TPU v7x, 32 devices: a whole 2x2x4 slice. The times are simulated.
32 devices in a mesh: dp: 4 (over y, core), row: 2 (over x), col: 4 (over z).
Axes of the slice: x: 2, y: 2, z: 4, core: 2. Of those that a mesh axis runs over, the one named last changes fastest.
Arguments:
- tokens: bfloat16 [16, 1024, 2048], P('dp', 'row', 'col'), may hold values from -6 to 6
- cotangent: bfloat16 [16, 1024, 2048], P('dp', 'row', 'col'), may hold values from -6 to 6
- lengths: int32 [16], replicated, may hold values from 512 to 1024, as said below
- deal_order: int32 [16], replicated, may hold values from 0 to 15, as said below
- gain_attn: bfloat16 [2048], replicated, may hold values from 0.25 to 1.75
- gain_ffn: bfloat16 [2048], replicated, may hold values from 0.25 to 1.75
- w_query: bfloat16 [2048, 2048], P('row', 'col'), may hold values from -0.4375 to 0.4375
- key_value_weight: bfloat16 [2048, 2, 512], P('row', None, 'col'), may hold values from -0.4375 to 0.4375
- w_out: bfloat16 [2048, 2048], P('row', 'col'), may hold values from -1.25 to 1.25
- w_gate_up: bfloat16 [2048, 2, 8192], P('row', None, 'col'), may hold values from -0.125 to 0.125
- w_down: bfloat16 [2048, 8192], P('row', 'col'), may hold values from -0.25 to 0.25
Outputs:
- layer_out: float32 [16, 1024, 2048], P('dp', 'row', 'col')
- input_grad: float32 [16, 1024, 2048], P('dp', 'row', 'col')
- grad_query: float32 [2048, 2048], P(('dp', 'row'), 'col')
- grad_kv: float32 [2048, 2, 512], P(('dp', 'row'), None, 'col')
- grad_out: float32 [2048, 2048], P(('dp', 'row'), 'col')
- grad_gate_up: float32 [2048, 2, 8192], P(('dp', 'row'), None, 'col')
- grad_down: float32 [2048, 8192], P(('dp', 'row'), 'col')
- grad_gain_attn: float32 [2048], replicated
- grad_gain_ffn: float32 [2048], replicated
Inputs may be any that keep to these rules, and one draw needn't show every extreme that they name: `lengths`: among the 4 sequences that deal_order gives each data group, at least one has length exactly 1024. `deal_order`: A permutation of the sequence numbers.
All inputs are finite; a program needn't handle non-finite values.
Results may differ from a plain program's by a relative error of at most 0.018.
Values may be sent and summed in bfloat16 or wider, within the bound.
A program may use at most 256 MiB of HBM per device.

v0:
```python
import jax
import jax.numpy as jnp
from jax import lax
from jax.sharding import PartitionSpec as P

HEAD_SIZE = 64


EPSILON = 1e-05
THETA = 10000000.0
ATTN_MULT = 0.015625
RES_MULT = 0.22
MASKED = -1e30


def rope_tables(positions, head_size):
    halves = jnp.arange(head_size // 2, dtype=jnp.float32)
    inverse_freq = THETA ** (-(halves * 2.0) / head_size)
    angles = positions.astype(jnp.float32)[:, None] * inverse_freq[None, :]
    return (jnp.cos(angles), jnp.sin(angles))


def rotary_embed(value_rows, cosine_table, sine_table):
    middle = value_rows.shape[-1] // 2
    first_half = value_rows[..., :middle]
    second_half = value_rows[..., middle:]
    cos_part = cosine_table[:, None, :]
    sin_part = sine_table[:, None, :]
    return jnp.concatenate(
        [
            first_half * cos_part - second_half * sin_part,
            second_half * cos_part + first_half * sin_part,
        ],
        axis=-1,
    )


def widen_cols(value_rows):
    return lax.all_gather(value_rows, "col", axis=1, tiled=True)


def narrow_cols(value_rows):
    return lax.psum_scatter(value_rows, "col", scatter_dimension=1, tiled=True)


def sum_over_cols(value_rows):
    return lax.psum(value_rows, "col")


def contract_local(operand, matrix):
    return lax.dot_general(
        operand, matrix, (((1,), (0,)), ((), ())), preferred_element_type=jnp.float32
    )


def expand_local(operand, matrix):
    trailing = tuple(range(1, operand.ndim))
    return lax.dot_general(
        operand, matrix, ((trailing, trailing), ((), ())), preferred_element_type=jnp.float32
    )


def token_outer(features, grads):
    return lax.dot_general(
        features, grads, (((0,), (0,)), ((), ())), preferred_element_type=jnp.float32
    )


def contract_rows(operand, matrix):
    return contract_local(operand, lax.all_gather(matrix, "row", axis=0, tiled=True))


def expand_rows(operand, matrix):
    return expand_local(operand, lax.all_gather(matrix, "row", axis=0, tiled=True))


def split_keys(key_seq, value_seq, key_pos):
    slot_len = key_seq.shape[0]
    width = min(512, slot_len)
    count = slot_len // width
    return (
        key_seq.reshape(count, width, key_seq.shape[1], key_seq.shape[2]),
        value_seq.reshape(count, width, value_seq.shape[1], value_seq.shape[2]),
        key_pos.reshape(count, width),
    )


def block_scores(query_seq, key_block, pos_block, query_pos, length):
    scores = (
        jnp.einsum("qkgd,tkd->kgqt", query_seq, key_block, preferred_element_type=jnp.float32)
        * ATTN_MULT
    )
    allowed = (pos_block[None, :] <= query_pos[:, None]) & (pos_block[None, :] < length)
    return jnp.where(allowed, scores, MASKED)


def attend(inputs, key_pos, query_pos):
    query_seq, key_seq, value_seq, length = inputs
    key_blocks, value_blocks, pos_blocks = split_keys(key_seq, value_seq, key_pos)
    stat_shape = (query_seq.shape[1], query_seq.shape[2], query_seq.shape[0], 1)

    def gather_stats(carry, entry):
        running_max, running_sum = carry
        key_block, pos_block = entry
        scores = block_scores(query_seq, key_block, pos_block, query_pos, length)
        new_max = jnp.maximum(running_max, jnp.max(scores, axis=-1, keepdims=True))
        new_sum = running_sum * jnp.exp(running_max - new_max) + jnp.sum(
            jnp.exp(scores - new_max), axis=-1, keepdims=True
        )
        return ((new_max, new_sum), None)

    start_stats = (jnp.full(stat_shape, MASKED, jnp.float32), jnp.zeros(stat_shape, jnp.float32))
    (row_max, row_sums), unused = lax.scan(gather_stats, start_stats, (key_blocks, pos_blocks))

    def mix_values(running, entry):
        key_block, value_block, pos_block = entry
        scores = block_scores(query_seq, key_block, pos_block, query_pos, length)
        weights = jnp.exp(scores - row_max) / row_sums
        return (
            running
            + jnp.einsum(
                "kgqt,tkd->qkgd",
                weights.astype(jnp.bfloat16),
                value_block,
                preferred_element_type=jnp.float32,
            ),
            None,
        )

    start_mix = jnp.zeros(query_seq.shape, jnp.float32)
    mixed_heads, unused = lax.scan(mix_values, start_mix, (key_blocks, value_blocks, pos_blocks))
    return (mixed_heads, row_max, row_sums)


def attend_back(inputs, key_pos, query_pos):
    query_seq, key_seq, value_seq, grad_mixed, row_max, row_sums, length = inputs
    key_blocks, value_blocks, pos_blocks = split_keys(key_seq, value_seq, key_pos)

    def block_weights(key_block, value_block, pos_block):
        scores = block_scores(query_seq, key_block, pos_block, query_pos, length)
        weights = jnp.exp(scores - row_max) / row_sums
        grad_weights = jnp.einsum(
            "qkgd,tkd->kgqt", grad_mixed, value_block, preferred_element_type=jnp.float32
        )
        return (weights, grad_weights)

    def gather_centre(running, entry):
        weights, grad_weights = block_weights(*entry)
        return (running + jnp.sum(weights * grad_weights, axis=-1, keepdims=True), None)

    start_centre = jnp.zeros(row_max.shape, jnp.float32)
    centre, unused = lax.scan(gather_centre, start_centre, (key_blocks, value_blocks, pos_blocks))

    def grads_block(running, entry):
        key_block = entry[0]
        weights, grad_weights = block_weights(*entry)
        grad_scores = (weights * (grad_weights - centre)).astype(jnp.bfloat16)
        grad_query = (
            running
            + jnp.einsum(
                "kgqt,tkd->qkgd", grad_scores, key_block, preferred_element_type=jnp.float32
            )
            * ATTN_MULT
        )
        grad_key = (
            jnp.einsum("kgqt,qkgd->tkd", grad_scores, query_seq, preferred_element_type=jnp.float32)
            * ATTN_MULT
        )
        grad_value = jnp.einsum(
            "kgqt,qkgd->tkd",
            weights.astype(jnp.bfloat16),
            grad_mixed,
            preferred_element_type=jnp.float32,
        )
        return (grad_query, (grad_key, grad_value))

    start_query = jnp.zeros(query_seq.shape, jnp.float32)
    grad_query, (grad_key, grad_value) = lax.scan(
        grads_block, start_query, (key_blocks, value_blocks, pos_blocks)
    )
    return (grad_query, grad_key.reshape(key_seq.shape), grad_value.reshape(value_seq.shape))


def body(
    tokens,
    cotangent,
    lengths,
    deal_order,
    gain_attn,
    gain_ffn,
    w_query,
    key_value_weight,
    w_out,
    w_gate_up,
    w_down,
):
    seq_group, rows_local, width_local = tokens.shape
    row_count = lax.axis_size("row")
    col_count = lax.axis_size("col")
    full_width = width_local * col_count
    slot_len = rows_local * row_count
    total_rows = seq_group * rows_local
    head_size = HEAD_SIZE
    query_width = w_query.shape[1]
    kv_width = key_value_weight.shape[2]
    kv_heads = kv_width // head_size
    group_size = query_width // kv_width
    group_index = lax.axis_index("dp")
    row_index = lax.axis_index("row")
    col_index = lax.axis_index("col")
    matrices = {
        "qkv": jnp.concatenate(
            [w_query, key_value_weight.reshape(key_value_weight.shape[0], 2 * kv_width)], axis=1
        ),
        "out": w_out,
        "gate_up": w_gate_up,
        "down": w_down,
    }

    def contract_with(operand, which_one):
        return contract_rows(operand, matrices[which_one])

    def expand_with(operand, which_one):
        return expand_rows(operand, matrices[which_one])

    everyone = lax.all_gather(tokens, "dp", axis=0, tiled=True)
    my_ids = lax.dynamic_slice_in_dim(deal_order, group_index * seq_group, seq_group)
    own_rows = jnp.take(everyone, my_ids, axis=0)
    seq_lens = jnp.take(lengths, my_ids)
    local_pos = row_index * rows_local + jnp.arange(rows_local, dtype=jnp.int32)
    key_pos = jnp.arange(slot_len, dtype=jnp.int32)
    live_rows = (local_pos[None, :] < seq_lens[:, None]).astype(jnp.float32).reshape(total_rows, 1)
    cosine_table, sine_table = rope_tables(jnp.tile(local_pos, seq_group), head_size)
    own_tokens = own_rows.reshape(total_rows, width_local)
    wide_float = widen_cols(own_tokens).astype(jnp.float32)
    scale_one = lax.rsqrt(jnp.mean(wide_float * wide_float, axis=1, keepdims=True) + EPSILON)
    gain_one = gain_attn.astype(jnp.float32)
    first_normed = wide_float * scale_one
    attn_input = (first_normed * gain_one).astype(jnp.bfloat16)
    projected = contract_with(attn_input, "qkv")
    query_lin = projected[:, :query_width].reshape(total_rows, query_width // head_size, head_size)
    key_lin = projected[:, query_width : query_width + kv_width].reshape(
        total_rows, kv_heads, head_size
    )
    value_lin = projected[:, query_width + kv_width :]
    query_rows = rotary_embed(query_lin, cosine_table, sine_table).astype(jnp.bfloat16)
    keys_own = (
        rotary_embed(key_lin, cosine_table, sine_table)
        .astype(jnp.bfloat16)
        .reshape(seq_group, rows_local, kv_width)
    )
    values_own = value_lin.astype(jnp.bfloat16).reshape(seq_group, rows_local, kv_width)
    all_keys, all_values = (
        lax.all_gather(keys_own, "row", axis=1, tiled=True),
        lax.all_gather(values_own, "row", axis=1, tiled=True),
    )
    query_split = query_rows.reshape(seq_group, rows_local, kv_heads, group_size, head_size)
    key_split = all_keys.reshape(seq_group, slot_len, kv_heads, head_size)
    value_split = all_values.reshape(seq_group, slot_len, kv_heads, head_size)

    def forward_seq(inputs):
        return attend(inputs, key_pos, local_pos)

    mixed_heads, row_max, row_sums = lax.map(
        forward_seq, (query_split, key_split, value_split, seq_lens)
    )
    heads_out = mixed_heads.reshape(total_rows, query_width).astype(jnp.bfloat16)
    attn_local = narrow_cols(expand_with(heads_out, "out"))
    resid = own_tokens.astype(jnp.float32) + RES_MULT * attn_local
    gain_two = lax.dynamic_slice_in_dim(
        gain_ffn.astype(jnp.float32), col_index * width_local, width_local
    )
    scale_two = lax.rsqrt(sum_over_cols(jnp.sum(resid * resid, axis=1)) / full_width + EPSILON)[
        :, None
    ]
    normed_two = resid * scale_two
    ffn_input = widen_cols((normed_two * gain_two).astype(jnp.bfloat16))
    gate_up = contract_with(ffn_input, "gate_up")
    gate = gate_up[:, 0]
    upward = gate_up[:, 1]
    sigmoid_gate = jax.nn.sigmoid(gate)
    silu_gate = gate * sigmoid_gate
    hidden = (silu_gate * upward).astype(jnp.bfloat16)
    ffn_local = narrow_cols(expand_with(hidden, "down"))
    layer_out = live_rows * (resid + RES_MULT * ffn_local)
    grad_rows = live_rows * cotangent.reshape(total_rows, width_local).astype(jnp.float32)
    grad_ffn = widen_cols((RES_MULT * grad_rows).astype(jnp.bfloat16))
    grad_hidden = contract_with(grad_ffn, "down")
    grad_down = token_outer(grad_ffn, hidden)
    slope = sigmoid_gate * (1.0 + gate * (1.0 - sigmoid_gate))
    grad_gate_rows = jnp.stack(
        [grad_hidden * upward * slope, grad_hidden * silu_gate], axis=1
    ).astype(jnp.bfloat16)
    grad_gate_up = token_outer(ffn_input, grad_gate_rows)
    grad_normed_two = narrow_cols(expand_with(grad_gate_rows, "gate_up"))
    weighted_two = grad_normed_two * gain_two
    inner_two = sum_over_cols(jnp.sum(weighted_two * resid, axis=1))[:, None]
    grad_resid = (
        grad_rows + scale_two * weighted_two - resid * scale_two**3 * inner_two / full_width
    )
    gain_two_part = jnp.sum(grad_normed_two * normed_two, axis=0)
    grad_attn = widen_cols((RES_MULT * grad_resid).astype(jnp.bfloat16))
    grad_heads = contract_with(grad_attn, "out").astype(jnp.bfloat16)
    grad_out = token_outer(grad_attn, heads_out)
    grad_split = grad_heads.reshape(seq_group, rows_local, kv_heads, group_size, head_size)

    def backward_seq(inputs):
        return attend_back(inputs, key_pos, local_pos)

    grad_query, grad_key, grad_value = lax.map(
        backward_seq, (query_split, key_split, value_split, grad_split, row_max, row_sums, seq_lens)
    )
    key_part, value_part = (
        lax.psum_scatter(
            grad_key.reshape(seq_group, slot_len, kv_width).astype(jnp.bfloat16),
            "row",
            scatter_dimension=1,
            tiled=True,
        ).astype(jnp.float32),
        lax.psum_scatter(
            grad_value.reshape(seq_group, slot_len, kv_width).astype(jnp.bfloat16),
            "row",
            scatter_dimension=1,
            tiled=True,
        ).astype(jnp.float32),
    )
    query_back = rotary_embed(
        grad_query.reshape(total_rows, query_width // head_size, head_size),
        cosine_table,
        -sine_table,
    ).reshape(total_rows, query_width)
    key_back = rotary_embed(
        key_part.reshape(total_rows, kv_heads, head_size), cosine_table, -sine_table
    ).reshape(total_rows, kv_width)
    grad_projected = jnp.concatenate(
        [query_back, key_back, value_part.reshape(total_rows, kv_width)], axis=1
    ).astype(jnp.bfloat16)
    grad_qkv = token_outer(attn_input, grad_projected)
    grad_normed_one = expand_with(grad_projected, "qkv")
    weighted_one = grad_normed_one * gain_one
    inner_one = jnp.sum(weighted_one * wide_float, axis=1, keepdims=True)
    input_part = scale_one * weighted_one - wide_float * scale_one**3 * inner_one / full_width
    input_grad = grad_resid + narrow_cols(input_part)
    gain_one_part = jnp.sum(grad_normed_one * first_normed, axis=0)
    gain_two_full = lax.dynamic_update_slice_in_dim(
        jnp.zeros((full_width,), jnp.float32), gain_two_part, col_index * width_local, 0
    )
    grad_gain_attn, grad_gain_ffn = lax.psum((gain_one_part, gain_two_full), ("dp", "row", "col"))
    sums_qkv, sums_out, sums_gate_up, sums_down = (
        lax.psum_scatter(
            grad_qkv.astype(jnp.bfloat16), ("dp", "row"), scatter_dimension=0, tiled=True
        ).astype(jnp.float32),
        lax.psum_scatter(
            grad_out.astype(jnp.bfloat16), ("dp", "row"), scatter_dimension=0, tiled=True
        ).astype(jnp.float32),
        lax.psum_scatter(
            grad_gate_up.astype(jnp.bfloat16), ("dp", "row"), scatter_dimension=0, tiled=True
        ).astype(jnp.float32),
        lax.psum_scatter(
            grad_down.astype(jnp.bfloat16), ("dp", "row"), scatter_dimension=0, tiled=True
        ).astype(jnp.float32),
    )
    out_query = sums_qkv[:, :query_width]
    out_kv = sums_qkv[:, query_width:].reshape(sums_qkv.shape[0], 2, kv_width)
    slots = jnp.arange(deal_order.shape[0], dtype=jnp.int32)
    inverse = jnp.sum(jnp.where(deal_order[None, :] == slots[:, None], slots[None, :], 0), axis=1)
    own_slots = lax.dynamic_slice_in_dim(inverse, group_index * seq_group, seq_group)
    every_out, every_grad = (
        lax.all_gather(
            layer_out.reshape(seq_group, rows_local, width_local).astype(jnp.bfloat16),
            "dp",
            axis=0,
            tiled=True,
        ).astype(jnp.float32),
        lax.all_gather(
            input_grad.reshape(seq_group, rows_local, width_local).astype(jnp.bfloat16),
            "dp",
            axis=0,
            tiled=True,
        ).astype(jnp.float32),
    )
    return (
        jnp.take(every_out, own_slots, axis=0),
        jnp.take(every_grad, own_slots, axis=0),
        out_query,
        out_kv,
        sums_out,
        sums_gate_up,
        sums_down,
        grad_gain_attn,
        grad_gain_ffn,
    )


def solution(mesh):
    placed = (
        P("dp", "row", "col"),
        P("dp", "row", "col"),
        P(),
        P(),
        P(),
        P(),
        P("row", "col"),
        P("row", None, "col"),
        P("row", "col"),
        P("row", None, "col"),
        P("row", "col"),
    )
    return jax.shard_map(
        body,
        mesh=mesh,
        in_specs=placed,
        out_specs=(
            P("dp", "row", "col"),
            P("dp", "row", "col"),
            P(("dp", "row"), "col"),
            P(("dp", "row"), None, "col"),
            P(("dp", "row"), "col"),
            P(("dp", "row"), None, "col"),
            P(("dp", "row"), "col"),
            P(),
            P(),
        ),
        check_vma=False,
    )
```

profile of v0, /device:TPU:0, one launch (start us, length us, event | category | flops | bytes accessed | tf_op | source)
XLA Modules:
  0.0 3310.9 jit_solution(13840233308920651617)
XLA Ops:
  8.9 61.7 %all-gather.14.cloned.1.call-done = bf16[16,512,512]{2,1,0:T(8,128)(2,1)} async-done(((bf16[4,512,512]{2,1,0:T(8,128)(2,1)}), bf16[16,512,512]{2,1,0:T(8,128)(2,1)}) %all-gather.14.cloned.1.call-update) | async-done | bytes 8388624 | tf_op jit(solution)/shard_map/all_gather | solution.py:226
  81.6 144.9 %all-gather.16.cloned.1.call-done = bf16[2048,2048]{1,0:T(8,128)(2,1)} async-done(((bf16[2048,512]{1,0:T(8,128)(2,1)}), bf16[2048,2048]{1,0:T(8,128)(2,1)}) %all-gather.16.cloned.1.call-update) | async-done | bytes 8388624 | tf_op jit(solution)/shard_map/all_gather | solution.py:39
  232.2 39.6 %all-gather.18.cloned.1.call-done = bf16[2048,768]{1,0:T(8,128)(2,1)} async-done(((bf16[1024,768]{1,0:T(8,128)(2,1)}), bf16[2048,768]{1,0:T(8,128)(2,1)}) %all-gather.18.cloned.1.call-update) | async-done | bytes 3145744 | tf_op jit(solution)/shard_map/all_gather | solution.py:70
  309.4 21.8 all-gather.22.cloned.1.call-done
  331.2 139.5 %while.92 = (s32[]{:T(128)}, bf16[4,512,2,4,64]{1,4,3,2,0:T(8,128)(2,1)}, f32[4,2,4,512,1]{3,2,1,4,0:T(4,128)}, f32[4,2,4,512,1]{3,2,1,4,0:T(4,128)}, bf16[4,102...) while((s32[]{:T(128)}, ...), condition=%wide.region_8.9_spmd.clone.clone, body=%wide.region_1.8_spmd.clone.clone.sunk | while | flops 832069120 | bytes 28256876 | solution.py:264
  333.2 22.3 while.96
  497.2 268.8 %reduce-scatter.11.cloned.1.call-done = f32[2048,512]{1,0:T(8,128)} async-done(((f32[2048,2048]{1,0:T(8,128)}), f32[2048,512]{1,0:T(8,128)}) %reduce-scatter.11.cloned.1.call-update) | async-done | bytes 4194320 | tf_op jit(solution)/shard_map/reduce_scatter | solution.py:43
  790.9 176.4 %all-gather.28.cloned.1.call-done = bf16[2048,2,2048]{2,0,1:T(8,128)(2,1)} async-done(((bf16[1024,2,2048]{2,0,1:T(8,128)(2,1)}), bf16[2048,2,2048]{2,0,1:T(8,128)(2,1)}) %all-gather.28.cloned.1.call-update) | async-done | bytes 16777232 | tf_op jit(solution)/shard_map/all_gather | solution.py:70
  967.3 151.9 %all-gather.26.cloned.1.call-done = bf16[2048,2048]{1,0:T(8,128)(2,1)} async-done(((bf16[2048,512]{1,0:T(8,128)(2,1)}), bf16[2048,2048]{1,0:T(8,128)(2,1)}) %all-gather.26.cloned.1.call-update) | async-done | bytes 8388624 | tf_op jit(solution)/shard_map/all_gather | solution.py:39
  1119.2 43.7 %fusion.92 = f32[2048,2,2048]{2,0,1:T(8,128)} fusion(bf16[2048,2,2048]{2,0,1:T(8,128)(2,1)} %all-gather.28.cloned.1.call-done, bf16[2048,2048]{1,0:T(8,128)(2,1)} %all-gather.26.cloned.1.call-done), kind=kOutput, calls=%fused_computation.133 | convolution fusion | flops 34359738368 | bytes 58720256 | tf_op jit(solution)/shard_map/dot_general | solution.py:51
  1162.9 60.0 %all-gather.30.cloned.1.call-done = bf16[2048,2048]{1,0:T(8,128)(2,1)} async-done(((bf16[1024,2048]{1,0:T(8,128)(2,1)}), bf16[2048,2048]{1,0:T(8,128)(2,1)}) %all-gather.30.cloned.1.call-update) | async-done | bytes 8388624 | tf_op jit(solution)/shard_map/all_gather | solution.py:74
  1222.9 151.9 %all-gather.34.cloned.1.call-done = bf16[2048,2048]{1,0:T(8,128)(2,1)} async-done(((bf16[2048,512]{1,0:T(8,128)(2,1)}), bf16[2048,2048]{1,0:T(8,128)(2,1)}) %all-gather.34.cloned.1.call-update) | async-done | bytes 8388624 | tf_op jit(solution)/shard_map/all_gather | solution.py:39
  1374.8 34.2 %fusion.94 = (bf16[2048,1,2048]{2,0,1:T(8,128)(2,1)}, bf16[2048,1,2048]{2,0,1:T(8,128)(2,1)}, bf16[2048,2048]{1,0:T(8,128)(2,1)}) fusion(f32[2048,2,2048]{2,0,1:T(8,128)} %fusion.92, bf16[2048,2048]{1,0:T(8,128)(2,1)} %all-gather.34.cloned.1.call-done, bf16[2048,2048]{1,0:T(8,128)(2,1)} %all-gather.30.cloned.1.call-done), kind=kOutput, calls=%fused_computation.135 | convolution fusion | flops 17242783744 | bytes 75497472 | tf_op jit(solution)/shard_map/dot_general | solution.py:51
  1409.0 45.0 %fusion.89 = f32[2048,2048]{1,0:T(8,128)} fusion(bf16[2048,2,2048]{2,0,1:T(8,128)(2,1)} %all-gather.28.cloned.1.call-done, bf16[2048,1,2048]{2,0,1:T(8,128)(2,1)} %get-tuple-element.1243, bf16[2048,1,2048]{2,0,1:T(8,128)(2,1)} %get-tuple-element.1242), kind=kOutput, calls=%fused_computation.130 | convolution fusion | flops 34368126976 | bytes 50331648 | tf_op jit(solution)/shard_map/dot_general | solution.py:58
  1454.1 24.9 fusion.111
  1479.1 253.6 %reduce-scatter.15.cloned.1.call-done = f32[2048,512]{1,0:T(8,128)} async-done(((f32[2048,2048]{1,0:T(8,128)}), f32[2048,512]{1,0:T(8,128)}) %reduce-scatter.15.cloned.1.call-update) | async-done | bytes 4194320 | tf_op jit(solution)/shard_map/reduce_scatter | solution.py:43
  1748.9 267.4 %reduce-scatter.13.cloned.1.call-done = f32[2048,512]{1,0:T(8,128)} async-done(((f32[2048,2048]{1,0:T(8,128)}), f32[2048,512]{1,0:T(8,128)}) %reduce-scatter.13.cloned.1.call-update) | async-done | bytes 4194320 | tf_op jit(solution)/shard_map/reduce_scatter | solution.py:43
  2024.1 150.5 %all-gather.36.cloned.1.call-done = bf16[2048,2048]{1,0:T(8,128)(2,1)} async-done(((bf16[2048,512]{1,0:T(8,128)(2,1)}), bf16[2048,2048]{1,0:T(8,128)(2,1)}) %all-gather.36.cloned.1.call-update) | async-done | bytes 8388624 | tf_op jit(solution)/shard_map/all_gather | solution.py:39
  2193.7 317.4 %while.95 = (s32[]{:T(128)}, f32[4,512,2,4,64]{1,0,4,3,2:T(4,128)}, bf16[4,1024,2,64]{1,3,2,0:T(8,128)(2,1)}, bf16[4,1024,2,64]{1,3,2,0:T(8,128)(2,1)}, bf16[4,1...) while((s32[]{:T(128)}, f32[4,512,2,4,64]{1,0,4,3,2:T(4,128)}, ...), condition=%wide.region_23.25_spmd.clone.clone, body=%wide.region_17.24_spmd.clone.clone.sunk | while | flops 1910316544 | bytes 125183912 | solution.py:310
  2209.0 39.0 %while.99 = (s32[]{:T(128)}, f32[512,2,4,64]{0,3,2,1:T(8,128)S(1)}, bf16[2,512,2,64]{1,3,2,0:T(8,128)(2,1)S(1)}, bf16[2,512,2,64]{1,3,2,0:T(8,128)(2,1)S(1)}, bf...) while((s32[]{:T(128)}, f32[512,2,4,64]{0,3,2,1:T(8,128)S(1)}, ...), condition=%wide.region_22.23_spmd.clone, body=%wide.region_21.22_spmd.clone.sunk | while | flops 1360331264 | bytes 93775096 | solution.py:178
  2288.3 39.0 %while.99 = (s32[]{:T(128)}, f32[512,2,4,64]{0,3,2,1:T(8,128)S(1)}, bf16[2,512,2,64]{1,3,2,0:T(8,128)(2,1)S(1)}, bf16[2,512,2,64]{1,3,2,0:T(8,128)(2,1)S(1)}, bf...) while((s32[]{:T(128)}, f32[512,2,4,64]{0,3,2,1:T(8,128)S(1)}, ...), condition=%wide.region_22.23_spmd.clone, body=%wide.region_21.22_spmd.clone.sunk | while | flops 1360331264 | bytes 93775096 | solution.py:178
  2367.6 39.0 %while.99 = (s32[]{:T(128)}, f32[512,2,4,64]{0,3,2,1:T(8,128)S(1)}, bf16[2,512,2,64]{1,3,2,0:T(8,128)(2,1)S(1)}, bf16[2,512,2,64]{1,3,2,0:T(8,128)(2,1)S(1)}, bf...) while((s32[]{:T(128)}, f32[512,2,4,64]{0,3,2,1:T(8,128)S(1)}, ...), condition=%wide.region_22.23_spmd.clone, body=%wide.region_21.22_spmd.clone.sunk | while | flops 1360331264 | bytes 93775096 | solution.py:178
  2446.9 39.0 %while.99 = (s32[]{:T(128)}, f32[512,2,4,64]{0,3,2,1:T(8,128)S(1)}, bf16[2,512,2,64]{1,3,2,0:T(8,128)(2,1)S(1)}, bf16[2,512,2,64]{1,3,2,0:T(8,128)(2,1)S(1)}, bf...) while((s32[]{:T(128)}, f32[512,2,4,64]{0,3,2,1:T(8,128)S(1)}, ...), condition=%wide.region_22.23_spmd.clone, body=%wide.region_21.22_spmd.clone.sunk | while | flops 1360331264 | bytes 93775096 | solution.py:178
  2584.7 24.2 convolution_convert_fusion
  2608.9 42.3 %fusion.88 = bf16[2048,2,2048]{2,0,1:T(8,128)(2,1)} fusion(bf16[2048,1,2048]{2,0,1:T(8,128)(2,1)} %get-tuple-element.1243, bf16[2048,1,2048]{2,0,1:T(8,128)(2,1)} %get-tuple-element.1242, bf16[2048,2048]{1,0:T(8,128)(2,1)} %all-gather.26.cloned.1.call-done), kind=kOutput, calls=%fused_computation.129 | convolution fusion | flops 34401681408 | bytes 41943040 | tf_op jit(solution)/shard_map/dot_general | solution.py:64
  2676.3 188.8 %reduce-scatter.21.cloned.1.call-done = f32[2048,512]{1,0:T(8,128)} async-done(((f32[2048,2048]{1,0:T(8,128)}), f32[2048,512]{1,0:T(8,128)}) %reduce-scatter.21.cloned.1.call-update) | async-done | bytes 4194320 | tf_op jit(solution)/shard_map/reduce_scatter | solution.py:43
  2870.8 69.6 %reduce-scatter.29.cloned.1.call-done = bf16[256,2048]{1,0:T(8,128)(2,1)} async-done(((bf16[2048,2048]{1,0:T(8,128)(2,1)}), bf16[256,2048]{1,0:T(8,128)(2,1)}) %reduce-scatter.29.cloned.1.call-update) | async-done | bytes 1048592 | tf_op jit(solution)/shard_map/reduce_scatter | solution.py:359
  2943.2 117.2 %reduce-scatter.27.cloned.1.call-done = bf16[256,2,2048]{2,0,1:T(8,128)(2,1)} async-done(((bf16[2048,2,2048]{2,0,1:T(8,128)(2,1)}), bf16[256,2,2048]{2,0,1:T(8,128)(2,1)}) %reduce-scatter.27.cloned.1.call-update) | async-done | bytes 2097168 | tf_op jit(solution)/shard_map/reduce_scatter | solution.py:356
  3066.4 53.8 %all-gather.32.cloned.1.call-done = bf16[16,512,512]{2,1,0:T(8,128)(2,1)} async-done(((bf16[4,512,512]{2,1,0:T(8,128)(2,1)}), bf16[16,512,512]{2,1,0:T(8,128)(2,1)}) %all-gather.32.cloned.1.call-update) | async-done | bytes 8388624 | tf_op jit(solution)/shard_map/all_gather | solution.py:369
  3141.2 39.5 %all-reduce = (f32[2048]{0:T(1024)}, f32[2048]{0:T(1024)}) all-reduce(f32[2048]{0:T(1024)S(1)} %get-tuple-element.1082, f32[2048]{0:T(1024)S(1)} %dynamic_update_slice.31), channel_id=1, replica_groups=mesh['dp'=4,'row'=2,'col'=4] {'dp','row','col'}, use_global_device_ids=true, to_apply=%region_33.35 | all-reduce | flops 4096 | bytes 32768 | tf_op jit(solution)/shard_map/psum | solution.py:348
  3182.6 33.1 reduce-scatter.23.cloned.1.call-done
  3219.2 56.4 %all-gather.38.cloned.1.call-done = bf16[16,512,512]{2,1,0:T(8,128)(2,1)} async-done(((bf16[4,512,512]{2,1,0:T(8,128)(2,1)}), bf16[16,512,512]{2,1,0:T(8,128)(2,1)}) %all-gather.38.cloned.1.call-update) | async-done | bytes 8388624 | tf_op jit(solution)/shard_map/all_gather | solution.py:375
  (590 shorter events, 914.1 us)
Async XLA Ops:
  7.2 282.4 %copy-start = (s32[16]{0:T(128)S(1)}, s32[16]{0:T(128)}, u32[]{:S(2)}) copy-start(s32[16]{0:T(128)} %param.27) | copy-start | bytes 196
  7.2 63.4 %all-gather.14.cloned.1.call-start = ((), (), s32[]{:S(2)}) async-start(), calls=%async_computation.10 | async-start | bytes 10485760 | tf_op jit(solution)/shard_map/all_gather | solution.py:226
  7.9 218.6 %all-gather.16.cloned.1.call-start = ((), (), s32[]{:S(2)}) async-start(), calls=%async_computation.11 | async-start | bytes 10485760 | tf_op jit(solution)/shard_map/all_gather | solution.py:39
  76.7 195.1 %all-gather.18.cloned.1.call-start = ((), (), s32[]{:S(2)}) async-start(), calls=%async_computation.12 | async-start | bytes 4718592 | tf_op jit(solution)/shard_map/all_gather | solution.py:70
  79.2 228.7 %all-gather.20.cloned.1.call-start = ((), (), s32[]{:S(2)}) async-start(), calls=%async_computation.13 | async-start | bytes 1572864 | tf_op jit(solution)/shard_map/all_gather | solution.py:254
  286.5 44.7 %all-gather.22.cloned.1.call-start = ((), (), s32[]{:S(2)}) async-start(), calls=%async_computation.14 | async-start | bytes 1572864 | tf_op jit(solution)/shard_map/all_gather | solution.py:255
  288.7 186.3 %all-gather.24.cloned.1.call-start = ((), (), s32[]{:S(2)}) async-start(), calls=%async_computation.15 | async-start | bytes 3145728 | tf_op jit(solution)/shard_map/all_gather | solution.py:74
  289.2 476.8 %reduce-scatter.11.cloned.1.call-start = ((), (), s32[]{:S(2)}) async-start(), calls=%async_computation.16 | async-start | bytes 20971520 | tf_op jit(solution)/shard_map/reduce_scatter | solution.py:43
  470.7 317.6 %copy-start.34 = (s32[4]{0:T(128)}, s32[4]{0:T(128)S(1)}, u32[]{:S(2)}) copy-start(s32[4]{0:T(128)S(1)} %get-tuple-element.2147) | copy-start | bytes 52
  485.5 481.7 %all-gather.28.cloned.1.call-start = ((), (), s32[]{:S(2)}) async-start(), calls=%async_computation.18 | async-start | bytes 25165824 | tf_op jit(solution)/shard_map/all_gather | solution.py:70
  496.2 269.8 %copy-start.5 = (bf16[4,512,512]{2,1,0:T(8,128)(2,1)S(1)}, bf16[4,512,512]{2,1,0:T(8,128)(2,1)}, u32[]{:S(2)}) copy-start(bf16[4,512,512]{2,1,0:T(8,128)(2,1)} %copy-done.4) | copy-start | bytes 6291460
  496.2 269.8 %copy-start.29 = (pred[1,4,4,128]{3,1,2,0:T(4,128)(4,1)S(1)}, pred[1,4,4,128]{3,1,2,0:T(4,128)(4,1)}, u32[]{:S(2)}) copy-start(pred[1,4,4,128]{3,1,2,0:T(4,128)(4,1)} %copy-done.28) | copy-start | bytes 6148
  496.3 622.9 %all-gather.26.cloned.1.call-start = ((), (), s32[]{:S(2)}) async-start(), calls=%async_computation.17 | async-start | bytes 10485760 | tf_op jit(solution)/shard_map/all_gather | solution.py:39
  497.2 290.4 %copy-start.26 = (f32[512]{0:T(512)}, f32[512]{0:T(512)S(1)}, u32[]{:S(2)}) copy-start(f32[512]{0:T(512)S(1)} %dynamic-slice_convert_fusion) | copy-start | bytes 6148
  787.6 435.3 %all-gather.30.cloned.1.call-start = ((), (), s32[]{:S(2)}) async-start(), calls=%async_computation.19 | async-start | bytes 12582912 | tf_op jit(solution)/shard_map/all_gather | solution.py:74
  788.2 586.6 %all-gather.34.cloned.1.call-start = ((), (), s32[]{:S(2)}) async-start(), calls=%async_computation.22 | async-start | bytes 10485760 | tf_op jit(solution)/shard_map/all_gather | solution.py:39
  790.9 941.8 %reduce-scatter.15.cloned.1.call-start = ((), (), s32[]{:S(2)}) async-start(), calls=%async_computation.23 | async-start | bytes 20971520 | tf_op jit(solution)/shard_map/reduce_scatter | solution.py:43
  1454.0 562.2 %reduce-scatter.13.cloned.1.call-start = ((), (), s32[]{:S(2)}) async-start(), calls=%async_computation.20 | async-start | bytes 20971520 | tf_op jit(solution)/shard_map/reduce_scatter | solution.py:43
  1479.0 253.7 %copy-start.27 = (f32[512]{0:T(512)S(1)}, f32[512]{0:T(512)}, u32[]{:S(2)}) copy-start(f32[512]{0:T(512)} %copy-done.26) | copy-start | bytes 6148
  1479.0 537.3 %copy-start.9 = (bf16[4,512,512]{2,1,0:T(8,128)(2,1)S(1)}, bf16[4,512,512]{2,1,0:T(8,128)(2,1)}, u32[]{:S(2)}) copy-start(bf16[4,512,512]{2,1,0:T(8,128)(2,1)} %param.26) | copy-start | bytes 6291460
  1479.0 537.3 %copy-start.19 = (f32[1,4,4,128]{3,1,2,0:T(4,128)S(1)}, f32[1,4,4,128]{3,1,2,0:T(4,128)}, u32[]{:S(2)}) copy-start(f32[1,4,4,128]{3,1,2,0:T(4,128)} %copy-done.18) | copy-start | bytes 24580
  1479.0 537.3 %copy-start.23 = (f32[2048]{0:T(1024)S(1)}, f32[2048]{0:T(1024)}, u32[]{:S(2)}) copy-start(f32[2048]{0:T(1024)} %get-tuple-element.1259) | copy-start | bytes 24580
  1479.0 695.6 %all-gather.36.cloned.1.call-start = ((), (), s32[]{:S(2)}) async-start(), calls=%async_computation.24 | async-start | bytes 10485760 | tf_op jit(solution)/shard_map/all_gather | solution.py:39
  2024.0 505.7 %reduce-scatter.17.cloned.1.call-start = ((), (), s32[]{:S(2)}) async-start(), calls=%async_computation.25 | async-start | bytes 1572864 | tf_op jit(solution)/shard_map/reduce_scatter | solution.py:314
  2511.1 41.1 %reduce-scatter.19.cloned.1.call-start = ((), (), s32[]{:S(2)}) async-start(), calls=%async_computation.26 | async-start | bytes 1572864 | tf_op jit(solution)/shard_map/reduce_scatter | solution.py:320
  2511.7 353.4 %reduce-scatter.21.cloned.1.call-start = ((), (), s32[]{:S(2)}) async-start(), calls=%async_computation.27 | async-start | bytes 20971520 | tf_op jit(solution)/shard_map/reduce_scatter | solution.py:43
  2584.6 355.8 %reduce-scatter.29.cloned.1.call-start = ((), (), s32[]{:S(2)}) async-start(), calls=%async_computation.32 | async-start | bytes 9437184 | tf_op jit(solution)/shard_map/reduce_scatter | solution.py:359
  2608.9 451.6 %reduce-scatter.27.cloned.1.call-start = ((), (), s32[]{:S(2)}) async-start(), calls=%async_computation.31 | async-start | bytes 18874368 | tf_op jit(solution)/shard_map/reduce_scatter | solution.py:356
  2651.2 469.0 %all-gather.32.cloned.1.call-start = ((), (), s32[]{:S(2)}) async-start(), calls=%async_computation.21 | async-start | bytes 10485760 | tf_op jit(solution)/shard_map/all_gather | solution.py:369
  2651.8 528.9 %reduce-scatter.25.cloned.1.call-start = ((), (), s32[]{:S(2)}) async-start(), calls=%async_computation.30 | async-start | bytes 2359296 | tf_op jit(solution)/shard_map/reduce_scatter | solution.py:353
  2662.4 553.3 %reduce-scatter.23.cloned.1.call-start = ((), (), s32[]{:S(2)}) async-start(), calls=%async_computation.29 | async-start | bytes 3538944 | tf_op jit(solution)/shard_map/reduce_scatter | solution.py:350
  2676.0 599.6 %all-gather.38.cloned.1.call-start = ((), (), s32[]{:S(2)}) async-start(), calls=%async_computation.28 | async-start | bytes 10485760 | tf_op jit(solution)/shard_map/all_gather | solution.py:375
  (48 other events, 1417.3 us)
Sparse Core Ops, SparseCore 0:
  9.6 60.9 all-gather.13
  76.8 149.6 all-gather.15
  228.6 43.1 all-gather.17
  286.6 21.2 all-gather.19
  309.9 21.2 all-gather.21
  332.6 33.1 all-gather.23
  485.7 280.3 reduce-scatter.10
  767.6 199.5 all-gather.27
  969.5 149.6 all-gather.25
  1120.6 102.1 all-gather.29
  1225.1 149.6 all-gather.33
  1454.1 278.4 reduce-scatter.14
  1735.0 281.1 reduce-scatter.12
  2024.1 150.4 all-gather.35
  2511.2 18.4 reduce-scatter.16
  2531.9 20.3 reduce-scatter.18
  2584.8 280.2 reduce-scatter.20
  2868.4 71.9 reduce-scatter.28
  2944.4 115.9 reduce-scatter.26
  3061.9 58.2 all-gather.31
  3123.8 41.5 reduce-scatter.24
  3169.4 46.2 reduce-scatter.22
  3217.3 58.2 all-gather.37
where the time goes:
time: 3320 us; the launch traced here: 3310 us
  waiting for transfers between devices  2310 us (70%)
  matrix products  506 us (15%)
  local copies, waits for them, and re-layouts  247 us (7%)
  other arithmetic  169 us (5%)
  blocking collectives  62.5 us (2%)
    reduce_scatter x4, waiting for transfers between devices, narrow_cols(): return lax.psum_scatter(value_rows, 'col', scatter_dimension=1, tiled=True)  979 us
    all_gather x4, waiting for transfers between devices, widen_cols(): return lax.all_gather(value_rows, 'col', axis=1, tiled=True)  599 us
    all_gather x2, waiting for transfers between devices, contract_rows(): lax.all_gather(matrix, 'row', axis=0, tiled=True)  216 us
    reduce_scatter x1, waiting for transfers between devices, body(): lax.psum_scatter(grad_gate_up.astype(jnp.bfloat16), ('dp', 'row'), scatte...  117 us
    dot_general x4, matrix products, expand_local(): lax.dot_general(operand, matrix, ((trailing, trailing), ((), ())), prefer...  97.5 us
    dot_general x4, matrix products, contract_local(): lax.dot_general(operand, matrix, (((1,), (0,)), ((), ())), preferred_elem...  96.8 us
    dynamic_update_slice x16, local copies, waits for them, and re-layouts, body(): lax.map(forward_seq, (query_split, key_split, value_split, seq_lens))  94.3 us
    dot_general x4, matrix products, token_outer(): lax.dot_general(features, grads, (((0,), (0,)), ((), ())), preferred_elem...  89.4 us
  transfers between devices with their start and end apart: 23, of which 21 were waited for; matrix products, arithmetic and copies ran while one was open for 12% of the time, Pallas kernels for 0%

commit v1 on v0

--- a/solution.py
+++ b/solution.py
@@ -1,6 +1,10 @@
+import functools
+
 import jax
 import jax.numpy as jnp
 from jax import lax
+from jax.experimental import pallas as pl
+from jax.experimental.pallas import tpu as pltpu
 from jax.sharding import PartitionSpec as P
 
 HEAD_SIZE = 64
@@ -181,7 +185,622 @@
     return (grad_query, grad_key.reshape(key_seq.shape), grad_value.reshape(value_seq.shape))
 
 
-def body(
+MESH_IDS = pl.DeviceIdType.MESH
+SIBLINGS = [(0, 1), (1, 0), (2, 3), (3, 2)]
+OVER_X = [(0, 1), (1, 0)]
+CROSSED = [((2 * y + c) * 2 + x, (2 * y + x) * 2 + c) for y in (0, 1) for c in (0, 1) for x in (0, 1)]
+SAME_CORE = [[0, 2], [1, 3]]
+
+
+def bring_cotangent(cotangent, deal_order, first):
+    everyone = lax.all_gather(cotangent, "dp", axis=0, tiled=True)
+    slots = jnp.arange(deal_order.shape[0], dtype=jnp.int32)
+    inverse = jnp.sum(jnp.where(deal_order[None, :] == slots[:, None], slots[None, :], 0), axis=1)
+    return jnp.concatenate(
+        [
+            lax.dynamic_slice_in_dim(
+                everyone, lax.dynamic_index_in_dim(inverse, first + at, keepdims=False), 1
+            )
+            for at in range(cotangent.shape[0])
+        ]
+    )
+
+
+def place():
+    group = lax.axis_index("dp")
+    core = lax.rem(group, 2)
+    row = lax.axis_index("row")
+    return group, core, group - core + row, row, lax.axis_index("col")
+
+
+def start_kernel(
+    cols, tok_ref, pq_ref, po_ref, x_ref, wq_ref, wo_ref, tok_sems, q_sems, o_sems, qx_sems, ox_sems, local_sems
+):
+    group, core, mate, row, col = place()
+    width = tok_ref.shape[2]
+    weight_rows = pq_ref.shape[0]
+
+    def line(step):
+        return lax.rem(col + step + cols, cols)
+
+    def start_at(block, size):
+        return pl.ds(pl.multiple_of(block * size, size), size)
+
+    barrier = pltpu.get_barrier_semaphore()
+
+    def greet(device):
+        pl.semaphore_signal(barrier, inc=1, device_id=device, device_id_type=MESH_IDS)
+
+    for step in range(1, cols):
+        greet((mate, core, line(step)))
+        greet((group, row, line(step)))
+    greet((group, 1 - row, col))
+
+    @pl.when(core != row)
+    def _():
+        greet((mate, core, col))
+
+    pl.semaphore_wait(barrier, 2 * cols - 1 + (core - row) * (core - row))
+
+    def remote(src, dst, sems, at, device):
+        return pltpu.make_async_remote_copy(
+            src_ref=src,
+            dst_ref=dst,
+            send_sem=sems.at[0, at],
+            recv_sem=sems.at[1, at],
+            device_id=device,
+            device_id_type=MESH_IDS,
+        )
+
+    def weight_copies(own, full, sems, x_sems):
+        wide = own.shape[1]
+
+        def block(of_row, of_col):
+            return full.at[start_at(of_row, weight_rows), start_at(of_col, wide)]
+
+        along = [
+            remote(own, block(row, col), sems, step, (group, row, line(step)))
+            for step in range(1, cols)
+        ]
+        arrive = [
+            remote(own, block(row, line(-step)), sems, step, (group, row, line(step)))
+            for step in range(1, cols)
+        ]
+        across = [remote(own, block(row, col), x_sems, 0, (group, 1 - row, col))] + [
+            remote(block(row, line(-step)), block(row, line(-step)), x_sems, step, (group, 1 - row, col))
+            for step in range(1, cols)
+        ]
+        landed = [
+            remote(own, block(1 - row, line(-step)), x_sems, step, (group, 1 - row, col))
+            for step in range(cols)
+        ]
+        return along, arrive, across, landed, block(row, col)
+
+    q_along, q_arrive, q_across, q_landed, q_own = weight_copies(pq_ref, wq_ref, q_sems, qx_sems)
+    o_along, o_arrive, o_across, o_landed, o_own = weight_copies(po_ref, wo_ref, o_sems, ox_sems)
+    own_q = pltpu.make_async_copy(pq_ref, q_own, local_sems.at[0])
+    own_o = pltpu.make_async_copy(po_ref, o_own, local_sems.at[1])
+
+    def token_copy(step, into):
+        return remote(
+            tok_ref.at[line(step)],
+            x_ref.at[:, start_at(into, width)],
+            tok_sems,
+            step,
+            (mate, core, line(step)),
+        )
+
+    own_tokens = pltpu.make_async_copy(
+        tok_ref.at[col], x_ref.at[:, start_at(col, width)], local_sems.at[2]
+    )
+    for step in range(1, cols):
+        token_copy(step, col).start()
+
+    @pl.when(core != row)
+    def _():
+        token_copy(0, col).start()
+
+    @pl.when(core == row)
+    def _():
+        own_tokens.start()
+
+    for copy in q_along:
+        copy.start()
+    q_across[0].start()
+    own_q.start()
+    own_o.start()
+    for copy in o_along:
+        copy.start()
+    o_across[0].start()
+    for step in range(1, cols):
+        q_arrive[step - 1].wait_recv()
+        q_across[step].start()
+    for step in range(1, cols):
+        o_arrive[step - 1].wait_recv()
+        o_across[step].start()
+    for step in range(1, cols):
+        token_copy(step, line(-step)).wait_recv()
+        token_copy(step, col).wait_send()
+
+    @pl.when(core != row)
+    def _():
+        token_copy(0, col).wait_recv()
+        token_copy(0, col).wait_send()
+
+    @pl.when(core == row)
+    def _():
+        own_tokens.wait()
+
+    own_q.wait()
+    own_o.wait()
+    for copy in q_along + o_along + q_across + o_across:
+        copy.wait_send()
+    for copy in q_landed + o_landed:
+        copy.wait_recv()
+
+
+def start_exchange(tokens, pack_q, pack_o, rows, cols):
+    anywhere = pl.BlockSpec(memory_space=pl.ANY)
+    seqs, length, width = tokens.shape
+    weight_rows = pack_q.shape[0]
+    return pl.pallas_call(
+        functools.partial(start_kernel, cols),
+        out_shape=(
+            jax.ShapeDtypeStruct((length, width * cols), tokens.dtype),
+            jax.ShapeDtypeStruct((weight_rows * rows, pack_q.shape[1] * cols), pack_q.dtype),
+            jax.ShapeDtypeStruct((weight_rows * rows, pack_o.shape[1] * cols), pack_o.dtype),
+        ),
+        in_specs=[anywhere] * 3,
+        out_specs=(anywhere,) * 3,
+        scratch_shapes=[pltpu.SemaphoreType.DMA((2, cols))] * 5 + [pltpu.SemaphoreType.DMA((3,))],
+        compiler_params=pltpu.CompilerParams(collective_id=1, has_side_effects=True),
+        name="start_exchange",
+    )(tokens, pack_q, pack_o)
+
+
+def half_turn(wide):
+    lanes = wide.shape[1]
+    half = HEAD_SIZE // 2
+    lane = lax.broadcasted_iota(jnp.int32, wide.shape, 1)
+    return jnp.where(
+        lax.rem(lane, HEAD_SIZE) < half,
+        pltpu.roll(wide, lanes - half, 1),
+        pltpu.roll(wide, half, 1),
+    )
+
+
+def both_heads(pair):
+    lane = lax.broadcasted_iota(jnp.int32, pair.shape, 1)
+    turned = pltpu.roll(pair, HEAD_SIZE, 1)
+    low = lane < HEAD_SIZE
+    return jnp.where(low, pair, turned), jnp.where(low, turned, pair)
+
+
+def keep_head(pair, side):
+    lane = lax.broadcasted_iota(jnp.int32, pair.shape, 1)
+    mine = lane < HEAD_SIZE if side == 0 else lane >= HEAD_SIZE
+    return jnp.where(mine, pair, jnp.zeros_like(pair))
+
+
+def dot_nn(a, b):
+    return lax.dot_general(a, b, (((1,), (0,)), ((), ())), preferred_element_type=jnp.float32)
+
+
+def dot_nt(a, b):
+    return lax.dot_general(a, b, (((1,), (1,)), ((), ())), preferred_element_type=jnp.float32)
+
+
+def dot_tn(a, b):
+    return lax.dot_general(a, b, (((0,), (0,)), ((), ())), preferred_element_type=jnp.float32)
+
+
+PAIR = 2 * HEAD_SIZE
+
+
+def attend_kernel(block, len_ref, a_ref, w_ref, cos_ref, sin_ref, qkv_ref, z_ref, q_all, k_two, v_two):
+    rows = a_ref.shape[0]
+    heads = q_all.shape[0]
+    length = len_ref[0]
+
+    @pl.loop(0, rows // block)
+    def _(at):
+        here = pl.ds(pl.multiple_of(at * block, block), block)
+        lin = dot_nn(a_ref[here, :], w_ref[...])
+        for part in range(heads // 2 + 1):
+            lanes = slice(part * PAIR, (part + 1) * PAIR)
+            now = lin[:, lanes]
+            now = now * cos_ref[here, lanes] + half_turn(now) * sin_ref[here, lanes]
+            qkv_ref[here, lanes] = now.astype(jnp.bfloat16)
+            if part < heads // 2:
+                for side in range(2):
+                    q_all[2 * part + side, here, :] = keep_head(now * ATTN_MULT, side).astype(
+                        jnp.bfloat16
+                    )
+            else:
+                keys, values = both_heads(now)
+                k_two[here, :] = keys.astype(jnp.bfloat16)
+                v_two[here, :] = values.astype(jnp.bfloat16)
+
+    for at in range(rows // block):
+        here = slice(at * block, (at + 1) * block)
+        upto = (at + 1) * block
+        row = lax.broadcasted_iota(jnp.int32, (block, upto), 0) + at * block
+        key = lax.broadcasted_iota(jnp.int32, (block, upto), 1)
+        allowed = key < jnp.minimum(row + 1, length)
+
+        def one_head(head):
+            scores = dot_nt(q_all[head, here, :], k_two[:upto, :])
+            scores = jnp.where(allowed, scores, MASKED)
+            top = jnp.max(scores, axis=1, keepdims=True)
+            power = jnp.exp(scores - top)
+            total = jnp.sum(power, axis=1, keepdims=True)
+            return dot_nn(power.astype(jnp.bfloat16), v_two[:upto, :]) / total
+
+        for pair in range(heads // 2):
+            low = one_head(2 * pair)
+            high = one_head(2 * pair + 1)
+            lane = lax.broadcasted_iota(jnp.int32, low.shape, 1)
+            z_ref[here, pair * PAIR : (pair + 1) * PAIR] = jnp.where(
+                lane < HEAD_SIZE, low, high
+            ).astype(jnp.bfloat16)
+
+
+def attend_fast(length, inputs, weights, cosines, sines, groups):
+    rows, depth = inputs.shape
+    wide = weights.shape[1] // groups
+    heads = (wide - PAIR) // HEAD_SIZE
+    block = min(256, rows)
+    return pl.pallas_call(
+        functools.partial(attend_kernel, block),
+        grid=(groups,),
+        out_shape=(
+            jax.ShapeDtypeStruct((rows, groups * wide), jnp.bfloat16),
+            jax.ShapeDtypeStruct((rows, groups * heads * HEAD_SIZE), jnp.bfloat16),
+        ),
+        in_specs=[
+            pl.BlockSpec(memory_space=pltpu.SMEM),
+            pl.BlockSpec((rows, depth), lambda g: (0, 0)),
+            pl.BlockSpec((depth, wide), lambda g: (0, g)),
+            pl.BlockSpec((rows, wide), lambda g: (0, 0)),
+            pl.BlockSpec((rows, wide), lambda g: (0, 0)),
+        ],
+        out_specs=(
+            pl.BlockSpec((rows, wide), lambda g: (0, g)),
+            pl.BlockSpec((rows, heads * HEAD_SIZE), lambda g: (0, g)),
+        ),
+        scratch_shapes=[
+            pltpu.VMEM((heads, rows, PAIR), jnp.bfloat16),
+            pltpu.VMEM((rows, PAIR), jnp.bfloat16),
+            pltpu.VMEM((rows, PAIR), jnp.bfloat16),
+        ],
+        compiler_params=pltpu.CompilerParams(vmem_limit_bytes=48 << 20),
+        cost_estimate=pl.CostEstimate(
+            flops=2 * rows * depth * wide * groups + 2 * groups * heads * rows * rows * 128,
+            bytes_accessed=2 * (rows * depth + depth * wide * groups + rows * wide * groups),
+            transcendentals=groups * heads * rows * rows // 2,
+        ),
+        name="attend",
+    )(length, inputs, weights, cosines, sines)
+
+
+def attend_back_kernel(
+    block, len_ref, qkv_ref, dz_ref, cos_ref, sin_ref, out_ref, q_all, z_all, k_two, v_two, k_acc, v_acc
+):
+    rows = qkv_ref.shape[0]
+    heads = q_all.shape[0]
+    length = len_ref[0]
+
+    @pl.loop(0, rows // block)
+    def _(at):
+        here = pl.ds(pl.multiple_of(at * block, block), block)
+        for part in range(heads // 2):
+            lanes = slice(part * PAIR, (part + 1) * PAIR)
+            queries = qkv_ref[here, lanes].astype(jnp.float32) * ATTN_MULT
+            mixed = dz_ref[here, lanes].astype(jnp.float32)
+            for side in range(2):
+                q_all[2 * part + side, here, :] = keep_head(queries, side).astype(jnp.bfloat16)
+                z_all[2 * part + side, here, :] = keep_head(mixed, side).astype(jnp.bfloat16)
+        keys, values = both_heads(qkv_ref[here, heads * HEAD_SIZE :].astype(jnp.float32))
+        k_two[here, :] = keys.astype(jnp.bfloat16)
+        v_two[here, :] = values.astype(jnp.bfloat16)
+        k_acc[here, :] = jnp.zeros((block, PAIR), jnp.float32)
+        v_acc[here, :] = jnp.zeros((block, PAIR), jnp.float32)
+
+    def turn_back(now, here, lanes):
+        return (now * cos_ref[here, lanes] - half_turn(now) * sin_ref[here, lanes]).astype(
+            jnp.bfloat16
+        )
+
+    for at in range(rows // block):
+        here = slice(at * block, (at + 1) * block)
+        upto = (at + 1) * block
+        key = lax.broadcasted_iota(jnp.int32, (upto, block), 0)
+        query = lax.broadcasted_iota(jnp.int32, (upto, block), 1) + at * block
+        allowed = key < jnp.minimum(query + 1, length)
+
+        def one_head(head):
+            queries, mixed = q_all[head, here, :], z_all[head, here, :]
+            scores = jnp.where(allowed, dot_nt(k_two[:upto, :], queries), MASKED)
+            power = jnp.exp(scores - jnp.max(scores, axis=0, keepdims=True))
+            weights = power * (1.0 / jnp.sum(power, axis=0, keepdims=True))
+            back = dot_nt(v_two[:upto, :], mixed)
+            centre = jnp.sum(weights * back, axis=0, keepdims=True)
+            slope = (weights * (back - centre)).astype(jnp.bfloat16)
+            k_acc[:upto, :] += dot_nn(slope, queries)
+            v_acc[:upto, :] += dot_nn(weights.astype(jnp.bfloat16), mixed)
+            return dot_tn(slope, k_two[:upto, :]) * ATTN_MULT
+
+        for pair in range(heads // 2):
+            low = one_head(2 * pair)
+            high = one_head(2 * pair + 1)
+            lane = lax.broadcasted_iota(jnp.int32, low.shape, 1)
+            lanes = slice(pair * PAIR, (pair + 1) * PAIR)
+            out_ref[here, lanes] = turn_back(jnp.where(lane < HEAD_SIZE, low, high), here, lanes)
+
+    @pl.loop(0, rows // block)
+    def _(at):
+        here = pl.ds(pl.multiple_of(at * block, block), block)
+        keys, values = k_acc[here, :], v_acc[here, :]
+        keys = keys + pltpu.roll(keys, HEAD_SIZE, 1)
+        values = values + pltpu.roll(values, HEAD_SIZE, 1)
+        lane = lax.broadcasted_iota(jnp.int32, keys.shape, 1)
+        lanes = slice(heads * HEAD_SIZE, heads * HEAD_SIZE + PAIR)
+        out_ref[here, lanes] = turn_back(jnp.where(lane < HEAD_SIZE, keys, values), here, lanes)
+
+
+def attend_back_fast(length, projected, grad_mixed, cosines, sines, groups):
+    rows = projected.shape[0]
+    wide = projected.shape[1] // groups
+    heads = (wide - PAIR) // HEAD_SIZE
+    block = min(256, rows)
+    return pl.pallas_call(
+        functools.partial(attend_back_kernel, block),
+        grid=(groups,),
+        out_shape=jax.ShapeDtypeStruct((rows, groups * wide), jnp.bfloat16),
+        in_specs=[
+            pl.BlockSpec(memory_space=pltpu.SMEM),
+            pl.BlockSpec((rows, wide), lambda g: (0, g)),
+            pl.BlockSpec((rows, heads * HEAD_SIZE), lambda g: (0, g)),
+            pl.BlockSpec((rows, wide), lambda g: (0, 0)),
+            pl.BlockSpec((rows, wide), lambda g: (0, 0)),
+        ],
+        out_specs=pl.BlockSpec((rows, wide), lambda g: (0, g)),
+        scratch_shapes=[
+            pltpu.VMEM((heads, rows, PAIR), jnp.bfloat16),
+            pltpu.VMEM((heads, rows, PAIR), jnp.bfloat16),
+            pltpu.VMEM((rows, PAIR), jnp.bfloat16),
+            pltpu.VMEM((rows, PAIR), jnp.bfloat16),
+            pltpu.VMEM((rows, PAIR), jnp.float32),
+            pltpu.VMEM((rows, PAIR), jnp.float32),
+        ],
+        compiler_params=pltpu.CompilerParams(vmem_limit_bytes=48 << 20),
+        cost_estimate=pl.CostEstimate(
+            flops=5 * groups * heads * rows * rows * 128,
+            bytes_accessed=2 * (2 * rows * wide * groups + rows * heads * HEAD_SIZE * groups),
+            transcendentals=groups * heads * rows * rows // 2,
+        ),
+        name="attend_back",
+    )(length, projected, grad_mixed, cosines, sines)
+
+
+def one_sequence_body(
+    tokens,
+    cotangent,
+    lengths,
+    deal_order,
+    gain_attn,
+    gain_ffn,
+    w_query,
+    key_value_weight,
+    w_out,
+    w_gate_up,
+    w_down,
+):
+    seq_group, rows_local, width_local = tokens.shape
+    row_count = lax.axis_size("row")
+    col_count = lax.axis_size("col")
+    full_width = width_local * col_count
+    slot_len = rows_local * row_count
+    group, core, mate, row, col = place()
+    query_half = w_query.shape[1] // 2
+    kv_half = key_value_weight.shape[2] // 2
+    hidden = w_down.shape[1]
+
+    def core_half(matrix, axis):
+        width = matrix.shape[axis] // 2
+        return lax.dynamic_slice_in_dim(matrix, core * width, width, axis)
+
+    def joined(mine, other, at):
+        return jnp.where(
+            at == 0, jnp.concatenate([mine, other]), jnp.concatenate([other, mine])
+        )
+
+    def from_sibling(value):
+        return lax.ppermute(value, "dp", SIBLINGS)
+
+    pack_q = jnp.concatenate(
+        [
+            core_half(w_query, 1),
+            core_half(key_value_weight[:, 0], 1),
+            core_half(key_value_weight[:, 1], 1),
+        ],
+        axis=1,
+    )
+    pack_o = core_half(w_out, 1)
+    own_tokens, weights_qkv, weights_out = start_exchange(
+        tokens, pack_q, pack_o, row_count, col_count
+    )
+
+    length = lax.dynamic_slice_in_dim(lengths, mate * seq_group + col, 1)
+    line_lengths = lax.dynamic_slice_in_dim(lengths, mate * seq_group, seq_group)
+    own_pos = core * rows_local + jnp.arange(rows_local, dtype=jnp.int32)
+    line_live = (own_pos[None, :] < line_lengths[:, None]).astype(jnp.float32)
+    own_live = (own_pos < length).astype(jnp.float32)[:, None]
+
+    def all_rows(matrix):
+        count = matrix.shape[0] // 4
+        part = lax.dynamic_slice_in_dim(matrix, group * count, count)
+        other = lax.all_gather(lax.ppermute(part, "row", OVER_X), "dp", axis=0, tiled=True)
+        return joined(matrix, other, row)
+
+    gate_up_weights = all_rows(w_gate_up)
+    down_weights = all_rows(w_down)
+
+    given = bring_cotangent(cotangent, deal_order, group * seq_group)
+    swapped = lax.ppermute(given, ("dp", "row"), CROSSED)
+    line_cot = lax.all_gather(swapped, "col", axis=2, tiled=True)
+    line_grad = line_live[:, :, None] * line_cot.astype(jnp.float32)
+    grad_ffn = (RES_MULT * line_grad).astype(jnp.bfloat16).reshape(-1, full_width)
+    own_grad = own_live * lax.dynamic_index_in_dim(line_cot, col, keepdims=False).astype(
+        jnp.float32
+    )
+
+    cosine_table, sine_table = rope_tables(jnp.arange(slot_len, dtype=jnp.int32), HEAD_SIZE)
+    turns = (query_half + kv_half) // HEAD_SIZE
+    cosines = jnp.concatenate(
+        [jnp.tile(cosine_table, (1, 2 * turns)), jnp.ones((slot_len, kv_half), jnp.float32)], axis=1
+    )
+    sines = jnp.concatenate(
+        [
+            jnp.tile(jnp.concatenate([-sine_table, sine_table], axis=1), (1, turns)),
+            jnp.zeros((slot_len, kv_half), jnp.float32),
+        ],
+        axis=1,
+    )
+
+    gain_one = gain_attn.astype(jnp.float32)
+    gain_two = gain_ffn.astype(jnp.float32)
+    own_float = own_tokens.astype(jnp.float32)
+    scale_one = lax.rsqrt(jnp.mean(own_float * own_float, axis=1, keepdims=True) + EPSILON)
+    own_input = (own_float * scale_one * gain_one).astype(jnp.bfloat16)
+    attn_input = joined(own_input, from_sibling(own_input), core)
+    projected, heads_out = attend_fast(
+        length, attn_input, weights_qkv, cosines, sines, col_count
+    )
+
+    def summed_rows(partial):
+        count = partial.shape[0] // 2
+        mine = lax.dynamic_slice_in_dim(partial, core * count, count)
+        other = lax.dynamic_slice_in_dim(partial, (1 - core) * count, count)
+        return mine.astype(jnp.float32) + from_sibling(other).astype(jnp.float32)
+
+    attn_rows = summed_rows(expand_local(heads_out, weights_out).astype(jnp.bfloat16))
+    resid = own_float + RES_MULT * attn_rows
+    scale_two = lax.rsqrt(jnp.mean(resid * resid, axis=1, keepdims=True) + EPSILON)
+    own_ffn = (resid * scale_two * gain_two).astype(jnp.bfloat16)
+
+    ffn_input = lax.all_gather(own_ffn, "col", axis=0, tiled=True)
+    gate_up = contract_local(ffn_input, gate_up_weights)
+    gate = gate_up[:, 0]
+    upward = gate_up[:, 1]
+    sigmoid_gate = jax.nn.sigmoid(gate)
+    silu_gate = gate * sigmoid_gate
+    hidden_rows = (silu_gate * upward).astype(jnp.bfloat16)
+    grad_hidden = contract_local(grad_ffn, down_weights)
+    slope = sigmoid_gate * (1.0 + gate * (1.0 - sigmoid_gate))
+    grad_gate_rows = jnp.stack(
+        [grad_hidden * upward * slope, grad_hidden * silu_gate], axis=1
+    ).astype(jnp.bfloat16)
+    back_partial = expand_local(grad_gate_rows, gate_up_weights).astype(jnp.bfloat16)
+    grad_normed_two = lax.psum_scatter(
+        back_partial, "col", scatter_dimension=0, tiled=True
+    ).astype(jnp.float32)
+
+    mlp_partial = RES_MULT * expand_local(hidden_rows, down_weights)
+    is_own = (jnp.arange(col_count) == col).astype(jnp.float32)[:, None, None]
+    out_partial = (
+        mlp_partial.reshape(col_count, rows_local, full_width) + is_own * resid[None]
+    ).astype(jnp.bfloat16)
+    out_cols = lax.psum_scatter(out_partial, "col", scatter_dimension=2, tiled=True)
+    given_pos = row * rows_local + jnp.arange(rows_local, dtype=jnp.int32)
+    given_lengths = lax.dynamic_slice_in_dim(lengths, group * seq_group, seq_group)
+    given_live = (given_pos[None, :] < given_lengths[:, None]).astype(jnp.float32)
+    layer_out = given_live[:, :, None] * lax.ppermute(
+        out_cols, ("dp", "row"), CROSSED
+    ).astype(jnp.float32)
+
+    def scatter_rows(matrix):
+        return lax.psum_scatter(
+            matrix.astype(jnp.bfloat16), ("dp", "row"), scatter_dimension=0, tiled=True
+        ).astype(jnp.float32)
+
+    sums_down = scatter_rows(token_outer(grad_ffn, hidden_rows))
+    sums_gate_up = scatter_rows(token_outer(ffn_input, grad_gate_rows))
+
+    weighted_two = grad_normed_two * gain_two
+    inner_two = jnp.sum(weighted_two * resid, axis=1, keepdims=True)
+    grad_resid = (
+        own_grad + scale_two * weighted_two - resid * scale_two**3 * inner_two / full_width
+    )
+    gain_two_part = jnp.sum(grad_normed_two * resid * scale_two, axis=0)
+    own_attn_grad = (RES_MULT * grad_resid).astype(jnp.bfloat16)
+    grad_attn = joined(own_attn_grad, from_sibling(own_attn_grad), core)
+    grad_heads = contract_local(grad_attn, weights_out).astype(jnp.bfloat16)
+    grad_out = token_outer(grad_attn, heads_out).astype(jnp.bfloat16)
+    grad_projected = attend_back_fast(
+        length, projected, grad_heads, cosines, sines, col_count
+    )
+    grad_normed_one = summed_rows(expand_local(grad_projected, weights_qkv).astype(jnp.bfloat16))
+    grad_qkv = token_outer(attn_input, grad_projected).astype(jnp.bfloat16)
+    weighted_one = grad_normed_one * gain_one
+    inner_one = jnp.sum(weighted_one * own_float, axis=1, keepdims=True)
+    own_input_grad = (
+        grad_resid
+        + scale_one * weighted_one
+        - own_float * scale_one**3 * inner_one / full_width
+    ).astype(jnp.bfloat16)
+    gain_one_part = jnp.sum(grad_normed_one * own_float * scale_one, axis=0)
+    given_grad = lax.all_to_all(
+        own_input_grad.reshape(rows_local, col_count, width_local), "col", 1, 0
+    )
+    input_grad = lax.ppermute(given_grad, ("dp", "row"), CROSSED).astype(jnp.float32)
+    grad_gain_attn, grad_gain_ffn = lax.psum((gain_one_part, gain_two_part), ("dp", "row", "col"))
+
+    both = jnp.concatenate(
+        [
+            grad_qkv.reshape(full_width, col_count, -1),
+            grad_out.reshape(full_width, col_count, -1),
+        ],
+        axis=2,
+    )
+    both = both.reshape(2, 2, row_count, -1, col_count, both.shape[2])
+    kept = lax.dynamic_index_in_dim(both, core, 1, keepdims=False)
+    sent = from_sibling(lax.dynamic_index_in_dim(both, 1 - core, 1, keepdims=False))
+    cores = jnp.where(
+        core == 0, jnp.stack([kept, sent], axis=4), jnp.stack([sent, kept], axis=4)
+    )
+    cores = lax.psum_scatter(
+        cores, "row", scatter_dimension=1, tiled=False
+    )
+    cores = lax.psum_scatter(
+        cores, "dp", scatter_dimension=0, axis_index_groups=SAME_CORE, tiled=False
+    )
+    cores = lax.psum_scatter(cores, "col", scatter_dimension=1, tiled=False).astype(jnp.float32)
+    grad_rows = cores.shape[0]
+    qk = query_half + kv_half
+    out_query = cores[:, :, :query_half].reshape(grad_rows, -1)
+    out_kv = jnp.stack(
+        [
+            cores[:, :, query_half:qk].reshape(grad_rows, -1),
+            cores[:, :, qk : qk + kv_half].reshape(grad_rows, -1),
+        ],
+        axis=1,
+    )
+    out_out = cores[:, :, qk + kv_half :].reshape(grad_rows, -1)
+    return (
+        layer_out,
+        input_grad,
+        out_query,
+        out_kv,
+        out_out,
+        sums_gate_up,
+        sums_down,
+        grad_gain_attn,
+        grad_gain_ffn,
+    )
+
+
+def general_body(
     tokens,
     cotangent,
     lengths,
@@ -223,10 +842,9 @@
     def expand_with(operand, which_one):
         return expand_rows(operand, matrices[which_one])
 
-    everyone = lax.all_gather(tokens, "dp", axis=0, tiled=True)
-    my_ids = lax.dynamic_slice_in_dim(deal_order, group_index * seq_group, seq_group)
-    own_rows = jnp.take(everyone, my_ids, axis=0)
-    seq_lens = jnp.take(lengths, my_ids)
+    own_cotangent = bring_cotangent(cotangent, deal_order, group_index * seq_group)
+    own_rows = tokens
+    seq_lens = lax.dynamic_slice_in_dim(lengths, group_index * seq_group, seq_group)
     local_pos = row_index * rows_local + jnp.arange(rows_local, dtype=jnp.int32)
     key_pos = jnp.arange(slot_len, dtype=jnp.int32)
     live_rows = (local_pos[None, :] < seq_lens[:, None]).astype(jnp.float32).reshape(total_rows, 1)
@@ -283,7 +901,7 @@
     hidden = (silu_gate * upward).astype(jnp.bfloat16)
     ffn_local = narrow_cols(expand_with(hidden, "down"))
     layer_out = live_rows * (resid + RES_MULT * ffn_local)
-    grad_rows = live_rows * cotangent.reshape(total_rows, width_local).astype(jnp.float32)
+    grad_rows = live_rows * own_cotangent.reshape(total_rows, width_local).astype(jnp.float32)
     grad_ffn = widen_cols((RES_MULT * grad_rows).astype(jnp.bfloat16))
     grad_hidden = contract_with(grad_ffn, "down")
     grad_down = token_outer(grad_ffn, hidden)
@@ -362,26 +980,9 @@
     )
     out_query = sums_qkv[:, :query_width]
     out_kv = sums_qkv[:, query_width:].reshape(sums_qkv.shape[0], 2, kv_width)
-    slots = jnp.arange(deal_order.shape[0], dtype=jnp.int32)
-    inverse = jnp.sum(jnp.where(deal_order[None, :] == slots[:, None], slots[None, :], 0), axis=1)
-    own_slots = lax.dynamic_slice_in_dim(inverse, group_index * seq_group, seq_group)
-    every_out, every_grad = (
-        lax.all_gather(
-            layer_out.reshape(seq_group, rows_local, width_local).astype(jnp.bfloat16),
-            "dp",
-            axis=0,
-            tiled=True,
-        ).astype(jnp.float32),
-        lax.all_gather(
-            input_grad.reshape(seq_group, rows_local, width_local).astype(jnp.bfloat16),
-            "dp",
-            axis=0,
-            tiled=True,
-        ).astype(jnp.float32),
-    )
     return (
-        jnp.take(every_out, own_slots, axis=0),
-        jnp.take(every_grad, own_slots, axis=0),
+        layer_out.reshape(seq_group, rows_local, width_local),
+        input_grad.reshape(seq_group, rows_local, width_local),
         out_query,
         out_kv,
         sums_out,
@@ -389,6 +990,16 @@
         sums_down,
         grad_gain_attn,
         grad_gain_ffn,
+    )
+
+
+def body(tokens, cotangent, lengths, deal_order, gain_attn, gain_ffn, w_query, key_value_weight, *rest):
+    sizes = (lax.axis_size("dp"), lax.axis_size("row"), lax.axis_size("col"))
+    one_each = sizes == (4, 2, 4) and tokens.shape[0] == sizes[2]
+    pairs = w_query.shape[1] == 8 * HEAD_SIZE and key_value_weight.shape[2] == 2 * HEAD_SIZE
+    chosen = one_sequence_body if one_each and pairs else general_body
+    return chosen(
+        tokens, cotangent, lengths, deal_order, gain_attn, gain_ffn, w_query, key_value_weight, *rest
     )
 
 

time: 3320 us -> 1880 us (0.57)
  waiting for transfers between devices: 2310 us -> 927 us
  Pallas kernels: 0 us -> 300 us
  matrix products: 506 us -> 269 us
  local copies, waits for them, and re-layouts: 247 us -> 94.4 us
  starting transfers between devices: 1.54 us -> 59.5 us
    all_gather x13 -> x5, waiting for transfers between devices: 1080 us -> 150 us  [the longest x1 105 us: one_sequence_body(): line_cot = lax.all_gather(swapped, 'col', axis=2, tiled=True)]
    reduce_scatter x10 -> x6, waiting for transfers between devices: 1230 us -> 442 us  [the longest x1 144 us: one_sequence_body(): lax.psum_scatter(back_partial, 'col', scatter_dimension=0, tiled=True)]
    pallas_call x0 -> x3, Pallas kernels: none -> 300 us  [the longest x1 193 us: start_exchange(): pl.pallas_call(functools.partial(start_kernel, cols), out_shape=(jax.Shap...]
    unnamed x23 -> x13, waiting for transfers between devices: 3.09 us -> 244 us
    dot_general x72 -> x0, matrix products: 222 us -> none  [the longest x24 83.5 us: block_scores(): jnp.einsum('qkgd,tkd->kgqt', query_seq, key_block, preferred_element_type...]
    dynamic_update_slice x33 -> x0, local copies, waits for them, and re-layouts: 103 us -> none  [the longest x16 94.3 us: body(): lax.map(forward_seq, (query_split, key_split, value_split, seq_lens))]
    ppermute x0 -> x10, waiting for transfers between devices: none -> 90.5 us  [the longest x2 69 us: all_rows(): lax.ppermute(part, 'row', OVER_X)]
    select_n x3, other arithmetic: 10.4 us -> 96.7 us  [the longest x2 86.3 us: joined(): jnp.where(at == 0, jnp.concatenate([mine, other]), jnp.concatenate([other...]
  transfers between devices with their start and end apart: 23 -> 23, of which waited for: 21 -> 15; matrix products, arithmetic and copies ran while one was open for 12% -> 17% of each run, Pallas kernels for 0% -> 13%
where the time goes in v1:
time: 1880 us; the launch traced here: 1870 us
  waiting for transfers between devices  927 us (49%)
  Pallas kernels  300 us (16%)
  matrix products  269 us (14%)
  other arithmetic  158 us (8%)
  local copies, waits for them, and re-layouts  94.4 us (5%)
  starting transfers between devices  59.5 us (3%)
  blocking collectives  40.8 us (2%)
  between operations  22.4 us (1%)
    unnamed x13, waiting for transfers between devices  244 us
    pallas_call x1, Pallas kernels, start_exchange(): pl.pallas_call(functools.partial(start_kernel, cols), out_shape=(jax.Shap...  193 us
    reduce_scatter x1, waiting for transfers between devices, one_sequence_body(): lax.psum_scatter(back_partial, 'col', scatter_dimension=0, tiled=True)  144 us
    reduce_scatter x2, waiting for transfers between devices, scatter_rows(): lax.psum_scatter(matrix.astype(jnp.bfloat16), ('dp', 'row'), scatter_dime...  142 us
    reduce_scatter x1, waiting for transfers between devices, one_sequence_body(): lax.psum_scatter(out_partial, 'col', scatter_dimension=2, tiled=True)  110 us
    all_gather x1, waiting for transfers between devices, one_sequence_body(): line_cot = lax.all_gather(swapped, 'col', axis=2, tiled=True)  105 us
    dot_general x4, matrix products, expand_local(): lax.dot_general(operand, matrix, ((trailing, trailing), ((), ())), prefer...  92.6 us
    dot_general x4, matrix products, token_outer(): lax.dot_general(features, grads, (((0,), (0,)), ((), ())), preferred_elem...  89.2 us
  transfers between devices with their start and end apart: 23, of which 15 were waited for; matrix products, arithmetic and copies ran while one was open for 17% of the time, Pallas kernels for 13%

profile of v1, /device:TPU:0, one launch (start us, length us, event | category | flops | bytes accessed | tf_op | source)
XLA Modules:
  0.0 1870.3 jit_solution(12764018198500074494)
XLA Ops:
  14.0 45.6 %collective-permute-done.2 = bf16[256,2,2048]{2,1,0:T(2,128)(2,1)S(1)} collective-permute-done((bf16[256,2,2048]{2,1,0:T(2,128)(2,1)S(1)}, bf16[256,2,2048]{2,1,0:T(2,128)(2,1)S(1)}, u32[]{:S(2)}, u32[]{:S(2)}) %collective-permute-start.2) | collective-permute-done | bytes 2097184 | tf_op jit(solution)/shard_map/ppermute | solution.py:643
  66.1 193.0 %start_exchange.1 = (bf16[512,2048]{1,0:T(8,128)(2,1)}, bf16[2048,1536]{1,0:T(8,128)(2,1)}, bf16[2048,1024]{1,0:T(8,128)(2,1)}) custom-call(bf16[4,512,512]{2,1,0:T(8,128)(2,1)} %tok_ref.1, bf16[1024,384]{1,0:T(8,128)(2,1)} %pad_maximum_fusion.8.pq_ref, bf16[1024,256]{1,0:T(8,128)(2,1)} %get-tuple-element.103.po_ref), custom_call_target="tpu_custom_call" | custom-call | tf_op jit(solution)/shard_map/start_exchange/pallas_call | solution.py:346
  276.2 43.2 %attend.1 = (bf16[1024,1536]{1,0:T(8,128)(2,1)}, bf16[1024,1024]{1,0:T(8,128)(2,1)S(1)}) custom-call(s32[1]{0:T(128)} %dynamic_slice.86.len_ref, bf16[1024,2048]{1,0:T(8,128)(2,1)} %maximum_select_fusion.2.a_ref, bf16[2048,1536]{1,0:T(8,128)(2,1)} %get-tuple-element.15.w_ref, f32[1024,384]{1,0:T(8,128)S(1)} %concatenate.50.cos_ref, ...), custom_call_target="tpu_custom_call" | custom-call | flops 10737418240 | bytes 13631488 | tf_op jit(solution)/shard_map/attend/pallas_call | solution.py:453
  354.4 27.9 %collective-permute-start.3 = (bf16[256,2048]{1,0:T(8,128)(2,1)}, bf16[256,2048]{1,0:T(8,128)(2,1)}, u32[]{:S(2)}, u32[]{:S(2)}) collective-permute-start(bf16[256,2048]{1,0:T(8,128)(2,1)} %constant_dynamic-slice_fusion.5), channel_id=1, source_target_pairs={{0,4},{4,0},{1,5},{5,1},{2,6},{6,2},{3,7},{7,3},{8,12},{12,8},{9,1... | collective-permute-start | bytes 3145736 | tf_op jit(solution)/shard_map/ppermute | solution.py:643
  383.0 23.4 %collective-permute-done.3 = bf16[256,2048]{1,0:T(8,128)(2,1)} collective-permute-done((bf16[256,2048]{1,0:T(8,128)(2,1)}, bf16[256,2048]{1,0:T(8,128)(2,1)}, u32[]{:S(2)}, u32[]{:S(2)}) %collective-permute-start.3) | collective-permute-done | bytes 1048608 | tf_op jit(solution)/shard_map/ppermute | solution.py:643
  406.5 79.9 %broadcast_select_fusion = bf16[2048,2,2048]{2,1,0:T(2,128)(2,1)} fusion(pred[]{:T(512)S(6)} %eq.33, bf16[1024,2,2048]{2,1,0:T(2,128)(2,1)} %all-gather.8.cloned.1.call-done, bf16[1024,2,2048]{2,1,0:T(2,128)(2,1)} %param.20), kind=kLoop, calls=%fused_computation | loop fusion | flops 25165824 | bytes 33554432 | tf_op jit(solution)/shard_map/jit(_where)/select_n | solution.py:614
  486.4 20.4 %all-gather.6.cloned.1.call-done = bf16[2048,2048]{1,0:T(8,128)(2,1)} async-done(((bf16[512,2048]{1,0:T(8,128)(2,1)}), bf16[2048,2048]{1,0:T(8,128)(2,1)}) %all-gather.6.cloned.1.call-update) | async-done | bytes 8388624 | tf_op jit(solution)/shard_map/all_gather | solution.py:692
  506.9 44.3 %fusion.10 = f32[2048,2,2048]{2,0,1:T(8,128)} fusion(bf16[2048,2,2048]{2,1,0:T(2,128)(2,1)} %broadcast_select_fusion, bf16[2048,2048]{1,0:T(8,128)(2,1)} %all-gather.6.cloned.1.call-done), kind=kOutput, calls=%fused_computation.22 | convolution fusion | flops 34359738368 | bytes 58720256 | tf_op jit(solution)/shard_map/dot_general | solution.py:55
  551.2 105.0 %all-gather.14.cloned.1.call-done = bf16[4,512,2048]{2,1,0:T(8,128)(2,1)} async-done(((bf16[4,512,512]{2,1,0:T(8,128)(2,1)}), bf16[4,512,2048]{2,1,0:T(8,128)(2,1)}) %all-gather.14.cloned.1.call-update) | async-done | bytes 8388624 | tf_op jit(solution)/shard_map/all_gather | solution.py:651
  656.2 9.3 multiply_convert_fusion.2
  665.5 24.8 %all-gather.10.cloned.1.call-done = bf16[1024,2048]{1,0:T(8,128)(2,1)} async-done(((bf16[256,2048]{1,0:T(8,128)(2,1)}), bf16[1024,2048]{1,0:T(8,128)(2,1)}) %all-gather.10.cloned.1.call-update) | async-done | bytes 4194320 | tf_op jit(solution)/shard_map/all_gather | solution.py:643
  690.3 33.7 %fusion.20 = (bf16[2048,1,2048]{2,0,1:T(8,128)(2,1)}, bf16[2048,1,2048]{2,0,1:T(8,128)(2,1)}) fusion(f32[2048,2,2048]{2,0,1:T(8,128)} %fusion.10, bf16[2048,2048]{1,0:T(8,128)(2,1)} %bitcast.117, bf16[1024,2048]{1,0:T(8,128)(2,1)} %all-gather.10.cloned.1.call-done, bf16[1024,2048]{1,0:T(8,128)(2,1)} %param.21, pred[]{:T(512)S(6)} %eq.33), kind=kOutput, calls=%fused_computation.40 | convolution fusion | flops 17272143872 | bytes 67108864 | tf_op jit(solution)/shard_map/dot_general | solution.py:55
  724.0 46.7 %bitcast_convert_fusion = bf16[2048,2048]{1,0:T(8,128)(2,1)} fusion(bf16[2048,2,2048]{2,1,0:T(2,128)(2,1)} %broadcast_select_fusion, bf16[2048,1,2048]{2,0,1:T(8,128)(2,1)} %get-tuple-element.75, bf16[2048,1,2048]{2,0,1:T(8,128)(2,1)} %get-tuple-element.74), kind=kOutput, calls=%fused_computation.2 | convolution fusion | flops 34372321280 | bytes 41943040 | tf_op jit(solution)/shard_map/dot_general | solution.py:62
  771.5 143.9 %reduce-scatter.12.cloned.1.call-done = bf16[512,2048]{1,0:T(8,128)(2,1)} async-done(((bf16[2048,2048]{1,0:T(8,128)(2,1)}), bf16[512,2048]{1,0:T(8,128)(2,1)}) %reduce-scatter.12.cloned.1.call-update) | async-done | bytes 2097168 | tf_op jit(solution)/shard_map/reduce_scatter | solution.py:705
  929.7 9.2 convolution_convert_fusion.4.dz_ref
  938.9 63.7 %attend_back.1 = bf16[1024,1536]{1,0:T(8,128)(2,1)} custom-call(s32[1]{0:T(128)} %dynamic_slice.86.len_ref, bf16[1024,1536]{1,0:T(8,128)(2,1)} %get-tuple-element.18.qkv_ref, bf16[1024,1024]{1,0:T(8,128)(2,1)S(1)} %convolution_convert_fusion.4.dz_ref, f32[1024,384]{1,0:T(8,128)S(1)} %concatenate.50.cos_ref, f32[1024,384]{1,0:T(8,128)S(1)} %concatenate.52.sin_ref), custom_call_target="tpu_custom_call" | custom-call | flops 10737418240 | bytes 8388608 | tf_op jit(solution)/shard_map/attend_back/pallas_call | solution.py:556
  1002.6 10.6 convolution_convert_fusion
  1013.2 11.3 concatenate.60
  1031.5 10.2 convolution_convert_fusion.2
  1054.7 9.6 dynamic-slice_bitcast_fusion.1
  1073.1 10.4 maximum_select_fusion
  1084.7 242.9 %all-reduce.6.cloned.1.call-done = bf16[2,2,256,4,2,640]{5,2,4,3,1,0:T(8,128)(2,1)} async-done(((bf16[2,2,256,4,2,640]{5,2,4,3,1,0:T(8,128)(2,1)}), bf16[2,2,256,4,2,640]{5,2,4,3,1,0:T(8,128)(2,1)}) %all-reduce.6.cloned.1.call-update) | async-done | bytes 10485776
  1341.6 32.2 %convolution_multiply_fusion = f32[2048,2048]{1,0:T(8,128)} fusion(f32[2048,2,2048]{2,0,1:T(8,128)} %fusion.10, bf16[1024,2048]{1,0:T(8,128)(2,1)} %all-gather.10.cloned.1.call-done, bf16[1024,2048]{1,0:T(8,128)(2,1)} %param.21, pred[]{:T(512)S(6)} %eq.33), kind=kOutput, calls=%fused_computation.27 | convolution fusion | flops 17246978048 | bytes 58720256 | tf_op jit(solution)/shard_map/dot_general | solution.py:62
  1373.8 11.0 add_convert_fusion
  1384.9 26.2 %fusion.21 = bf16[2048,2048]{1,0:T(8,128)(2,1)} fusion(bf16[2048,2048]{1,0:T(8,128)(2,1)} %bitcast.118, f32[2048,2,2048]{2,0,1:T(8,128)} %fusion.10), kind=kOutput, calls=%fused_computation.41 | convolution fusion | flops 17209229312 | bytes 50331648 | tf_op jit(solution)/shard_map/dot_general | solution.py:68
  1411.4 42.1 %fusion.13 = bf16[2048,2,2048]{2,0,1:T(8,128)(2,1)} fusion(bf16[2048,1,2048]{2,0,1:T(8,128)(2,1)} %get-tuple-element.75, bf16[2048,1,2048]{2,0,1:T(8,128)(2,1)} %get-tuple-element.74, bf16[2048,2048]{1,0:T(8,128)(2,1)} %all-gather.6.cloned.1.call-done), kind=kOutput, calls=%fused_computation.25 | convolution fusion | flops 34401681408 | bytes 41943040 | tf_op jit(solution)/shard_map/dot_general | solution.py:68
  1483.6 109.7 %reduce-scatter.10.cloned.1.call-done = bf16[4,512,512]{2,1,0:T(8,128)(2,1)} async-done(((bf16[4,512,2048]{2,1,0:T(8,128)(2,1)}), bf16[4,512,512]{2,1,0:T(8,128)(2,1)}) %reduce-scatter.10.cloned.1.call-update) | async-done | bytes 2097168 | tf_op jit(solution)/shard_map/reduce_scatter | solution.py:714
  1593.3 17.2 collective-permute-start.4
  1618.9 65.6 %reduce-scatter.20.cloned.1.call-done = bf16[256,2048]{1,0:T(8,128)(2,1)} async-done(((bf16[2048,2048]{1,0:T(8,128)(2,1)}), bf16[256,2048]{1,0:T(8,128)(2,1)}) %reduce-scatter.20.cloned.1.call-update) | async-done | bytes 1048592 | tf_op jit(solution)/shard_map/reduce_scatter | solution.py:723
  1687.2 40.8 %all-reduce.3 = (f32[2048]{0:T(1024)}, f32[2048]{0:T(1024)}) all-reduce(f32[2048]{0:T(1024)S(1)} %get-tuple-element.64, f32[2048]{0:T(1024)S(1)} %copy-done.22), channel_id=1, replica_groups=mesh['dp'=4,'row'=2,'col'=4] {'dp','row','col'}, use_global_device_ids=true, to_apply=%region_13.14 | all-reduce | flops 4096 | bytes 32768 | tf_op jit(solution)/shard_map/psum | solution.py:757
  1728.0 76.6 %reduce-scatter.18.cloned.1.call-done = bf16[256,2,2048]{2,0,1:T(8,128)(2,1)} async-done(((bf16[2048,2,2048]{2,0,1:T(8,128)(2,1)}), bf16[256,2,2048]{2,0,1:T(8,128)(2,1)}) %reduce-scatter.18.cloned.1.call-update) | async-done | bytes 2097168 | tf_op jit(solution)/shard_map/reduce_scatter | solution.py:723
  1813.0 46.0 %reduce-scatter.16.cloned.1.call-done = bf16[256,1,2,640]{0,3,2,1:T(8,128)(2,1)} async-done(((bf16[256,4,2,640]{0,3,2,1:T(8,128)(2,1)}), bf16[256,1,2,640]{0,3,2,1:T(8,128)(2,1)}) %reduce-scatter.16.cloned.1.call-update) | async-done | bytes 655376 | tf_op jit(solution)/shard_map/reduce_scatter | solution.py:778
  (177 shorter events, 171.4 us)
Async XLA Ops:
  7.2 53.9 %copy-start.12 = (bf16[1024,2,128]{2,1,0:T(2,128)(2,1)S(1)}, bf16[1024,2,128]{2,1,0:T(2,128)(2,1)}, u32[]{:S(2)}) copy-start(bf16[1024,2,128]{2,1,0:T(2,128)(2,1)} %param.18) | copy-start | bytes 1572868
  7.2 340.9 %all-gather.12.cloned.1.call-start = ((), (), s32[]{:S(2)}) async-start(), calls=%async_computation.11 | async-start | bytes 10485760 | tf_op jit(solution)/shard_map/all_gather | solution.py:196
  7.9 398.6 %all-gather.8.cloned.1.call-start = ((), (), s32[]{:S(2)}) async-start(), calls=%async_computation.8 | async-start | bytes 10485760 | tf_op jit(solution)/shard_map/all_gather | solution.py:643
  11.0 52.1 %copy-start.25 = (bf16[2048]{0:T(1024)(128)(2,1)S(1)}, bf16[2048]{0:T(1024)(128)(2,1)}, u32[]{:S(2)}) copy-start(bf16[2048]{0:T(1024)(128)(2,1)} %param.15) | copy-start | bytes 12292
  11.0 48.6 %collective-permute-start.2 = (bf16[256,2,2048]{2,1,0:T(2,128)(2,1)S(1)}, bf16[256,2,2048]{2,1,0:T(2,128)(2,1)S(1)}, u32[]{:S(2)}, u32[]{:S(2)}) collective-permute-start(bf16[256,2,2048]{2,1,0:T(2,128)(2,1)S(1)} %constant_dynamic-slice_fusion.6), channel_id=1, source_target_pairs={{0,4},{4,0},{1,5},{5,1},{2,6},{6,2},{3,7},{7,3},{8,12},{12,8},{9,1... | collective-permute-start | bytes 6291464 | tf_op jit(solution)/shard_map/ppermute | solution.py:643
  61.0 445.9 %all-gather.6.cloned.1.call-start = ((), (), s32[]{:S(2)}) async-start(), calls=%async_computation.7 | async-start | bytes 10485760 | tf_op jit(solution)/shard_map/all_gather | solution.py:692
  63.1 198.7 %copy-start.16 = (f32[2048]{0:T(1024)}, f32[2048]{0:T(1024)S(1)}, u32[]{:S(2)}) copy-start(f32[2048]{0:T(1024)S(1)} %convert_element_type.143) | copy-start | bytes 24580
  265.3 4.5 collective-permute-start
  326.9 4.6 collective-permute-start.1
  339.3 316.9 %all-gather.14.cloned.1.call-start = ((), (), s32[]{:S(2)}) async-start(), calls=%async_computation.12 | async-start | bytes 10485760 | tf_op jit(solution)/shard_map/all_gather | solution.py:651
  350.0 2.0 collective-permute-start.5
  352.0 338.3 %all-gather.10.cloned.1.call-start = ((), (), s32[]{:S(2)}) async-start(), calls=%async_computation.9 | async-start | bytes 5242880 | tf_op jit(solution)/shard_map/all_gather | solution.py:643
  354.4 52.0 %collective-permute-start.3 = (bf16[256,2048]{1,0:T(8,128)(2,1)}, bf16[256,2048]{1,0:T(8,128)(2,1)}, u32[]{:S(2)}, u32[]{:S(2)}) collective-permute-start(bf16[256,2048]{1,0:T(8,128)(2,1)} %constant_dynamic-slice_fusion.5), channel_id=1, source_target_pairs={{0,4},{4,0},{1,5},{5,1},{2,6},{6,2},{3,7},{7,3},{8,12},{12,8},{9,1... | collective-permute-start | bytes 3145736 | tf_op jit(solution)/shard_map/ppermute | solution.py:643
  406.4 509.0 %reduce-scatter.12.cloned.1.call-start = ((), (), s32[]{:S(2)}) async-start(), calls=%async_computation.13 | async-start | bytes 10485760 | tf_op jit(solution)/shard_map/reduce_scatter | solution.py:705
  770.7 144.7 %copy-start.15 = (f32[2048]{0:T(1024)S(1)}, f32[2048]{0:T(1024)}, u32[]{:S(2)}) copy-start(f32[2048]{0:T(1024)} %copy-done.14) | copy-start | bytes 24580
  770.7 144.7 %copy-start.21 = (f32[512]{0:T(512)S(1)}, f32[512]{0:T(512)}, u32[]{:S(2)}) copy-start(f32[512]{0:T(512)} %copy-done.20) | copy-start | bytes 6148
  770.8 149.5 %copy-start.24 = (f32[512]{0:T(512)S(1)}, f32[512]{0:T(512)}, u32[]{:S(2)}) copy-start(f32[512]{0:T(512)} %get-tuple-element.93) | copy-start | bytes 6148
  770.8 556.8 %all-reduce.6.cloned.1.call-start = ((), (), s32[]{:S(2)}) async-start(), calls=%async_computation.18 | async-start | bytes 20971520
  925.2 4.5 collective-permute-start.6
  938.9 63.7 %copy-start.8 = (bf16[1024,2048]{1,0:T(8,128)(2,1)S(1)}, bf16[1024,2048]{1,0:T(8,128)(2,1)}, u32[]{:S(2)}) copy-start(bf16[1024,2048]{1,0:T(8,128)(2,1)} %maximum_select_fusion.2.a_ref) | copy-start | bytes 12582916
  1064.2 8.9 collective-permute-start.9
  1083.5 399.5 %reduce-scatter.14.cloned.1.call-start = ((), (), s32[]{:S(2)}) async-start(), calls=%async_computation.14 | async-start | bytes 7864320 | tf_op jit(solution)/shard_map/reduce_scatter | solution.py:775
  1341.6 251.8 %reduce-scatter.10.cloned.1.call-start = ((), (), s32[]{:S(2)}) async-start(), calls=%async_computation.10 | async-start | bytes 10485760 | tf_op jit(solution)/shard_map/reduce_scatter | solution.py:714
  1384.8 299.6 %reduce-scatter.20.cloned.1.call-start = ((), (), s32[]{:S(2)}) async-start(), calls=%async_computation.17 | async-start | bytes 9437184 | tf_op jit(solution)/shard_map/reduce_scatter | solution.py:723
  1411.1 393.5 %reduce-scatter.18.cloned.1.call-start = ((), (), s32[]{:S(2)}) async-start(), calls=%async_computation.16 | async-start | bytes 18874368 | tf_op jit(solution)/shard_map/reduce_scatter | solution.py:723
  1464.5 4.2 collective-permute-start.7
  1478.3 136.1 %copy-start.28 = (s32[4]{0:T(128)S(1)}, s32[4]{0:T(128)}, u32[]{:S(2)}) copy-start(s32[4]{0:T(128)} %get-tuple-element.96) | copy-start | bytes 52
  1478.3 132.2 %all-to-all-start = ((bf16[1,512,4,512]{3,1,0,2:T(8,128)(2,1)}), bf16[1,512,4,512]{3,1,0,2:T(8,128)(2,1)S(1)}, u32[]{:S(2)}, u32[]{:S(2)}) async-start(bf16[1,512,4,512]{3,1,0,2:T(8,128)(2,1)} %copy.86), calls=%async_computation.2 | async-start | bytes 4194304 | tf_op jit(solution)/shard_map/all_to_all | solution.py:753
  1483.1 376.0 %reduce-scatter.16.cloned.1.call-start = ((), (), s32[]{:S(2)}) async-start(), calls=%async_computation.15 | async-start | bytes 3276800 | tf_op jit(solution)/shard_map/reduce_scatter | solution.py:778
  1593.3 21.2 %collective-permute-start.4 = (bf16[4,512,512]{2,1,0:T(8,128)(2,1)}, bf16[4,512,512]{2,1,0:T(8,128)(2,1)}, u32[]{:S(2)}, u32[]{:S(2)}) collective-permute-start(bf16[4,512,512]{2,1,0:T(8,128)(2,1)} %reduce-scatter.10.cloned.1.call-done), channel_id=1, source_target_pairs={{0,0},{4,8},{8,4},{12,12},{16,16},{20,24},{24,20},{28,28},{1,1},{5... | collective-permute-start | bytes 6291464 | tf_op jit(solution)/shard_map/ppermute | solution.py:718
  1611.9 198.6 %collective-permute-start.8 = (bf16[4,512,512]{2,1,0:T(8,128)(2,1)}, bf16[4,512,512]{2,1,0:T(8,128)(2,1)S(1)}, u32[]{:S(2)}, u32[]{:S(2)}) collective-permute-start(bf16[4,512,512]{2,1,0:T(8,128)(2,1)} %bitcast.123), channel_id=1, source_target_pairs={{0,0},{4,8},{8,4},{12,12},{16,16},{20,24},{24,20},{28,28},{1,1},{5... | collective-permute-start | bytes 6291464 | tf_op jit(solution)/shard_map/ppermute | solution.py:756
  1614.5 72.7 %copy-start.22 = (f32[2048]{0:T(1024)S(1)}, f32[2048]{0:T(1024)}, u32[]{:S(2)}) copy-start(f32[2048]{0:T(1024)} %get-tuple-element.66) | copy-start | bytes 24580
  (24 other events, 124.8 us)
Sparse Core Ops, SparseCore 0:
  9.6 60.9 all-gather.11
  72.7 58.2 all-gather.7
  339.4 167.4 all-gather.5
  508.3 147.8 all-gather.13
  657.6 32.6 all-gather.9
  770.9 144.4 reduce-scatter.11
  1083.6 243.9 all-reduce.5
  1341.7 66.3 reduce-scatter.13
  1410.5 182.8 reduce-scatter.9
  1596.6 87.7 reduce-scatter.19
  1688.5 116.1 reduce-scatter.17
  1806.9 52.0 reduce-scatter.15

commit v2 on v1

--- a/solution.py
+++ b/solution.py
@@ -214,7 +214,24 @@
 
 
 def start_kernel(
-    cols, tok_ref, pq_ref, po_ref, x_ref, wq_ref, wo_ref, tok_sems, q_sems, o_sems, qx_sems, ox_sems, local_sems
+    cols,
+    tok_ref,
+    pq_ref,
+    po_ref,
+    gain_ref,
+    x_ref,
+    a_ref,
+    wq_ref,
+    wo_ref,
+    x_buf,
+    a_buf,
+    tok_sems,
+    q_sems,
+    o_sems,
+    qx_sems,
+    ox_sems,
+    a_sems,
+    local_sems,
 ):
     group, core, mate, row, col = place()
     width = tok_ref.shape[2]
@@ -234,13 +251,15 @@
     for step in range(1, cols):
         greet((mate, core, line(step)))
         greet((group, row, line(step)))
+    sibling = (group + 1 - 2 * core, row, col)
     greet((group, 1 - row, col))
+    greet(sibling)
 
     @pl.when(core != row)
     def _():
         greet((mate, core, col))
 
-    pl.semaphore_wait(barrier, 2 * cols - 1 + (core - row) * (core - row))
+    pl.semaphore_wait(barrier, 2 * cols + (core - row) * (core - row))
 
     def remote(src, dst, sems, at, device):
         return pltpu.make_async_remote_copy(
@@ -284,14 +303,14 @@
     def token_copy(step, into):
         return remote(
             tok_ref.at[line(step)],
-            x_ref.at[:, start_at(into, width)],
+            x_buf.at[:, start_at(into, width)],
             tok_sems,
             step,
             (mate, core, line(step)),
         )
 
     own_tokens = pltpu.make_async_copy(
-        tok_ref.at[col], x_ref.at[:, start_at(col, width)], local_sems.at[2]
+        tok_ref.at[col], x_buf.at[:, start_at(col, width)], local_sems.at[2]
     )
     for step in range(1, cols):
         token_copy(step, col).start()
@@ -313,24 +332,51 @@
         copy.start()
     o_across[0].start()
     for step in range(1, cols):
+        token_copy(step, line(-step)).wait_recv()
+
+    @pl.when(core != row)
+    def _():
+        token_copy(0, col).wait_recv()
+
+    @pl.when(core == row)
+    def _():
+        own_tokens.wait()
+
+    keep_x = pltpu.make_async_copy(x_buf, x_ref, local_sems.at[3])
+    keep_x.start()
+    length = x_buf.shape[0]
+    tall = min(64, length)
+
+    @pl.loop(0, length // tall)
+    def _(at):
+        here = pl.ds(pl.multiple_of(at * tall, tall), tall)
+        now = x_buf[here, :].astype(jnp.float32)
+        scale = lax.rsqrt(jnp.mean(now * now, axis=1, keepdims=True) + EPSILON)
+        a_buf[here, :] = (now * scale * gain_ref[...]).astype(jnp.bfloat16)
+
+    def a_copy(of_core):
+        return remote(a_buf, a_ref.at[start_at(of_core, length)], a_sems, 0, sibling)
+
+    own_a = pltpu.make_async_copy(a_buf, a_ref.at[start_at(core, length)], local_sems.at[4])
+    a_copy(core).start()
+    own_a.start()
+    for step in range(1, cols):
         q_arrive[step - 1].wait_recv()
         q_across[step].start()
     for step in range(1, cols):
         o_arrive[step - 1].wait_recv()
         o_across[step].start()
     for step in range(1, cols):
-        token_copy(step, line(-step)).wait_recv()
         token_copy(step, col).wait_send()
 
     @pl.when(core != row)
     def _():
-        token_copy(0, col).wait_recv()
         token_copy(0, col).wait_send()
 
-    @pl.when(core == row)
-    def _():
-        own_tokens.wait()
-
+    keep_x.wait()
+    own_a.wait()
+    a_copy(core).wait_send()
+    a_copy(1 - core).wait_recv()
     own_q.wait()
     own_o.wait()
     for copy in q_along + o_along + q_across + o_across:
@@ -339,23 +385,33 @@
         copy.wait_recv()
 
 
-def start_exchange(tokens, pack_q, pack_o, rows, cols):
+def start_exchange(tokens, pack_q, pack_o, gain, rows, cols):
     anywhere = pl.BlockSpec(memory_space=pl.ANY)
     seqs, length, width = tokens.shape
     weight_rows = pack_q.shape[0]
+    full = width * cols
     return pl.pallas_call(
         functools.partial(start_kernel, cols),
         out_shape=(
-            jax.ShapeDtypeStruct((length, width * cols), tokens.dtype),
+            jax.ShapeDtypeStruct((length, full), tokens.dtype),
+            jax.ShapeDtypeStruct((2 * length, full), tokens.dtype),
             jax.ShapeDtypeStruct((weight_rows * rows, pack_q.shape[1] * cols), pack_q.dtype),
             jax.ShapeDtypeStruct((weight_rows * rows, pack_o.shape[1] * cols), pack_o.dtype),
         ),
-        in_specs=[anywhere] * 3,
-        out_specs=(anywhere,) * 3,
-        scratch_shapes=[pltpu.SemaphoreType.DMA((2, cols))] * 5 + [pltpu.SemaphoreType.DMA((3,))],
-        compiler_params=pltpu.CompilerParams(collective_id=1, has_side_effects=True),
+        in_specs=[anywhere] * 3 + [pl.BlockSpec(memory_space=pltpu.VMEM)],
+        out_specs=(anywhere,) * 4,
+        scratch_shapes=[
+            pltpu.VMEM((length, full), tokens.dtype),
+            pltpu.VMEM((length, full), tokens.dtype),
+        ]
+        + [pltpu.SemaphoreType.DMA((2, cols))] * 5
+        + [pltpu.SemaphoreType.DMA((2, 1)), pltpu.SemaphoreType.DMA((5,))],
+        compiler_params=pltpu.CompilerParams(
+            collective_id=1, has_side_effects=True, vmem_limit_bytes=16 << 20
+        ),
+        cost_estimate=pl.CostEstimate(flops=0, bytes_accessed=400 << 20, transcendentals=0),
         name="start_exchange",
-    )(tokens, pack_q, pack_o)
+    )(tokens, pack_q, pack_o, gain.reshape(1, full))
 
 
 def half_turn(wide):
@@ -409,7 +465,8 @@
         for part in range(heads // 2 + 1):
             lanes = slice(part * PAIR, (part + 1) * PAIR)
             now = lin[:, lanes]
-            now = now * cos_ref[here, lanes] + half_turn(now) * sin_ref[here, lanes]
+            table = slice(0, PAIR) if part < heads // 2 else slice(PAIR, 2 * PAIR)
+            now = now * cos_ref[here, table] + half_turn(now) * sin_ref[here, table]
             qkv_ref[here, lanes] = now.astype(jnp.bfloat16)
             if part < heads // 2:
                 for side in range(2):
@@ -461,8 +518,8 @@
             pl.BlockSpec(memory_space=pltpu.SMEM),
             pl.BlockSpec((rows, depth), lambda g: (0, 0)),
             pl.BlockSpec((depth, wide), lambda g: (0, g)),
-            pl.BlockSpec((rows, wide), lambda g: (0, 0)),
-            pl.BlockSpec((rows, wide), lambda g: (0, 0)),
+            pl.BlockSpec((rows, 2 * PAIR), lambda g: (0, 0)),
+            pl.BlockSpec((rows, 2 * PAIR), lambda g: (0, 0)),
         ],
         out_specs=(
             pl.BlockSpec((rows, wide), lambda g: (0, g)),
@@ -506,8 +563,8 @@
         k_acc[here, :] = jnp.zeros((block, PAIR), jnp.float32)
         v_acc[here, :] = jnp.zeros((block, PAIR), jnp.float32)
 
-    def turn_back(now, here, lanes):
-        return (now * cos_ref[here, lanes] - half_turn(now) * sin_ref[here, lanes]).astype(
+    def turn_back(now, here, table):
+        return (now * cos_ref[here, table] - half_turn(now) * sin_ref[here, table]).astype(
             jnp.bfloat16
         )
 
@@ -535,7 +592,9 @@
             high = one_head(2 * pair + 1)
             lane = lax.broadcasted_iota(jnp.int32, low.shape, 1)
             lanes = slice(pair * PAIR, (pair + 1) * PAIR)
-            out_ref[here, lanes] = turn_back(jnp.where(lane < HEAD_SIZE, low, high), here, lanes)
+            out_ref[here, lanes] = turn_back(
+                jnp.where(lane < HEAD_SIZE, low, high), here, slice(0, PAIR)
+            )
 
     @pl.loop(0, rows // block)
     def _(at):
@@ -545,7 +604,9 @@
         values = values + pltpu.roll(values, HEAD_SIZE, 1)
         lane = lax.broadcasted_iota(jnp.int32, keys.shape, 1)
         lanes = slice(heads * HEAD_SIZE, heads * HEAD_SIZE + PAIR)
-        out_ref[here, lanes] = turn_back(jnp.where(lane < HEAD_SIZE, keys, values), here, lanes)
+        out_ref[here, lanes] = turn_back(
+            jnp.where(lane < HEAD_SIZE, keys, values), here, slice(PAIR, 2 * PAIR)
+        )
 
 
 def attend_back_fast(length, projected, grad_mixed, cosines, sines, groups):
@@ -561,8 +622,8 @@
             pl.BlockSpec(memory_space=pltpu.SMEM),
             pl.BlockSpec((rows, wide), lambda g: (0, g)),
             pl.BlockSpec((rows, heads * HEAD_SIZE), lambda g: (0, g)),
-            pl.BlockSpec((rows, wide), lambda g: (0, 0)),
-            pl.BlockSpec((rows, wide), lambda g: (0, 0)),
+            pl.BlockSpec((rows, 2 * PAIR), lambda g: (0, 0)),
+            pl.BlockSpec((rows, 2 * PAIR), lambda g: (0, 0)),
         ],
         out_specs=pl.BlockSpec((rows, wide), lambda g: (0, g)),
         scratch_shapes=[
@@ -581,6 +642,583 @@
         ),
         name="attend_back",
     )(length, projected, grad_mixed, cosines, sines)
+
+
+def ffn_kernel(
+    cols,
+    own_ref,
+    resid_ref,
+    grad_ref,
+    wg_own,
+    wu_own,
+    wd_own,
+    wg_far,
+    wu_far,
+    wd_far,
+    wg_sib,
+    wu_sib,
+    wd_sib,
+    b_all,
+    u_all,
+    dgu_all,
+    mlp_all,
+    back_all,
+    wg,
+    wu,
+    wd,
+    b_buf,
+    g_buf,
+    u_buf,
+    dg_buf,
+    du_buf,
+    mlp_buf,
+    back_buf,
+    w_sems,
+    ag_send,
+    ag_recv,
+    back_send,
+    back_recv,
+    io_sems,
+):
+    group, core, mate, row, col = place()
+    last = cols - 1
+    depth = wg_own.shape[0]
+    half = depth // 2
+    units = wg_own.shape[1]
+    tile = min(512, units)
+
+    barrier = pltpu.get_barrier_semaphore()
+    for step in range(1, cols):
+        pl.semaphore_signal(
+            barrier,
+            inc=1,
+            device_id=(group, row, lax.rem(col + step, cols)),
+            device_id_type=MESH_IDS,
+        )
+    pl.semaphore_wait(barrier, cols - 1)
+
+    def pass_on(src, at, to, way):
+        return pltpu.make_async_remote_copy(
+            src_ref=src,
+            dst_ref=b_all.at[at],
+            send_sem=ag_send.at[way, at],
+            recv_sem=ag_recv.at[at],
+            device_id=(group, row, to),
+            device_id_type=MESH_IDS,
+        )
+
+    @pl.when(col < last)
+    def _():
+        pass_on(own_ref, col, col + 1, 0).start()
+
+    @pl.when(col > 0)
+    def _():
+        pass_on(own_ref, col, col - 1, 1).start()
+
+    def rows_at(first, size):
+        return pl.ds(pl.multiple_of(first, half), size)
+
+    own_copy = pltpu.make_async_copy(own_ref, b_all.at[col], io_sems.at[0])
+    own_copy.start()
+    load_resid = pltpu.make_async_copy(resid_ref, mlp_buf, io_sems.at[8])
+    load_resid.start()
+    far = (1 - row) * depth
+    loads = []
+    for at, (full, mine, across, sibling) in enumerate(
+        ((wg, wg_own, wg_far, wg_sib), (wu, wu_own, wu_far, wu_sib), (wd, wd_own, wd_far, wd_sib))
+    ):
+        loads += [
+            pltpu.make_async_copy(mine, full.at[rows_at(row * depth, depth)], w_sems.at[3 * at]),
+            pltpu.make_async_copy(
+                across, full.at[rows_at(far + core * half, half)], w_sems.at[3 * at + 1]
+            ),
+            pltpu.make_async_copy(
+                sibling, full.at[rows_at(far + (1 - core) * half, half)], w_sems.at[3 * at + 2]
+            ),
+        ]
+    for load in loads:
+        load.start()
+    own_copy.wait()
+    for load in loads:
+        load.wait()
+
+    def order(at):
+        inner_low = jnp.where(at < 2, 1 - at, at)
+        inner_high = jnp.where(at == 3, 0, jnp.where(at == 0, 2, jnp.where(at == 1, 1, 3)))
+        return jnp.where(
+            col == 0,
+            at,
+            jnp.where(col == last, last - at, jnp.where(col == 1, inner_low, inner_high)),
+        )
+
+    def arrive(chunk):
+        pass_on(b_all.at[chunk], chunk, col, 0).wait_recv()
+
+        @pl.when((chunk < col) & (col < last))
+        def _():
+            pass_on(b_all.at[chunk], chunk, col + 1, 0).start()
+
+        @pl.when((chunk > col) & (col > 0))
+        def _():
+            pass_on(b_all.at[chunk], chunk, col - 1, 1).start()
+
+    def outputs(chunk):
+        return (
+            pltpu.make_async_copy(u_buf, u_all.at[chunk], io_sems.at[1]),
+            pltpu.make_async_copy(dg_buf, dgu_all.at[chunk, :, 0:units], io_sems.at[2]),
+            pltpu.make_async_copy(du_buf, dgu_all.at[chunk, :, units : 2 * units], io_sems.at[3]),
+        )
+
+    def mlp_out(chunk):
+        return pltpu.make_async_copy(mlp_buf, mlp_all.at[chunk], io_sems.at[4])
+
+    def back_out(at, chunk):
+        return pltpu.make_async_remote_copy(
+            src_ref=back_buf.at[at],
+            dst_ref=back_all.at[col],
+            send_sem=back_send.at[at],
+            recv_sem=back_recv.at[col],
+            device_id=(group, row, chunk),
+            device_id_type=MESH_IDS,
+        )
+
+    own_back = pltpu.make_async_copy(back_buf.at[0], back_all.at[col], io_sems.at[5])
+    at_end = (col == 0) | (col == last)
+
+    def one_chunk(at, unused):
+        chunk = order(at)
+
+        @pl.when(at_end & (at > 0))
+        def _():
+            arrive(order(at))
+
+        @pl.when(jnp.logical_not(at_end) & (at == 1))
+        def _():
+            arrive(order(1))
+            arrive(order(2))
+
+        @pl.when(jnp.logical_not(at_end) & (at == 3))
+        def _():
+            arrive(order(3))
+
+        load_b = pltpu.make_async_copy(b_all.at[chunk], b_buf, io_sems.at[6])
+        load_g = pltpu.make_async_copy(grad_ref.at[chunk], g_buf, io_sems.at[7])
+        load_b.start()
+        load_g.start()
+
+        @pl.when(at > 0)
+        def _():
+            for copy in outputs(order(at - 1)):
+                copy.wait()
+
+        load_b.wait()
+        load_g.wait()
+
+        @pl.loop(0, units // tile)
+        def _(step):
+            lanes = pl.ds(pl.multiple_of(step * tile, tile), tile)
+            gate = dot_nn(b_buf[...], wg[:, lanes])
+            upward = dot_nn(b_buf[...], wu[:, lanes])
+            back = dot_nn(g_buf[...], wd[:, lanes])
+            opened = 1.0 / (1.0 + jnp.exp(-gate))
+            silu = gate * opened
+            u_buf[:, lanes] = (silu * upward).astype(jnp.bfloat16)
+            slope = opened * (1.0 + gate * (1.0 - opened))
+            dg_buf[:, lanes] = (back * upward * slope).astype(jnp.bfloat16)
+            du_buf[:, lanes] = (back * silu).astype(jnp.bfloat16)
+
+        for copy in outputs(chunk):
+            copy.start()
+
+        @pl.when(at > 0)
+        def _():
+            mlp_out(order(at - 1)).wait()
+
+        @pl.when(at == 0)
+        def _():
+            load_resid.wait()
+
+        @pl.loop(0, 2 * depth // tile)
+        def _(step):
+            here = pl.ds(pl.multiple_of(step * tile, tile), tile)
+            back = dot_nt(dg_buf[...], wg[here, :]) + dot_nt(du_buf[...], wu[here, :])
+            back_buf[at, :, here] = back.astype(jnp.bfloat16)
+            added = jnp.where(at == 0, mlp_buf[:, here].astype(jnp.float32), 0.0)
+            mlp_buf[:, here] = (added + RES_MULT * dot_nt(u_buf[...], wd[here, :])).astype(
+                jnp.bfloat16
+            )
+
+        mlp_out(chunk).start()
+
+        @pl.when(at == 0)
+        def _():
+            own_back.start()
+
+        @pl.when(at > 0)
+        def _():
+            back_out(at, chunk).start()
+
+        return unused
+
+    lax.fori_loop(0, cols, one_chunk, 0)
+    for copy in outputs(order(last)):
+        copy.wait()
+    mlp_out(order(last)).wait()
+    own_back.wait()
+    for at in range(1, cols):
+        back_out(at, order(at)).wait_send()
+        source = lax.rem(col + at, cols)
+        pltpu.make_async_remote_copy(
+            src_ref=back_buf.at[at],
+            dst_ref=back_all.at[source],
+            send_sem=back_send.at[at],
+            recv_sem=back_recv.at[source],
+            device_id=(group, row, source),
+            device_id_type=MESH_IDS,
+        ).wait_recv()
+    for chunk in range(cols):
+
+        @pl.when((col >= chunk) & (col < last))
+        def _():
+            pass_on(own_ref, chunk, col + 1, 0).wait_send()
+
+        @pl.when((col <= chunk) & (col > 0))
+        def _():
+            pass_on(own_ref, chunk, col - 1, 1).wait_send()
+
+
+def feed_forward(own_input, resid, grad_rows, weights, cols):
+    rows, width = own_input.shape
+    units = weights[0].shape[1]
+    anywhere = pl.BlockSpec(memory_space=pl.ANY)
+    bf16 = jnp.bfloat16
+    return pl.pallas_call(
+        functools.partial(ffn_kernel, cols),
+        out_shape=(
+            jax.ShapeDtypeStruct((cols, rows, width), bf16),
+            jax.ShapeDtypeStruct((cols, rows, units), bf16),
+            jax.ShapeDtypeStruct((cols, rows, 2 * units), bf16),
+            jax.ShapeDtypeStruct((cols, rows, width), bf16),
+            jax.ShapeDtypeStruct((cols, rows, width), bf16),
+        ),
+        in_specs=[anywhere] * 12,
+        out_specs=(anywhere,) * 5,
+        scratch_shapes=[
+            pltpu.VMEM((width, units), bf16),
+            pltpu.VMEM((width, units), bf16),
+            pltpu.VMEM((width, units), bf16),
+            pltpu.VMEM((rows, width), bf16),
+            pltpu.VMEM((rows, width), bf16),
+            pltpu.VMEM((rows, units), bf16),
+            pltpu.VMEM((rows, units), bf16),
+            pltpu.VMEM((rows, units), bf16),
+            pltpu.VMEM((rows, width), bf16),
+            pltpu.VMEM((cols, rows, width), bf16),
+            pltpu.SemaphoreType.DMA((9,)),
+            pltpu.SemaphoreType.DMA((2, cols)),
+            pltpu.SemaphoreType.DMA((cols,)),
+            pltpu.SemaphoreType.DMA((cols,)),
+            pltpu.SemaphoreType.DMA((cols,)),
+            pltpu.SemaphoreType.DMA((9,)),
+        ],
+        compiler_params=pltpu.CompilerParams(
+            collective_id=2, has_side_effects=True, vmem_limit_bytes=60 << 20
+        ),
+        cost_estimate=pl.CostEstimate(
+            flops=12 * cols * rows * width * units,
+            bytes_accessed=800 << 20,
+            transcendentals=cols * rows * units,
+        ),
+        name="feed_forward",
+    )(own_input, resid, grad_rows, *weights)
+
+
+def finish_kernel(
+    cols,
+    ig_ref,
+    gq_ref,
+    go_ref,
+    gain_ref,
+    gin_ref,
+    sq_ref,
+    so_ref,
+    gsum_ref,
+    q_keep,
+    q_sib,
+    q_a1,
+    q_a2,
+    q_b1,
+    q_b2,
+    q_z,
+    o_keep,
+    o_sib,
+    o_a1,
+    o_a2,
+    o_b1,
+    o_b2,
+    o_z,
+    gain_now,
+    gain_in,
+    ig_sems,
+    gain_sems,
+    q_sems,
+    o_sems,
+    qz_sems,
+    oz_sems,
+    local_sems,
+):
+    group, core, mate, row, col = place()
+    pair = group - core
+    high = pair // 2
+    sibling = (pair + 1 - core, row, col)
+    over_x = (group, 1 - row, col)
+    over_y = (2 * (1 - high) + core, row, col)
+    width = gin_ref.shape[2]
+
+    def line(step):
+        return lax.rem(col + step + cols, cols)
+
+    barrier = pltpu.get_barrier_semaphore()
+
+    def greet(device):
+        pl.semaphore_signal(barrier, inc=1, device_id=device, device_id_type=MESH_IDS)
+
+    greet(sibling)
+    greet(over_x)
+    greet(over_y)
+    for step in range(1, cols):
+        greet((mate, core, line(step)))
+        greet((group, row, line(step)))
+
+    @pl.when(core != row)
+    def _():
+        greet((mate, core, col))
+
+    pl.semaphore_wait(barrier, 2 * cols + 1 + (core - row) * (core - row))
+
+    def remote(src, dst, sems, at, device):
+        return pltpu.make_async_remote_copy(
+            src_ref=src,
+            dst_ref=dst,
+            send_sem=sems.at[0, at],
+            recv_sem=sems.at[1, at],
+            device_id=device,
+            device_id_type=MESH_IDS,
+        )
+
+    def lanes(block, size):
+        return pl.ds(pl.multiple_of(block * size, size), size)
+
+    matrices = (
+        (gq_ref, sq_ref, q_keep, q_sib, q_a1, q_a2, q_b1, q_b2, q_z, q_sems, qz_sems),
+        (go_ref, so_ref, o_keep, o_sib, o_a1, o_a2, o_b1, o_b2, o_z, o_sems, oz_sems),
+    )
+
+    def moves(m):
+        grads, out, keep, sib, a1, a2, b1, b2, zb, sems, z_sems = matrices[m]
+        return dict(
+            s0=remote(grads.at[:, 1 - core], sib, sems, 0, sibling),
+            a1=remote(grads.at[:, core, 1 - row], a1, sems, 1, over_x),
+            a2=remote(keep.at[1 - high, row], a2, sems, 2, over_y),
+            b1=remote(sib.at[1 - high], b1, sems, 3, over_y),
+            b2=remote(sib.at[high, 1 - row], b2, sems, 4, over_x),
+            own=pltpu.make_async_copy(grads.at[:, core], keep, local_sems.at[m]),
+        )
+
+    copies = (moves(0), moves(1))
+
+    def rows_plus(into, more):
+        rows = into.shape[0]
+        step = min(32, rows)
+
+        @pl.loop(0, rows // step)
+        def _(at):
+            here = pl.ds(pl.multiple_of(at * step, step), step)
+            into[here, :] = (
+                into[here, :].astype(jnp.float32) + more[here, :].astype(jnp.float32)
+            ).astype(into.dtype)
+
+    def token_copy(step, at):
+        return remote(
+            ig_ref.at[:, lanes(line(step), width)],
+            gin_ref.at[at],
+            ig_sems,
+            step,
+            (mate, core, line(step)),
+        )
+
+    own_tokens = pltpu.make_async_copy(
+        ig_ref.at[:, lanes(col, width)], gin_ref.at[col], local_sems.at[2]
+    )
+
+    for m in range(2):
+        copies[m]["s0"].start()
+        copies[m]["a1"].start()
+        copies[m]["own"].start()
+    for step in range(1, cols):
+        token_copy(step, col).start()
+
+    @pl.when(core != row)
+    def _():
+        token_copy(0, col).start()
+
+    @pl.when(core == row)
+    def _():
+        own_tokens.start()
+
+    gain_load = pltpu.make_async_copy(gain_ref, gain_now.at[0], local_sems.at[3])
+    gain_load.start()
+    gain_load.wait()
+    near = (
+        sibling,
+        over_x,
+        over_y,
+        (group, row, col + 1 - 2 * lax.rem(col, 2)),
+        (group, row, lax.rem(col + cols // 2, cols)),
+    )
+
+    def gain_round(at):
+        exchange = remote(gain_now.at[at], gain_in.at[at], gain_sems, at, near[at])
+        exchange.start()
+        exchange.wait()
+        gain_now[at + 1] = gain_now[at] + gain_in[at]
+
+    gain_round(0)
+    for m in range(2):
+        copies[m]["s0"].wait()
+        copies[m]["b1"].start()
+    gain_round(1)
+    for m in range(2):
+        grads, out, keep, sib, a1, a2, b1, b2, zb, sems, z_sems = matrices[m]
+        copies[m]["own"].wait()
+        copies[m]["a1"].wait()
+        rows_plus(keep.at[1 - high, row], a1.at[1 - high])
+        copies[m]["a2"].start()
+    for m in range(2):
+        grads, out, keep, sib, a1, a2, b1, b2, zb, sems, z_sems = matrices[m]
+        copies[m]["b1"].wait()
+        rows_plus(sib.at[high, 1 - row], b1.at[1 - row])
+        copies[m]["b2"].start()
+    gain_round(2)
+    for m in range(2):
+        grads, out, keep, sib, a1, a2, b1, b2, zb, sems, z_sems = matrices[m]
+        rows_plus(keep.at[high, row], a1.at[high])
+        rows_plus(sib.at[high, row], b1.at[row])
+
+    def z_moves(m, side, source):
+        grads, out, keep, sib, a1, a2, b1, b2, zb, sems, z_sems = matrices[m]
+        held = (keep, sib)[side]
+        wide = zb.shape[3]
+        return [
+            pltpu.make_async_remote_copy(
+                src_ref=held.at[high, row, :, lanes(line(step), wide)],
+                dst_ref=zb.at[side, line(source(step))],
+                send_sem=z_sems.at[0, side, step],
+                recv_sem=z_sems.at[1, side, step],
+                device_id=(group, row, line(step)),
+                device_id_type=MESH_IDS,
+            )
+            for step in range(1, cols)
+        ]
+
+    for side, last_copy in ((0, "a2"), (1, "b2")):
+        for m in range(2):
+            grads, out, keep, sib, a1, a2, b1, b2, zb, sems, z_sems = matrices[m]
+            copies[m][last_copy].wait()
+            rows_plus((keep, sib)[side].at[high, row], (a2, b2)[side])
+            for copy in z_moves(m, side, lambda step: 0):
+                copy.start()
+    gain_round(3)
+    gain_round(4)
+    gsum_ref[...] = gain_now[5]
+    for side in range(2):
+        for m in range(2):
+            grads, out, keep, sib, a1, a2, b1, b2, zb, sems, z_sems = matrices[m]
+            for copy in z_moves(m, side, lambda step: 0):
+                copy.wait_send()
+            for copy in z_moves(m, side, lambda step: -step):
+                copy.wait_recv()
+            held = (keep, sib)[side]
+            wide = zb.shape[3]
+            at_core = core if side == 0 else 1 - core
+            rows = zb.shape[2]
+            tall = min(32, rows)
+
+            @pl.loop(0, rows // tall)
+            def _(at):
+                here = pl.ds(pl.multiple_of(at * tall, tall), tall)
+                total = held[high, row, here, lanes(col, wide)].astype(jnp.float32)
+                for step in range(1, cols):
+                    total = total + zb[side, line(-step), here, :].astype(jnp.float32)
+                out[at_core, here, :] = total
+
+    for step in range(1, cols):
+        token_copy(step, line(-step)).wait_recv()
+        token_copy(step, col).wait_send()
+
+    @pl.when(core != row)
+    def _():
+        token_copy(0, col).wait_recv()
+        token_copy(0, col).wait_send()
+
+    @pl.when(core == row)
+    def _():
+        own_tokens.wait()
+
+
+def finish(input_grad, grad_q, grad_o, gains, cols):
+    anywhere = pl.BlockSpec(memory_space=pl.ANY)
+    in_vmem = pl.BlockSpec(memory_space=pltpu.VMEM)
+    bf16, f32 = jnp.bfloat16, jnp.float32
+    length, full = input_grad.shape
+    rows = grad_q.shape[0] // 8
+
+    def buffers(wide):
+        return [
+            pltpu.VMEM((2, 2, rows, wide), bf16),
+            pltpu.VMEM((2, 2, rows, wide), bf16),
+            pltpu.VMEM((2, rows, wide), bf16),
+            pltpu.VMEM((rows, wide), bf16),
+            pltpu.VMEM((2, rows, wide), bf16),
+            pltpu.VMEM((rows, wide), bf16),
+            pltpu.VMEM((2, cols, rows, wide // cols), bf16),
+        ]
+
+    wide_q, wide_o = grad_q.shape[1], grad_o.shape[1]
+    return pl.pallas_call(
+        functools.partial(finish_kernel, cols),
+        out_shape=(
+            jax.ShapeDtypeStruct((cols, length, full // cols), bf16),
+            jax.ShapeDtypeStruct((2, rows, wide_q // cols), f32),
+            jax.ShapeDtypeStruct((2, rows, wide_o // cols), f32),
+            jax.ShapeDtypeStruct(gains.shape, f32),
+        ),
+        in_specs=[anywhere] * 4,
+        out_specs=(anywhere, in_vmem, in_vmem, in_vmem),
+        scratch_shapes=buffers(wide_q)
+        + buffers(wide_o)
+        + [
+            pltpu.VMEM((6,) + gains.shape, f32),
+            pltpu.VMEM((5,) + gains.shape, f32),
+            pltpu.SemaphoreType.DMA((2, cols)),
+            pltpu.SemaphoreType.DMA((2, 5)),
+            pltpu.SemaphoreType.DMA((2, 5)),
+            pltpu.SemaphoreType.DMA((2, 5)),
+            pltpu.SemaphoreType.DMA((2, 2, cols)),
+            pltpu.SemaphoreType.DMA((2, 2, cols)),
+            pltpu.SemaphoreType.DMA((4,)),
+        ],
+        compiler_params=pltpu.CompilerParams(
+            collective_id=3, has_side_effects=True, vmem_limit_bytes=40 << 20
+        ),
+        cost_estimate=pl.CostEstimate(flops=0, bytes_accessed=300 << 20, transcendentals=0),
+        name="finish",
+    )(
+        input_grad,
+        grad_q.reshape(2, 2, 2, rows, wide_q),
+        grad_o.reshape(2, 2, 2, rows, wide_o),
+        gains,
+    )
 
 
 def one_sequence_body(
@@ -618,6 +1256,9 @@
     def from_sibling(value):
         return lax.ppermute(value, "dp", SIBLINGS)
 
+    def half_rows(matrix):
+        return core_half(matrix, 0)
+
     pack_q = jnp.concatenate(
         [
             core_half(w_query, 1),
@@ -627,8 +1268,10 @@
         axis=1,
     )
     pack_o = core_half(w_out, 1)
-    own_tokens, weights_qkv, weights_out = start_exchange(
-        tokens, pack_q, pack_o, row_count, col_count
+    gain_one = gain_attn.astype(jnp.float32)
+    gain_two = gain_ffn.astype(jnp.float32)
+    own_tokens, attn_input, weights_qkv, weights_out = start_exchange(
+        tokens, pack_q, pack_o, gain_one, row_count, col_count
     )
 
     length = lax.dynamic_slice_in_dim(lengths, mate * seq_group + col, 1)
@@ -637,16 +1280,14 @@
     line_live = (own_pos[None, :] < line_lengths[:, None]).astype(jnp.float32)
     own_live = (own_pos < length).astype(jnp.float32)[:, None]
 
-    def all_rows(matrix):
-        count = matrix.shape[0] // 4
-        part = lax.dynamic_slice_in_dim(matrix, group * count, count)
-        other = lax.all_gather(lax.ppermute(part, "row", OVER_X), "dp", axis=0, tiled=True)
-        return joined(matrix, other, row)
-
-    gate_up_weights = all_rows(w_gate_up)
-    down_weights = all_rows(w_down)
+    own_mats = (w_gate_up[:, 0], w_gate_up[:, 1], w_down)
+    halves = tuple(half_rows(matrix) for matrix in own_mats)
+    halves, attn_input = lax.optimization_barrier((halves, attn_input))
+    far_mats = tuple(lax.ppermute(matrix, "row", OVER_X) for matrix in halves)
+    sibling_mats = tuple(from_sibling(matrix) for matrix in far_mats)
 
     given = bring_cotangent(cotangent, deal_order, group * seq_group)
+    given, attn_input = lax.optimization_barrier((given, attn_input))
     swapped = lax.ppermute(given, ("dp", "row"), CROSSED)
     line_cot = lax.all_gather(swapped, "col", axis=2, tiled=True)
     line_grad = line_live[:, :, None] * line_cot.astype(jnp.float32)
@@ -656,24 +1297,16 @@
     )
 
     cosine_table, sine_table = rope_tables(jnp.arange(slot_len, dtype=jnp.int32), HEAD_SIZE)
-    turns = (query_half + kv_half) // HEAD_SIZE
+    cosine_table, sine_table = lax.optimization_barrier((cosine_table, sine_table))
     cosines = jnp.concatenate(
-        [jnp.tile(cosine_table, (1, 2 * turns)), jnp.ones((slot_len, kv_half), jnp.float32)], axis=1
-    )
+        [jnp.tile(cosine_table, (1, 6)), jnp.ones((slot_len, HEAD_SIZE), jnp.float32)], axis=1
+    )
+    turning = jnp.concatenate([-sine_table, sine_table], axis=1)
     sines = jnp.concatenate(
-        [
-            jnp.tile(jnp.concatenate([-sine_table, sine_table], axis=1), (1, turns)),
-            jnp.zeros((slot_len, kv_half), jnp.float32),
-        ],
-        axis=1,
-    )
-
-    gain_one = gain_attn.astype(jnp.float32)
-    gain_two = gain_ffn.astype(jnp.float32)
+        [jnp.tile(turning, (1, 3)), jnp.zeros((slot_len, HEAD_SIZE), jnp.float32)], axis=1
+    )
     own_float = own_tokens.astype(jnp.float32)
     scale_one = lax.rsqrt(jnp.mean(own_float * own_float, axis=1, keepdims=True) + EPSILON)
-    own_input = (own_float * scale_one * gain_one).astype(jnp.bfloat16)
-    attn_input = joined(own_input, from_sibling(own_input), core)
     projected, heads_out = attend_fast(
         length, attn_input, weights_qkv, cosines, sines, col_count
     )
@@ -689,29 +1322,19 @@
     scale_two = lax.rsqrt(jnp.mean(resid * resid, axis=1, keepdims=True) + EPSILON)
     own_ffn = (resid * scale_two * gain_two).astype(jnp.bfloat16)
 
-    ffn_input = lax.all_gather(own_ffn, "col", axis=0, tiled=True)
-    gate_up = contract_local(ffn_input, gate_up_weights)
-    gate = gate_up[:, 0]
-    upward = gate_up[:, 1]
-    sigmoid_gate = jax.nn.sigmoid(gate)
-    silu_gate = gate * sigmoid_gate
-    hidden_rows = (silu_gate * upward).astype(jnp.bfloat16)
-    grad_hidden = contract_local(grad_ffn, down_weights)
-    slope = sigmoid_gate * (1.0 + gate * (1.0 - sigmoid_gate))
-    grad_gate_rows = jnp.stack(
-        [grad_hidden * upward * slope, grad_hidden * silu_gate], axis=1
-    ).astype(jnp.bfloat16)
-    back_partial = expand_local(grad_gate_rows, gate_up_weights).astype(jnp.bfloat16)
-    grad_normed_two = lax.psum_scatter(
-        back_partial, "col", scatter_dimension=0, tiled=True
-    ).astype(jnp.float32)
-
-    mlp_partial = RES_MULT * expand_local(hidden_rows, down_weights)
-    is_own = (jnp.arange(col_count) == col).astype(jnp.float32)[:, None, None]
-    out_partial = (
-        mlp_partial.reshape(col_count, rows_local, full_width) + is_own * resid[None]
-    ).astype(jnp.bfloat16)
-    out_cols = lax.psum_scatter(out_partial, "col", scatter_dimension=2, tiled=True)
+    ffn_input, hidden_rows, grad_gate_rows, mlp_part, back_part = feed_forward(
+        own_ffn,
+        resid.astype(jnp.bfloat16),
+        grad_ffn.reshape(col_count, rows_local, full_width),
+        own_mats + far_mats + sibling_mats,
+        col_count,
+    )
+    ffn_input = ffn_input.reshape(-1, full_width)
+    hidden_rows = hidden_rows.reshape(-1, hidden)
+    grad_gate_rows = grad_gate_rows.reshape(-1, 2 * hidden)
+    grad_normed_two = jnp.sum(back_part.astype(jnp.float32), axis=0)
+
+    out_cols = lax.psum_scatter(mlp_part, "col", scatter_dimension=2, tiled=True)
     given_pos = row * rows_local + jnp.arange(rows_local, dtype=jnp.int32)
     given_lengths = lax.dynamic_slice_in_dim(lengths, group * seq_group, seq_group)
     given_live = (given_pos[None, :] < given_lengths[:, None]).astype(jnp.float32)
@@ -726,6 +1349,7 @@
 
     sums_down = scatter_rows(token_outer(grad_ffn, hidden_rows))
     sums_gate_up = scatter_rows(token_outer(ffn_input, grad_gate_rows))
+    sums_gate_up = sums_gate_up.reshape(-1, 2, hidden)
 
     weighted_two = grad_normed_two * gain_two
     inner_two = jnp.sum(weighted_two * resid, axis=1, keepdims=True)
@@ -750,43 +1374,26 @@
         - own_float * scale_one**3 * inner_one / full_width
     ).astype(jnp.bfloat16)
     gain_one_part = jnp.sum(grad_normed_one * own_float * scale_one, axis=0)
-    given_grad = lax.all_to_all(
-        own_input_grad.reshape(rows_local, col_count, width_local), "col", 1, 0
-    )
-    input_grad = lax.ppermute(given_grad, ("dp", "row"), CROSSED).astype(jnp.float32)
-    grad_gain_attn, grad_gain_ffn = lax.psum((gain_one_part, gain_two_part), ("dp", "row", "col"))
-
-    both = jnp.concatenate(
-        [
-            grad_qkv.reshape(full_width, col_count, -1),
-            grad_out.reshape(full_width, col_count, -1),
-        ],
-        axis=2,
-    )
-    both = both.reshape(2, 2, row_count, -1, col_count, both.shape[2])
-    kept = lax.dynamic_index_in_dim(both, core, 1, keepdims=False)
-    sent = from_sibling(lax.dynamic_index_in_dim(both, 1 - core, 1, keepdims=False))
-    cores = jnp.where(
-        core == 0, jnp.stack([kept, sent], axis=4), jnp.stack([sent, kept], axis=4)
-    )
-    cores = lax.psum_scatter(
-        cores, "row", scatter_dimension=1, tiled=False
-    )
-    cores = lax.psum_scatter(
-        cores, "dp", scatter_dimension=0, axis_index_groups=SAME_CORE, tiled=False
-    )
-    cores = lax.psum_scatter(cores, "col", scatter_dimension=1, tiled=False).astype(jnp.float32)
-    grad_rows = cores.shape[0]
+    gains = jnp.stack([gain_one_part, gain_two_part]).reshape(8, -1)
+    given_grad, sums_q, sums_o, gain_sums = finish(
+        own_input_grad, grad_qkv, grad_out, gains, col_count
+    )
+    input_grad = given_grad.astype(jnp.float32)
+    grad_gain_attn, grad_gain_ffn = gain_sums.reshape(2, full_width)
+
+    def both_cores(sums):
+        return jnp.concatenate([sums[0], sums[1]], axis=1)
+
     qk = query_half + kv_half
-    out_query = cores[:, :, :query_half].reshape(grad_rows, -1)
+    out_query = both_cores(sums_q[:, :, :query_half])
     out_kv = jnp.stack(
         [
-            cores[:, :, query_half:qk].reshape(grad_rows, -1),
-            cores[:, :, qk : qk + kv_half].reshape(grad_rows, -1),
+            both_cores(sums_q[:, :, query_half:qk]),
+            both_cores(sums_q[:, :, qk:]),
         ],
         axis=1,
     )
-    out_out = cores[:, :, qk + kv_half :].reshape(grad_rows, -1)
+    out_out = both_cores(sums_o)
     return (
         layer_out,
         input_grad,

time: 1880 us -> 1280 us (0.68)
  waiting for transfers between devices: 927 us -> 80.9 us
  Pallas kernels: 300 us -> 862 us
  matrix products: 269 us -> 107 us
  other arithmetic: 158 us -> 48.8 us
  blocking collectives: 40.8 us -> 0 us
    pallas_call x0 -> x2, Pallas kernels: none -> 562 us  [the longest x1 328 us: feed_forward(): pl.pallas_call(functools.partial(ffn_kernel, cols), out_shape=(jax.ShapeD...]
    reduce_scatter x4 -> x1, waiting for transfers between devices: 300 us -> 0.02 us  [one_sequence_body(): lax.psum_scatter(mlp_part, 'col', scatter_dimension=2, tiled=True)]
    unnamed x13 -> x5, waiting for transfers between devices: 244 us -> 0.75 us
    reduce_scatter x2, waiting for transfers between devices: 142 us -> 0.01 us  [scatter_rows(): lax.psum_scatter(matrix.astype(jnp.bfloat16), ('dp', 'row'), scatter_dime...]
    select_n x3 -> x0, other arithmetic: 96.7 us -> none  [the longest x2 86.3 us: joined(): jnp.where(at == 0, jnp.concatenate([mine, other]), jnp.concatenate([other...]
    all_gather x1, waiting for transfers between devices: 105 us -> 18.9 us  [one_sequence_body(): line_cot = lax.all_gather(swapped, 'col', axis=2, tiled=True)]
    dot_general x4 -> x2, matrix products: 92.6 us -> 13.3 us  [expand_local(): lax.dot_general(operand, matrix, ((trailing, trailing), ((), ())), prefer...]
    dot_general x3 -> x1, matrix products: 87.2 us -> 8.31 us  [contract_local(): lax.dot_general(operand, matrix, (((1,), (0,)), ((), ())), preferred_elem...]
  transfers between devices with their start and end apart: 23 -> 16, of which waited for: 15 -> 4; matrix products, arithmetic and copies ran while one was open for 17% -> 18% of each run, Pallas kernels for 13% -> 42%
where the time goes in v2:
time: 1280 us; the launch traced here: 1260 us
  Pallas kernels  862 us (67%)
  matrix products  107 us (8%)
  local copies, waits for them, and re-layouts  91.5 us (7%)
  waiting for transfers between devices  80.9 us (6%)
  starting transfers between devices  50.2 us (4%)
  other arithmetic  48.8 us (4%)
  between operations  22.7 us (2%)
    pallas_call x1, Pallas kernels, feed_forward(): pl.pallas_call(functools.partial(ffn_kernel, cols), out_shape=(jax.ShapeD...  328 us
    pallas_call x1, Pallas kernels, finish(): pl.pallas_call(functools.partial(finish_kernel, cols), out_shape=(jax.Sha...  234 us
    pallas_call x1, Pallas kernels, start_exchange(): pl.pallas_call(functools.partial(start_kernel, cols), out_shape=(jax.Shap...  194 us
    dot_general x4, matrix products, token_outer(): lax.dot_general(features, grads, (((0,), (0,)), ((), ())), preferred_elem...  85.8 us
    pallas_call x1, Pallas kernels, attend_back_fast(): pl.pallas_call(functools.partial(attend_back_kernel, block), grid=(groups...  63.3 us
    ppermute x3, waiting for transfers between devices, one_sequence_body(): far_mats = tuple((lax.ppermute(matrix, 'row', OVER_X) for matrix in halves))  57 us
    unnamed x84, local copies, waits for them, and re-layouts  44.9 us
    pallas_call x1, Pallas kernels, attend_fast(): pl.pallas_call(functools.partial(attend_kernel, block), grid=(groups,), o...  43.2 us
  transfers between devices with their start and end apart: 16, of which 4 were waited for; matrix products, arithmetic and copies ran while one was open for 18% of the time, Pallas kernels for 42%

profile of v2, /device:TPU:0, one launch (start us, length us, event | category | flops | bytes accessed | tf_op | source)
XLA Modules:
  0.0 1263.9 jit_solution(5209313334800105542)
XLA Ops:
  18.0 16.4 %fusion.15 = (bf16[1024,1,2048]{2,1,0:T(2,128)(2,1)S(1)}, bf16[1024,1,2048]{2,1,0:T(2,128)(2,1)S(1)}) fusion(bf16[1024,2,2048]{2,1,0:T(2,128)(2,1)} %param.20), kind=kLoop, calls=%fused_computation.86 | loop fusion | bytes 16777216 | tf_op jit(solution)/shard_map/slice | solution.py:1283
  34.4 5.4 copy.64
  41.7 4.6 copy.65
  48.3 193.8 %start_exchange.1 = (bf16[512,2048]{1,0:T(8,128)(2,1)S(1)}, bf16[1024,2048]{1,0:T(8,128)(2,1)S(1)}, bf16[2048,1536]{1,0:T(8,128)(2,1)S(1)}, bf16[2048,1024]{1,0:T(8,128)(2,1)S(1)}) custom-call(bf16[4,512,512]{2,1,0:T(8,128)(2,1)S(1)} %copy-done.3, bf16[1024,384]{1,0:T(8,128)(2,1)S(1)} %pad_maximum_fusion.1.pq_ref, ...), custom_call_target="tpu_custom_call" | custom-call | bytes 419430400 | tf_op jit(solution)/shard_map/start_exchange/pallas_call | solution.py:393
  248.9 3.9 constant_dynamic-slice_fusion.2
  252.8 4.2 dynamic-slice_bitcast_fusion
  264.2 27.7 %collective-permute-start.2 = (bf16[512,2048]{1,0:T(8,128)(2,1)}, bf16[512,2048]{1,0:T(8,128)(2,1)}, u32[]{:S(2)}, u32[]{:S(2)}) collective-permute-start(bf16[512,2048]{1,0:T(8,128)(2,1)} %get-tuple-element.42), channel_id=1, source_target_pairs={{0,4},{4,0},{1,5},{5,1},{2,6},{6,2},{3,7},{7,3},{8,12},{12,8},{9,1... | collective-permute-start | bytes 6291464 | tf_op jit(solution)/shard_map/ppermute | solution.py:1286
  302.7 43.2 %attend.1 = (bf16[1024,1536]{1,0:T(8,128)(2,1)}, bf16[1024,1024]{1,0:T(8,128)(2,1)S(1)}) custom-call(s32[1]{0:T(128)} %dynamic_slice.86.len_ref, bf16[1024,2048]{1,0:T(8,128)(2,1)} %copy-done.9, bf16[2048,1536]{1,0:T(8,128)(2,1)} %copy-done.8, f32[1024,256]{1,0:T(8,128)S(1)} %copy-done.4, f32[1024,256]{1,0:T(8,128)S(1)} %concatenate.37.sin_ref), custom_call_target="tpu_custom_call" | custom-call | flops 10737418240 | bytes 13631488 | tf_op jit(solution)/shard_map/attend/pallas_call | solution.py:510
  345.9 5.0 convolution_convert_fusion.3
  353.5 8.1 copy.76
  361.6 8.0 copy.77
  371.0 12.6 collective-permute-done.3.wu_far
  383.6 44.4 %collective-permute-done.4.wd_far = bf16[512,2048]{1,0:T(8,128)(2,1)} collective-permute-done((bf16[512,2048]{1,0:T(8,128)(2,1)}, bf16[512,2048]{1,0:T(8,128)(2,1)}, u32[]{:S(2)}, u32[]{:S(2)}) %collective-permute-start.4) | collective-permute-done | bytes 2097184 | tf_op jit(solution)/shard_map/ppermute | solution.py:1286
  428.0 5.8 fusion.14
  437.5 18.9 %all-gather.5.cloned.1.call-done = bf16[4,512,2048]{2,1,0:T(8,128)(2,1)} async-done(((bf16[4,512,512]{2,1,0:T(8,128)(2,1)}), bf16[4,512,2048]{2,1,0:T(8,128)(2,1)}) %all-gather.5.cloned.1.call-update) | async-done | bytes 8388624 | tf_op jit(solution)/shard_map/all_gather | solution.py:1292
  456.4 8.6 multiply_convert_fusion.grad_ref
  465.1 328.0 %feed_forward.1 = (bf16[4,512,2048]{2,1,0:T(8,128)(2,1)}, bf16[4,512,2048]{2,1,0:T(8,128)(2,1)}, bf16[4,512,4096]{2,1,0:T(8,128)(2,1)}, bf16[4,512,2048]{2,1,0:T(8,128)(2,1)}, bf16[4,512,2048]{2,1,0:T(8,128)(2,1)}) custom-call(bf16[512,2048]{1,0:T(8,128)(2,1)} %multiply_convert_fusion.2.own_ref, bf16[512,2048]{1,0:T(8,128)(2,1)} %get-tuple-element.97.resid_ref, ...), custom_call_target="tpu_custom_call" | custom-call | flops 103079215104 | bytes 838860800 | tf_op jit(solution)/shard_map/feed_forward/pallas_call | solution.py:895
  793.2 23.7 %bitcast_convert_fusion.1 = bf16[2048,2048]{1,0:T(8,128)(2,1)} fusion(bf16[4,512,2048]{2,1,0:T(8,128)(2,1)} %multiply_convert_fusion.grad_ref, bf16[4,512,2048]{2,1,0:T(8,128)(2,1)} %get-tuple-element.53), kind=kOutput, calls=%fused_computation.1 | convolution fusion | flops 17184063488 | bytes 25165824 | tf_op jit(solution)/shard_map/dot_general | solution.py:68
  817.0 42.5 %bitcast_convert_fusion = bf16[2048,4096]{1,0:T(8,128)(2,1)} fusion(bf16[4,512,2048]{2,1,0:T(8,128)(2,1)} %get-tuple-element.51, bf16[4,512,4096]{2,1,0:T(8,128)(2,1)} %get-tuple-element.52), kind=kOutput, calls=%fused_computation | convolution fusion | flops 34368126976 | bytes 41943040 | tf_op jit(solution)/shard_map/dot_general | solution.py:68
  860.3 5.8 convert_reduce_fusion
  867.2 4.6 multiply_convert_fusion.1
  871.9 4.2 collective-permute-done.9
  876.1 8.3 convolution_convert_fusion.4.dz_ref
  884.4 63.3 %attend_back.1 = bf16[1024,1536]{1,0:T(8,128)(2,1)} custom-call(s32[1]{0:T(128)} %dynamic_slice.86.len_ref, bf16[1024,1536]{1,0:T(8,128)(2,1)} %get-tuple-element.47.qkv_ref, bf16[1024,1024]{1,0:T(8,128)(2,1)S(1)} %convolution_convert_fusion.4.dz_ref, f32[1024,256]{1,0:T(8,128)S(1)} %copy-done.5, f32[1024,256]{1,0:T(8,128)S(1)} %concatenate.37.sin_ref), custom_call_target="tpu_custom_call" | custom-call | flops 10737418240 | bytes 8388608 | tf_op jit(solution)/shard_map/attend_back/pallas_call | solution.py:617
  947.7 8.3 convolution_convert_fusion.1
  959.2 10.5 convolution_convert_fusion.2
  969.7 9.1 convolution_convert_fusion
  980.5 17.2 %collective-permute-start.8 = (bf16[4,512,512]{2,1,0:T(8,128)(2,1)}, bf16[4,512,512]{2,1,0:T(8,128)(2,1)}, u32[]{:S(2)}, u32[]{:S(2)}) collective-permute-start(bf16[4,512,512]{2,1,0:T(8,128)(2,1)} %reduce-scatter.4.cloned.1.call-done), channel_id=1, source_target_pairs={{0,0},{4,8},{8,4},{12,12},{16,16},{20,24},{24,20},{28,28},{1,1},{5... | collective-permute-start | bytes 6291464 | tf_op jit(solution)/shard_map/ppermute | solution.py:1341
  997.8 4.5 fusion.4.ig_ref
  1002.7 234.0 %finish.1 = (bf16[4,512,512]{2,1,0:T(8,128)(2,1)S(1)}, f32[2,256,384]{2,1,0:T(8,128)S(1)}, f32[2,256,256]{2,1,0:T(8,128)S(1)}, f32[8,512]{1,0:T(8,128)S(1)}) custom-call(bf16[512,2048]{1,0:T(8,128)(2,1)S(1)} %fusion.4.ig_ref, bf16[2,2,2,256,1536]{4,3,2,1,0:T(8,128)(2,1)} %bitcast.80, bf16[2,2,2,256,1024]{4,3,2,1,0:T(8,128)(2,1)S(1)} %bitcast.76, ...), custom_call_target="tpu_custom_call" | custom-call | bytes 314572800 | tf_op jit(solution)/shard_map/finish/pallas_call | solution.py:1188
  1246.4 4.0 convert_multiply_fusion.5
  1250.4 6.6 reshape.183
  (162 shorter events, 55.8 us)
Async XLA Ops:
  7.2 10.8 copy-start.31
  7.2 252.5 %all-gather.3.cloned.1.call-start = ((), (), s32[]{:S(2)}) async-start(), calls=%async_computation.3 | async-start | bytes 10485760 | tf_op jit(solution)/shard_map/all_gather | solution.py:196
  7.9 448.5 %all-gather.5.cloned.1.call-start = ((), (), s32[]{:S(2)}) async-start(), calls=%async_computation.4 | async-start | bytes 10485760 | tf_op jit(solution)/shard_map/all_gather | solution.py:1292
  18.0 28.6 %copy-start.6 = (f32[2048]{0:T(1024)}, f32[2048]{0:T(1024)S(1)}, u32[]{:S(2)}) copy-start(f32[2048]{0:T(1024)S(1)} %convert_element_type.110) | copy-start | bytes 24580
  48.3 204.6 %copy-start.19 = (bf16[1024,1,2048]{2,0,1:T(8,128)(2,1)S(1)}, bf16[1024,1,2048]{2,0,1:T(8,128)(2,1)}, u32[]{:S(2)}) copy-start(bf16[1024,1,2048]{2,0,1:T(8,128)(2,1)} %copy.64) | copy-start | bytes 12582916
  248.9 179.1 %copy-start = (bf16[512,2048]{1,0:T(8,128)(2,1)}, bf16[512,2048]{1,0:T(8,128)(2,1)S(1)}, u32[]{:S(2)}) copy-start(bf16[512,2048]{1,0:T(8,128)(2,1)S(1)} %get-tuple-element.32) | copy-start | bytes 6291460
  261.6 2.0 collective-permute-start.1
  263.6 33.7 %copy-start.33 = (s32[16]{0:T(128)S(1)}, s32[16]{0:T(128)}, u32[]{:S(2)}) copy-start(s32[16]{0:T(128)} %param.13) | copy-start | bytes 196
  263.6 716.9 %reduce-scatter.4.cloned.1.call-start = ((), (), s32[]{:S(2)}) async-start(), calls=%async_computation.5 | async-start | bytes 10485760 | tf_op jit(solution)/shard_map/reduce_scatter | solution.py:1337
  264.2 106.3 %collective-permute-start.2 = (bf16[512,2048]{1,0:T(8,128)(2,1)}, bf16[512,2048]{1,0:T(8,128)(2,1)}, u32[]{:S(2)}, u32[]{:S(2)}) collective-permute-start(bf16[512,2048]{1,0:T(8,128)(2,1)} %get-tuple-element.42), channel_id=1, source_target_pairs={{0,4},{4,0},{1,5},{5,1},{2,6},{6,2},{3,7},{7,3},{8,12},{12,8},{9,1... | collective-permute-start | bytes 6291464 | tf_op jit(solution)/shard_map/ppermute | solution.py:1286
  291.9 91.7 %collective-permute-start.3 = (bf16[512,2048]{1,0:T(8,128)(2,1)}, bf16[512,2048]{1,0:T(8,128)(2,1)}, u32[]{:S(2)}, u32[]{:S(2)}) collective-permute-start(bf16[512,2048]{1,0:T(8,128)(2,1)} %get-tuple-element.43), channel_id=1, source_target_pairs={{0,4},{4,0},{1,5},{5,1},{2,6},{6,2},{3,7},{7,3},{8,12},{12,8},{9,1... | collective-permute-start | bytes 6291464 | tf_op jit(solution)/shard_map/ppermute | solution.py:1286
  292.0 136.0 %collective-permute-start.4 = (bf16[512,2048]{1,0:T(8,128)(2,1)}, bf16[512,2048]{1,0:T(8,128)(2,1)}, u32[]{:S(2)}, u32[]{:S(2)}) collective-permute-start(bf16[512,2048]{1,0:T(8,128)(2,1)} %constant_dynamic-slice_fusion.2), channel_id=1, source_target_pairs={{0,4},{4,0},{1,5},{5,1},{2,6},{6,2},{3,7},{7,3},{8,12},{12,8},{9,1... | collective-permute-start | bytes 6291464 | tf_op jit(solution)/shard_map/ppermute | solution.py:1286
  302.7 43.2 %copy-start.12 = (bf16[2048,1024]{1,0:T(8,128)(2,1)S(1)}, bf16[2048,1024]{1,0:T(8,128)(2,1)}, u32[]{:S(2)}) copy-start(bf16[2048,1024]{1,0:T(8,128)(2,1)} %copy-done.11) | copy-start | bytes 12582916
  353.5 74.5 %collective-permute-start = (bf16[512,2048]{1,0:T(8,128)(2,1)}, bf16[512,2048]{1,0:T(8,128)(2,1)}, u32[]{:S(2)}, u32[]{:S(2)}) collective-permute-start(bf16[512,2048]{1,0:T(8,128)(2,1)} %constant_dynamic-slice_fusion.1), channel_id=1, source_target_pairs={{0,8},{8,0},{16,24},{24,16},{1,9},{9,1},{17,25},{25,17},{2,10},{10... | collective-permute-start | bytes 6291464 | tf_op jit(solution)/shard_map/ppermute | solution.py:1257
  369.7 65.3 %copy-start.25 = (f32[2048]{0:T(1024)}, f32[2048]{0:T(1024)S(1)}, u32[]{:S(2)}) copy-start(f32[2048]{0:T(1024)S(1)} %convert_element_type.116) | copy-start | bytes 24580
  370.4 94.6 %collective-permute-start.5 = (bf16[512,2048]{1,0:T(8,128)(2,1)}, bf16[512,2048]{1,0:T(8,128)(2,1)}, u32[]{:S(2)}, u32[]{:S(2)}) collective-permute-start(bf16[512,2048]{1,0:T(8,128)(2,1)} %collective-permute-done.2.wg_far), channel_id=1, source_target_pairs={{0,8},{8,0},{16,24},{24,16},{1,9},{9,1},{17,25},{25,17},{2,10},{10... | collective-permute-start | bytes 6291464 | tf_op jit(solution)/shard_map/ppermute | solution.py:1257
  383.6 81.5 %collective-permute-start.6 = (bf16[512,2048]{1,0:T(8,128)(2,1)}, bf16[512,2048]{1,0:T(8,128)(2,1)}, u32[]{:S(2)}, u32[]{:S(2)}) collective-permute-start(bf16[512,2048]{1,0:T(8,128)(2,1)} %collective-permute-done.3.wu_far), channel_id=1, source_target_pairs={{0,8},{8,0},{16,24},{24,16},{1,9},{9,1},{17,25},{25,17},{2,10},{10... | collective-permute-start | bytes 6291464 | tf_op jit(solution)/shard_map/ppermute | solution.py:1257
  428.0 37.1 %collective-permute-start.7 = (bf16[512,2048]{1,0:T(8,128)(2,1)}, bf16[512,2048]{1,0:T(8,128)(2,1)}, u32[]{:S(2)}, u32[]{:S(2)}) collective-permute-start(bf16[512,2048]{1,0:T(8,128)(2,1)} %collective-permute-done.4.wd_far), channel_id=1, source_target_pairs={{0,8},{8,0},{16,24},{24,16},{1,9},{9,1},{17,25},{25,17},{2,10},{10... | collective-permute-start | bytes 6291464 | tf_op jit(solution)/shard_map/ppermute | solution.py:1257
  435.0 30.0 %copy-start.27 = (f32[512]{0:T(512)}, f32[512]{0:T(512)S(1)}, u32[]{:S(2)}) copy-start(f32[512]{0:T(512)S(1)} %get-tuple-element.123) | copy-start | bytes 6148
  793.2 450.5 %reduce-scatter.8.cloned.1.call-start = ((), (), s32[]{:S(2)}) async-start(), calls=%async_computation.7 | async-start | bytes 9437184 | tf_op jit(solution)/shard_map/reduce_scatter | solution.py:1346
  817.0 433.4 %reduce-scatter.6.cloned.1.call-start = ((), (), s32[]{:S(2)}) async-start(), calls=%async_computation.6 | async-start | bytes 18874368 | tf_op jit(solution)/shard_map/reduce_scatter | solution.py:1346
  871.8 4.3 collective-permute-start.9
  871.9 12.5 copy-start.5
  876.1 71.6 %slice-start = ((s8[6291456]{0:T(1024)(128)(4,1)}), s8[4194304]{0:T(1024)(128)(4,1)S(1)}, s32[]{:S(2)}) async-start(s8[6291456]{0:T(1024)(128)(4,1)} %bitcast.78), calls=%async_computation.8 | async-start | bytes 8388608
  884.4 63.3 %slice-start.1 = ((s8[6291456]{0:T(1024)(128)(4,1)}), s8[2097152]{0:T(1024)(128)(4,1)S(1)}, s32[]{:S(2)}) async-start(s8[6291456]{0:T(1024)(128)(4,1)} %bitcast.78), calls=%async_computation.9 | async-start | bytes 4194304
  956.1 22.7 %copy-start.20 = (bf16[1024,2048]{1,0:T(8,128)(2,1)}, bf16[1024,2048]{1,0:T(8,128)(2,1)S(1)}, u32[]{:S(2)}) copy-start(bf16[1024,2048]{1,0:T(8,128)(2,1)S(1)} %convolution_convert_fusion.1) | copy-start | bytes 12582916
  956.4 13.3 %copy-start.10 = (bf16[1024,2048]{1,0:T(8,128)(2,1)S(1)}, bf16[1024,2048]{1,0:T(8,128)(2,1)}, u32[]{:S(2)}) copy-start(bf16[1024,2048]{1,0:T(8,128)(2,1)} %copy-done.9) | copy-start | bytes 12582916
  956.4 13.3 %copy-start.35 = (bf16[1024,1536]{1,0:T(8,128)(2,1)S(1)}, bf16[1024,1536]{1,0:T(8,128)(2,1)}, u32[]{:S(2)}) copy-start(bf16[1024,1536]{1,0:T(8,128)(2,1)} %attend_back.1) | copy-start | bytes 9437188
  956.4 22.4 %collective-permute-start.10 = (bf16[512,2048]{1,0:T(8,128)(2,1)S(1)}, bf16[512,2048]{1,0:T(8,128)(2,1)S(1)}, u32[]{:S(2)}, u32[]{:S(2)}) collective-permute-start(bf16[512,2048]{1,0:T(8,128)(2,1)S(1)} %constant_dynamic-slice_fusion), channel_id=1, source_target_pairs={{0,8},{8,0},{16,24},{24,16},{1,9},{9,1},{17,25},{25,17},{2,10},{10... | collective-permute-start | bytes 6291464 | tf_op jit(solution)/shard_map/ppermute | solution.py:1257
  969.7 9.1 copy-start.1
  969.7 9.1 copy-start.7
  980.5 265.9 %collective-permute-start.8 = (bf16[4,512,512]{2,1,0:T(8,128)(2,1)}, bf16[4,512,512]{2,1,0:T(8,128)(2,1)}, u32[]{:S(2)}, u32[]{:S(2)}) collective-permute-start(bf16[4,512,512]{2,1,0:T(8,128)(2,1)} %reduce-scatter.4.cloned.1.call-done), channel_id=1, source_target_pairs={{0,0},{4,8},{8,4},{12,12},{16,16},{20,24},{24,20},{28,28},{1,1},{5... | collective-permute-start | bytes 6291464 | tf_op jit(solution)/shard_map/ppermute | solution.py:1341
  (22 other events, 87.1 us)
Sparse Core Ops, SparseCore 0:
  9.6 60.9 all-gather.2
  263.8 192.5 all-gather.4
  793.3 156.7 reduce-scatter.3
  953.4 109.5 reduce-scatter.7
  1066.8 157.9 reduce-scatter.5

commit v3 on v2

--- a/solution.py
+++ b/solution.py
@@ -189,11 +189,9 @@
 SIBLINGS = [(0, 1), (1, 0), (2, 3), (3, 2)]
 OVER_X = [(0, 1), (1, 0)]
 CROSSED = [((2 * y + c) * 2 + x, (2 * y + x) * 2 + c) for y in (0, 1) for c in (0, 1) for x in (0, 1)]
-SAME_CORE = [[0, 2], [1, 3]]
-
-
-def bring_cotangent(cotangent, deal_order, first):
-    everyone = lax.all_gather(cotangent, "dp", axis=0, tiled=True)
+
+
+def pick_sequences(everyone, deal_order, first, count):
     slots = jnp.arange(deal_order.shape[0], dtype=jnp.int32)
     inverse = jnp.sum(jnp.where(deal_order[None, :] == slots[:, None], slots[None, :], 0), axis=1)
     return jnp.concatenate(
@@ -201,9 +199,14 @@
             lax.dynamic_slice_in_dim(
                 everyone, lax.dynamic_index_in_dim(inverse, first + at, keepdims=False), 1
             )
-            for at in range(cotangent.shape[0])
+            for at in range(count)
         ]
     )
+
+
+def bring_cotangent(cotangent, deal_order, first):
+    everyone = lax.all_gather(cotangent, "dp", axis=0, tiled=True)
+    return pick_sequences(everyone, deal_order, first, cotangent.shape[0])
 
 
 def place():
@@ -213,45 +216,79 @@
     return group, core, group - core + row, row, lax.axis_index("col")
 
 
+def lined(index, step, count):
+    return lax.rem(index + step + count, count)
+
+
+def aligned(block, size):
+    return pl.ds(pl.multiple_of(block * size, size), size)
+
+
+def greet(device):
+    pl.semaphore_signal(
+        pltpu.get_barrier_semaphore(), inc=1, device_id=device, device_id_type=MESH_IDS
+    )
+
+
+def remote(src, dst, sems, at, device):
+    return pltpu.make_async_remote_copy(
+        src_ref=src,
+        dst_ref=dst,
+        send_sem=sems.at[0, at],
+        recv_sem=sems.at[1, at],
+        device_id=device,
+        device_id_type=MESH_IDS,
+    )
+
+
+def weight_copies(cols, own, full, sems, x_sems):
+    group, core, mate, row, col = place()
+    tall, wide = own.shape
+
+    def block(of_row, of_col):
+        return full.at[aligned(of_row, tall), aligned(of_col, wide)]
+
+    def line(step):
+        return lined(col, step, cols)
+
+    over = (group, 1 - row, col)
+    steps = range(1, cols)
+    along = [remote(own, block(row, col), sems, k, (group, row, line(k))) for k in steps]
+    arrive = [remote(own, block(row, line(-k)), sems, k, (group, row, line(k))) for k in steps]
+    across = [remote(own, block(row, col), x_sems, 0, over)] + [
+        remote(block(row, line(-k)), block(row, line(-k)), x_sems, k, over) for k in steps
+    ]
+    landed = [remote(own, block(1 - row, line(-k)), x_sems, k, over) for k in range(cols)]
+    return along, arrive, across, landed, block(row, col)
+
+
 def start_kernel(
     cols,
     tok_ref,
     pq_ref,
-    po_ref,
     gain_ref,
     x_ref,
     a_ref,
     wq_ref,
-    wo_ref,
     x_buf,
     a_buf,
     tok_sems,
     q_sems,
-    o_sems,
     qx_sems,
-    ox_sems,
     a_sems,
     local_sems,
 ):
     group, core, mate, row, col = place()
     width = tok_ref.shape[2]
-    weight_rows = pq_ref.shape[0]
+    length = x_buf.shape[0]
+    sibling = (group + 1 - 2 * core, row, col)
 
     def line(step):
-        return lax.rem(col + step + cols, cols)
-
-    def start_at(block, size):
-        return pl.ds(pl.multiple_of(block * size, size), size)
-
-    barrier = pltpu.get_barrier_semaphore()
-
-    def greet(device):
-        pl.semaphore_signal(barrier, inc=1, device_id=device, device_id_type=MESH_IDS)
+        return lined(col, step, cols)
 
     for step in range(1, cols):
         greet((mate, core, line(step)))
         greet((group, row, line(step)))
-    sibling = (group + 1 - 2 * core, row, col)
     greet((group, 1 - row, col))
     greet(sibling)
 
@@ -259,58 +296,24 @@
     def _():
         greet((mate, core, col))
 
-    pl.semaphore_wait(barrier, 2 * cols + (core - row) * (core - row))
-
-    def remote(src, dst, sems, at, device):
-        return pltpu.make_async_remote_copy(
-            src_ref=src,
-            dst_ref=dst,
-            send_sem=sems.at[0, at],
-            recv_sem=sems.at[1, at],
-            device_id=device,
-            device_id_type=MESH_IDS,
-        )
-
-    def weight_copies(own, full, sems, x_sems):
-        wide = own.shape[1]
-
-        def block(of_row, of_col):
-            return full.at[start_at(of_row, weight_rows), start_at(of_col, wide)]
-
-        along = [
-            remote(own, block(row, col), sems, step, (group, row, line(step)))
-            for step in range(1, cols)
-        ]
-        arrive = [
-            remote(own, block(row, line(-step)), sems, step, (group, row, line(step)))
-            for step in range(1, cols)
-        ]
-        across = [remote(own, block(row, col), x_sems, 0, (group, 1 - row, col))] + [
-            remote(block(row, line(-step)), block(row, line(-step)), x_sems, step, (group, 1 - row, col))
-            for step in range(1, cols)
-        ]
-        landed = [
-            remote(own, block(1 - row, line(-step)), x_sems, step, (group, 1 - row, col))
-            for step in range(cols)
-        ]
-        return along, arrive, across, landed, block(row, col)
-
-    q_along, q_arrive, q_across, q_landed, q_own = weight_copies(pq_ref, wq_ref, q_sems, qx_sems)
-    o_along, o_arrive, o_across, o_landed, o_own = weight_copies(po_ref, wo_ref, o_sems, ox_sems)
-    own_q = pltpu.make_async_copy(pq_ref, q_own, local_sems.at[0])
-    own_o = pltpu.make_async_copy(po_ref, o_own, local_sems.at[1])
+    pl.semaphore_wait(
+        pltpu.get_barrier_semaphore(), 2 * cols + (core - row) * (core - row)
+    )
+
+    along, arrive, across, landed, own_place = weight_copies(cols, pq_ref, wq_ref, q_sems, qx_sems)
+    own_q = pltpu.make_async_copy(pq_ref, own_place, local_sems.at[0])
 
     def token_copy(step, into):
         return remote(
             tok_ref.at[line(step)],
-            x_buf.at[:, start_at(into, width)],
+            x_buf.at[:, aligned(into, width)],
             tok_sems,
             step,
             (mate, core, line(step)),
         )
 
     own_tokens = pltpu.make_async_copy(
-        tok_ref.at[col], x_buf.at[:, start_at(col, width)], local_sems.at[2]
+        tok_ref.at[col], x_buf.at[:, aligned(col, width)], local_sems.at[1]
     )
     for step in range(1, cols):
         token_copy(step, col).start()
@@ -323,14 +326,10 @@
     def _():
         own_tokens.start()
 
-    for copy in q_along:
+    for copy in along:
         copy.start()
-    q_across[0].start()
+    across[0].start()
     own_q.start()
-    own_o.start()
-    for copy in o_along:
-        copy.start()
-    o_across[0].start()
     for step in range(1, cols):
         token_copy(step, line(-step)).wait_recv()
 
@@ -342,30 +341,26 @@
     def _():
         own_tokens.wait()
 
-    keep_x = pltpu.make_async_copy(x_buf, x_ref, local_sems.at[3])
+    keep_x = pltpu.make_async_copy(x_buf, x_ref, local_sems.at[2])
     keep_x.start()
-    length = x_buf.shape[0]
     tall = min(64, length)
 
     @pl.loop(0, length // tall)
     def _(at):
-        here = pl.ds(pl.multiple_of(at * tall, tall), tall)
+        here = aligned(at, tall)
         now = x_buf[here, :].astype(jnp.float32)
         scale = lax.rsqrt(jnp.mean(now * now, axis=1, keepdims=True) + EPSILON)
         a_buf[here, :] = (now * scale * gain_ref[...]).astype(jnp.bfloat16)
 
     def a_copy(of_core):
-        return remote(a_buf, a_ref.at[start_at(of_core, length)], a_sems, 0, sibling)
-
-    own_a = pltpu.make_async_copy(a_buf, a_ref.at[start_at(core, length)], local_sems.at[4])
+        return remote(a_buf, a_ref.at[aligned(of_core, length)], a_sems, 0, sibling)
+
+    own_a = pltpu.make_async_copy(a_buf, a_ref.at[aligned(core, length)], local_sems.at[3])
     a_copy(core).start()
     own_a.start()
     for step in range(1, cols):
-        q_arrive[step - 1].wait_recv()
-        q_across[step].start()
-    for step in range(1, cols):
-        o_arrive[step - 1].wait_recv()
-        o_across[step].start()
+        arrive[step - 1].wait_recv()
+        across[step].start()
     for step in range(1, cols):
         token_copy(step, col).wait_send()
 
@@ -378,14 +373,13 @@
     a_copy(core).wait_send()
     a_copy(1 - core).wait_recv()
     own_q.wait()
-    own_o.wait()
-    for copy in q_along + o_along + q_across + o_across:
+    for copy in along + across:
         copy.wait_send()
-    for copy in q_landed + o_landed:
+    for copy in landed:
         copy.wait_recv()
 
 
-def start_exchange(tokens, pack_q, pack_o, gain, rows, cols):
+def start_exchange(tokens, pack_q, gain, rows, cols):
     anywhere = pl.BlockSpec(memory_space=pl.ANY)
     seqs, length, width = tokens.shape
     weight_rows = pack_q.shape[0]
@@ -396,22 +390,61 @@
             jax.ShapeDtypeStruct((length, full), tokens.dtype),
             jax.ShapeDtypeStruct((2 * length, full), tokens.dtype),
             jax.ShapeDtypeStruct((weight_rows * rows, pack_q.shape[1] * cols), pack_q.dtype),
-            jax.ShapeDtypeStruct((weight_rows * rows, pack_o.shape[1] * cols), pack_o.dtype),
         ),
-        in_specs=[anywhere] * 3 + [pl.BlockSpec(memory_space=pltpu.VMEM)],
-        out_specs=(anywhere,) * 4,
+        in_specs=[anywhere] * 2 + [pl.BlockSpec(memory_space=pltpu.VMEM)],
+        out_specs=(anywhere,) * 3,
         scratch_shapes=[
             pltpu.VMEM((length, full), tokens.dtype),
             pltpu.VMEM((length, full), tokens.dtype),
         ]
-        + [pltpu.SemaphoreType.DMA((2, cols))] * 5
-        + [pltpu.SemaphoreType.DMA((2, 1)), pltpu.SemaphoreType.DMA((5,))],
+        + [pltpu.SemaphoreType.DMA((2, cols))] * 3
+        + [pltpu.SemaphoreType.DMA((2, 1)), pltpu.SemaphoreType.DMA((4,))],
         compiler_params=pltpu.CompilerParams(
             collective_id=1, has_side_effects=True, vmem_limit_bytes=16 << 20
         ),
         cost_estimate=pl.CostEstimate(flops=0, bytes_accessed=400 << 20, transcendentals=0),
         name="start_exchange",
-    )(tokens, pack_q, pack_o, gain.reshape(1, full))
+    )(tokens, pack_q, gain.reshape(1, full))
+
+
+def gather_kernel(cols, own_ref, after_ref, full_ref, sems, x_sems, local_sem):
+    group, core, mate, row, col = place()
+    for step in range(1, cols):
+        greet((group, row, lined(col, step, cols)))
+    greet((group, 1 - row, col))
+    pl.semaphore_wait(pltpu.get_barrier_semaphore(), cols)
+    along, arrive, across, landed, own_place = weight_copies(cols, own_ref, full_ref, sems, x_sems)
+    own = pltpu.make_async_copy(own_ref, own_place, local_sem)
+    for copy in along:
+        copy.start()
+    across[0].start()
+    own.start()
+    for step in range(1, cols):
+        arrive[step - 1].wait_recv()
+        across[step].start()
+    own.wait()
+    for copy in along + across:
+        copy.wait_send()
+    for copy in landed:
+        copy.wait_recv()
+
+
+def gather_weights(own, after, rows, cols):
+    anywhere = pl.BlockSpec(memory_space=pl.ANY)
+    return pl.pallas_call(
+        functools.partial(gather_kernel, cols),
+        out_shape=jax.ShapeDtypeStruct((own.shape[0] * rows, own.shape[1] * cols), own.dtype),
+        in_specs=[anywhere] * 2,
+        out_specs=anywhere,
+        scratch_shapes=[
+            pltpu.SemaphoreType.DMA((2, cols)),
+            pltpu.SemaphoreType.DMA((2, cols)),
+            pltpu.SemaphoreType.DMA(()),
+        ],
+        compiler_params=pltpu.CompilerParams(collective_id=4, has_side_effects=True),
+        cost_estimate=pl.CostEstimate(flops=0, bytes_accessed=200 << 20, transcendentals=0),
+        name="gather_weights",
+    )(own, after)
 
 
 def half_turn(wide):
@@ -663,6 +696,8 @@
     dgu_all,
     mlp_all,
     back_all,
+    ggu_ref,
+    gdn_ref,
     wg,
     wu,
     wd,
@@ -673,6 +708,7 @@
     du_buf,
     mlp_buf,
     back_buf,
+    turn_buf,
     w_sems,
     ag_send,
     ag_recv,
@@ -774,13 +810,16 @@
 
     def back_out(at, chunk):
         return pltpu.make_async_remote_copy(
-            src_ref=back_buf.at[at],
+            src_ref=back_buf.at[slot_of(at)],
             dst_ref=back_all.at[col],
             send_sem=back_send.at[at],
             recv_sem=back_recv.at[col],
             device_id=(group, row, chunk),
             device_id_type=MESH_IDS,
         )
+
+    def slot_of(at):
+        return lax.rem(at, cols - 1)
 
     own_back = pltpu.make_async_copy(back_buf.at[0], back_all.at[col], io_sems.at[5])
     at_end = (col == 0) | (col == last)
@@ -838,11 +877,15 @@
         def _():
             load_resid.wait()
 
+        @pl.when(at == last)
+        def _():
+            own_back.wait()
+
         @pl.loop(0, 2 * depth // tile)
         def _(step):
             here = pl.ds(pl.multiple_of(step * tile, tile), tile)
             back = dot_nt(dg_buf[...], wg[here, :]) + dot_nt(du_buf[...], wu[here, :])
-            back_buf[at, :, here] = back.astype(jnp.bfloat16)
+            back_buf[slot_of(at), :, here] = back.astype(jnp.bfloat16)
             added = jnp.where(at == 0, mlp_buf[:, here].astype(jnp.float32), 0.0)
             mlp_buf[:, here] = (added + RES_MULT * dot_nt(u_buf[...], wd[here, :])).astype(
                 jnp.bfloat16
@@ -864,12 +907,68 @@
     for copy in outputs(order(last)):
         copy.wait()
     mlp_out(order(last)).wait()
-    own_back.wait()
+
+    rows = b_buf.shape[0]
+    loads = []
+    for chunk in range(cols):
+        here = slice(chunk * rows, (chunk + 1) * rows)
+        loads += [
+            pltpu.make_async_copy(
+                dgu_all.at[chunk, :, 0:units], wg.at[here], w_sems.at[chunk]
+            ),
+            pltpu.make_async_copy(
+                dgu_all.at[chunk, :, units : 2 * units], wu.at[here], w_sems.at[cols + chunk]
+            ),
+            pltpu.make_async_copy(u_all.at[chunk], wd.at[here], w_sems.at[2 * cols + chunk]),
+        ]
+    for load in loads:
+        load.start()
+    for load in loads:
+        load.wait()
+
+    def results(at):
+        here = aligned(at, rows)
+        return (
+            pltpu.make_async_copy(dg_buf, ggu_ref.at[here, 0:units], io_sems.at[1]),
+            pltpu.make_async_copy(du_buf, ggu_ref.at[here, units : 2 * units], io_sems.at[2]),
+            pltpu.make_async_copy(u_buf, gdn_ref.at[here], io_sems.at[3]),
+        )
+
+    def turned(source, into, at):
+        load = pltpu.make_async_copy(source.at[:, :, aligned(at, rows)], turn_buf, io_sems.at[4])
+        load.start()
+        load.wait()
+        for chunk in range(cols):
+            into[:, chunk * rows : (chunk + 1) * rows] = turn_buf[chunk].T
+
+    def one_block(at, unused):
+        turned(b_all, b_buf, at)
+        turned(grad_ref, g_buf, at)
+
+        @pl.when(at > 0)
+        def _():
+            for copy in results(at - 1):
+                copy.wait()
+
+        @pl.loop(0, units // tile)
+        def _(step):
+            lanes = aligned(step, tile)
+            dg_buf[:, lanes] = dot_nn(b_buf[...], wg[:, lanes]).astype(jnp.bfloat16)
+            du_buf[:, lanes] = dot_nn(b_buf[...], wu[:, lanes]).astype(jnp.bfloat16)
+            u_buf[:, lanes] = dot_nn(g_buf[...], wd[:, lanes]).astype(jnp.bfloat16)
+
+        for copy in results(at):
+            copy.start()
+        return unused
+
+    lax.fori_loop(0, cols, one_block, 0)
+    for copy in results(last):
+        copy.wait()
     for at in range(1, cols):
         back_out(at, order(at)).wait_send()
         source = lax.rem(col + at, cols)
         pltpu.make_async_remote_copy(
-            src_ref=back_buf.at[at],
+            src_ref=back_buf.at[slot_of(at)],
             dst_ref=back_all.at[source],
             send_sem=back_send.at[at],
             recv_sem=back_recv.at[source],
@@ -900,9 +999,11 @@
             jax.ShapeDtypeStruct((cols, rows, 2 * units), bf16),
             jax.ShapeDtypeStruct((cols, rows, width), bf16),
             jax.ShapeDtypeStruct((cols, rows, width), bf16),
+            jax.ShapeDtypeStruct((width, 2 * units), bf16),
+            jax.ShapeDtypeStruct((width, units), bf16),
         ),
         in_specs=[anywhere] * 12,
-        out_specs=(anywhere,) * 5,
+        out_specs=(anywhere,) * 7,
         scratch_shapes=[
             pltpu.VMEM((width, units), bf16),
             pltpu.VMEM((width, units), bf16),
@@ -913,8 +1014,9 @@
             pltpu.VMEM((rows, units), bf16),
             pltpu.VMEM((rows, units), bf16),
             pltpu.VMEM((rows, width), bf16),
-            pltpu.VMEM((cols, rows, width), bf16),
-            pltpu.SemaphoreType.DMA((9,)),
+            pltpu.VMEM((cols - 1, rows, width), bf16),
+            pltpu.VMEM((cols, rows, rows), bf16),
+            pltpu.SemaphoreType.DMA((12,)),
             pltpu.SemaphoreType.DMA((2, cols)),
             pltpu.SemaphoreType.DMA((cols,)),
             pltpu.SemaphoreType.DMA((cols,)),
@@ -925,7 +1027,7 @@
             collective_id=2, has_side_effects=True, vmem_limit_bytes=60 << 20
         ),
         cost_estimate=pl.CostEstimate(
-            flops=12 * cols * rows * width * units,
+            flops=18 * cols * rows * width * units,
             bytes_accessed=800 << 20,
             transcendentals=cols * rows * units,
         ),
@@ -1270,8 +1372,8 @@
     pack_o = core_half(w_out, 1)
     gain_one = gain_attn.astype(jnp.float32)
     gain_two = gain_ffn.astype(jnp.float32)
-    own_tokens, attn_input, weights_qkv, weights_out = start_exchange(
-        tokens, pack_q, pack_o, gain_one, row_count, col_count
+    own_tokens, attn_input, weights_qkv = start_exchange(
+        tokens, pack_q, gain_one, row_count, col_count
     )
 
     length = lax.dynamic_slice_in_dim(lengths, mate * seq_group + col, 1)
@@ -1280,16 +1382,19 @@
     line_live = (own_pos[None, :] < line_lengths[:, None]).astype(jnp.float32)
     own_live = (own_pos < length).astype(jnp.float32)[:, None]
 
+    w_gate_up, attn_input = lax.optimization_barrier((w_gate_up, attn_input))
     own_mats = (w_gate_up[:, 0], w_gate_up[:, 1], w_down)
     halves = tuple(half_rows(matrix) for matrix in own_mats)
     halves, attn_input = lax.optimization_barrier((halves, attn_input))
     far_mats = tuple(lax.ppermute(matrix, "row", OVER_X) for matrix in halves)
     sibling_mats = tuple(from_sibling(matrix) for matrix in far_mats)
 
-    given = bring_cotangent(cotangent, deal_order, group * seq_group)
-    given, attn_input = lax.optimization_barrier((given, attn_input))
-    swapped = lax.ppermute(given, ("dp", "row"), CROSSED)
-    line_cot = lax.all_gather(swapped, "col", axis=2, tiled=True)
+    everyone = lax.all_gather(cotangent, "dp", axis=0, tiled=True)
+    everyone, attn_input = lax.optimization_barrier((everyone, attn_input))
+    given = lax.ppermute(
+        pick_sequences(everyone, deal_order, group * seq_group, seq_group), ("dp", "row"), CROSSED
+    )
+    line_cot = lax.all_gather(given, "col", axis=2, tiled=True)
     line_grad = line_live[:, :, None] * line_cot.astype(jnp.float32)
     grad_ffn = (RES_MULT * line_grad).astype(jnp.bfloat16).reshape(-1, full_width)
     own_grad = own_live * lax.dynamic_index_in_dim(line_cot, col, keepdims=False).astype(
@@ -1317,21 +1422,19 @@
         other = lax.dynamic_slice_in_dim(partial, (1 - core) * count, count)
         return mine.astype(jnp.float32) + from_sibling(other).astype(jnp.float32)
 
+    weights_out = gather_weights(pack_o, heads_out, row_count, col_count)
     attn_rows = summed_rows(expand_local(heads_out, weights_out).astype(jnp.bfloat16))
     resid = own_float + RES_MULT * attn_rows
     scale_two = lax.rsqrt(jnp.mean(resid * resid, axis=1, keepdims=True) + EPSILON)
     own_ffn = (resid * scale_two * gain_two).astype(jnp.bfloat16)
 
-    ffn_input, hidden_rows, grad_gate_rows, mlp_part, back_part = feed_forward(
+    unused_b, unused_u, unused_gu, mlp_part, back_part, grad_gu, grad_dn = feed_forward(
         own_ffn,
         resid.astype(jnp.bfloat16),
         grad_ffn.reshape(col_count, rows_local, full_width),
         own_mats + far_mats + sibling_mats,
         col_count,
     )
-    ffn_input = ffn_input.reshape(-1, full_width)
-    hidden_rows = hidden_rows.reshape(-1, hidden)
-    grad_gate_rows = grad_gate_rows.reshape(-1, 2 * hidden)
     grad_normed_two = jnp.sum(back_part.astype(jnp.float32), axis=0)
 
     out_cols = lax.psum_scatter(mlp_part, "col", scatter_dimension=2, tiled=True)
@@ -1344,11 +1447,11 @@
 
     def scatter_rows(matrix):
         return lax.psum_scatter(
-            matrix.astype(jnp.bfloat16), ("dp", "row"), scatter_dimension=0, tiled=True
+            matrix, ("dp", "row"), scatter_dimension=0, tiled=True
         ).astype(jnp.float32)
 
-    sums_down = scatter_rows(token_outer(grad_ffn, hidden_rows))
-    sums_gate_up = scatter_rows(token_outer(ffn_input, grad_gate_rows))
+    sums_down = scatter_rows(grad_dn)
+    sums_gate_up = scatter_rows(grad_gu)
     sums_gate_up = sums_gate_up.reshape(-1, 2, hidden)
 
     weighted_two = grad_normed_two * gain_two

time: 1280 us -> 1230 us (0.961)
  Pallas kernels: 862 us -> 944 us
  matrix products: 107 us -> 44 us
  waiting for transfers between devices: 80.9 us -> 47.6 us
  local copies, waits for them, and re-layouts: 91.5 us -> 65.8 us
    pallas_call x0 -> x1, Pallas kernels: none -> 122 us  [gather_weights(): pl.pallas_call(functools.partial(gather_kernel, cols), out_shape=jax.Shap...]
    dot_general x4 -> x2, matrix products: 85.8 us -> 19.1 us  [token_outer(): lax.dot_general(features, grads, (((0,), (0,)), ((), ())), preferred_elem...]
    ppermute x3, waiting for transfers between devices: 57 us -> 0.01 us  [one_sequence_body(): far_mats = tuple((lax.ppermute(matrix, 'row', OVER_X) for matrix in halves))]
    pallas_call x1, Pallas kernels: 194 us -> 138 us  [start_exchange(): pl.pallas_call(functools.partial(start_kernel, cols), out_shape=(jax.Shap...]
    pallas_call x1, Pallas kernels: 328 us -> 365 us  [feed_forward(): pl.pallas_call(functools.partial(ffn_kernel, cols), out_shape=(jax.ShapeD...]
    reduce_scatter x1, waiting for transfers between devices: 0.02 us -> 35.9 us  [one_sequence_body(): lax.psum_scatter(mlp_part, 'col', scatter_dimension=2, tiled=True)]
    unnamed x84 -> x68, local copies, waits for them, and re-layouts: 44.9 us -> 17.2 us
    pallas_call x1, Pallas kernels: 234 us -> 211 us  [finish(): pl.pallas_call(functools.partial(finish_kernel, cols), out_shape=(jax.Sha...]
  transfers between devices with their start and end apart: 16 -> 16, of which waited for: 4 -> 4; matrix products, arithmetic and copies ran while one was open for 18% -> 11% of each run, Pallas kernels for 42% -> 47%
where the time goes in v3:
time: 1230 us; the launch traced here: 1220 us
  Pallas kernels  944 us (77%)
  local copies, waits for them, and re-layouts  65.8 us (5%)
  starting transfers between devices  50.6 us (4%)
  other arithmetic  50.4 us (4%)
  waiting for transfers between devices  47.6 us (4%)
  matrix products  44 us (4%)
  between operations  22.4 us (2%)
    pallas_call x1, Pallas kernels, feed_forward(): pl.pallas_call(functools.partial(ffn_kernel, cols), out_shape=(jax.ShapeD...  365 us
    pallas_call x1, Pallas kernels, finish(): pl.pallas_call(functools.partial(finish_kernel, cols), out_shape=(jax.Sha...  211 us
    pallas_call x1, Pallas kernels, start_exchange(): pl.pallas_call(functools.partial(start_kernel, cols), out_shape=(jax.Shap...  138 us
    pallas_call x1, Pallas kernels, gather_weights(): pl.pallas_call(functools.partial(gather_kernel, cols), out_shape=jax.Shap...  122 us
    pallas_call x1, Pallas kernels, attend_back_fast(): pl.pallas_call(functools.partial(attend_back_kernel, block), grid=(groups...  63.8 us
    pallas_call x1, Pallas kernels, attend_fast(): pl.pallas_call(functools.partial(attend_kernel, block), grid=(groups,), o...  43.5 us
    reduce_scatter x1, waiting for transfers between devices, one_sequence_body(): lax.psum_scatter(mlp_part, 'col', scatter_dimension=2, tiled=True)  35.9 us
    ppermute x3, starting transfers between devices, one_sequence_body(): far_mats = tuple((lax.ppermute(matrix, 'row', OVER_X) for matrix in halves))  29.8 us
  transfers between devices with their start and end apart: 16, of which 4 were waited for; matrix products, arithmetic and copies ran while one was open for 11% of the time, Pallas kernels for 47%

profile of v3, /device:TPU:0, one launch (start us, length us, event | category | flops | bytes accessed | tf_op | source)
XLA Modules:
  0.0 1224.3 jit_solution(7056043100385688932)
XLA Ops:
  14.6 2.1 fusion.15
  20.1 137.6 %start_exchange.1 = (bf16[512,2048]{1,0:T(8,128)(2,1)S(1)}, bf16[1024,2048]{1,0:T(8,128)(2,1)S(1)}, bf16[2048,1536]{1,0:T(8,128)(2,1)S(1)}) custom-call(bf16[4,512,512]{2,1,0:T(8,128)(2,1)S(1)} %copy-done.5, bf16[1024,384]{1,0:T(8,128)(2,1)S(1)} %pad_maximum_fusion.1.pq_ref, f32[1,2048]{1,0:T(1,128)S(1)} %bitcast.67), custom_call_target="tpu_custom_call" | custom-call | bytes 419430400 | tf_op jit(solution)/shard_map/start_exchange/pallas_call | solution.py:387
  157.7 2.8 copy-done.10
  162.5 11.3 copy.45
  173.8 6.9 slice_bitcast_fusion.10
  192.7 27.8 %collective-permute-start.2 = (bf16[512,2048]{1,0:T(8,128)(2,1)}, bf16[512,2048]{1,0:T(8,128)(2,1)}, u32[]{:S(2)}, u32[]{:S(2)}) collective-permute-start(bf16[512,2048]{1,0:T(8,128)(2,1)} %dynamic-slice_bitcast_fusion.1), channel_id=1, source_target_pairs={{0,4},{4,0},{1,5},{5,1},{2,6},{6,2},{3,7},{7,3},{8,12},{12,8},{9,1... | collective-permute-start | bytes 6291464 | tf_op jit(solution)/shard_map/ppermute | solution.py:1389
  226.5 2.4 copy.47
  234.9 43.5 %attend.1 = (bf16[1024,1536]{1,0:T(8,128)(2,1)}, bf16[1024,1024]{1,0:T(8,128)(2,1)S(1)}) custom-call(s32[1]{0:T(128)} %dynamic_slice.85.len_ref, bf16[1024,2048]{1,0:T(8,128)(2,1)} %copy-done.11, bf16[2048,1536]{1,0:T(8,128)(2,1)} %copy-done.10, f32[1024,256]{1,0:T(8,128)S(1)} %concatenate.34.cos_ref, f32[1024,256]{1,0:T(8,128)S(1)} %copy-done.8), custom_call_target="tpu_custom_call" | custom-call | flops 10737418240 | bytes 13631488 | tf_op jit(solution)/shard_map/attend/pallas_call | solution.py:543
  279.8 121.9 %gather_weights.1 = bf16[2048,1024]{1,0:T(8,128)(2,1)} custom-call(bf16[1024,256]{1,0:T(8,128)(2,1)} %constant_dynamic-slice_fusion.6.own_ref, bf16[1024,1024]{1,0:T(8,128)(2,1)} %copy-done.6), custom_call_target="tpu_custom_call" | custom-call | bytes 209715200 | tf_op jit(solution)/shard_map/gather_weights/pallas_call | solution.py:434
  401.6 7.4 convolution_convert_fusion.3
  414.3 2.8 collective-permute-done
  417.0 5.8 fusion.14
  426.6 2.9 all-gather.5.cloned.1.call-done
  429.5 8.6 multiply_convert_fusion.grad_ref
  438.2 365.4 %feed_forward.1 = (bf16[4,512,2048]{2,1,0:T(8,128)(2,1)}, bf16[4,512,2048]{2,1,0:T(8,128)(2,1)}, bf16[4,512,4096]{2,1,0:T(8,128)(2,1)}, bf16[4,512,2048]{2,1,0:T...) custom-call(bf16[512,2048]{1,0:T(8,128)(2,1)} %multiply_convert_fusion.2.own_ref, ...), custom_call_target="tpu_custom_call" | custom-call | flops 154618822656 | bytes 838860800 | tf_op jit(solution)/shard_map/feed_forward/pallas_call | solution.py:994
  805.5 6.0 convert_reduce_fusion
  812.6 4.7 multiply_convert_fusion.1
  817.4 4.2 collective-permute-done.9
  821.6 9.1 convolution_convert_fusion.4.dz_ref
  830.7 63.8 %attend_back.1 = bf16[1024,1536]{1,0:T(8,128)(2,1)} custom-call(s32[1]{0:T(128)} %dynamic_slice.85.len_ref, bf16[1024,1536]{1,0:T(8,128)(2,1)} %get-tuple-element.48.qkv_ref, bf16[1024,1024]{1,0:T(8,128)(2,1)S(1)} %convolution_convert_fusion.4.dz_ref, f32[1024,256]{1,0:T(8,128)S(1)} %concatenate.34.cos_ref, f32[1024,256]{1,0:T(8,128)S(1)} %copy-done.9), custom_call_target="tpu_custom_call" | custom-call | flops 10737418240 | bytes 8388608 | tf_op jit(solution)/shard_map/attend_back/pallas_call | solution.py:650
  894.5 8.6 convolution_convert_fusion.1
  903.4 2.7 copy-done.7
  906.1 10.2 convolution_convert_fusion.2
  916.4 8.8 convolution_convert_fusion
  927.0 35.9 %reduce-scatter.4.cloned.1.call-done = bf16[4,512,512]{2,1,0:T(8,128)(2,1)} async-done(((bf16[4,512,2048]{2,1,0:T(8,128)(2,1)}), bf16[4,512,512]{2,1,0:T(8,128)(2,1)}) %reduce-scatter.4.cloned.1.call-update) | async-done | bytes 2097168 | tf_op jit(solution)/shard_map/reduce_scatter | solution.py:1440
  962.9 17.3 %collective-permute-start.8 = (bf16[4,512,512]{2,1,0:T(8,128)(2,1)}, bf16[4,512,512]{2,1,0:T(8,128)(2,1)}, u32[]{:S(2)}, u32[]{:S(2)}) collective-permute-start(bf16[4,512,512]{2,1,0:T(8,128)(2,1)} %reduce-scatter.4.cloned.1.call-done), channel_id=1, source_target_pairs={{0,0},{4,8},{8,4},{12,12},{16,16},{20,24},{24,20},{28,28},{1,1},{5... | collective-permute-start | bytes 6291464 | tf_op jit(solution)/shard_map/ppermute | solution.py:1444
  980.2 5.5 fusion.4.ig_ref
  985.8 211.4 %finish.1 = (bf16[4,512,512]{2,1,0:T(8,128)(2,1)S(1)}, f32[2,256,384]{2,1,0:T(8,128)S(1)}, f32[2,256,256]{2,1,0:T(8,128)S(1)}, f32[8,512]{1,0:T(8,128)S(1)}) custom-call(bf16[512,2048]{1,0:T(8,128)(2,1)S(1)} %fusion.4.ig_ref, bf16[2,2,2,256,1536]{4,3,2,1,0:T(8,128)(2,1)} %bitcast.70, bf16[2,2,2,256,1024]{4,3,2,1,0:T(8,128)(2,1)S(1)} %bitcast.66, ...), custom_call_target="tpu_custom_call" | custom-call | bytes 314572800 | tf_op jit(solution)/shard_map/finish/pallas_call | solution.py:1290
  1198.5 2.6 convert_element_type.129
  1204.1 2.8 convert_element_type.130
  1206.9 4.1 convert_multiply_fusion.5
  1211.0 6.6 reshape.179
  (148 shorter events, 48.5 us)
Async XLA Ops:
  7.2 10.8 copy-start
  7.2 10.8 copy-start.25
  7.2 181.2 %all-gather.3.cloned.1.call-start = ((), (), s32[]{:S(2)}) async-start(), calls=%async_computation.3 | async-start | bytes 10485760 | tf_op jit(solution)/shard_map/all_gather | solution.py:1392
  7.9 421.6 %all-gather.5.cloned.1.call-start = ((), (), s32[]{:S(2)}) async-start(), calls=%async_computation.4 | async-start | bytes 10485760 | tf_op jit(solution)/shard_map/all_gather | solution.py:1397
  162.5 254.6 %copy-start.2 = (bf16[512,2048]{1,0:T(8,128)(2,1)}, bf16[512,2048]{1,0:T(8,128)(2,1)S(1)}, u32[]{:S(2)}) copy-start(bf16[512,2048]{1,0:T(8,128)(2,1)S(1)} %get-tuple-element.32) | copy-start | bytes 6291460
  190.4 2.0 collective-permute-start.1
  192.4 36.5 %copy-start.27 = (s32[16]{0:T(128)S(1)}, s32[16]{0:T(128)}, u32[]{:S(2)}) copy-start(s32[16]{0:T(128)} %param.13) | copy-start | bytes 196
  192.4 770.5 %reduce-scatter.4.cloned.1.call-start = ((), (), s32[]{:S(2)}) async-start(), calls=%async_computation.5 | async-start | bytes 10485760 | tf_op jit(solution)/shard_map/reduce_scatter | solution.py:1440
  192.7 220.6 %collective-permute-start.2 = (bf16[512,2048]{1,0:T(8,128)(2,1)}, bf16[512,2048]{1,0:T(8,128)(2,1)}, u32[]{:S(2)}, u32[]{:S(2)}) collective-permute-start(bf16[512,2048]{1,0:T(8,128)(2,1)} %dynamic-slice_bitcast_fusion.1), channel_id=1, source_target_pairs={{0,4},{4,0},{1,5},{5,1},{2,6},{6,2},{3,7},{7,3},{8,12},{12,8},{9,1... | collective-permute-start | bytes 6291464 | tf_op jit(solution)/shard_map/ppermute | solution.py:1389
  220.4 193.3 %collective-permute-start.3 = (bf16[512,2048]{1,0:T(8,128)(2,1)}, bf16[512,2048]{1,0:T(8,128)(2,1)}, u32[]{:S(2)}, u32[]{:S(2)}) collective-permute-start(bf16[512,2048]{1,0:T(8,128)(2,1)} %dynamic-slice_bitcast_fusion), channel_id=1, source_target_pairs={{0,4},{4,0},{1,5},{5,1},{2,6},{6,2},{3,7},{7,3},{8,12},{12,8},{9,1... | collective-permute-start | bytes 6291464 | tf_op jit(solution)/shard_map/ppermute | solution.py:1389
  220.5 193.3 %collective-permute-start.4 = (bf16[512,2048]{1,0:T(8,128)(2,1)}, bf16[512,2048]{1,0:T(8,128)(2,1)}, u32[]{:S(2)}, u32[]{:S(2)}) collective-permute-start(bf16[512,2048]{1,0:T(8,128)(2,1)} %constant_dynamic-slice_fusion.7), channel_id=1, source_target_pairs={{0,4},{4,0},{1,5},{5,1},{2,6},{6,2},{3,7},{7,3},{8,12},{12,8},{9,1... | collective-permute-start | bytes 6291464 | tf_op jit(solution)/shard_map/ppermute | solution.py:1389
  412.5 4.5 collective-permute-start
  412.5 11.5 copy-start.19
  413.3 24.9 %collective-permute-start.5 = (bf16[512,2048]{1,0:T(8,128)(2,1)}, bf16[512,2048]{1,0:T(8,128)(2,1)}, u32[]{:S(2)}, u32[]{:S(2)}) collective-permute-start(bf16[512,2048]{1,0:T(8,128)(2,1)} %collective-permute-done.2.wg_far), channel_id=1, source_target_pairs={{0,8},{8,0},{16,24},{24,16},{1,9},{9,1},{17,25},{25,17},{2,10},{10... | collective-permute-start | bytes 6291464 | tf_op jit(solution)/shard_map/ppermute | solution.py:1359
  413.8 24.4 %collective-permute-start.6 = (bf16[512,2048]{1,0:T(8,128)(2,1)}, bf16[512,2048]{1,0:T(8,128)(2,1)}, u32[]{:S(2)}, u32[]{:S(2)}) collective-permute-start(bf16[512,2048]{1,0:T(8,128)(2,1)} %collective-permute-done.3.wu_far), channel_id=1, source_target_pairs={{0,8},{8,0},{16,24},{24,16},{1,9},{9,1},{17,25},{25,17},{2,10},{10... | collective-permute-start | bytes 6291464 | tf_op jit(solution)/shard_map/ppermute | solution.py:1359
  413.8 24.4 %collective-permute-start.7 = (bf16[512,2048]{1,0:T(8,128)(2,1)}, bf16[512,2048]{1,0:T(8,128)(2,1)}, u32[]{:S(2)}, u32[]{:S(2)}) collective-permute-start(bf16[512,2048]{1,0:T(8,128)(2,1)} %collective-permute-done.4.wd_far), channel_id=1, source_target_pairs={{0,8},{8,0},{16,24},{24,16},{1,9},{9,1},{17,25},{25,17},{2,10},{10... | collective-permute-start | bytes 6291464 | tf_op jit(solution)/shard_map/ppermute | solution.py:1359
  803.6 400.5 %reduce-scatter.8.cloned.1.call-start = ((), (), s32[]{:S(2)}) async-start(), calls=%async_computation.7 | async-start | bytes 9437184 | tf_op jit(solution)/shard_map/reduce_scatter | solution.py:1449
  804.2 406.8 %reduce-scatter.6.cloned.1.call-start = ((), (), s32[]{:S(2)}) async-start(), calls=%async_computation.6 | async-start | bytes 18874368 | tf_op jit(solution)/shard_map/reduce_scatter | solution.py:1449
  805.4 6.0 copy-start.14
  805.5 6.0 copy-start.20
  805.5 6.0 copy-start.22
  817.3 4.3 collective-permute-start.9
  817.4 13.3 %copy-start.9 = (f32[1024,256]{1,0:T(8,128)S(1)}, f32[1024,256]{1,0:T(8,128)}, u32[]{:S(2)}) copy-start(f32[1024,256]{1,0:T(8,128)} %concatenate.36.sin_ref) | copy-start | bytes 3145732
  821.6 72.9 %slice-start = ((s8[6291456]{0:T(1024)(128)(4,1)}), s8[4194304]{0:T(1024)(128)(4,1)S(1)}, s32[]{:S(2)}) async-start(s8[6291456]{0:T(1024)(128)(4,1)} %bitcast.68), calls=%async_computation.8 | async-start | bytes 8388608
  830.6 63.8 %slice-start.1 = ((s8[6291456]{0:T(1024)(128)(4,1)}), s8[2097152]{0:T(1024)(128)(4,1)S(1)}, s32[]{:S(2)}) async-start(s8[6291456]{0:T(1024)(128)(4,1)} %bitcast.68), calls=%async_computation.9 | async-start | bytes 4194304
  903.0 22.2 %copy-start.15 = (bf16[1024,2048]{1,0:T(8,128)(2,1)}, bf16[1024,2048]{1,0:T(8,128)(2,1)S(1)}, u32[]{:S(2)}) copy-start(bf16[1024,2048]{1,0:T(8,128)(2,1)S(1)} %convolution_convert_fusion.1) | copy-start | bytes 12582916
  903.3 13.1 %copy-start.12 = (bf16[1024,2048]{1,0:T(8,128)(2,1)S(1)}, bf16[1024,2048]{1,0:T(8,128)(2,1)}, u32[]{:S(2)}) copy-start(bf16[1024,2048]{1,0:T(8,128)(2,1)} %copy-done.11) | copy-start | bytes 12582916
  903.3 13.1 %copy-start.29 = (bf16[1024,1536]{1,0:T(8,128)(2,1)S(1)}, bf16[1024,1536]{1,0:T(8,128)(2,1)}, u32[]{:S(2)}) copy-start(bf16[1024,1536]{1,0:T(8,128)(2,1)} %attend_back.1) | copy-start | bytes 9437188
  903.3 21.9 %collective-permute-start.10 = (bf16[512,2048]{1,0:T(8,128)(2,1)S(1)}, bf16[512,2048]{1,0:T(8,128)(2,1)S(1)}, u32[]{:S(2)}, u32[]{:S(2)}) collective-permute-start(bf16[512,2048]{1,0:T(8,128)(2,1)S(1)} %constant_dynamic-slice_fusion), channel_id=1, source_target_pairs={{0,8},{8,0},{16,24},{24,16},{1,9},{9,1},{17,25},{25,17},{2,10},{10... | collective-permute-start | bytes 6291464 | tf_op jit(solution)/shard_map/ppermute | solution.py:1359
  916.4 8.8 copy-start.3
  962.9 244.1 %collective-permute-start.8 = (bf16[4,512,512]{2,1,0:T(8,128)(2,1)}, bf16[4,512,512]{2,1,0:T(8,128)(2,1)}, u32[]{:S(2)}, u32[]{:S(2)}) collective-permute-start(bf16[4,512,512]{2,1,0:T(8,128)(2,1)} %reduce-scatter.4.cloned.1.call-done), channel_id=1, source_target_pairs={{0,0},{4,8},{8,4},{12,12},{16,16},{20,24},{24,20},{28,28},{1,1},{5... | collective-permute-start | bytes 6291464 | tf_op jit(solution)/shard_map/ppermute | solution.py:1444
  1206.9 10.7 copy-start.1
  (16 other events, 39.8 us)
Sparse Core Ops, SparseCore 0:
  9.6 60.9 all-gather.2
  192.5 236.9 all-gather.4
  803.7 159.0 reduce-scatter.3
  966.2 120.5 reduce-scatter.7
  1090.6 120.2 reduce-scatter.5

commit v4 on v3

--- a/solution.py
+++ b/solution.py
@@ -186,6 +186,7 @@
 
 
 MESH_IDS = pl.DeviceIdType.MESH
+CORES = [[(2 * y + c) * 2 + x for y in (0, 1) for x in (0, 1)] for c in (0, 1)]
 SIBLINGS = [(0, 1), (1, 0), (2, 3), (3, 2)]
 OVER_X = [(0, 1), (1, 0)]
 CROSSED = [((2 * y + c) * 2 + x, (2 * y + x) * 2 + c) for y in (0, 1) for c in (0, 1) for x in (0, 1)]
@@ -696,8 +697,8 @@
     dgu_all,
     mlp_all,
     back_all,
-    ggu_ref,
-    gdn_ref,
+    land_ref,
+    sums_ref,
     wg,
     wu,
     wd,
@@ -714,9 +715,11 @@
     ag_recv,
     back_send,
     back_recv,
+    pair_sems,
     io_sems,
 ):
     group, core, mate, row, col = place()
+    sibling = (group + 1 - 2 * core, row, col)
     last = cols - 1
     depth = wg_own.shape[0]
     half = depth // 2
@@ -731,7 +734,8 @@
             device_id=(group, row, lax.rem(col + step, cols)),
             device_id_type=MESH_IDS,
         )
-    pl.semaphore_wait(barrier, cols - 1)
+    greet(sibling)
+    pl.semaphore_wait(barrier, cols)
 
     def pass_on(src, at, to, way):
         return pltpu.make_async_remote_copy(
@@ -760,7 +764,7 @@
     load_resid.start()
     far = (1 - row) * depth
     loads = []
-    for at, (full, mine, across, sibling) in enumerate(
+    for at, (full, mine, across, shared) in enumerate(
         ((wg, wg_own, wg_far, wg_sib), (wu, wu_own, wu_far, wu_sib), (wd, wd_own, wd_far, wd_sib))
     ):
         loads += [
@@ -769,7 +773,7 @@
                 across, full.at[rows_at(far + core * half, half)], w_sems.at[3 * at + 1]
             ),
             pltpu.make_async_copy(
-                sibling, full.at[rows_at(far + (1 - core) * half, half)], w_sems.at[3 * at + 2]
+                shared, full.at[rows_at(far + (1 - core) * half, half)], w_sems.at[3 * at + 2]
             ),
         ]
     for load in loads:
@@ -858,7 +862,7 @@
             lanes = pl.ds(pl.multiple_of(step * tile, tile), tile)
             gate = dot_nn(b_buf[...], wg[:, lanes])
             upward = dot_nn(b_buf[...], wu[:, lanes])
-            back = dot_nn(g_buf[...], wd[:, lanes])
+            back = RES_MULT * dot_nn(g_buf[...], wd[:, lanes])
             opened = 1.0 / (1.0 + jnp.exp(-gate))
             silu = gate * opened
             u_buf[:, lanes] = (silu * upward).astype(jnp.bfloat16)
@@ -926,12 +930,25 @@
     for load in loads:
         load.wait()
 
-    def results(at):
-        here = aligned(at, rows)
-        return (
-            pltpu.make_async_copy(dg_buf, ggu_ref.at[here, 0:units], io_sems.at[1]),
-            pltpu.make_async_copy(du_buf, ggu_ref.at[here, units : 2 * units], io_sems.at[2]),
-            pltpu.make_async_copy(u_buf, gdn_ref.at[here], io_sems.at[3]),
+    buffers = (dg_buf, du_buf, u_buf)
+
+    def to_sibling(at, part):
+        return pltpu.make_async_remote_copy(
+            src_ref=buffers[part],
+            dst_ref=land_ref.at[at, part],
+            send_sem=pair_sems.at[0, at, part],
+            recv_sem=pair_sems.at[1, at, part],
+            device_id=sibling,
+            device_id_type=MESH_IDS,
+        )
+
+    def landed(at, part):
+        return pltpu.make_async_copy(land_ref.at[at, part], buffers[part], io_sems.at[5 + part])
+
+    def results(at, part):
+        here = slice(part * units, (part + 1) * units)
+        return pltpu.make_async_copy(
+            buffers[part], sums_ref.at[at, :, here], io_sems.at[1 + part]
         )
 
     def turned(source, into, at):
@@ -941,29 +958,60 @@
         for chunk in range(cols):
             into[:, chunk * rows : (chunk + 1) * rows] = turn_buf[chunk].T
 
+    parts = range(3)
+
     def one_block(at, unused):
-        turned(b_all, b_buf, at)
-        turned(grad_ref, g_buf, at)
-
-        @pl.when(at > 0)
+        high = lax.rem(at, 2)
+        is_own = at >= 2
+        block = 2 * high + jnp.where(is_own, core, 1 - core)
+        turned(b_all, b_buf, block)
+        turned(grad_ref, g_buf, block)
+
+        @pl.when((at == 1) | (at == 2))
         def _():
-            for copy in results(at - 1):
-                copy.wait()
+            for part in parts:
+                to_sibling(at - 1, part).wait_send()
+
+        @pl.when(at == 3)
+        def _():
+            for part in parts:
+                results(0, part).wait()
+
+        @pl.when(is_own)
+        def _():
+            for part in parts:
+                to_sibling(high, part).wait_recv()
+                landed(high, part).start()
+            for part in parts:
+                landed(high, part).wait()
 
         @pl.loop(0, units // tile)
         def _(step):
             lanes = aligned(step, tile)
-            dg_buf[:, lanes] = dot_nn(b_buf[...], wg[:, lanes]).astype(jnp.bfloat16)
-            du_buf[:, lanes] = dot_nn(b_buf[...], wu[:, lanes]).astype(jnp.bfloat16)
-            u_buf[:, lanes] = dot_nn(g_buf[...], wd[:, lanes]).astype(jnp.bfloat16)
-
-        for copy in results(at):
-            copy.start()
+
+            def put(buffer, value):
+                other = jnp.where(is_own, buffer[:, lanes].astype(jnp.float32), 0.0)
+                buffer[:, lanes] = (other + value).astype(jnp.bfloat16)
+
+            put(dg_buf, dot_nn(b_buf[...], wg[:, lanes]))
+            put(du_buf, dot_nn(b_buf[...], wu[:, lanes]))
+            put(u_buf, RES_MULT * dot_nn(g_buf[...], wd[:, lanes]))
+
+        @pl.when(jnp.logical_not(is_own))
+        def _():
+            for part in parts:
+                to_sibling(at, part).start()
+
+        @pl.when(is_own)
+        def _():
+            for part in parts:
+                results(high, part).start()
+
         return unused
 
-    lax.fori_loop(0, cols, one_block, 0)
-    for copy in results(last):
-        copy.wait()
+    lax.fori_loop(0, 4, one_block, 0)
+    for part in parts:
+        results(1, part).wait()
     for at in range(1, cols):
         back_out(at, order(at)).wait_send()
         source = lax.rem(col + at, cols)
@@ -999,8 +1047,8 @@
             jax.ShapeDtypeStruct((cols, rows, 2 * units), bf16),
             jax.ShapeDtypeStruct((cols, rows, width), bf16),
             jax.ShapeDtypeStruct((cols, rows, width), bf16),
-            jax.ShapeDtypeStruct((width, 2 * units), bf16),
-            jax.ShapeDtypeStruct((width, units), bf16),
+            jax.ShapeDtypeStruct((2, 3, rows, units), bf16),
+            jax.ShapeDtypeStruct((2, rows, 3 * units), bf16),
         ),
         in_specs=[anywhere] * 12,
         out_specs=(anywhere,) * 7,
@@ -1021,6 +1069,7 @@
             pltpu.SemaphoreType.DMA((cols,)),
             pltpu.SemaphoreType.DMA((cols,)),
             pltpu.SemaphoreType.DMA((cols,)),
+            pltpu.SemaphoreType.DMA((2, 2, 3)),
             pltpu.SemaphoreType.DMA((9,)),
         ],
         compiler_params=pltpu.CompilerParams(
@@ -1377,29 +1426,27 @@
     )
 
     length = lax.dynamic_slice_in_dim(lengths, mate * seq_group + col, 1)
-    line_lengths = lax.dynamic_slice_in_dim(lengths, mate * seq_group, seq_group)
-    own_pos = core * rows_local + jnp.arange(rows_local, dtype=jnp.int32)
-    line_live = (own_pos[None, :] < line_lengths[:, None]).astype(jnp.float32)
-    own_live = (own_pos < length).astype(jnp.float32)[:, None]
-
-    w_gate_up, attn_input = lax.optimization_barrier((w_gate_up, attn_input))
-    own_mats = (w_gate_up[:, 0], w_gate_up[:, 1], w_down)
-    halves = tuple(half_rows(matrix) for matrix in own_mats)
-    halves, attn_input = lax.optimization_barrier((halves, attn_input))
-    far_mats = tuple(lax.ppermute(matrix, "row", OVER_X) for matrix in halves)
-    sibling_mats = tuple(from_sibling(matrix) for matrix in far_mats)
-
+    given_pos = row * rows_local + jnp.arange(rows_local, dtype=jnp.int32)
+    given_lengths = lax.dynamic_slice_in_dim(lengths, group * seq_group, seq_group)
+    given_live = given_pos[None, :, None] < given_lengths[:, None, None]
     everyone = lax.all_gather(cotangent, "dp", axis=0, tiled=True)
     everyone, attn_input = lax.optimization_barrier((everyone, attn_input))
-    given = lax.ppermute(
-        pick_sequences(everyone, deal_order, group * seq_group, seq_group), ("dp", "row"), CROSSED
-    )
+    picked = pick_sequences(everyone, deal_order, group * seq_group, seq_group)
+    picked = jnp.where(given_live, picked, jnp.zeros_like(picked))
+    given = lax.ppermute(picked, ("dp", "row"), CROSSED)
+    weights_out = gather_weights(pack_o, picked, row_count, col_count)
+    given, weights_out = lax.optimization_barrier((given, weights_out))
     line_cot = lax.all_gather(given, "col", axis=2, tiled=True)
-    line_grad = line_live[:, :, None] * line_cot.astype(jnp.float32)
-    grad_ffn = (RES_MULT * line_grad).astype(jnp.bfloat16).reshape(-1, full_width)
-    own_grad = own_live * lax.dynamic_index_in_dim(line_cot, col, keepdims=False).astype(
-        jnp.float32
-    )
+    own_grad = lax.dynamic_index_in_dim(line_cot, col, keepdims=False).astype(jnp.float32)
+
+    w_gate_up, w_down, attn_input, weights_out = lax.optimization_barrier(
+        (w_gate_up, w_down, attn_input, weights_out)
+    )
+    far_gate_up = lax.ppermute(half_rows(w_gate_up), "row", OVER_X)
+    far_down = lax.ppermute(half_rows(w_down), "row", OVER_X)
+    own_mats = (w_gate_up[:, 0], w_gate_up[:, 1], w_down)
+    far_mats = (far_gate_up[:, 0], far_gate_up[:, 1], far_down)
+    sibling_mats = tuple(from_sibling(matrix) for matrix in far_mats)
 
     cosine_table, sine_table = rope_tables(jnp.arange(slot_len, dtype=jnp.int32), HEAD_SIZE)
     cosine_table, sine_table = lax.optimization_barrier((cosine_table, sine_table))
@@ -1422,37 +1469,27 @@
         other = lax.dynamic_slice_in_dim(partial, (1 - core) * count, count)
         return mine.astype(jnp.float32) + from_sibling(other).astype(jnp.float32)
 
-    weights_out = gather_weights(pack_o, heads_out, row_count, col_count)
     attn_rows = summed_rows(expand_local(heads_out, weights_out).astype(jnp.bfloat16))
     resid = own_float + RES_MULT * attn_rows
     scale_two = lax.rsqrt(jnp.mean(resid * resid, axis=1, keepdims=True) + EPSILON)
     own_ffn = (resid * scale_two * gain_two).astype(jnp.bfloat16)
 
-    unused_b, unused_u, unused_gu, mlp_part, back_part, grad_gu, grad_dn = feed_forward(
+    unused_b, unused_u, unused_gu, mlp_part, back_part, unused_land, grad_sums = feed_forward(
         own_ffn,
         resid.astype(jnp.bfloat16),
-        grad_ffn.reshape(col_count, rows_local, full_width),
+        line_cot,
         own_mats + far_mats + sibling_mats,
         col_count,
     )
     grad_normed_two = jnp.sum(back_part.astype(jnp.float32), axis=0)
 
-    out_cols = lax.psum_scatter(mlp_part, "col", scatter_dimension=2, tiled=True)
-    given_pos = row * rows_local + jnp.arange(rows_local, dtype=jnp.int32)
-    given_lengths = lax.dynamic_slice_in_dim(lengths, group * seq_group, seq_group)
-    given_live = (given_pos[None, :] < given_lengths[:, None]).astype(jnp.float32)
-    layer_out = given_live[:, :, None] * lax.ppermute(
-        out_cols, ("dp", "row"), CROSSED
-    ).astype(jnp.float32)
-
-    def scatter_rows(matrix):
-        return lax.psum_scatter(
-            matrix, ("dp", "row"), scatter_dimension=0, tiled=True
-        ).astype(jnp.float32)
-
-    sums_down = scatter_rows(grad_dn)
-    sums_gate_up = scatter_rows(grad_gu)
-    sums_gate_up = sums_gate_up.reshape(-1, 2, hidden)
+    sums_ffn = lax.psum_scatter(
+        grad_sums.reshape(-1, 3 * hidden),
+        ("dp", "row"),
+        scatter_dimension=0,
+        axis_index_groups=CORES,
+        tiled=True,
+    )
 
     weighted_two = grad_normed_two * gain_two
     inner_two = jnp.sum(weighted_two * resid, axis=1, keepdims=True)
@@ -1467,6 +1504,10 @@
     grad_projected = attend_back_fast(
         length, projected, grad_heads, cosines, sines, col_count
     )
+    mlp_part, sums_ffn, grad_projected = lax.optimization_barrier(
+        (mlp_part, sums_ffn, grad_projected)
+    )
+    out_cols = lax.psum_scatter(mlp_part, "col", scatter_dimension=2, tiled=True)
     grad_normed_one = summed_rows(expand_local(grad_projected, weights_qkv).astype(jnp.bfloat16))
     grad_qkv = token_outer(attn_input, grad_projected).astype(jnp.bfloat16)
     weighted_one = grad_normed_one * gain_one
@@ -1477,9 +1518,16 @@
         - own_float * scale_one**3 * inner_one / full_width
     ).astype(jnp.bfloat16)
     gain_one_part = jnp.sum(grad_normed_one * own_float * scale_one, axis=0)
+    sums_ffn = sums_ffn.astype(jnp.float32)
+    sums_gate_up = sums_ffn[:, : 2 * hidden].reshape(-1, 2, hidden)
+    sums_down = sums_ffn[:, 2 * hidden :]
     gains = jnp.stack([gain_one_part, gain_two_part]).reshape(8, -1)
     given_grad, sums_q, sums_o, gain_sums = finish(
         own_input_grad, grad_qkv, grad_out, gains, col_count
+    )
+    out_cols, given_grad = lax.optimization_barrier((out_cols, given_grad))
+    layer_out = jnp.where(
+        given_live, lax.ppermute(out_cols, ("dp", "row"), CROSSED).astype(jnp.float32), 0.0
     )
     input_grad = given_grad.astype(jnp.float32)
     grad_gain_attn, grad_gain_ffn = gain_sums.reshape(2, full_width)

time: 1230 us -> 1250 us (1.016)
  waiting for transfers between devices: 47.6 us -> 129 us
  Pallas kernels: 944 us -> 907 us
  other arithmetic: 50.4 us -> 35.6 us
  starting transfers between devices: 50.6 us -> 37.9 us
    ppermute x4 -> x3, waiting for transfers between devices: 0.01 us -> 75.3 us  [the longest x1 75.3 us: one_sequence_body(): far_down = lax.ppermute(half_rows(w_down), 'row', OVER_X)]
    reduce_scatter x2 -> x1, waiting for transfers between devices: 0.01 us -> 48.9 us  [one_sequence_body(): lax.psum_scatter(grad_sums.reshape(-1, 3 * hidden), ('dp', 'row'), scatte...]
    pallas_call x1, Pallas kernels: 122 us -> 79.8 us  [gather_weights(): pl.pallas_call(functools.partial(gather_kernel, cols), out_shape=jax.Shap...]
    reduce_scatter x1, waiting for transfers between devices: 35.9 us -> 0.01 us  [one_sequence_body(): lax.psum_scatter(mlp_part, 'col', scatter_dimension=2, tiled=True)]
    ppermute x4 -> x3, starting transfers between devices: 31.8 us -> 19.2 us  [the longest x1 17.1 us: one_sequence_body(): given = lax.ppermute(picked, ('dp', 'row'), CROSSED)]
  transfers between devices with their start and end apart: 16 -> 14, of which waited for: 4 -> 3; matrix products, arithmetic and copies ran while one was open for 11% -> 10% of each run, Pallas kernels for 47% -> 43%
where the time goes in v4:
time: 1250 us; the launch traced here: 1240 us
  Pallas kernels  907 us (73%)
  waiting for transfers between devices  129 us (10%)
  local copies, waits for them, and re-layouts  68.9 us (6%)
  matrix products  41.8 us (3%)
  starting transfers between devices  37.9 us (3%)
  other arithmetic  35.6 us (3%)
  between operations  22.7 us (2%)
    pallas_call x1, Pallas kernels, feed_forward(): pl.pallas_call(functools.partial(ffn_kernel, cols), out_shape=(jax.ShapeD...  372 us
    pallas_call x1, Pallas kernels, finish(): pl.pallas_call(functools.partial(finish_kernel, cols), out_shape=(jax.Sha...  210 us
    pallas_call x1, Pallas kernels, start_exchange(): pl.pallas_call(functools.partial(start_kernel, cols), out_shape=(jax.Shap...  138 us
    pallas_call x1, Pallas kernels, gather_weights(): pl.pallas_call(functools.partial(gather_kernel, cols), out_shape=jax.Shap...  79.8 us
    ppermute x1, waiting for transfers between devices, one_sequence_body(): far_down = lax.ppermute(half_rows(w_down), 'row', OVER_X)  75.3 us
    pallas_call x1, Pallas kernels, attend_back_fast(): pl.pallas_call(functools.partial(attend_back_kernel, block), grid=(groups...  63.4 us
    reduce_scatter x1, waiting for transfers between devices, one_sequence_body(): lax.psum_scatter(grad_sums.reshape(-1, 3 * hidden), ('dp', 'row'), scatte...  48.9 us
    pallas_call x1, Pallas kernels, attend_fast(): pl.pallas_call(functools.partial(attend_kernel, block), grid=(groups,), o...  43.7 us
  transfers between devices with their start and end apart: 14, of which 3 were waited for; matrix products, arithmetic and copies ran while one was open for 10% of the time, Pallas kernels for 43%

profile of v4, /device:TPU:0, one launch (start us, length us, event | category | flops | bytes accessed | tf_op | source)
XLA Modules:
  0.0 1242.9 jit_solution(13647039879552583709)
XLA Ops:
  22.9 137.6 %start_exchange.1 = (bf16[512,2048]{1,0:T(8,128)(2,1)S(1)}, bf16[1024,2048]{1,0:T(8,128)(2,1)S(1)}, bf16[2048,1536]{1,0:T(8,128)(2,1)S(1)}) custom-call(bf16[4,512,512]{2,1,0:T(8,128)(2,1)S(1)} %copy-done.5, bf16[1024,384]{1,0:T(8,128)(2,1)S(1)} %pad_maximum_fusion.pq_ref, f32[1,2048]{1,0:T(1,128)S(1)} %bitcast.67), custom_call_target="tpu_custom_call" | custom-call | bytes 419430400 | tf_op jit(solution)/shard_map/start_exchange/pallas_call | solution.py:388
  160.5 2.7 copy-done.9
  165.3 2.4 constant_dynamic-slice_fusion.8
  169.2 17.1 %collective-permute-start = (bf16[4,512,512]{2,1,0:T(8,128)(2,1)}, bf16[4,512,512]{2,1,0:T(8,128)(2,1)}, u32[]{:S(2)}, u32[]{:S(2)}) collective-permute-start(bf16[4,512,512]{2,1,0:T(8,128)(2,1)} %maximum_select_fusion.1.after_ref), channel_id=1, source_target_pairs={{0,0},{4,8},{8,4},{12,12},{16,16},{20,24},{24,20},{28,28},{1,1},{5... | collective-permute-start | bytes 6291464 | tf_op jit(solution)/shard_map/ppermute | solution.py:1436
  187.2 79.8 %gather_weights.1 = bf16[2048,1024]{1,0:T(8,128)(2,1)} custom-call(bf16[1024,256]{1,0:T(8,128)(2,1)} %constant_dynamic-slice_fusion.4.own_ref, bf16[4,512,512]{2,1,0:T(8,128)(2,1)} %maximum_select_fusion.1.after_ref), custom_call_target="tpu_custom_call" | custom-call | bytes 209715200 | tf_op jit(solution)/shard_map/gather_weights/pallas_call | solution.py:435
  267.1 10.8 copy.50
  277.9 5.4 constant_dynamic-slice_fusion.2
  291.7 3.2 constant_dynamic-slice_fusion.1
  296.1 43.7 %attend.1 = (bf16[1024,1536]{1,0:T(8,128)(2,1)}, bf16[1024,1024]{1,0:T(8,128)(2,1)S(1)}) custom-call(s32[1]{0:T(128)} %dynamic_slice.75.len_ref, bf16[1024,2048]{1,0:T(8,128)(2,1)} %copy-done.10, bf16[2048,1536]{1,0:T(8,128)(2,1)} %copy-done.9, f32[1024,256]{1,0:T(8,128)S(1)} %copy-done.6, f32[1024,256]{1,0:T(8,128)S(1)} %concatenate.37.sin_ref), custom_call_target="tpu_custom_call" | custom-call | flops 10737418240 | bytes 13631488 | tf_op jit(solution)/shard_map/attend/pallas_call | solution.py:544
  339.9 4.8 convolution_convert_fusion.3
  345.4 75.3 %collective-permute-done.3.wd_far = bf16[512,2048]{1,0:T(8,128)(2,1)} collective-permute-done((bf16[512,2048]{1,0:T(8,128)(2,1)}, bf16[512,2048]{1,0:T(8,128)(2,1)}, u32[]{:S(2)}, u32[]{:S(2)}) %collective-permute-start.3) | collective-permute-done | bytes 2097184 | tf_op jit(solution)/shard_map/ppermute | solution.py:1446
  420.7 2.5 slice_bitcast_fusion.2
  423.9 4.1 slice_bitcast_fusion
  428.1 3.5 fusion.13
  435.8 372.4 %feed_forward.1 = (bf16[4,512,2048]{2,1,0:T(8,128)(2,1)}, bf16[4,512,2048]{2,1,0:T(8,128)(2,1)}, bf16[4,512,4096]{2,1,0:T(8,128)(2,1)}, bf16[4,512,2048]{2,1,0:T...) custom-call(bf16[512,2048]{1,0:T(8,128)(2,1)} %multiply_convert_fusion, ...), custom_call_target="tpu_custom_call" | custom-call | flops 154618822656 | bytes 838860800 | tf_op jit(solution)/shard_map/feed_forward/pallas_call | solution.py:1042
  808.7 6.0 convert_reduce_fusion
  815.8 4.3 multiply_convert_fusion
  820.1 4.3 collective-permute-done.7
  824.4 8.2 convolution_convert_fusion.4.dz_ref
  832.6 63.4 %attend_back.1 = bf16[1024,1536]{1,0:T(8,128)(2,1)} custom-call(s32[1]{0:T(128)} %dynamic_slice.75.len_ref, bf16[1024,1536]{1,0:T(8,128)(2,1)} %get-tuple-element.52.qkv_ref, bf16[1024,1024]{1,0:T(8,128)(2,1)S(1)} %convolution_convert_fusion.4.dz_ref, f32[1024,256]{1,0:T(8,128)S(1)} %copy-done.7, f32[1024,256]{1,0:T(8,128)S(1)} %concatenate.37.sin_ref), custom_call_target="tpu_custom_call" | custom-call | flops 10737418240 | bytes 8388608 | tf_op jit(solution)/shard_map/attend_back/pallas_call | solution.py:651
  896.1 48.9 %reduce-scatter.3.cloned.1.call-done = bf16[256,6144]{1,0:T(8,128)(2,1)} async-done(((bf16[1024,6144]{1,0:T(8,128)(2,1)}), bf16[256,6144]{1,0:T(8,128)(2,1)}) %reduce-scatter.3.cloned.1.call-update) | async-done | bytes 3145744 | tf_op jit(solution)/shard_map/reduce_scatter | solution.py:1486
  945.7 9.8 convolution_convert_fusion.1
  955.8 2.7 copy-done.13
  958.6 10.2 convolution_convert_fusion.2
  968.8 8.8 convolution_convert_fusion
  979.4 4.9 fusion.4.ig_ref
  984.3 209.7 %finish.1 = (bf16[4,512,512]{2,1,0:T(8,128)(2,1)S(1)}, f32[2,256,384]{2,1,0:T(8,128)S(1)}, f32[2,256,256]{2,1,0:T(8,128)S(1)}, f32[8,512]{1,0:T(8,128)S(1)}) custom-call(bf16[512,2048]{1,0:T(8,128)(2,1)S(1)} %fusion.4.ig_ref, bf16[2,2,2,256,1536]{4,3,2,1,0:T(8,128)(2,1)} %bitcast.71, bf16[2,2,2,256,1024]{4,3,2,1,0:T(8,128)(2,1)S(1)} %bitcast.66, ...), custom_call_target="tpu_custom_call" | custom-call | bytes 314572800 | tf_op jit(solution)/shard_map/finish/pallas_call | solution.py:1339
  1194.9 17.4 %collective-permute-start.9 = (bf16[4,512,512]{2,1,0:T(8,128)(2,1)}, bf16[4,512,512]{2,1,0:T(8,128)(2,1)}, u32[]{:S(2)}, u32[]{:S(2)}) collective-permute-start(bf16[4,512,512]{2,1,0:T(8,128)(2,1)} %reduce-scatter.5.cloned.1.call-done), channel_id=1, source_target_pairs={{0,0},{4,8},{8,4},{12,12},{16,16},{20,24},{24,20},{28,28},{1,1},{5... | collective-permute-start | bytes 6291464 | tf_op jit(solution)/shard_map/ppermute | solution.py:1530
  1212.3 4.1 slice.79
  1217.9 6.6 reshape.139
  1229.8 2.6 convert_element_type.96
  1232.4 3.5 convert_select_fusion
  (152 shorter events, 39.3 us)
Async XLA Ops:
  7.2 13.6 %copy-start = (bf16[1024,512]{1,0:T(8,128)(2,1)S(1)}, bf16[1024,512]{1,0:T(8,128)(2,1)}, u32[]{:S(2)}) copy-start(bf16[1024,512]{1,0:T(8,128)(2,1)} %param.17) | copy-start | bytes 3145732
  7.2 10.8 copy-start.31
  7.2 10.8 copy-start.34
  7.2 158.1 %all-gather.3.cloned.1.call-start = ((), (), s32[]{:S(2)}) async-start(), calls=%async_computation.2 | async-start | bytes 10485760 | tf_op jit(solution)/shard_map/all_gather | solution.py:1432
  7.9 427.8 %all-gather.5.cloned.1.call-start = ((), (), s32[]{:S(2)}) async-start(), calls=%async_computation.3 | async-start | bytes 10485760 | tf_op jit(solution)/shard_map/all_gather | solution.py:1439
  165.2 262.8 %copy-start.2 = (bf16[512,2048]{1,0:T(8,128)(2,1)}, bf16[512,2048]{1,0:T(8,128)(2,1)S(1)}, u32[]{:S(2)}) copy-start(bf16[512,2048]{1,0:T(8,128)(2,1)S(1)} %get-tuple-element.36) | copy-start | bytes 6291460
  165.3 21.1 %copy-start.22 = (bf16[1024,512]{1,0:T(8,128)(2,1)S(1)}, bf16[1024,512]{1,0:T(8,128)(2,1)}, u32[]{:S(2)}) copy-start(bf16[1024,512]{1,0:T(8,128)(2,1)} %param.19) | copy-start | bytes 3145732
  169.2 97.8 %collective-permute-start = (bf16[4,512,512]{2,1,0:T(8,128)(2,1)}, bf16[4,512,512]{2,1,0:T(8,128)(2,1)}, u32[]{:S(2)}, u32[]{:S(2)}) collective-permute-start(bf16[4,512,512]{2,1,0:T(8,128)(2,1)} %maximum_select_fusion.1.after_ref), channel_id=1, source_target_pairs={{0,0},{4,8},{8,4},{12,12},{16,16},{20,24},{24,20},{28,28},{1,1},{5... | collective-permute-start | bytes 6291464 | tf_op jit(solution)/shard_map/ppermute | solution.py:1436
  267.0 678.0 %reduce-scatter.3.cloned.1.call-start = ((), (), s32[]{:S(2)}) async-start(), calls=%async_computation.4 | async-start | bytes 15728640 | tf_op jit(solution)/shard_map/reduce_scatter | solution.py:1486
  283.3 137.4 %collective-permute-start.2 = (bf16[512,2,2048]{2,0,1:T(8,128)(2,1)}, bf16[512,2,2048]{2,0,1:T(8,128)(2,1)}, u32[]{:S(2)}, u32[]{:S(2)}) collective-permute-start(bf16[512,2,2048]{2,0,1:T(8,128)(2,1)} %constant_dynamic-slice_fusion.2), channel_id=1, source_target_pairs={{0,4},{4,0},{1,5},{5,1},{2,6},{6,2},{3,7},{7,3},{8,12},{12,8},{9,1... | collective-permute-start | bytes 12582920 | tf_op jit(solution)/shard_map/ppermute | solution.py:1445
  295.0 125.7 %collective-permute-start.3 = (bf16[512,2048]{1,0:T(8,128)(2,1)}, bf16[512,2048]{1,0:T(8,128)(2,1)}, u32[]{:S(2)}, u32[]{:S(2)}) collective-permute-start(bf16[512,2048]{1,0:T(8,128)(2,1)} %constant_dynamic-slice_fusion.1), channel_id=1, source_target_pairs={{0,4},{4,0},{1,5},{5,1},{2,6},{6,2},{3,7},{7,3},{8,12},{12,8},{9,1... | collective-permute-start | bytes 6291464 | tf_op jit(solution)/shard_map/ppermute | solution.py:1446
  296.1 43.8 %copy-start.19 = (bf16[2048,1024]{1,0:T(8,128)(2,1)S(1)}, bf16[2048,1024]{1,0:T(8,128)(2,1)}, u32[]{:S(2)}) copy-start(bf16[2048,1024]{1,0:T(8,128)(2,1)} %gather_weights.1) | copy-start | bytes 12582916
  339.9 84.1 %slice-start = ((s8[8388608]{0:T(1024)(128)(4,1)}), s8[4194304]{0:T(1024)(128)(4,1)S(1)}, s32[]{:S(2)}) async-start(s8[8388608]{0:T(1024)(128)(4,1)} %bitcast.68), calls=%async_computation.6 | async-start | bytes 8388608
  339.9 84.0 %slice-start.1 = ((s8[8388608]{0:T(1024)(128)(4,1)}), s8[4194304]{0:T(1024)(128)(4,1)S(1)}, s32[]{:S(2)}) async-start(s8[8388608]{0:T(1024)(128)(4,1)} %bitcast.68), calls=%async_computation.7 | async-start | bytes 8388608
  344.9 83.2 %collective-permute-start.1 = (bf16[512,2048]{1,0:T(8,128)(2,1)S(1)}, bf16[512,2048]{1,0:T(8,128)(2,1)S(1)}, u32[]{:S(2)}, u32[]{:S(2)}) collective-permute-start(bf16[512,2048]{1,0:T(8,128)(2,1)S(1)} %constant_dynamic-slice_fusion.3), channel_id=1, source_target_pairs={{0,8},{8,0},{16,24},{24,16},{1,9},{9,1},{17,25},{25,17},{2,10},{10... | collective-permute-start | bytes 6291464 | tf_op jit(solution)/shard_map/ppermute | solution.py:1408
  345.4 87.4 %copy-start.23 = (f32[2048]{0:T(1024)}, f32[2048]{0:T(1024)S(1)}, u32[]{:S(2)}) copy-start(f32[2048]{0:T(1024)S(1)} %convert_element_type.81) | copy-start | bytes 24580
  420.7 13.8 %collective-permute-start.6 = (bf16[512,2048]{1,0:T(8,128)(2,1)}, bf16[512,2048]{1,0:T(8,128)(2,1)S(1)}, u32[]{:S(2)}, u32[]{:S(2)}) collective-permute-start(bf16[512,2048]{1,0:T(8,128)(2,1)} %collective-permute-done.3.wd_far), channel_id=1, source_target_pairs={{0,8},{8,0},{16,24},{24,16},{1,9},{9,1},{17,25},{25,17},{2,10},{10... | collective-permute-start | bytes 6291464 | tf_op jit(solution)/shard_map/ppermute | solution.py:1408
  423.3 11.2 collective-permute-start.4
  423.8 12.0 collective-permute-start.5
  808.2 386.6 %reduce-scatter.5.cloned.1.call-start = ((), (), s32[]{:S(2)}) async-start(), calls=%async_computation.5 | async-start | bytes 10485760 | tf_op jit(solution)/shard_map/reduce_scatter | solution.py:1510
  808.7 6.0 copy-start.15
  808.7 6.0 copy-start.24
  820.1 4.3 collective-permute-start.7
  820.1 12.5 %copy-start.7 = (f32[1024,256]{1,0:T(8,128)S(1)}, f32[1024,256]{1,0:T(8,128)}, u32[]{:S(2)}) copy-start(f32[1024,256]{1,0:T(8,128)} %concatenate.35.cos_ref) | copy-start | bytes 3145732
  955.5 22.2 %copy-start.17 = (bf16[1024,2048]{1,0:T(8,128)(2,1)}, bf16[1024,2048]{1,0:T(8,128)(2,1)S(1)}, u32[]{:S(2)}) copy-start(bf16[1024,2048]{1,0:T(8,128)(2,1)S(1)} %convolution_convert_fusion.1) | copy-start | bytes 12582916
  955.7 13.1 %copy-start.11 = (bf16[1024,2048]{1,0:T(8,128)(2,1)S(1)}, bf16[1024,2048]{1,0:T(8,128)(2,1)}, u32[]{:S(2)}) copy-start(bf16[1024,2048]{1,0:T(8,128)(2,1)} %copy-done.10) | copy-start | bytes 12582916
  955.8 13.1 %copy-start.35 = (bf16[1024,1536]{1,0:T(8,128)(2,1)S(1)}, bf16[1024,1536]{1,0:T(8,128)(2,1)}, u32[]{:S(2)}) copy-start(bf16[1024,1536]{1,0:T(8,128)(2,1)} %attend_back.1) | copy-start | bytes 9437188
  955.8 21.9 %collective-permute-start.8 = (bf16[512,2048]{1,0:T(8,128)(2,1)S(1)}, bf16[512,2048]{1,0:T(8,128)(2,1)S(1)}, u32[]{:S(2)}, u32[]{:S(2)}) collective-permute-start(bf16[512,2048]{1,0:T(8,128)(2,1)S(1)} %constant_dynamic-slice_fusion), channel_id=1, source_target_pairs={{0,8},{8,0},{16,24},{24,16},{1,9},{9,1},{17,25},{25,17},{2,10},{10... | collective-permute-start | bytes 6291464 | tf_op jit(solution)/shard_map/ppermute | solution.py:1408
  968.8 8.8 copy-start.3
  1194.8 21.5 %copy-start.16 = (bf16[256,6144]{1,0:T(8,128)(2,1)S(1)}, bf16[256,6144]{1,0:T(8,128)(2,1)}, u32[]{:S(2)}) copy-start(bf16[256,6144]{1,0:T(8,128)(2,1)} %reduce-scatter.3.cloned.1.call-done) | copy-start | bytes 9437188
  1194.9 37.6 %collective-permute-start.9 = (bf16[4,512,512]{2,1,0:T(8,128)(2,1)}, bf16[4,512,512]{2,1,0:T(8,128)(2,1)}, u32[]{:S(2)}, u32[]{:S(2)}) collective-permute-start(bf16[4,512,512]{2,1,0:T(8,128)(2,1)} %reduce-scatter.5.cloned.1.call-done), channel_id=1, source_target_pairs={{0,0},{4,8},{8,4},{12,12},{16,16},{20,24},{24,20},{28,28},{1,1},{5... | collective-permute-start | bytes 6291464 | tf_op jit(solution)/shard_map/ppermute | solution.py:1530
  1229.8 6.1 copy-start.1
  (20 other events, 57.7 us)
Sparse Core Ops, SparseCore 0:
  9.6 60.9 all-gather.2
  267.1 152.5 all-gather.4
  808.3 136.6 reduce-scatter.2
  947.2 223.7 reduce-scatter.4

commit v5 on v4

--- a/solution.py
+++ b/solution.py
@@ -186,9 +186,9 @@
 
 
 MESH_IDS = pl.DeviceIdType.MESH
-CORES = [[(2 * y + c) * 2 + x for y in (0, 1) for x in (0, 1)] for c in (0, 1)]
 SIBLINGS = [(0, 1), (1, 0), (2, 3), (3, 2)]
 OVER_X = [(0, 1), (1, 0)]
+OVER_Y = [(0, 2), (2, 0), (1, 3), (3, 1)]
 CROSSED = [((2 * y + c) * 2 + x, (2 * y + x) * 2 + c) for y in (0, 1) for c in (0, 1) for x in (0, 1)]
 
 
@@ -242,42 +242,16 @@
     )
 
 
-def weight_copies(cols, own, full, sems, x_sems):
-    group, core, mate, row, col = place()
-    tall, wide = own.shape
-
-    def block(of_row, of_col):
-        return full.at[aligned(of_row, tall), aligned(of_col, wide)]
-
-    def line(step):
-        return lined(col, step, cols)
-
-    over = (group, 1 - row, col)
-    steps = range(1, cols)
-    along = [remote(own, block(row, col), sems, k, (group, row, line(k))) for k in steps]
-    arrive = [remote(own, block(row, line(-k)), sems, k, (group, row, line(k))) for k in steps]
-    across = [remote(own, block(row, col), x_sems, 0, over)] + [
-        remote(block(row, line(-k)), block(row, line(-k)), x_sems, k, over) for k in steps
-    ]
-    landed = [remote(own, block(1 - row, line(-k)), x_sems, k, over) for k in range(cols)]
-    return along, arrive, across, landed, block(row, col)
+def line_order(col, last, at):
+    inner_low = jnp.where(at < 2, 1 - at, at)
+    inner_high = jnp.where(at == 3, 0, jnp.where(at == 0, 2, jnp.where(at == 1, 1, 3)))
+    return jnp.where(
+        col == 0, at, jnp.where(col == last, last - at, jnp.where(col == 1, inner_low, inner_high))
+    )
 
 
 def start_kernel(
-    cols,
-    tok_ref,
-    pq_ref,
-    gain_ref,
-    x_ref,
-    a_ref,
-    wq_ref,
-    x_buf,
-    a_buf,
-    tok_sems,
-    q_sems,
-    qx_sems,
-    a_sems,
-    local_sems,
+    cols, tok_ref, gain_ref, x_ref, a_ref, x_buf, a_buf, tok_sems, a_sems, local_sems
 ):
     group, core, mate, row, col = place()
     width = tok_ref.shape[2]
@@ -289,20 +263,13 @@
 
     for step in range(1, cols):
         greet((mate, core, line(step)))
-        greet((group, row, line(step)))
-    greet((group, 1 - row, col))
     greet(sibling)
 
     @pl.when(core != row)
     def _():
         greet((mate, core, col))
 
-    pl.semaphore_wait(
-        pltpu.get_barrier_semaphore(), 2 * cols + (core - row) * (core - row)
-    )
-
-    along, arrive, across, landed, own_place = weight_copies(cols, pq_ref, wq_ref, q_sems, qx_sems)
-    own_q = pltpu.make_async_copy(pq_ref, own_place, local_sems.at[0])
+    pl.semaphore_wait(pltpu.get_barrier_semaphore(), cols + (core - row) * (core - row))
 
     def token_copy(step, into):
         return remote(
@@ -314,7 +281,7 @@
         )
 
     own_tokens = pltpu.make_async_copy(
-        tok_ref.at[col], x_buf.at[:, aligned(col, width)], local_sems.at[1]
+        tok_ref.at[col], x_buf.at[:, aligned(col, width)], local_sems.at[0]
     )
     for step in range(1, cols):
         token_copy(step, col).start()
@@ -327,10 +294,6 @@
     def _():
         own_tokens.start()
 
-    for copy in along:
-        copy.start()
-    across[0].start()
-    own_q.start()
     for step in range(1, cols):
         token_copy(step, line(-step)).wait_recv()
 
@@ -342,7 +305,7 @@
     def _():
         own_tokens.wait()
 
-    keep_x = pltpu.make_async_copy(x_buf, x_ref, local_sems.at[2])
+    keep_x = pltpu.make_async_copy(x_buf, x_ref, local_sems.at[1])
     keep_x.start()
     tall = min(64, length)
 
@@ -356,12 +319,9 @@
     def a_copy(of_core):
         return remote(a_buf, a_ref.at[aligned(of_core, length)], a_sems, 0, sibling)
 
-    own_a = pltpu.make_async_copy(a_buf, a_ref.at[aligned(core, length)], local_sems.at[3])
+    own_a = pltpu.make_async_copy(a_buf, a_ref.at[aligned(core, length)], local_sems.at[2])
     a_copy(core).start()
     own_a.start()
-    for step in range(1, cols):
-        arrive[step - 1].wait_recv()
-        across[step].start()
     for step in range(1, cols):
         token_copy(step, col).wait_send()
 
@@ -373,79 +333,148 @@
     own_a.wait()
     a_copy(core).wait_send()
     a_copy(1 - core).wait_recv()
-    own_q.wait()
-    for copy in along + across:
-        copy.wait_send()
-    for copy in landed:
-        copy.wait_recv()
-
-
-def start_exchange(tokens, pack_q, gain, rows, cols):
+
+
+def start_exchange(tokens, gain, cols):
     anywhere = pl.BlockSpec(memory_space=pl.ANY)
     seqs, length, width = tokens.shape
-    weight_rows = pack_q.shape[0]
     full = width * cols
     return pl.pallas_call(
         functools.partial(start_kernel, cols),
         out_shape=(
             jax.ShapeDtypeStruct((length, full), tokens.dtype),
             jax.ShapeDtypeStruct((2 * length, full), tokens.dtype),
-            jax.ShapeDtypeStruct((weight_rows * rows, pack_q.shape[1] * cols), pack_q.dtype),
         ),
-        in_specs=[anywhere] * 2 + [pl.BlockSpec(memory_space=pltpu.VMEM)],
-        out_specs=(anywhere,) * 3,
+        in_specs=[anywhere, pl.BlockSpec(memory_space=pltpu.VMEM)],
+        out_specs=(anywhere,) * 2,
         scratch_shapes=[
             pltpu.VMEM((length, full), tokens.dtype),
             pltpu.VMEM((length, full), tokens.dtype),
-        ]
-        + [pltpu.SemaphoreType.DMA((2, cols))] * 3
-        + [pltpu.SemaphoreType.DMA((2, 1)), pltpu.SemaphoreType.DMA((4,))],
+            pltpu.SemaphoreType.DMA((2, cols)),
+            pltpu.SemaphoreType.DMA((2, 1)),
+            pltpu.SemaphoreType.DMA((3,)),
+        ],
         compiler_params=pltpu.CompilerParams(
             collective_id=1, has_side_effects=True, vmem_limit_bytes=16 << 20
         ),
-        cost_estimate=pl.CostEstimate(flops=0, bytes_accessed=400 << 20, transcendentals=0),
+        cost_estimate=pl.CostEstimate(flops=0, bytes_accessed=200 << 20, transcendentals=0),
         name="start_exchange",
-    )(tokens, pack_q, gain.reshape(1, full))
-
-
-def gather_kernel(cols, own_ref, after_ref, full_ref, sems, x_sems, local_sem):
+    )(tokens, gain.reshape(1, full))
+
+
+def gather_kernel(
+    cols, q_ref, o_ref, after_ref, wq_ref, wo_ref, q_send, q_recv, q_over, o_send, o_recv, o_over, local_sems
+):
     group, core, mate, row, col = place()
-    for step in range(1, cols):
-        greet((group, row, lined(col, step, cols)))
-    greet((group, 1 - row, col))
-    pl.semaphore_wait(pltpu.get_barrier_semaphore(), cols)
-    along, arrive, across, landed, own_place = weight_copies(cols, own_ref, full_ref, sems, x_sems)
-    own = pltpu.make_async_copy(own_ref, own_place, local_sem)
-    for copy in along:
-        copy.start()
-    across[0].start()
-    own.start()
-    for step in range(1, cols):
-        arrive[step - 1].wait_recv()
-        across[step].start()
-    own.wait()
-    for copy in along + across:
-        copy.wait_send()
-    for copy in landed:
-        copy.wait_recv()
-
-
-def gather_weights(own, after, rows, cols):
+    last = cols - 1
+    over = (group, 1 - row, col)
+    greet(over)
+
+    @pl.when(col < last)
+    def _():
+        greet((group, row, col + 1))
+
+    @pl.when(col > 0)
+    def _():
+        greet((group, row, col - 1))
+
+    pl.semaphore_wait(
+        pltpu.get_barrier_semaphore(),
+        1 + jnp.minimum(col, 1) + jnp.minimum(last - col, 1),
+    )
+
+    def moves(own, full, send, recv, over_sems):
+        tall, wide = own.shape
+
+        def block(of_row, of_col):
+            return full.at[aligned(of_row, tall), aligned(of_col, wide)]
+
+        def along(src, chunk, to, way):
+            return pltpu.make_async_remote_copy(
+                src_ref=src,
+                dst_ref=block(row, chunk),
+                send_sem=send.at[way, chunk],
+                recv_sem=recv.at[chunk],
+                device_id=(group, row, to),
+                device_id_type=MESH_IDS,
+            )
+
+        def across(src, of_row, chunk):
+            return remote(src, block(of_row, chunk), over_sems, chunk, over)
+
+        return block, along, across
+
+    both = (
+        (q_ref, moves(q_ref, wq_ref, q_send, q_recv, q_over)),
+        (o_ref, moves(o_ref, wo_ref, o_send, o_recv, o_over)),
+    )
+    own_copies = []
+    for at, (own, (block, along, across)) in enumerate(both):
+
+        @pl.when(col < last)
+        def _():
+            along(own, col, col + 1, 0).start()
+
+        @pl.when(col > 0)
+        def _():
+            along(own, col, col - 1, 1).start()
+
+        across(own, row, col).start()
+        own_copies.append(pltpu.make_async_copy(own, block(row, col), local_sems.at[at]))
+        own_copies[-1].start()
+    for at in range(1, cols):
+        chunk = line_order(col, last, at)
+        for own, (block, along, across) in both:
+            along(own, chunk, col, 0).wait_recv()
+
+            @pl.when((chunk < col) & (col < last))
+            def _():
+                along(block(row, chunk), chunk, col + 1, 0).start()
+
+            @pl.when((chunk > col) & (col > 0))
+            def _():
+                along(block(row, chunk), chunk, col - 1, 1).start()
+
+            across(block(row, chunk), row, chunk).start()
+    for copy in own_copies:
+        copy.wait()
+    for own, (block, along, across) in both:
+        for chunk in range(cols):
+
+            @pl.when((col >= chunk) & (col < last))
+            def _():
+                along(own, chunk, col + 1, 0).wait_send()
+
+            @pl.when((col <= chunk) & (col > 0))
+            def _():
+                along(own, chunk, col - 1, 1).wait_send()
+
+            across(own, row, chunk).wait_send()
+            across(own, 1 - row, chunk).wait_recv()
+
+
+def gather_weights(own_q, own_o, after, rows, cols):
     anywhere = pl.BlockSpec(memory_space=pl.ANY)
+
+    def whole(own):
+        return jax.ShapeDtypeStruct((own.shape[0] * rows, own.shape[1] * cols), own.dtype)
+
     return pl.pallas_call(
         functools.partial(gather_kernel, cols),
-        out_shape=jax.ShapeDtypeStruct((own.shape[0] * rows, own.shape[1] * cols), own.dtype),
-        in_specs=[anywhere] * 2,
-        out_specs=anywhere,
+        out_shape=(whole(own_q), whole(own_o)),
+        in_specs=[anywhere] * 3,
+        out_specs=(anywhere,) * 2,
         scratch_shapes=[
             pltpu.SemaphoreType.DMA((2, cols)),
+            pltpu.SemaphoreType.DMA((cols,)),
             pltpu.SemaphoreType.DMA((2, cols)),
-            pltpu.SemaphoreType.DMA(()),
-        ],
+        ]
+        * 2
+        + [pltpu.SemaphoreType.DMA((2,))],
         compiler_params=pltpu.CompilerParams(collective_id=4, has_side_effects=True),
-        cost_estimate=pl.CostEstimate(flops=0, bytes_accessed=200 << 20, transcendentals=0),
+        cost_estimate=pl.CostEstimate(flops=0, bytes_accessed=300 << 20, transcendentals=0),
         name="gather_weights",
-    )(own, after)
+    )(own_q, own_o, after)
 
 
 def half_turn(wide):
@@ -698,7 +727,10 @@
     mlp_all,
     back_all,
     land_ref,
-    sums_ref,
+    a_keep,
+    a_send,
+    b_keep,
+    b_send,
     wg,
     wu,
     wd,
@@ -716,6 +748,7 @@
     back_send,
     back_recv,
     pair_sems,
+    lane_sems,
     io_sems,
 ):
     group, core, mate, row, col = place()
@@ -783,13 +816,7 @@
         load.wait()
 
     def order(at):
-        inner_low = jnp.where(at < 2, 1 - at, at)
-        inner_high = jnp.where(at == 3, 0, jnp.where(at == 0, 2, jnp.where(at == 1, 1, 3)))
-        return jnp.where(
-            col == 0,
-            at,
-            jnp.where(col == last, last - at, jnp.where(col == 1, inner_low, inner_high)),
-        )
+        return line_order(col, last, at)
 
     def arrive(chunk):
         pass_on(b_all.at[chunk], chunk, col, 0).wait_recv()
@@ -945,11 +972,65 @@
     def landed(at, part):
         return pltpu.make_async_copy(land_ref.at[at, part], buffers[part], io_sems.at[5 + part])
 
-    def results(at, part):
-        here = slice(part * units, (part + 1) * units)
-        return pltpu.make_async_copy(
-            buffers[part], sums_ref.at[at, :, here], io_sems.at[1 + part]
-        )
+    halfway = units // 2
+    small = rows // 2
+    mine, others = aligned(row, small), aligned(1 - row, small)
+
+    def x_lane(high):
+        return (
+            pltpu.make_async_copy(
+                dg_buf.at[mine], a_keep.at[high, :, 0:units], lane_sems.at[0]
+            ),
+            pltpu.make_async_copy(
+                dg_buf.at[others], a_send.at[high, :, 0:units], lane_sems.at[1]
+            ),
+            pltpu.make_async_copy(
+                u_buf.at[mine, 0:halfway],
+                a_keep.at[high, :, units : units + halfway],
+                lane_sems.at[2],
+            ),
+            pltpu.make_async_copy(
+                u_buf.at[others, 0:halfway],
+                a_send.at[high, :, units : units + halfway],
+                lane_sems.at[3],
+            ),
+        )
+
+    def y_lane(target):
+        copies = []
+        for side in range(2):
+            here = slice(side * small, (side + 1) * small)
+            copies += [
+                pltpu.make_async_copy(
+                    du_buf.at[here], target.at[side, :, 0:units], lane_sems.at[4 + 2 * side]
+                ),
+                pltpu.make_async_copy(
+                    u_buf.at[here, halfway:units],
+                    target.at[side, :, units : units + halfway],
+                    lane_sems.at[5 + 2 * side],
+                ),
+            ]
+        return copies
+
+    def put_results(high, act):
+        for copy in x_lane(high):
+            act(copy)
+
+        @pl.when(high == (group - core) // 2)
+        def _():
+            for copy in y_lane(b_keep):
+                act(copy)
+
+        @pl.when(high != (group - core) // 2)
+        def _():
+            for copy in y_lane(b_send):
+                act(copy)
+
+    def start_it(copy):
+        copy.start()
+
+    def wait_for(copy):
+        copy.wait()
 
     def turned(source, into, at):
         load = pltpu.make_async_copy(source.at[:, :, aligned(at, rows)], turn_buf, io_sems.at[4])
@@ -974,8 +1055,7 @@
 
         @pl.when(at == 3)
         def _():
-            for part in parts:
-                results(0, part).wait()
+            put_results(0, wait_for)
 
         @pl.when(is_own)
         def _():
@@ -1004,14 +1084,12 @@
 
         @pl.when(is_own)
         def _():
-            for part in parts:
-                results(high, part).start()
+            put_results(high, start_it)
 
         return unused
 
     lax.fori_loop(0, 4, one_block, 0)
-    for part in parts:
-        results(1, part).wait()
+    put_results(1, wait_for)
     for at in range(1, cols):
         back_out(at, order(at)).wait_send()
         source = lax.rem(col + at, cols)
@@ -1048,10 +1126,10 @@
             jax.ShapeDtypeStruct((cols, rows, width), bf16),
             jax.ShapeDtypeStruct((cols, rows, width), bf16),
             jax.ShapeDtypeStruct((2, 3, rows, units), bf16),
-            jax.ShapeDtypeStruct((2, rows, 3 * units), bf16),
-        ),
+        )
+        + (jax.ShapeDtypeStruct((2, rows // 2, units + units // 2), bf16),) * 4,
         in_specs=[anywhere] * 12,
-        out_specs=(anywhere,) * 7,
+        out_specs=(anywhere,) * 10,
         scratch_shapes=[
             pltpu.VMEM((width, units), bf16),
             pltpu.VMEM((width, units), bf16),
@@ -1070,6 +1148,7 @@
             pltpu.SemaphoreType.DMA((cols,)),
             pltpu.SemaphoreType.DMA((cols,)),
             pltpu.SemaphoreType.DMA((2, 2, 3)),
+            pltpu.SemaphoreType.DMA((8,)),
             pltpu.SemaphoreType.DMA((9,)),
         ],
         compiler_params=pltpu.CompilerParams(
@@ -1090,7 +1169,9 @@
     gq_ref,
     go_ref,
     gain_ref,
+    out_ref,
     gin_ref,
+    crossed_ref,
     sq_ref,
     so_ref,
     gsum_ref,
@@ -1116,6 +1197,7 @@
     o_sems,
     qz_sems,
     oz_sems,
+    cross_sems,
     local_sems,
 ):
     group, core, mate, row, col = place()
@@ -1202,6 +1284,8 @@
         ig_ref.at[:, lanes(col, width)], gin_ref.at[col], local_sems.at[2]
     )
 
+    cross = remote(out_ref, crossed_ref, cross_sems, 0, (mate, core, col))
+    stay = pltpu.make_async_copy(out_ref, crossed_ref, local_sems.at[4])
     for m in range(2):
         copies[m]["s0"].start()
         copies[m]["a1"].start()
@@ -1212,10 +1296,12 @@
     @pl.when(core != row)
     def _():
         token_copy(0, col).start()
+        cross.start()
 
     @pl.when(core == row)
     def _():
         own_tokens.start()
+        stay.start()
 
     gain_load = pltpu.make_async_copy(gain_ref, gain_now.at[0], local_sems.at[3])
     gain_load.start()
@@ -1311,13 +1397,15 @@
     def _():
         token_copy(0, col).wait_recv()
         token_copy(0, col).wait_send()
+        cross.wait()
 
     @pl.when(core == row)
     def _():
         own_tokens.wait()
-
-
-def finish(input_grad, grad_q, grad_o, gains, cols):
+        stay.wait()
+
+
+def finish(input_grad, grad_q, grad_o, gains, output, cols):
     anywhere = pl.BlockSpec(memory_space=pl.ANY)
     in_vmem = pl.BlockSpec(memory_space=pltpu.VMEM)
     bf16, f32 = jnp.bfloat16, jnp.float32
@@ -1340,12 +1428,13 @@
         functools.partial(finish_kernel, cols),
         out_shape=(
             jax.ShapeDtypeStruct((cols, length, full // cols), bf16),
+            jax.ShapeDtypeStruct(output.shape, bf16),
             jax.ShapeDtypeStruct((2, rows, wide_q // cols), f32),
             jax.ShapeDtypeStruct((2, rows, wide_o // cols), f32),
             jax.ShapeDtypeStruct(gains.shape, f32),
         ),
-        in_specs=[anywhere] * 4,
-        out_specs=(anywhere, in_vmem, in_vmem, in_vmem),
+        in_specs=[anywhere] * 5,
+        out_specs=(anywhere, anywhere, in_vmem, in_vmem, in_vmem),
         scratch_shapes=buffers(wide_q)
         + buffers(wide_o)
         + [
@@ -1357,7 +1446,8 @@
             pltpu.SemaphoreType.DMA((2, 5)),
             pltpu.SemaphoreType.DMA((2, 2, cols)),
             pltpu.SemaphoreType.DMA((2, 2, cols)),
-            pltpu.SemaphoreType.DMA((4,)),
+            pltpu.SemaphoreType.DMA((2, 1)),
+            pltpu.SemaphoreType.DMA((5,)),
         ],
         compiler_params=pltpu.CompilerParams(
             collective_id=3, has_side_effects=True, vmem_limit_bytes=40 << 20
@@ -1369,6 +1459,7 @@
         grad_q.reshape(2, 2, 2, rows, wide_q),
         grad_o.reshape(2, 2, 2, rows, wide_o),
         gains,
+        output,
     )
 
 
@@ -1421,9 +1512,7 @@
     pack_o = core_half(w_out, 1)
     gain_one = gain_attn.astype(jnp.float32)
     gain_two = gain_ffn.astype(jnp.float32)
-    own_tokens, attn_input, weights_qkv = start_exchange(
-        tokens, pack_q, gain_one, row_count, col_count
-    )
+    own_tokens, attn_input = start_exchange(tokens, gain_one, col_count)
 
     length = lax.dynamic_slice_in_dim(lengths, mate * seq_group + col, 1)
     given_pos = row * rows_local + jnp.arange(rows_local, dtype=jnp.int32)
@@ -1434,14 +1523,12 @@
     picked = pick_sequences(everyone, deal_order, group * seq_group, seq_group)
     picked = jnp.where(given_live, picked, jnp.zeros_like(picked))
     given = lax.ppermute(picked, ("dp", "row"), CROSSED)
-    weights_out = gather_weights(pack_o, picked, row_count, col_count)
-    given, weights_out = lax.optimization_barrier((given, weights_out))
+    weights_qkv, weights_out = gather_weights(pack_q, pack_o, picked, row_count, col_count)
+    given, weights_qkv = lax.optimization_barrier((given, weights_qkv))
     line_cot = lax.all_gather(given, "col", axis=2, tiled=True)
     own_grad = lax.dynamic_index_in_dim(line_cot, col, keepdims=False).astype(jnp.float32)
 
-    w_gate_up, w_down, attn_input, weights_out = lax.optimization_barrier(
-        (w_gate_up, w_down, attn_input, weights_out)
-    )
+    w_gate_up, w_down, weights_qkv = lax.optimization_barrier((w_gate_up, w_down, weights_qkv))
     far_gate_up = lax.ppermute(half_rows(w_gate_up), "row", OVER_X)
     far_down = lax.ppermute(half_rows(w_down), "row", OVER_X)
     own_mats = (w_gate_up[:, 0], w_gate_up[:, 1], w_down)
@@ -1474,22 +1561,22 @@
     scale_two = lax.rsqrt(jnp.mean(resid * resid, axis=1, keepdims=True) + EPSILON)
     own_ffn = (resid * scale_two * gain_two).astype(jnp.bfloat16)
 
-    unused_b, unused_u, unused_gu, mlp_part, back_part, unused_land, grad_sums = feed_forward(
+    *unused, a_keep, a_send, b_keep, b_send = feed_forward(
         own_ffn,
         resid.astype(jnp.bfloat16),
         line_cot,
         own_mats + far_mats + sibling_mats,
         col_count,
     )
+    mlp_part, back_part = unused[3:5]
     grad_normed_two = jnp.sum(back_part.astype(jnp.float32), axis=0)
-
-    sums_ffn = lax.psum_scatter(
-        grad_sums.reshape(-1, 3 * hidden),
-        ("dp", "row"),
-        scatter_dimension=0,
-        axis_index_groups=CORES,
-        tiled=True,
-    )
+    out_cols = lax.psum_scatter(mlp_part, "col", scatter_dimension=2, tiled=True)
+
+    def plus(kept, came):
+        return (kept.astype(jnp.float32) + came.astype(jnp.float32)).astype(jnp.bfloat16)
+
+    a_came = lax.ppermute(a_send, "row", OVER_X)
+    b_came = lax.ppermute(b_send, "dp", OVER_Y)
 
     weighted_two = grad_normed_two * gain_two
     inner_two = jnp.sum(weighted_two * resid, axis=1, keepdims=True)
@@ -1504,10 +1591,6 @@
     grad_projected = attend_back_fast(
         length, projected, grad_heads, cosines, sines, col_count
     )
-    mlp_part, sums_ffn, grad_projected = lax.optimization_barrier(
-        (mlp_part, sums_ffn, grad_projected)
-    )
-    out_cols = lax.psum_scatter(mlp_part, "col", scatter_dimension=2, tiled=True)
     grad_normed_one = summed_rows(expand_local(grad_projected, weights_qkv).astype(jnp.bfloat16))
     grad_qkv = token_outer(attn_input, grad_projected).astype(jnp.bfloat16)
     weighted_one = grad_normed_one * gain_one
@@ -1518,18 +1601,26 @@
         - own_float * scale_one**3 * inner_one / full_width
     ).astype(jnp.bfloat16)
     gain_one_part = jnp.sum(grad_normed_one * own_float * scale_one, axis=0)
-    sums_ffn = sums_ffn.astype(jnp.float32)
-    sums_gate_up = sums_ffn[:, : 2 * hidden].reshape(-1, 2, hidden)
-    sums_down = sums_ffn[:, 2 * hidden :]
+    a_sum, b_sum, own_input_grad = lax.optimization_barrier(
+        (plus(a_keep, a_came), plus(b_keep, b_came), own_input_grad)
+    )
+    high = group // 2
+
+    def one_of(pair, at):
+        return lax.dynamic_index_in_dim(pair, at, keepdims=False)
+
+    a_last = lax.ppermute(one_of(a_sum, 1 - high), "dp", OVER_Y)
+    b_last = lax.ppermute(one_of(b_sum, 1 - row), "row", OVER_X)
     gains = jnp.stack([gain_one_part, gain_two_part]).reshape(8, -1)
-    given_grad, sums_q, sums_o, gain_sums = finish(
-        own_input_grad, grad_qkv, grad_out, gains, col_count
-    )
-    out_cols, given_grad = lax.optimization_barrier((out_cols, given_grad))
-    layer_out = jnp.where(
-        given_live, lax.ppermute(out_cols, ("dp", "row"), CROSSED).astype(jnp.float32), 0.0
-    )
+    given_grad, given_out, sums_q, sums_o, gain_sums = finish(
+        own_input_grad, grad_qkv, grad_out, gains, out_cols, col_count
+    )
+    layer_out = jnp.where(given_live, given_out.astype(jnp.float32), 0.0)
     input_grad = given_grad.astype(jnp.float32)
+    a_total = one_of(a_sum, high).astype(jnp.float32) + a_last.astype(jnp.float32)
+    b_total = one_of(b_sum, row).astype(jnp.float32) + b_last.astype(jnp.float32)
+    sums_gate_up = jnp.stack([a_total[:, :hidden], b_total[:, :hidden]], axis=1)
+    sums_down = jnp.concatenate([a_total[:, hidden:], b_total[:, hidden:]], axis=1)
     grad_gain_attn, grad_gain_ffn = gain_sums.reshape(2, full_width)
 
     def both_cores(sums):

time: 1250 us -> 1190 us (0.952)
  Pallas kernels: 907 us -> 871 us
  waiting for transfers between devices: 129 us -> 104 us
    pallas_call x1, Pallas kernels: 138 us -> 46.2 us  [start_exchange(): pl.pallas_call(functools.partial(start_kernel, cols), out_shape=(jax.Shap...]
    reduce_scatter x1 -> x0, waiting for transfers between devices: 48.9 us -> none  [one_sequence_body(): lax.psum_scatter(grad_sums.reshape(-1, 3 * hidden), ('dp', 'row'), scatte...]
    pallas_call x1, Pallas kernels: 79.8 us -> 118 us  [gather_weights(): pl.pallas_call(functools.partial(gather_kernel, cols), out_shape=(whole(o...]
    ppermute x1 -> x4, waiting for transfers between devices: 0.01 us -> 23.7 us  [the longest x1 23.4 us: one_sequence_body(): a_last = lax.ppermute(one_of(a_sum, 1 - high), 'dp', OVER_Y)]
    pallas_call x1, Pallas kernels: 372 us -> 391 us  [feed_forward(): pl.pallas_call(functools.partial(ffn_kernel, cols), out_shape=(jax.ShapeD...]
  transfers between devices with their start and end apart: 14 -> 16, of which waited for: 3 -> 6; matrix products, arithmetic and copies ran while one was open for 10% -> 10% of each run, Pallas kernels for 43% -> 23%
where the time goes in v5:
time: 1190 us; the launch traced here: 1180 us
  Pallas kernels  871 us (73%)
  waiting for transfers between devices  104 us (9%)
  local copies, waits for them, and re-layouts  73 us (6%)
  other arithmetic  44 us (4%)
  matrix products  40.8 us (3%)
  starting transfers between devices  27 us (2%)
  between operations  22.5 us (2%)
    pallas_call x1, Pallas kernels, feed_forward(): pl.pallas_call(functools.partial(ffn_kernel, cols), out_shape=(jax.ShapeD...  391 us
    pallas_call x1, Pallas kernels, finish(): pl.pallas_call(functools.partial(finish_kernel, cols), out_shape=(jax.Sha...  209 us
    pallas_call x1, Pallas kernels, gather_weights(): pl.pallas_call(functools.partial(gather_kernel, cols), out_shape=(whole(o...  118 us
    ppermute x1, waiting for transfers between devices, one_sequence_body(): far_down = lax.ppermute(half_rows(w_down), 'row', OVER_X)  74.2 us
    pallas_call x1, Pallas kernels, attend_back_fast(): pl.pallas_call(functools.partial(attend_back_kernel, block), grid=(groups...  63.2 us
    pallas_call x1, Pallas kernels, start_exchange(): pl.pallas_call(functools.partial(start_kernel, cols), out_shape=(jax.Shap...  46.2 us
    pallas_call x1, Pallas kernels, attend_fast(): pl.pallas_call(functools.partial(attend_kernel, block), grid=(groups,), o...  43.4 us
    unnamed x93, local copies, waits for them, and re-layouts  24.6 us
  transfers between devices with their start and end apart: 16, of which 6 were waited for; matrix products, arithmetic and copies ran while one was open for 10% of the time, Pallas kernels for 23%

profile of v5, /device:TPU:0, one launch (start us, length us, event | category | flops | bytes accessed | tf_op | source)
XLA Modules:
  0.0 1181.7 jit_solution(4258883247993399249)
XLA Ops:
  20.4 46.2 %start_exchange.1 = (bf16[512,2048]{1,0:T(8,128)(2,1)S(1)}, bf16[1024,2048]{1,0:T(8,128)(2,1)S(1)}) custom-call(bf16[4,512,512]{2,1,0:T(8,128)(2,1)S(1)} %copy-done.3, f32[1,2048]{1,0:T(1,128)S(1)} %bitcast.80), custom_call_target="tpu_custom_call" | custom-call | bytes 209715200 | tf_op jit(solution)/shard_map/start_exchange/pallas_call | solution.py:342
  73.9 17.2 %collective-permute-start = (bf16[4,512,512]{2,1,0:T(8,128)(2,1)}, bf16[4,512,512]{2,1,0:T(8,128)(2,1)}, u32[]{:S(2)}, u32[]{:S(2)}) collective-permute-start(bf16[4,512,512]{2,1,0:T(8,128)(2,1)} %maximum_select_fusion.1.after_ref), channel_id=1, source_target_pairs={{0,0},{4,8},{8,4},{12,12},{16,16},{20,24},{24,20},{28,28},{1,1},{5... | collective-permute-start | bytes 6291464 | tf_op jit(solution)/shard_map/ppermute | solution.py:1525
  93.1 2.1 constant_dynamic-slice_fusion.4
  96.2 117.9 %gather_weights.1 = (bf16[2048,1536]{1,0:T(8,128)(2,1)}, bf16[2048,1024]{1,0:T(8,128)(2,1)}) custom-call(bf16[1024,384]{1,0:T(8,128)(2,1)} %pad_maximum_fusion.2.q_ref, bf16[1024,256]{1,0:T(8,128)(2,1)} %get-tuple-element.144.o_ref, bf16[4,512,512]{2,1,0:T(8,128)(2,1)} %maximum_select_fusion.1.after_ref), custom_call_target="tpu_custom_call" | custom-call | bytes 314572800 | tf_op jit(solution)/shard_map/gather_weights/pallas_call | solution.py:462
  214.2 10.6 copy.53
  224.8 4.8 constant_dynamic-slice_fusion.2
  236.7 2.4 concatenate.38.cos_ref
  239.1 3.3 constant_dynamic-slice_fusion.1
  242.7 43.4 %attend.1 = (bf16[1024,1536]{1,0:T(8,128)(2,1)}, bf16[1024,1024]{1,0:T(8,128)(2,1)S(1)}) custom-call(s32[1]{0:T(128)} %dynamic_slice.83.len_ref, bf16[1024,2048]{1,0:T(8,128)(2,1)} %copy-done.9, bf16[2048,1536]{1,0:T(8,128)(2,1)} %get-tuple-element.44.w_ref, f32[1024,256]{1,0:T(8,128)S(1)} %copy-done.5, f32[1024,256]{1,0:T(8,128)S(1)} %concatenate.40.sin_ref), custom_call_target="tpu_custom_call" | custom-call | flops 10737418240 | bytes 13631488 | tf_op jit(solution)/shard_map/attend/pallas_call | solution.py:573
  286.1 4.8 convolution_convert_fusion.3
  293.6 74.2 %collective-permute-done.3.wd_far = bf16[512,2048]{1,0:T(8,128)(2,1)} collective-permute-done((bf16[512,2048]{1,0:T(8,128)(2,1)}, bf16[512,2048]{1,0:T(8,128)(2,1)}, u32[]{:S(2)}, u32[]{:S(2)}) %collective-permute-start.3) | collective-permute-done | bytes 2097184 | tf_op jit(solution)/shard_map/ppermute | solution.py:1533
  367.8 2.7 slice_bitcast_fusion.4
  371.2 7.3 slice_bitcast_fusion
  378.6 5.2 fusion.13
  389.3 390.7 %feed_forward.1 = (bf16[4,512,2048]{2,1,0:T(8,128)(2,1)}, bf16[4,512,2048]{2,1,0:T(8,128)(2,1)}, bf16[4,512,4096]{2,1,0:T(8,128)(2,1)}, bf16[4,512,2048]{2,1,0:T...) custom-call(bf16[512,2048]{1,0:T(8,128)(2,1)} %multiply_convert_fusi, ...), custom_call_target="tpu_custom_call" | custom-call | flops 154618822656 | bytes 838860800 | tf_op jit(solution)/shard_map/feed_forward/pallas_call | solution.py:1120
  780.1 5.8 convert_reduce_fusion
  787.0 4.2 multiply_convert_fusion
  795.5 8.0 convolution_convert_fusion.4.dz_ref
  803.5 63.2 %attend_back.1 = bf16[1024,1536]{1,0:T(8,128)(2,1)} custom-call(s32[1]{0:T(128)} %dynamic_slice.83.len_ref, bf16[1024,1536]{1,0:T(8,128)(2,1)} %get-tuple-element.57.qkv_ref, bf16[1024,1024]{1,0:T(8,128)(2,1)S(1)} %convolution_convert_fusion.4.dz_ref, f32[1024,256]{1,0:T(8,128)S(1)} %copy-done.6, f32[1024,256]{1,0:T(8,128)S(1)} %concatenate.40.sin_ref), custom_call_target="tpu_custom_call" | custom-call | flops 10737418240 | bytes 8388608 | tf_op jit(solution)/shard_map/attend_back/pallas_call | solution.py:680
  866.7 10.2 convolution_convert_fusion.1
  879.1 8.8 convolution_convert_fusion
  894.5 2.1 fusion.4.ig_ref
  902.7 9.1 convolution_convert_fusion.2
  911.8 23.4 %collective-permute-done.11 = bf16[256,3072]{1,0:T(8,128)(2,1)} collective-permute-done((bf16[256,3072]{1,0:T(8,128)(2,1)}, bf16[256,3072]{1,0:T(8,128)(2,1)}, u32[]{:S(2)}, u32[]{:S(2)}) %collective-permute-start.11) | collective-permute-done | bytes 1572896 | tf_op jit(solution)/shard_map/ppermute | solution.py:1612
  935.2 2.5 convert_add_fusion.4
  938.0 2.8 convert_add_fusion.3
  942.9 5.2 copy.57
  949.7 3.0 reduce-scatter.2.cloned.1.call-done.out_ref
  952.7 2.2 copy-done.2
  956.5 209.2 %finish.1 = (bf16[4,512,512]{2,1,0:T(8,128)(2,1)S(1)}, bf16[4,512,512]{2,1,0:T(8,128)(2,1)S(1)}, f32[2,256,384]{2,1,0:T(8,128)S(1)}, f32[2,256,256]{2,1,0:T(8,128)S(1)}, f32[8,512]{1,0:T(8,128)S(1)}) custom-call(bf16[512,2048]{1,0:T(8,128)(2,1)S(1)} %fusion.4.ig_ref, bf16[2,2,2,256,1536]{4,3,2,1,0:T(8,128)(2,1)} %bitcast.81, ...), custom_call_target="tpu_custom_call" | custom-call | bytes 314572800 | tf_op jit(solution)/shard_map/finish/pallas_call | solution.py:1427
  1167.1 2.6 convert_element_type.135
  1169.7 2.3 convert_select_fusion
  (177 shorter events, 61.8 us)
Async XLA Ops:
  7.2 63.4 %all-gather.3.cloned.1.call-start = ((), (), s32[]{:S(2)}) async-start(), calls=%async_computation.1 | async-start | bytes 10485760 | tf_op jit(solution)/shard_map/all_gather | solution.py:1521
  7.9 381.4 %all-gather.5.cloned.1.call-start = ((), (), s32[]{:S(2)}) async-start(), calls=%async_computation.2 | async-start | bytes 10485760 | tf_op jit(solution)/shard_map/all_gather | solution.py:1528
  15.2 58.7 %copy-start.7 = (f32[2048]{0:T(1024)}, f32[2048]{0:T(1024)S(1)}, u32[]{:S(2)}) copy-start(f32[2048]{0:T(1024)S(1)} %convert_element_type.108) | copy-start | bytes 24580
  68.7 309.9 %copy-start = (bf16[512,2048]{1,0:T(8,128)(2,1)}, bf16[512,2048]{1,0:T(8,128)(2,1)S(1)}, u32[]{:S(2)}) copy-start(bf16[512,2048]{1,0:T(8,128)(2,1)S(1)} %get-tuple-element.38) | copy-start | bytes 6291460
  70.6 20.5 %copy-start.25 = (bf16[1024,2,128]{2,1,0:T(2,128)(2,1)S(1)}, bf16[1024,2,128]{2,1,0:T(2,128)(2,1)}, u32[]{:S(2)}) copy-start(bf16[1024,2,128]{2,1,0:T(2,128)(2,1)} %param.18) | copy-start | bytes 1572868
  73.9 140.2 %collective-permute-start = (bf16[4,512,512]{2,1,0:T(8,128)(2,1)}, bf16[4,512,512]{2,1,0:T(8,128)(2,1)}, u32[]{:S(2)}, u32[]{:S(2)}) collective-permute-start(bf16[4,512,512]{2,1,0:T(8,128)(2,1)} %maximum_select_fusion.1.after_ref), channel_id=1, source_target_pairs={{0,0},{4,8},{8,4},{12,12},{16,16},{20,24},{24,20},{28,28},{1,1},{5... | collective-permute-start | bytes 6291464 | tf_op jit(solution)/shard_map/ppermute | solution.py:1525
  214.1 738.6 %reduce-scatter.2.cloned.1.call-start = ((), (), s32[]{:S(2)}) async-start(), calls=%async_computation.3 | async-start | bytes 10485760 | tf_op jit(solution)/shard_map/reduce_scatter | solution.py:1573
  224.8 6.4 copy-start.42
  229.6 138.2 %collective-permute-start.2 = (bf16[512,2,2048]{2,0,1:T(8,128)(2,1)}, bf16[512,2,2048]{2,0,1:T(8,128)(2,1)}, u32[]{:S(2)}, u32[]{:S(2)}) collective-permute-start(bf16[512,2,2048]{2,0,1:T(8,128)(2,1)} %constant_dynamic-slice_fusion.2), channel_id=1, source_target_pairs={{0,4},{4,0},{1,5},{5,1},{2,6},{6,2},{3,7},{7,3},{8,12},{12,8},{9,1... | collective-permute-start | bytes 12582920 | tf_op jit(solution)/shard_map/ppermute | solution.py:1532
  242.3 43.8 %copy-start.39 = (bf16[2048,1024]{1,0:T(8,128)(2,1)S(1)}, bf16[2048,1024]{1,0:T(8,128)(2,1)}, u32[]{:S(2)}) copy-start(bf16[2048,1024]{1,0:T(8,128)(2,1)} %get-tuple-element.48) | copy-start | bytes 12582916
  242.3 125.4 %collective-permute-start.3 = (bf16[512,2048]{1,0:T(8,128)(2,1)}, bf16[512,2048]{1,0:T(8,128)(2,1)}, u32[]{:S(2)}, u32[]{:S(2)}) collective-permute-start(bf16[512,2048]{1,0:T(8,128)(2,1)} %constant_dynamic-slice_fusion.1), channel_id=1, source_target_pairs={{0,4},{4,0},{1,5},{5,1},{2,6},{6,2},{3,7},{7,3},{8,12},{12,8},{9,1... | collective-permute-start | bytes 6291464 | tf_op jit(solution)/shard_map/ppermute | solution.py:1533
  293.5 85.0 %collective-permute-start.1 = (bf16[512,2048]{1,0:T(8,128)(2,1)}, bf16[512,2048]{1,0:T(8,128)(2,1)}, u32[]{:S(2)}, u32[]{:S(2)}) collective-permute-start(bf16[512,2048]{1,0:T(8,128)(2,1)} %constant_dynamic-slice_fusion.3), channel_id=1, source_target_pairs={{0,8},{8,0},{16,24},{24,16},{1,9},{9,1},{17,25},{25,17},{2,10},{10... | collective-permute-start | bytes 6291464 | tf_op jit(solution)/shard_map/ppermute | solution.py:1499
  293.6 91.4 %copy-start.30 = (f32[2048]{0:T(1024)}, f32[2048]{0:T(1024)S(1)}, u32[]{:S(2)}) copy-start(f32[2048]{0:T(1024)S(1)} %convert_element_type.114) | copy-start | bytes 24580
  367.8 18.9 %collective-permute-start.6 = (bf16[512,2048]{1,0:T(8,128)(2,1)}, bf16[512,2048]{1,0:T(8,128)(2,1)S(1)}, u32[]{:S(2)}, u32[]{:S(2)}) collective-permute-start(bf16[512,2048]{1,0:T(8,128)(2,1)} %collective-permute-done.3.wd_far), channel_id=1, source_target_pairs={{0,8},{8,0},{16,24},{24,16},{1,9},{9,1},{17,25},{25,17},{2,10},{10... | collective-permute-start | bytes 6291464 | tf_op jit(solution)/shard_map/ppermute | solution.py:1499
  370.5 8.0 copy-start.26
  370.5 8.0 copy-start.27
  370.5 16.2 %collective-permute-start.4 = (bf16[512,2048]{1,0:T(8,128)(2,1)S(1)}, bf16[512,2048]{1,0:T(8,128)(2,1)S(1)}, u32[]{:S(2)}, u32[]{:S(2)}) collective-permute-start(bf16[512,2048]{1,0:T(8,128)(2,1)S(1)} %get-tuple-element.118.wg_far), channel_id=1, source_target_pairs={{0,8},{8,0},{16,24},{24,16},{1,9},{9,1},{17,25},{25,17},{2,10},{10... | collective-permute-start | bytes 6291464 | tf_op jit(solution)/shard_map/ppermute | solution.py:1499
  371.1 7.5 copy-start.22
  371.1 18.2 %collective-permute-start.5 = (bf16[512,2048]{1,0:T(8,128)(2,1)S(1)}, bf16[512,2048]{1,0:T(8,128)(2,1)}, u32[]{:S(2)}, u32[]{:S(2)}) collective-permute-start(bf16[512,2048]{1,0:T(8,128)(2,1)S(1)} %get-tuple-element.117.wu_far), channel_id=1, source_target_pairs={{0,8},{8,0},{16,24},{24,16},{1,9},{9,1},{17,25},{25,17},{2,10},{10... | collective-permute-start | bytes 6291464 | tf_op jit(solution)/shard_map/ppermute | solution.py:1499
  791.2 4.3 collective-permute-start.9
  792.0 96.0 %collective-permute-start.8 = (bf16[2,256,3072]{2,1,0:T(8,128)(2,1)}, bf16[2,256,3072]{2,1,0:T(8,128)(2,1)S(1)}, u32[]{:S(2)}, u32[]{:S(2)}) collective-permute-start(bf16[2,256,3072]{2,1,0:T(8,128)(2,1)} %get-tuple-element.55), channel_id=1, source_target_pairs={{0,16},{16,0},{8,24},{24,8},{1,17},{17,1},{9,25},{25,9},{2,18},{18... | collective-permute-start | bytes 9437192 | tf_op jit(solution)/shard_map/ppermute | solution.py:1579
  793.6 9.8 copy-start.6
  793.6 95.5 %collective-permute-start.7 = (bf16[2,256,3072]{2,1,0:T(8,128)(2,1)}, bf16[2,256,3072]{2,1,0:T(8,128)(2,1)S(1)}, u32[]{:S(2)}, u32[]{:S(2)}) collective-permute-start(bf16[2,256,3072]{2,1,0:T(8,128)(2,1)} %get-tuple-element.53), channel_id=1, source_target_pairs={{0,4},{4,0},{1,5},{5,1},{2,6},{6,2},{3,7},{7,3},{8,12},{12,8},{9,1... | collective-permute-start | bytes 9437192 | tf_op jit(solution)/shard_map/ppermute | solution.py:1578
  866.7 10.7 copy-start.43
  877.2 10.7 copy-start.24
  877.2 13.8 %collective-permute-start.10 = (bf16[512,2048]{1,0:T(8,128)(2,1)S(1)}, bf16[512,2048]{1,0:T(8,128)(2,1)S(1)}, u32[]{:S(2)}, u32[]{:S(2)}) collective-permute-start(bf16[512,2048]{1,0:T(8,128)(2,1)S(1)} %constant_dynamic-slice_fusion), channel_id=1, source_target_pairs={{0,8},{8,0},{16,24},{24,16},{1,9},{9,1},{17,25},{25,17},{2,10},{10... | collective-permute-start | bytes 6291464 | tf_op jit(solution)/shard_map/ppermute | solution.py:1499
  889.1 10.5 copy-start.18
  896.7 6.0 copy-start.12
  896.7 6.0 copy-start.29
  898.0 37.3 %collective-permute-start.11 = (bf16[256,3072]{1,0:T(8,128)(2,1)}, bf16[256,3072]{1,0:T(8,128)(2,1)}, u32[]{:S(2)}, u32[]{:S(2)}) collective-permute-start(bf16[256,3072]{1,0:T(8,128)(2,1)} %dynamic-slice_bitcast_fusion.1), channel_id=1, source_target_pairs={{0,16},{16,0},{8,24},{24,8},{1,17},{17,1},{9,25},{25,9},{2,18},{18... | collective-permute-start | bytes 4718600 | tf_op jit(solution)/shard_map/ppermute | solution.py:1612
  900.9 37.1 %collective-permute-start.12 = (bf16[256,3072]{1,0:T(8,128)(2,1)}, bf16[256,3072]{1,0:T(8,128)(2,1)}, u32[]{:S(2)}, u32[]{:S(2)}) collective-permute-start(bf16[256,3072]{1,0:T(8,128)(2,1)} %dynamic-slice_bitcast_fusion), channel_id=1, source_target_pairs={{0,4},{4,0},{1,5},{5,1},{2,6},{6,2},{3,7},{7,3},{8,12},{12,8},{9,1... | collective-permute-start | bytes 4718600 | tf_op jit(solution)/shard_map/ppermute | solution.py:1613
  911.8 26.2 %copy-start.19 = (bf16[2,256,3072]{2,1,0:T(8,128)(2,1)S(1)}, bf16[2,256,3072]{2,1,0:T(8,128)(2,1)}, u32[]{:S(2)}) copy-start(bf16[2,256,3072]{2,1,0:T(8,128)(2,1)} %copy-done.18) | copy-start | bytes 9437188
  (30 other events, 93.7 us)
Sparse Core Ops, SparseCore 0:
  9.6 60.9 all-gather.2
  214.2 159.3 all-gather.4
  791.4 161.2 reduce-scatter.1

commit v6 on v5

--- a/solution.py
+++ b/solution.py
@@ -721,11 +721,11 @@
     wg_sib,
     wu_sib,
     wd_sib,
-    b_all,
     u_all,
     dgu_all,
     mlp_all,
     back_all,
+    relay_ref,
     land_ref,
     a_keep,
     a_send,
@@ -734,19 +734,20 @@
     wg,
     wu,
     wd,
-    b_buf,
-    g_buf,
+    b_all,
+    b_turn,
+    g_two,
     u_buf,
     dg_buf,
     du_buf,
     mlp_buf,
     back_buf,
-    turn_buf,
     w_sems,
     ag_send,
     ag_recv,
     back_send,
     back_recv,
+    relay_recv,
     pair_sems,
     lane_sems,
     io_sems,
@@ -757,18 +758,16 @@
     depth = wg_own.shape[0]
     half = depth // 2
     units = wg_own.shape[1]
+    rows = own_ref.shape[0]
     tile = min(512, units)
-
-    barrier = pltpu.get_barrier_semaphore()
+    beside = col + 1 - 2 * lax.rem(col, 2)
+    facing = last - col
+    inner = (col > 0) & (col < last)
+
     for step in range(1, cols):
-        pl.semaphore_signal(
-            barrier,
-            inc=1,
-            device_id=(group, row, lax.rem(col + step, cols)),
-            device_id_type=MESH_IDS,
-        )
+        greet((group, row, lined(col, step, cols)))
     greet(sibling)
-    pl.semaphore_wait(barrier, cols)
+    pl.semaphore_wait(pltpu.get_barrier_semaphore(), cols)
 
     def pass_on(src, at, to, way):
         return pltpu.make_async_remote_copy(
@@ -788,13 +787,19 @@
     def _():
         pass_on(own_ref, col, col - 1, 1).start()
 
+    def order(at):
+        return line_order(col, last, at)
+
+    def load_g(at):
+        side = lax.rem(at, 2)
+        return pltpu.make_async_copy(grad_ref.at[order(at)], g_two.at[side], io_sems.at[6 + side])
+
     def rows_at(first, size):
         return pl.ds(pl.multiple_of(first, half), size)
 
     own_copy = pltpu.make_async_copy(own_ref, b_all.at[col], io_sems.at[0])
     own_copy.start()
     load_resid = pltpu.make_async_copy(resid_ref, mlp_buf, io_sems.at[8])
-    load_resid.start()
     far = (1 - row) * depth
     loads = []
     for at, (full, mine, across, shared) in enumerate(
@@ -811,12 +816,11 @@
         ]
     for load in loads:
         load.start()
+    load_g(0).start()
+    load_resid.start()
     own_copy.wait()
     for load in loads:
         load.wait()
-
-    def order(at):
-        return line_order(col, last, at)
 
     def arrive(chunk):
         pass_on(b_all.at[chunk], chunk, col, 0).wait_recv()
@@ -839,57 +843,66 @@
     def mlp_out(chunk):
         return pltpu.make_async_copy(mlp_buf, mlp_all.at[chunk], io_sems.at[4])
 
-    def back_out(at, chunk):
-        return pltpu.make_async_remote_copy(
-            src_ref=back_buf.at[slot_of(at)],
-            dst_ref=back_all.at[col],
-            send_sem=back_send.at[at],
-            recv_sem=back_recv.at[col],
-            device_id=(group, row, chunk),
-            device_id_type=MESH_IDS,
-        )
-
     def slot_of(at):
         return lax.rem(at, cols - 1)
 
-    own_back = pltpu.make_async_copy(back_buf.at[0], back_all.at[col], io_sems.at[5])
-    at_end = (col == 0) | (col == last)
+    def deliver(slot, to, place_there, at):
+        return pltpu.make_async_remote_copy(
+            src_ref=back_buf.at[slot],
+            dst_ref=back_all.at[place_there],
+            send_sem=back_send.at[at],
+            recv_sem=back_recv.at[place_there],
+            device_id=(group, row, to),
+            device_id_type=MESH_IDS,
+        )
+
+    def hand_over(slot, to, box, at):
+        return pltpu.make_async_remote_copy(
+            src_ref=back_buf.at[slot],
+            dst_ref=relay_ref.at[box],
+            send_sem=back_send.at[at],
+            recv_sem=relay_recv.at[box],
+            device_id=(group, row, to),
+            device_id_type=MESH_IDS,
+        )
+
+    own_back = pltpu.make_async_copy(back_buf.at[0], back_all.at[0], io_sems.at[5])
+    at_end = jnp.logical_not(inner)
 
     def one_chunk(at, unused):
         chunk = order(at)
+        side = lax.rem(at, 2)
 
         @pl.when(at_end & (at > 0))
         def _():
             arrive(order(at))
 
-        @pl.when(jnp.logical_not(at_end) & (at == 1))
+        @pl.when(inner & (at == 1))
         def _():
             arrive(order(1))
             arrive(order(2))
 
-        @pl.when(jnp.logical_not(at_end) & (at == 3))
+        @pl.when(inner & (at == 3))
         def _():
             arrive(order(3))
 
-        load_b = pltpu.make_async_copy(b_all.at[chunk], b_buf, io_sems.at[6])
-        load_g = pltpu.make_async_copy(grad_ref.at[chunk], g_buf, io_sems.at[7])
-        load_b.start()
-        load_g.start()
+        load_g(at).wait()
+
+        @pl.when(at < last)
+        def _():
+            load_g(at + 1).start()
 
         @pl.when(at > 0)
         def _():
             for copy in outputs(order(at - 1)):
                 copy.wait()
 
-        load_b.wait()
-        load_g.wait()
-
         @pl.loop(0, units // tile)
         def _(step):
-            lanes = pl.ds(pl.multiple_of(step * tile, tile), tile)
-            gate = dot_nn(b_buf[...], wg[:, lanes])
-            upward = dot_nn(b_buf[...], wu[:, lanes])
-            back = RES_MULT * dot_nn(g_buf[...], wd[:, lanes])
+            lanes = aligned(step, tile)
+            gate = dot_nn(b_all[chunk], wg[:, lanes])
+            upward = dot_nn(b_all[chunk], wu[:, lanes])
+            back = RES_MULT * dot_nn(g_two[side], wd[:, lanes])
             opened = 1.0 / (1.0 + jnp.exp(-gate))
             silu = gate * opened
             u_buf[:, lanes] = (silu * upward).astype(jnp.bfloat16)
@@ -914,7 +927,7 @@
 
         @pl.loop(0, 2 * depth // tile)
         def _(step):
-            here = pl.ds(pl.multiple_of(step * tile, tile), tile)
+            here = aligned(step, tile)
             back = dot_nt(dg_buf[...], wg[here, :]) + dot_nt(du_buf[...], wu[here, :])
             back_buf[slot_of(at), :, here] = back.astype(jnp.bfloat16)
             added = jnp.where(at == 0, mlp_buf[:, here].astype(jnp.float32), 0.0)
@@ -928,9 +941,21 @@
         def _():
             own_back.start()
 
-        @pl.when(at > 0)
-        def _():
-            back_out(at, chunk).start()
+        @pl.when(at_end & (at == 1))
+        def _():
+            deliver(1, beside, 1, 1).start()
+
+        @pl.when(at_end & (at == 2))
+        def _():
+            hand_over(2, beside, 1, 2).start()
+
+        @pl.when(at_end & (at == 3))
+        def _():
+            deliver(0, facing, 2, 3).start()
+
+        @pl.when(inner & (at == 3))
+        def _():
+            hand_over(0, facing, 0, 3).start()
 
         return unused
 
@@ -939,7 +964,6 @@
         copy.wait()
     mlp_out(order(last)).wait()
 
-    rows = b_buf.shape[0]
     loads = []
     for chunk in range(cols):
         here = slice(chunk * rows, (chunk + 1) * rows)
@@ -957,6 +981,21 @@
     for load in loads:
         load.wait()
 
+    def relay(box, slot):
+        hand_over(slot, facing, box, 3).wait_recv()
+        load = pltpu.make_async_copy(relay_ref.at[box], mlp_buf, io_sems.at[4])
+        load.start()
+        load.wait()
+        tall = min(64, rows)
+
+        @pl.loop(0, rows // tall)
+        def _(at):
+            here = aligned(at, tall)
+            back_buf[slot, here, :] = (
+                back_buf[slot, here, :].astype(jnp.float32)
+                + mlp_buf[here, :].astype(jnp.float32)
+            ).astype(jnp.bfloat16)
+
     buffers = (dg_buf, du_buf, u_buf)
 
     def to_sibling(at, part):
@@ -970,7 +1009,7 @@
         )
 
     def landed(at, part):
-        return pltpu.make_async_copy(land_ref.at[at, part], buffers[part], io_sems.at[5 + part])
+        return pltpu.make_async_copy(land_ref.at[at, part], buffers[part], io_sems.at[1 + part])
 
     halfway = units // 2
     small = rows // 2
@@ -1032,12 +1071,15 @@
     def wait_for(copy):
         copy.wait()
 
-    def turned(source, into, at):
-        load = pltpu.make_async_copy(source.at[:, :, aligned(at, rows)], turn_buf, io_sems.at[4])
-        load.start()
-        load.wait()
-        for chunk in range(cols):
-            into[:, chunk * rows : (chunk + 1) * rows] = turn_buf[chunk].T
+    def part_of(chunk):
+        return slice(chunk * rows, (chunk + 1) * rows)
+
+    def grad_tile(block, chunk):
+        return pltpu.make_async_copy(
+            grad_ref.at[chunk, :, aligned(block, rows)],
+            mlp_buf.at[:, part_of(chunk)],
+            w_sems.at[chunk],
+        )
 
     parts = range(3)
 
@@ -1045,8 +1087,22 @@
         high = lax.rem(at, 2)
         is_own = at >= 2
         block = 2 * high + jnp.where(is_own, core, 1 - core)
-        turned(b_all, b_buf, block)
-        turned(grad_ref, g_buf, block)
+
+        @pl.when(inner & (at == 1))
+        def _():
+            relay(0, col)
+            deliver(col, beside, 1, 1).start()
+            relay(1, last - col)
+            deliver(last - col, facing, 2, 2).start()
+
+        for chunk in range(cols):
+            grad_tile(block, chunk).start()
+        for chunk in range(cols):
+            b_turn[:, part_of(chunk)] = b_all[chunk, :, aligned(block, rows)].T
+        for chunk in range(cols):
+            grad_tile(block, chunk).wait()
+        for chunk in range(cols):
+            g_two[0, :, part_of(chunk)] = mlp_buf[:, part_of(chunk)].T
 
         @pl.when((at == 1) | (at == 2))
         def _():
@@ -1073,9 +1129,9 @@
                 other = jnp.where(is_own, buffer[:, lanes].astype(jnp.float32), 0.0)
                 buffer[:, lanes] = (other + value).astype(jnp.bfloat16)
 
-            put(dg_buf, dot_nn(b_buf[...], wg[:, lanes]))
-            put(du_buf, dot_nn(b_buf[...], wu[:, lanes]))
-            put(u_buf, RES_MULT * dot_nn(g_buf[...], wd[:, lanes]))
+            put(dg_buf, dot_nn(b_turn[...], wg[:, lanes]))
+            put(du_buf, dot_nn(b_turn[...], wu[:, lanes]))
+            put(u_buf, RES_MULT * dot_nn(g_two[0], wd[:, lanes]))
 
         @pl.when(jnp.logical_not(is_own))
         def _():
@@ -1091,16 +1147,9 @@
     lax.fori_loop(0, 4, one_block, 0)
     put_results(1, wait_for)
     for at in range(1, cols):
-        back_out(at, order(at)).wait_send()
-        source = lax.rem(col + at, cols)
-        pltpu.make_async_remote_copy(
-            src_ref=back_buf.at[slot_of(at)],
-            dst_ref=back_all.at[source],
-            send_sem=back_send.at[at],
-            recv_sem=back_recv.at[source],
-            device_id=(group, row, source),
-            device_id_type=MESH_IDS,
-        ).wait_recv()
+        deliver(0, beside, 1, at).wait_send()
+    for at in range(1, 3):
+        deliver(0, beside, at, at).wait_recv()
     for chunk in range(cols):
 
         @pl.when((col >= chunk) & (col < last))
@@ -1117,36 +1166,38 @@
     units = weights[0].shape[1]
     anywhere = pl.BlockSpec(memory_space=pl.ANY)
     bf16 = jnp.bfloat16
+    lane = jax.ShapeDtypeStruct((2, rows // 2, units + units // 2), bf16)
     return pl.pallas_call(
         functools.partial(ffn_kernel, cols),
         out_shape=(
-            jax.ShapeDtypeStruct((cols, rows, width), bf16),
             jax.ShapeDtypeStruct((cols, rows, units), bf16),
             jax.ShapeDtypeStruct((cols, rows, 2 * units), bf16),
             jax.ShapeDtypeStruct((cols, rows, width), bf16),
-            jax.ShapeDtypeStruct((cols, rows, width), bf16),
+            jax.ShapeDtypeStruct((3, rows, width), bf16),
+            jax.ShapeDtypeStruct((2, rows, width), bf16),
             jax.ShapeDtypeStruct((2, 3, rows, units), bf16),
         )
-        + (jax.ShapeDtypeStruct((2, rows // 2, units + units // 2), bf16),) * 4,
+        + (lane,) * 4,
         in_specs=[anywhere] * 12,
         out_specs=(anywhere,) * 10,
         scratch_shapes=[
             pltpu.VMEM((width, units), bf16),
             pltpu.VMEM((width, units), bf16),
             pltpu.VMEM((width, units), bf16),
+            pltpu.VMEM((cols, rows, width), bf16),
             pltpu.VMEM((rows, width), bf16),
-            pltpu.VMEM((rows, width), bf16),
+            pltpu.VMEM((2, rows, width), bf16),
             pltpu.VMEM((rows, units), bf16),
             pltpu.VMEM((rows, units), bf16),
             pltpu.VMEM((rows, units), bf16),
             pltpu.VMEM((rows, width), bf16),
             pltpu.VMEM((cols - 1, rows, width), bf16),
-            pltpu.VMEM((cols, rows, rows), bf16),
             pltpu.SemaphoreType.DMA((12,)),
             pltpu.SemaphoreType.DMA((2, cols)),
             pltpu.SemaphoreType.DMA((cols,)),
             pltpu.SemaphoreType.DMA((cols,)),
             pltpu.SemaphoreType.DMA((cols,)),
+            pltpu.SemaphoreType.DMA((2,)),
             pltpu.SemaphoreType.DMA((2, 2, 3)),
             pltpu.SemaphoreType.DMA((8,)),
             pltpu.SemaphoreType.DMA((9,)),
@@ -1290,18 +1341,12 @@
         copies[m]["s0"].start()
         copies[m]["a1"].start()
         copies[m]["own"].start()
-    for step in range(1, cols):
-        token_copy(step, col).start()
-
-    @pl.when(core != row)
-    def _():
-        token_copy(0, col).start()
-        cross.start()
-
     @pl.when(core == row)
     def _():
         own_tokens.start()
         stay.start()
+        for step in range(1, cols):
+            token_copy(step, col).start()
 
     gain_load = pltpu.make_async_copy(gain_ref, gain_now.at[0], local_sems.at[3])
     gain_load.start()
@@ -1336,6 +1381,13 @@
         copies[m]["b1"].wait()
         rows_plus(sib.at[high, 1 - row], b1.at[1 - row])
         copies[m]["b2"].start()
+
+    @pl.when(core != row)
+    def _():
+        for step in range(cols):
+            token_copy(step, col).start()
+        cross.start()
+
     gain_round(2)
     for m in range(2):
         grads, out, keep, sib, a1, a2, b1, b2, zb, sems, z_sems = matrices[m]
@@ -1532,8 +1584,6 @@
     far_gate_up = lax.ppermute(half_rows(w_gate_up), "row", OVER_X)
     far_down = lax.ppermute(half_rows(w_down), "row", OVER_X)
     own_mats = (w_gate_up[:, 0], w_gate_up[:, 1], w_down)
-    far_mats = (far_gate_up[:, 0], far_gate_up[:, 1], far_down)
-    sibling_mats = tuple(from_sibling(matrix) for matrix in far_mats)
 
     cosine_table, sine_table = rope_tables(jnp.arange(slot_len, dtype=jnp.int32), HEAD_SIZE)
     cosine_table, sine_table = lax.optimization_barrier((cosine_table, sine_table))
@@ -1561,6 +1611,11 @@
     scale_two = lax.rsqrt(jnp.mean(resid * resid, axis=1, keepdims=True) + EPSILON)
     own_ffn = (resid * scale_two * gain_two).astype(jnp.bfloat16)
 
+    far_gate_up, far_down, own_ffn, own_mats = lax.optimization_barrier(
+        (far_gate_up, far_down, own_ffn, own_mats)
+    )
+    far_mats = (far_gate_up[:, 0], far_gate_up[:, 1], far_down)
+    sibling_mats = tuple(from_sibling(matrix) for matrix in far_mats)
     *unused, a_keep, a_send, b_keep, b_send = feed_forward(
         own_ffn,
         resid.astype(jnp.bfloat16),
@@ -1568,7 +1623,7 @@
         own_mats + far_mats + sibling_mats,
         col_count,
     )
-    mlp_part, back_part = unused[3:5]
+    mlp_part, back_part = unused[2:4]
     grad_normed_two = jnp.sum(back_part.astype(jnp.float32), axis=0)
     out_cols = lax.psum_scatter(mlp_part, "col", scatter_dimension=2, tiled=True)
 

time: 1190 us -> 1040 us (0.87)
  Pallas kernels: 871 us -> 718 us
    pallas_call x1, Pallas kernels: 391 us -> 289 us  [feed_forward(): pl.pallas_call(functools.partial(ffn_kernel, cols), out_shape=(jax.ShapeD...]
    pallas_call x1, Pallas kernels: 209 us -> 159 us  [finish(): pl.pallas_call(functools.partial(finish_kernel, cols), out_shape=(jax.Sha...]
    unnamed x93 -> x87, local copies, waits for them, and re-layouts: 24.6 us -> 23.1 us
  transfers between devices with their start and end apart: 16 -> 16, of which waited for: 6 -> 8; matrix products, arithmetic and copies ran while one was open for 10% -> 11% of each run, Pallas kernels for 23% -> 26%
where the time goes in v6:
time: 1040 us; the launch traced here: 1030 us
  Pallas kernels  718 us (69%)
  waiting for transfers between devices  109 us (10%)
  local copies, waits for them, and re-layouts  65.6 us (6%)
  matrix products  44.9 us (4%)
  other arithmetic  41.8 us (4%)
  starting transfers between devices  26.2 us (3%)
  between operations  22.7 us (2%)
    pallas_call x1, Pallas kernels, feed_forward(): pl.pallas_call(functools.partial(ffn_kernel, cols), out_shape=(jax.ShapeD...  289 us
    pallas_call x1, Pallas kernels, finish(): pl.pallas_call(functools.partial(finish_kernel, cols), out_shape=(jax.Sha...  159 us
    pallas_call x1, Pallas kernels, gather_weights(): pl.pallas_call(functools.partial(gather_kernel, cols), out_shape=(whole(o...  118 us
    ppermute x1, waiting for transfers between devices, one_sequence_body(): far_down = lax.ppermute(half_rows(w_down), 'row', OVER_X)  72.2 us
    pallas_call x1, Pallas kernels, attend_back_fast(): pl.pallas_call(functools.partial(attend_back_kernel, block), grid=(groups...  63.1 us
    pallas_call x1, Pallas kernels, start_exchange(): pl.pallas_call(functools.partial(start_kernel, cols), out_shape=(jax.Shap...  46.2 us
    pallas_call x1, Pallas kernels, attend_fast(): pl.pallas_call(functools.partial(attend_kernel, block), grid=(groups,), o...  43 us
    ppermute x1, waiting for transfers between devices, one_sequence_body(): a_last = lax.ppermute(one_of(a_sum, 1 - high), 'dp', OVER_Y)  23.2 us
  transfers between devices with their start and end apart: 16, of which 8 were waited for; matrix products, arithmetic and copies ran while one was open for 11% of the time, Pallas kernels for 26%

profile of v6, /device:TPU:0, one launch (start us, length us, event | category | flops | bytes accessed | tf_op | source)
XLA Modules:
  0.0 1028.1 jit_solution(7443896939629763387)
XLA Ops:
  20.4 46.2 %start_exchange.1 = (bf16[512,2048]{1,0:T(8,128)(2,1)S(1)}, bf16[1024,2048]{1,0:T(8,128)(2,1)S(1)}) custom-call(bf16[4,512,512]{2,1,0:T(8,128)(2,1)S(1)} %copy-done.3, f32[1,2048]{1,0:T(1,128)S(1)} %bitcast.80), custom_call_target="tpu_custom_call" | custom-call | bytes 209715200 | tf_op jit(solution)/shard_map/start_exchange/pallas_call | solution.py:342
  73.9 17.1 %collective-permute-start = (bf16[4,512,512]{2,1,0:T(8,128)(2,1)}, bf16[4,512,512]{2,1,0:T(8,128)(2,1)}, u32[]{:S(2)}, u32[]{:S(2)}) collective-permute-start(bf16[4,512,512]{2,1,0:T(8,128)(2,1)} %maximum_select_fusion.1.after_ref), channel_id=1, source_target_pairs={{0,0},{4,8},{8,4},{12,12},{16,16},{20,24},{24,20},{28,28},{1,1},{5... | collective-permute-start | bytes 6291464 | tf_op jit(solution)/shard_map/ppermute | solution.py:1577
  93.0 2.1 constant_dynamic-slice_fusion.4
  96.1 117.9 %gather_weights.1 = (bf16[2048,1536]{1,0:T(8,128)(2,1)}, bf16[2048,1024]{1,0:T(8,128)(2,1)}) custom-call(bf16[1024,384]{1,0:T(8,128)(2,1)} %pad_maximum_fusion.2.q_ref, bf16[1024,256]{1,0:T(8,128)(2,1)} %get-tuple-element.156.o_ref, bf16[4,512,512]{2,1,0:T(8,128)(2,1)} %maximum_select_fusion.1.after_ref), custom_call_target="tpu_custom_call" | custom-call | bytes 314572800 | tf_op jit(solution)/shard_map/gather_weights/pallas_call | solution.py:462
  219.5 2.3 concatenate.38.cos_ref
  221.8 11.2 %copy.51 = bf16[1024,2,2048]{2,0,1:T(8,128)(2,1)} copy(bf16[1024,2,2048]{2,1,0:T(2,128)(2,1)} %param.20) | data formatting | bytes 16777216 | tf_op jit(solution)/shard_map/optimization_barrier | solution.py:1583
  233.0 5.2 constant_dynamic-slice_fusion.3
  239.8 43.0 %attend.1 = (bf16[1024,1536]{1,0:T(8,128)(2,1)}, bf16[1024,1024]{1,0:T(8,128)(2,1)S(1)}) custom-call(s32[1]{0:T(128)} %dynamic_slice.99.len_ref, bf16[1024,2048]{1,0:T(8,128)(2,1)} %copy-done.9, bf16[2048,1536]{1,0:T(8,128)(2,1)} %get-tuple-element.52.w_ref, f32[1024,256]{1,0:T(8,128)S(1)} %copy-done.5, f32[1024,256]{1,0:T(8,128)S(1)} %concatenate.40.sin_ref), custom_call_target="tpu_custom_call" | custom-call | flops 10737418240 | bytes 13631488 | tf_op jit(solution)/shard_map/attend/pallas_call | solution.py:573
  282.9 7.8 convolution_convert_fusion.3
  293.5 4.1 slice_bitcast_fusion
  297.6 3.6 fusion.13
  304.2 72.2 %collective-permute-done.2.wd_far = bf16[512,2048]{1,0:T(8,128)(2,1)} collective-permute-done((bf16[512,2048]{1,0:T(8,128)(2,1)S(1)}, bf16[512,2048]{1,0:T(8,128)(2,1)}, u32[]{:S(2)}, u32[]{:S(2)}) %collective-permute-start.2) | collective-permute-done | bytes 2097184 | tf_op jit(solution)/shard_map/ppermute | solution.py:1585
  376.5 4.0 slice_bitcast_fusion.4
  381.0 6.2 collective-permute-done.4.wg_sib
  387.2 3.1 collective-permute-done.5.wu_sib
  391.0 288.7 %feed_forward.1 = (bf16[4,512,2048]{2,1,0:T(8,128)(2,1)}, bf16[4,512,4096]{2,1,0:T(8,128)(2,1)}, bf16[4,512,2048]{2,1,0:T(8,128)(2,1)}, bf16[3,512,2048]{2,1,0:T...) custom-call(bf16[512,2048]{1,0:T(8,128)(2,1)} %multiply_convert_fusi, ...), custom_call_target="tpu_custom_call" | custom-call | flops 154618822656 | bytes 838860800 | tf_op jit(solution)/shard_map/feed_forward/pallas_call | solution.py:1170
  679.7 4.8 convert_reduce_fusion
  685.6 4.4 multiply_convert_fusion
  694.3 8.7 convolution_convert_fusion.4.dz_ref
  703.0 63.1 %attend_back.1 = bf16[1024,1536]{1,0:T(8,128)(2,1)} custom-call(s32[1]{0:T(128)} %dynamic_slice.99.len_ref, bf16[1024,1536]{1,0:T(8,128)(2,1)} %get-tuple-element.69.qkv_ref, bf16[1024,1024]{1,0:T(8,128)(2,1)S(1)} %convolution_convert_fusion.4.dz_ref, f32[1024,256]{1,0:T(8,128)S(1)} %copy-done.6, f32[1024,256]{1,0:T(8,128)S(1)} %concatenate.40.sin_ref), custom_call_target="tpu_custom_call" | custom-call | flops 10737418240 | bytes 8388608 | tf_op jit(solution)/shard_map/attend_back/pallas_call | solution.py:680
  766.1 10.5 %convolution_convert_fusion.1 = bf16[1024,2048]{1,0:T(8,128)(2,1)S(1)} fusion(bf16[1024,1536]{1,0:T(8,128)(2,1)} %attend_back.1, bf16[2048,1536]{1,0:T(8,128)(2,1)} %get-tuple-element.52.w_ref), kind=kOutput, calls=%fused_computation.31 | convolution fusion | flops 6444548096 | bytes 13631488 | tf_op jit(solution)/shard_map/dot_general | solution.py:62
  778.9 8.8 convolution_convert_fusion
  794.3 2.2 fusion.4.ig_ref
  802.0 9.1 convolution_convert_fusion.2
  811.2 23.2 %collective-permute-done.11 = bf16[256,3072]{1,0:T(8,128)(2,1)} collective-permute-done((bf16[256,3072]{1,0:T(8,128)(2,1)}, bf16[256,3072]{1,0:T(8,128)(2,1)}, u32[]{:S(2)}, u32[]{:S(2)}) %collective-permute-start.11) | collective-permute-done | bytes 1572896 | tf_op jit(solution)/shard_map/ppermute | solution.py:1667
  834.5 2.4 convert_add_fusion.4
  837.0 2.9 convert_add_fusion.3
  842.1 5.2 copy.57
  848.9 2.2 copy-done.2
  852.6 159.3 %finish.1 = (bf16[4,512,512]{2,1,0:T(8,128)(2,1)S(1)}, bf16[4,512,512]{2,1,0:T(8,128)(2,1)S(1)}, f32[2,256,384]{2,1,0:T(8,128)S(1)}, f32[2,256,256]{2,1,0:T(8,128)S(1)}, f32[8,512]{1,0:T(8,128)S(1)}) custom-call(bf16[512,2048]{1,0:T(8,128)(2,1)S(1)} %fusion.4.ig_ref, bf16[2,2,2,256,1536]{4,3,2,1,0:T(8,128)(2,1)} %bitcast.83, ...), custom_call_target="tpu_custom_call" | custom-call | bytes 314572800 | tf_op jit(solution)/shard_map/finish/pallas_call | solution.py:1479
  1013.3 2.6 convert_element_type.135
  1015.9 2.3 convert_select_fusion
  (172 shorter events, 58.8 us)
Async XLA Ops:
  7.2 63.4 %all-gather.3.cloned.1.call-start = ((), (), s32[]{:S(2)}) async-start(), calls=%async_computation.1 | async-start | bytes 10485760 | tf_op jit(solution)/shard_map/all_gather | solution.py:1573
  7.9 383.0 %all-gather.5.cloned.1.call-start = ((), (), s32[]{:S(2)}) async-start(), calls=%async_computation.2 | async-start | bytes 10485760 | tf_op jit(solution)/shard_map/all_gather | solution.py:1580
  15.2 58.7 %copy-start.7 = (f32[2048]{0:T(1024)}, f32[2048]{0:T(1024)S(1)}, u32[]{:S(2)}) copy-start(f32[2048]{0:T(1024)S(1)} %convert_element_type.108) | copy-start | bytes 24580
  68.7 229.0 %copy-start = (bf16[512,2048]{1,0:T(8,128)(2,1)}, bf16[512,2048]{1,0:T(8,128)(2,1)S(1)}, u32[]{:S(2)}) copy-start(bf16[512,2048]{1,0:T(8,128)(2,1)S(1)} %get-tuple-element.50) | copy-start | bytes 6291460
  70.6 20.4 %copy-start.23 = (bf16[1024,2,128]{2,1,0:T(2,128)(2,1)S(1)}, bf16[1024,2,128]{2,1,0:T(2,128)(2,1)}, u32[]{:S(2)}) copy-start(bf16[1024,2,128]{2,1,0:T(2,128)(2,1)} %param.18) | copy-start | bytes 1572868
  73.9 140.2 %collective-permute-start = (bf16[4,512,512]{2,1,0:T(8,128)(2,1)}, bf16[4,512,512]{2,1,0:T(8,128)(2,1)}, u32[]{:S(2)}, u32[]{:S(2)}) collective-permute-start(bf16[4,512,512]{2,1,0:T(8,128)(2,1)} %maximum_select_fusion.1.after_ref), channel_id=1, source_target_pairs={{0,0},{4,8},{8,4},{12,12},{16,16},{20,24},{24,20},{28,28},{1,1},{5... | collective-permute-start | bytes 6291464 | tf_op jit(solution)/shard_map/ppermute | solution.py:1577
  95.1 119.0 %copy-start.37 = (s32[16]{0:T(128)S(1)}, s32[16]{0:T(128)}, u32[]{:S(2)}) copy-start(s32[16]{0:T(128)} %param.13) | copy-start | bytes 196
  214.1 634.8 %reduce-scatter.2.cloned.1.call-start = ((), (), s32[]{:S(2)}) async-start(), calls=%async_computation.3 | async-start | bytes 10485760 | tf_op jit(solution)/shard_map/reduce_scatter | solution.py:1628
  238.2 138.3 %collective-permute-start.1 = (bf16[512,2,2048]{2,0,1:T(8,128)(2,1)}, bf16[512,2,2048]{2,0,1:T(8,128)(2,1)}, u32[]{:S(2)}, u32[]{:S(2)}) collective-permute-start(bf16[512,2,2048]{2,0,1:T(8,128)(2,1)} %constant_dynamic-slice_fusion.3), channel_id=1, source_target_pairs={{0,4},{4,0},{1,5},{5,1},{2,6},{6,2},{3,7},{7,3},{8,12},{12,8},{9,1... | collective-permute-start | bytes 12582920 | tf_op jit(solution)/shard_map/ppermute | solution.py:1584
  282.9 7.9 copy-start.11
  282.9 10.6 %slice-start = ((s8[8388608]{0:T(1024)(128)(4,1)}), s8[4194304]{0:T(1024)(128)(4,1)S(1)}, s32[]{:S(2)}) async-start(s8[8388608]{0:T(1024)(128)(4,1)} %bitcast.81), calls=%async_computation.4 | async-start | bytes 8388608
  282.9 8.2 copy-start.36
  282.9 10.6 %slice-start.1 = ((s8[8388608]{0:T(1024)(128)(4,1)}), s8[4194304]{0:T(1024)(128)(4,1)S(1)}, s32[]{:S(2)}) async-start(s8[8388608]{0:T(1024)(128)(4,1)} %bitcast.81), calls=%async_computation.5 | async-start | bytes 8388608
  291.0 6.6 collective-permute-start.3
  292.9 9.6 copy-start.28
  293.1 83.4 %collective-permute-start.2 = (bf16[512,2048]{1,0:T(8,128)(2,1)S(1)}, bf16[512,2048]{1,0:T(8,128)(2,1)}, u32[]{:S(2)}, u32[]{:S(2)}) collective-permute-start(bf16[512,2048]{1,0:T(8,128)(2,1)S(1)} %constant_dynamic-slice_fusion.2), channel_id=1, source_target_pairs={{0,4},{4,0},{1,5},{5,1},{2,6},{6,2},{3,7},{7,3},{8,12},{12,8},{9,1... | collective-permute-start | bytes 6291464 | tf_op jit(solution)/shard_map/ppermute | solution.py:1585
  302.5 78.0 %copy-start.30 = (f32[512]{0:T(512)}, f32[512]{0:T(512)S(1)}, u32[]{:S(2)}) copy-start(f32[512]{0:T(512)S(1)} %get-tuple-element.149) | copy-start | bytes 6148
  380.4 10.5 %copy-start.24 = (bf16[512,2048]{1,0:T(8,128)(2,1)}, bf16[512,2048]{1,0:T(8,128)(2,1)S(1)}, u32[]{:S(2)}) copy-start(bf16[512,2048]{1,0:T(8,128)(2,1)S(1)} %get-tuple-element.129.wu_far) | copy-start | bytes 6291460
  380.4 6.8 collective-permute-start.4
  380.5 9.9 collective-permute-start.5
  381.0 10.0 collective-permute-start.6
  690.0 4.3 collective-permute-start.9
  690.7 97.0 %collective-permute-start.8 = (bf16[2,256,3072]{2,1,0:T(8,128)(2,1)}, bf16[2,256,3072]{2,1,0:T(8,128)(2,1)S(1)}, u32[]{:S(2)}, u32[]{:S(2)}) collective-permute-start(bf16[2,256,3072]{2,1,0:T(8,128)(2,1)} %get-tuple-element.67), channel_id=1, source_target_pairs={{0,16},{16,0},{8,24},{24,8},{1,17},{17,1},{9,25},{25,9},{2,18},{18... | collective-permute-start | bytes 9437192 | tf_op jit(solution)/shard_map/ppermute | solution.py:1634
  692.3 10.7 %copy-start.6 = (f32[1024,256]{1,0:T(8,128)S(1)}, f32[1024,256]{1,0:T(8,128)}, u32[]{:S(2)}) copy-start(f32[1024,256]{1,0:T(8,128)} %concatenate.38.cos_ref) | copy-start | bytes 3145732
  692.3 96.6 %collective-permute-start.7 = (bf16[2,256,3072]{2,1,0:T(8,128)(2,1)}, bf16[2,256,3072]{2,1,0:T(8,128)(2,1)S(1)}, u32[]{:S(2)}, u32[]{:S(2)}) collective-permute-start(bf16[2,256,3072]{2,1,0:T(8,128)(2,1)} %get-tuple-element.65), channel_id=1, source_target_pairs={{0,4},{4,0},{1,5},{5,1},{2,6},{6,2},{3,7},{7,3},{8,12},{12,8},{9,1... | collective-permute-start | bytes 9437192 | tf_op jit(solution)/shard_map/ppermute | solution.py:1633
  766.1 11.0 %copy-start.38 = (bf16[1024,1536]{1,0:T(8,128)(2,1)S(1)}, bf16[1024,1536]{1,0:T(8,128)(2,1)}, u32[]{:S(2)}) copy-start(bf16[1024,1536]{1,0:T(8,128)(2,1)} %attend_back.1) | copy-start | bytes 9437188
  776.9 10.8 %copy-start.22 = (bf16[2,256,3072]{2,1,0:T(8,128)(2,1)S(1)}, bf16[2,256,3072]{2,1,0:T(8,128)(2,1)}, u32[]{:S(2)}) copy-start(bf16[2,256,3072]{2,1,0:T(8,128)(2,1)} %get-tuple-element.66) | copy-start | bytes 9437188
  776.9 13.9 %collective-permute-start.10 = (bf16[512,2048]{1,0:T(8,128)(2,1)S(1)}, bf16[512,2048]{1,0:T(8,128)(2,1)S(1)}, u32[]{:S(2)}, u32[]{:S(2)}) collective-permute-start(bf16[512,2048]{1,0:T(8,128)(2,1)S(1)} %constant_dynamic-slice_fusion), channel_id=1, source_target_pairs={{0,8},{8,0},{16,24},{24,16},{1,9},{9,1},{17,25},{25,17},{2,10},{10... | collective-permute-start | bytes 6291464 | tf_op jit(solution)/shard_map/ppermute | solution.py:1551
  788.8 10.5 %copy-start.18 = (bf16[2,256,3072]{2,1,0:T(8,128)(2,1)}, bf16[2,256,3072]{2,1,0:T(8,128)(2,1)S(1)}, u32[]{:S(2)}) copy-start(bf16[2,256,3072]{2,1,0:T(8,128)(2,1)S(1)} %add_convert_fusion) | copy-start | bytes 9437188
  797.8 36.7 %collective-permute-start.11 = (bf16[256,3072]{1,0:T(8,128)(2,1)}, bf16[256,3072]{1,0:T(8,128)(2,1)}, u32[]{:S(2)}, u32[]{:S(2)}) collective-permute-start(bf16[256,3072]{1,0:T(8,128)(2,1)} %dynamic-slice_bitcast_fusion.1), channel_id=1, source_target_pairs={{0,16},{16,0},{8,24},{24,8},{1,17},{17,1},{9,25},{25,9},{2,18},{18... | collective-permute-start | bytes 4718600 | tf_op jit(solution)/shard_map/ppermute | solution.py:1667
  800.6 36.4 %collective-permute-start.12 = (bf16[256,3072]{1,0:T(8,128)(2,1)}, bf16[256,3072]{1,0:T(8,128)(2,1)}, u32[]{:S(2)}, u32[]{:S(2)}) collective-permute-start(bf16[256,3072]{1,0:T(8,128)(2,1)} %dynamic-slice_bitcast_fusion), channel_id=1, source_target_pairs={{0,4},{4,0},{1,5},{5,1},{2,6},{6,2},{3,7},{7,3},{8,12},{12,8},{9,1... | collective-permute-start | bytes 4718600 | tf_op jit(solution)/shard_map/ppermute | solution.py:1668
  811.2 25.8 %copy-start.19 = (bf16[2,256,3072]{2,1,0:T(8,128)(2,1)S(1)}, bf16[2,256,3072]{2,1,0:T(8,128)(2,1)}, u32[]{:S(2)}) copy-start(bf16[2,256,3072]{2,1,0:T(8,128)(2,1)} %copy-done.18) | copy-start | bytes 9437188
  (27 other events, 92.8 us)
Sparse Core Ops, SparseCore 0:
  9.6 60.9 all-gather.2
  214.2 159.4 all-gather.4
  690.1 143.6 reduce-scatter.1

commit v7 on v6

--- a/solution.py
+++ b/solution.py
@@ -362,12 +362,11 @@
     )(tokens, gain.reshape(1, full))
 
 
-def gather_kernel(
-    cols, q_ref, o_ref, after_ref, wq_ref, wo_ref, q_send, q_recv, q_over, o_send, o_recv, o_over, local_sems
-):
+def gather_kernel(cols, own_ref, after_ref, full_ref, send, recv, over_sems, local_sem):
     group, core, mate, row, col = place()
     last = cols - 1
     over = (group, 1 - row, col)
+    tall, wide = own_ref.shape
     greet(over)
 
     @pl.when(col < last)
@@ -383,98 +382,78 @@
         1 + jnp.minimum(col, 1) + jnp.minimum(last - col, 1),
     )
 
-    def moves(own, full, send, recv, over_sems):
-        tall, wide = own.shape
-
-        def block(of_row, of_col):
-            return full.at[aligned(of_row, tall), aligned(of_col, wide)]
-
-        def along(src, chunk, to, way):
-            return pltpu.make_async_remote_copy(
-                src_ref=src,
-                dst_ref=block(row, chunk),
-                send_sem=send.at[way, chunk],
-                recv_sem=recv.at[chunk],
-                device_id=(group, row, to),
-                device_id_type=MESH_IDS,
-            )
-
-        def across(src, of_row, chunk):
-            return remote(src, block(of_row, chunk), over_sems, chunk, over)
-
-        return block, along, across
-
-    both = (
-        (q_ref, moves(q_ref, wq_ref, q_send, q_recv, q_over)),
-        (o_ref, moves(o_ref, wo_ref, o_send, o_recv, o_over)),
-    )
-    own_copies = []
-    for at, (own, (block, along, across)) in enumerate(both):
-
-        @pl.when(col < last)
-        def _():
-            along(own, col, col + 1, 0).start()
-
-        @pl.when(col > 0)
-        def _():
-            along(own, col, col - 1, 1).start()
-
-        across(own, row, col).start()
-        own_copies.append(pltpu.make_async_copy(own, block(row, col), local_sems.at[at]))
-        own_copies[-1].start()
+    def block(of_row, of_col):
+        return full_ref.at[aligned(of_row, tall), aligned(of_col, wide)]
+
+    def along(src, chunk, to, way):
+        return pltpu.make_async_remote_copy(
+            src_ref=src,
+            dst_ref=block(row, chunk),
+            send_sem=send.at[way, chunk],
+            recv_sem=recv.at[chunk],
+            device_id=(group, row, to),
+            device_id_type=MESH_IDS,
+        )
+
+    def across(src, of_row, chunk):
+        return remote(src, block(of_row, chunk), over_sems, chunk, over)
+
+    @pl.when(col < last)
+    def _():
+        along(own_ref, col, col + 1, 0).start()
+
+    @pl.when(col > 0)
+    def _():
+        along(own_ref, col, col - 1, 1).start()
+
+    across(own_ref, row, col).start()
+    own_copy = pltpu.make_async_copy(own_ref, block(row, col), local_sem)
+    own_copy.start()
     for at in range(1, cols):
         chunk = line_order(col, last, at)
-        for own, (block, along, across) in both:
-            along(own, chunk, col, 0).wait_recv()
-
-            @pl.when((chunk < col) & (col < last))
-            def _():
-                along(block(row, chunk), chunk, col + 1, 0).start()
-
-            @pl.when((chunk > col) & (col > 0))
-            def _():
-                along(block(row, chunk), chunk, col - 1, 1).start()
-
-            across(block(row, chunk), row, chunk).start()
-    for copy in own_copies:
-        copy.wait()
-    for own, (block, along, across) in both:
-        for chunk in range(cols):
-
-            @pl.when((col >= chunk) & (col < last))
-            def _():
-                along(own, chunk, col + 1, 0).wait_send()
-
-            @pl.when((col <= chunk) & (col > 0))
-            def _():
-                along(own, chunk, col - 1, 1).wait_send()
-
-            across(own, row, chunk).wait_send()
-            across(own, 1 - row, chunk).wait_recv()
-
-
-def gather_weights(own_q, own_o, after, rows, cols):
+        along(own_ref, chunk, col, 0).wait_recv()
+
+        @pl.when((chunk < col) & (col < last))
+        def _():
+            along(block(row, chunk), chunk, col + 1, 0).start()
+
+        @pl.when((chunk > col) & (col > 0))
+        def _():
+            along(block(row, chunk), chunk, col - 1, 1).start()
+
+        across(block(row, chunk), row, chunk).start()
+    own_copy.wait()
+    for chunk in range(cols):
+
+        @pl.when((col >= chunk) & (col < last))
+        def _():
+            along(own_ref, chunk, col + 1, 0).wait_send()
+
+        @pl.when((col <= chunk) & (col > 0))
+        def _():
+            along(own_ref, chunk, col - 1, 1).wait_send()
+
+        across(own_ref, row, chunk).wait_send()
+        across(own_ref, 1 - row, chunk).wait_recv()
+
+
+def gather_weights(own, after, rows, cols, collective_id):
     anywhere = pl.BlockSpec(memory_space=pl.ANY)
-
-    def whole(own):
-        return jax.ShapeDtypeStruct((own.shape[0] * rows, own.shape[1] * cols), own.dtype)
-
     return pl.pallas_call(
         functools.partial(gather_kernel, cols),
-        out_shape=(whole(own_q), whole(own_o)),
-        in_specs=[anywhere] * 3,
-        out_specs=(anywhere,) * 2,
+        out_shape=jax.ShapeDtypeStruct((own.shape[0] * rows, own.shape[1] * cols), own.dtype),
+        in_specs=[anywhere] * 2,
+        out_specs=anywhere,
         scratch_shapes=[
             pltpu.SemaphoreType.DMA((2, cols)),
             pltpu.SemaphoreType.DMA((cols,)),
             pltpu.SemaphoreType.DMA((2, cols)),
-        ]
-        * 2
-        + [pltpu.SemaphoreType.DMA((2,))],
-        compiler_params=pltpu.CompilerParams(collective_id=4, has_side_effects=True),
-        cost_estimate=pl.CostEstimate(flops=0, bytes_accessed=300 << 20, transcendentals=0),
+            pltpu.SemaphoreType.DMA(()),
+        ],
+        compiler_params=pltpu.CompilerParams(collective_id=collective_id, has_side_effects=True),
+        cost_estimate=pl.CostEstimate(flops=0, bytes_accessed=200 << 20, transcendentals=0),
         name="gather_weights",
-    )(own_q, own_o, after)
+    )(own, after)
 
 
 def half_turn(wide):
@@ -750,6 +729,7 @@
     relay_recv,
     pair_sems,
     lane_sems,
+    tile_sems,
     io_sems,
 ):
     group, core, mate, row, col = place()
@@ -759,7 +739,7 @@
     half = depth // 2
     units = wg_own.shape[1]
     rows = own_ref.shape[0]
-    tile = min(512, units)
+    tile = units // cols
     beside = col + 1 - 2 * lax.rem(col, 2)
     facing = last - col
     inner = (col > 0) & (col < last)
@@ -978,8 +958,6 @@
         ]
     for load in loads:
         load.start()
-    for load in loads:
-        load.wait()
 
     def relay(box, slot):
         hand_over(slot, facing, box, 3).wait_recv()
@@ -1078,15 +1056,30 @@
         return pltpu.make_async_copy(
             grad_ref.at[chunk, :, aligned(block, rows)],
             mlp_buf.at[:, part_of(chunk)],
-            w_sems.at[chunk],
+            tile_sems.at[chunk],
         )
 
     parts = range(3)
+
+    def block_of(at):
+        return 2 * lax.rem(at, 2) + jnp.where(at >= 2, core, 1 - core)
+
+    for chunk in range(cols):
+        grad_tile(block_of(0), chunk).start()
+    for chunk in range(cols):
+        b_turn[0, :, part_of(chunk)] = b_all[chunk, :, aligned(block_of(0), rows)].T
+    for chunk in range(cols):
+        grad_tile(block_of(0), chunk).wait()
+    for chunk in range(cols):
+        g_two[0, :, part_of(chunk)] = mlp_buf[:, part_of(chunk)].T
+    for load in loads:
+        load.wait()
 
     def one_block(at, unused):
         high = lax.rem(at, 2)
         is_own = at >= 2
-        block = 2 * high + jnp.where(is_own, core, 1 - core)
+        side = lax.rem(at, 2)
+        following = block_of(jnp.minimum(at + 1, 3))
 
         @pl.when(inner & (at == 1))
         def _():
@@ -1095,14 +1088,10 @@
             relay(1, last - col)
             deliver(last - col, facing, 2, 2).start()
 
-        for chunk in range(cols):
-            grad_tile(block, chunk).start()
-        for chunk in range(cols):
-            b_turn[:, part_of(chunk)] = b_all[chunk, :, aligned(block, rows)].T
-        for chunk in range(cols):
-            grad_tile(block, chunk).wait()
-        for chunk in range(cols):
-            g_two[0, :, part_of(chunk)] = mlp_buf[:, part_of(chunk)].T
+        @pl.when(at < 3)
+        def _():
+            for chunk in range(cols):
+                grad_tile(following, chunk).start()
 
         @pl.when((at == 1) | (at == 2))
         def _():
@@ -1121,17 +1110,25 @@
             for part in parts:
                 landed(high, part).wait()
 
-        @pl.loop(0, units // tile)
+        @pl.when(at < 3)
+        def _():
+            for chunk in range(cols):
+                grad_tile(following, chunk).wait()
+
+        @pl.loop(0, cols)
         def _(step):
             lanes = aligned(step, tile)
+            tokens = aligned(step, rows)
 
             def put(buffer, value):
                 other = jnp.where(is_own, buffer[:, lanes].astype(jnp.float32), 0.0)
                 buffer[:, lanes] = (other + value).astype(jnp.bfloat16)
 
-            put(dg_buf, dot_nn(b_turn[...], wg[:, lanes]))
-            put(du_buf, dot_nn(b_turn[...], wu[:, lanes]))
-            put(u_buf, RES_MULT * dot_nn(g_two[0], wd[:, lanes]))
+            put(dg_buf, dot_nn(b_turn[side], wg[:, lanes]))
+            b_turn[1 - side, :, tokens] = b_all[step, :, aligned(following, rows)].T
+            put(du_buf, dot_nn(b_turn[side], wu[:, lanes]))
+            g_two[1 - side, :, tokens] = mlp_buf[:, tokens].T
+            put(u_buf, RES_MULT * dot_nn(g_two[side], wd[:, lanes]))
 
         @pl.when(jnp.logical_not(is_own))
         def _():
@@ -1185,7 +1182,7 @@
             pltpu.VMEM((width, units), bf16),
             pltpu.VMEM((width, units), bf16),
             pltpu.VMEM((cols, rows, width), bf16),
-            pltpu.VMEM((rows, width), bf16),
+            pltpu.VMEM((2, rows, width), bf16),
             pltpu.VMEM((2, rows, width), bf16),
             pltpu.VMEM((rows, units), bf16),
             pltpu.VMEM((rows, units), bf16),
@@ -1200,6 +1197,7 @@
             pltpu.SemaphoreType.DMA((2,)),
             pltpu.SemaphoreType.DMA((2, 2, 3)),
             pltpu.SemaphoreType.DMA((8,)),
+            pltpu.SemaphoreType.DMA((cols,)),
             pltpu.SemaphoreType.DMA((9,)),
         ],
         compiler_params=pltpu.CompilerParams(
@@ -1220,9 +1218,7 @@
     gq_ref,
     go_ref,
     gain_ref,
-    out_ref,
     gin_ref,
-    crossed_ref,
     sq_ref,
     so_ref,
     gsum_ref,
@@ -1248,7 +1244,6 @@
     o_sems,
     qz_sems,
     oz_sems,
-    cross_sems,
     local_sems,
 ):
     group, core, mate, row, col = place()
@@ -1335,8 +1330,6 @@
         ig_ref.at[:, lanes(col, width)], gin_ref.at[col], local_sems.at[2]
     )
 
-    cross = remote(out_ref, crossed_ref, cross_sems, 0, (mate, core, col))
-    stay = pltpu.make_async_copy(out_ref, crossed_ref, local_sems.at[4])
     for m in range(2):
         copies[m]["s0"].start()
         copies[m]["a1"].start()
@@ -1344,7 +1337,6 @@
     @pl.when(core == row)
     def _():
         own_tokens.start()
-        stay.start()
         for step in range(1, cols):
             token_copy(step, col).start()
 
@@ -1386,7 +1378,6 @@
     def _():
         for step in range(cols):
             token_copy(step, col).start()
-        cross.start()
 
     gain_round(2)
     for m in range(2):
@@ -1449,15 +1440,13 @@
     def _():
         token_copy(0, col).wait_recv()
         token_copy(0, col).wait_send()
-        cross.wait()
 
     @pl.when(core == row)
     def _():
         own_tokens.wait()
-        stay.wait()
-
-
-def finish(input_grad, grad_q, grad_o, gains, output, cols):
+
+
+def finish(input_grad, grad_q, grad_o, gains, cols):
     anywhere = pl.BlockSpec(memory_space=pl.ANY)
     in_vmem = pl.BlockSpec(memory_space=pltpu.VMEM)
     bf16, f32 = jnp.bfloat16, jnp.float32
@@ -1480,13 +1469,12 @@
         functools.partial(finish_kernel, cols),
         out_shape=(
             jax.ShapeDtypeStruct((cols, length, full // cols), bf16),
-            jax.ShapeDtypeStruct(output.shape, bf16),
             jax.ShapeDtypeStruct((2, rows, wide_q // cols), f32),
             jax.ShapeDtypeStruct((2, rows, wide_o // cols), f32),
             jax.ShapeDtypeStruct(gains.shape, f32),
         ),
-        in_specs=[anywhere] * 5,
-        out_specs=(anywhere, anywhere, in_vmem, in_vmem, in_vmem),
+        in_specs=[anywhere] * 4,
+        out_specs=(anywhere, in_vmem, in_vmem, in_vmem),
         scratch_shapes=buffers(wide_q)
         + buffers(wide_o)
         + [
@@ -1498,8 +1486,7 @@
             pltpu.SemaphoreType.DMA((2, 5)),
             pltpu.SemaphoreType.DMA((2, 2, cols)),
             pltpu.SemaphoreType.DMA((2, 2, cols)),
-            pltpu.SemaphoreType.DMA((2, 1)),
-            pltpu.SemaphoreType.DMA((5,)),
+            pltpu.SemaphoreType.DMA((4,)),
         ],
         compiler_params=pltpu.CompilerParams(
             collective_id=3, has_side_effects=True, vmem_limit_bytes=40 << 20
@@ -1511,7 +1498,6 @@
         grad_q.reshape(2, 2, 2, rows, wide_q),
         grad_o.reshape(2, 2, 2, rows, wide_o),
         gains,
-        output,
     )
 
 
@@ -1575,7 +1561,7 @@
     picked = pick_sequences(everyone, deal_order, group * seq_group, seq_group)
     picked = jnp.where(given_live, picked, jnp.zeros_like(picked))
     given = lax.ppermute(picked, ("dp", "row"), CROSSED)
-    weights_qkv, weights_out = gather_weights(pack_q, pack_o, picked, row_count, col_count)
+    weights_qkv = gather_weights(pack_q, picked, row_count, col_count, 4)
     given, weights_qkv = lax.optimization_barrier((given, weights_qkv))
     line_cot = lax.all_gather(given, "col", axis=2, tiled=True)
     own_grad = lax.dynamic_index_in_dim(line_cot, col, keepdims=False).astype(jnp.float32)
@@ -1606,6 +1592,7 @@
         other = lax.dynamic_slice_in_dim(partial, (1 - core) * count, count)
         return mine.astype(jnp.float32) + from_sibling(other).astype(jnp.float32)
 
+    weights_out = gather_weights(pack_o, heads_out, row_count, col_count, 5)
     attn_rows = summed_rows(expand_local(heads_out, weights_out).astype(jnp.bfloat16))
     resid = own_float + RES_MULT * attn_rows
     scale_two = lax.rsqrt(jnp.mean(resid * resid, axis=1, keepdims=True) + EPSILON)
@@ -1667,9 +1654,13 @@
     a_last = lax.ppermute(one_of(a_sum, 1 - high), "dp", OVER_Y)
     b_last = lax.ppermute(one_of(b_sum, 1 - row), "row", OVER_X)
     gains = jnp.stack([gain_one_part, gain_two_part]).reshape(8, -1)
-    given_grad, given_out, sums_q, sums_o, gain_sums = finish(
-        own_input_grad, grad_qkv, grad_out, gains, out_cols, col_count
-    )
+    given_grad, sums_q, sums_o, gain_sums = finish(
+        own_input_grad, grad_qkv, grad_out, gains, col_count
+    )
+    out_cols, a_last, b_last, a_sum, b_sum, given_grad = lax.optimization_barrier(
+        (out_cols, a_last, b_last, a_sum, b_sum, given_grad)
+    )
+    given_out = lax.ppermute(out_cols, ("dp", "row"), CROSSED)
     layer_out = jnp.where(given_live, given_out.astype(jnp.float32), 0.0)
     input_grad = given_grad.astype(jnp.float32)
     a_total = one_of(a_sum, high).astype(jnp.float32) + a_last.astype(jnp.float32)

time: 1040 us -> 1090 us (1.048)
  Pallas kernels: 718 us -> 818 us
  waiting for transfers between devices: 109 us -> 48.1 us
    pallas_call x1 -> x2, Pallas kernels: 118 us -> 207 us  [gather_weights(): pl.pallas_call(functools.partial(gather_kernel, cols), out_shape=jax.Shap...]
    ppermute x1, waiting for transfers between devices: 72.2 us -> 33.5 us  [one_sequence_body(): far_down = lax.ppermute(half_rows(w_down), 'row', OVER_X)]
    ppermute x1, waiting for transfers between devices: 23.2 us -> 0.01 us  [one_sequence_body(): a_last = lax.ppermute(one_of(a_sum, 1 - high), 'dp', OVER_Y)]
    pallas_call x1, Pallas kernels: 159 us -> 178 us  [finish(): pl.pallas_call(functools.partial(finish_kernel, cols), out_shape=(jax.Sha...]
    unnamed x87 -> x81, local copies, waits for them, and re-layouts: 23.1 us -> 23.5 us
  transfers between devices with their start and end apart: 16 -> 17, of which waited for: 8 -> 6; matrix products, arithmetic and copies ran while one was open for 11% -> 13% of each run, Pallas kernels for 26% -> 50%
where the time goes in v7:
time: 1090 us; the launch traced here: 1080 us
  Pallas kernels  818 us (75%)
  local copies, waits for them, and re-layouts  71.4 us (7%)
  waiting for transfers between devices  48.1 us (4%)
  other arithmetic  44.9 us (4%)
  matrix products  42.7 us (4%)
  starting transfers between devices  27.7 us (3%)
  between operations  22.5 us (2%)
    pallas_call x1, Pallas kernels, feed_forward(): pl.pallas_call(functools.partial(ffn_kernel, cols), out_shape=(jax.ShapeD...  280 us
    pallas_call x2, Pallas kernels, gather_weights(): pl.pallas_call(functools.partial(gather_kernel, cols), out_shape=jax.Shap...  207 us
    pallas_call x1, Pallas kernels, finish(): pl.pallas_call(functools.partial(finish_kernel, cols), out_shape=(jax.Sha...  178 us
    pallas_call x1, Pallas kernels, attend_back_fast(): pl.pallas_call(functools.partial(attend_back_kernel, block), grid=(groups...  63.7 us
    pallas_call x1, Pallas kernels, start_exchange(): pl.pallas_call(functools.partial(start_kernel, cols), out_shape=(jax.Shap...  46.2 us
    pallas_call x1, Pallas kernels, attend_fast(): pl.pallas_call(functools.partial(attend_kernel, block), grid=(groups,), o...  43.3 us
    ppermute x1, waiting for transfers between devices, one_sequence_body(): far_down = lax.ppermute(half_rows(w_down), 'row', OVER_X)  33.5 us
    unnamed x81, local copies, waits for them, and re-layouts  23.5 us
  transfers between devices with their start and end apart: 17, of which 6 were waited for; matrix products, arithmetic and copies ran while one was open for 13% of the time, Pallas kernels for 50%

profile of v7, /device:TPU:0, one launch (start us, length us, event | category | flops | bytes accessed | tf_op | source)
XLA Modules:
  0.0 1075.4 jit_solution(17701465275941068334)
XLA Ops:
  20.4 46.2 %start_exchange.1 = (bf16[512,2048]{1,0:T(8,128)(2,1)S(1)}, bf16[1024,2048]{1,0:T(8,128)(2,1)S(1)}) custom-call(bf16[4,512,512]{2,1,0:T(8,128)(2,1)S(1)} %copy-done.7, f32[1,2048]{1,0:T(1,128)S(1)} %bitcast.80), custom_call_target="tpu_custom_call" | custom-call | bytes 209715200 | tf_op jit(solution)/shard_map/start_exchange/pallas_call | solution.py:342
  73.8 17.1 %collective-permute-start = (bf16[4,512,512]{2,1,0:T(8,128)(2,1)}, bf16[4,512,512]{2,1,0:T(8,128)(2,1)}, u32[]{:S(2)}, u32[]{:S(2)}) collective-permute-start(bf16[4,512,512]{2,1,0:T(8,128)(2,1)} %maximum_select_fusion.1.after_ref), channel_id=1, source_target_pairs={{0,0},{4,8},{8,4},{12,12},{16,16},{20,24},{24,20},{28,28},{1,1},{5... | collective-permute-start | bytes 6291464 | tf_op jit(solution)/shard_map/ppermute | solution.py:1563
  97.1 84.9 %gather_weights.2.w_ref = bf16[2048,1536]{1,0:T(8,128)(2,1)} custom-call(bf16[1024,384]{1,0:T(8,128)(2,1)} %pad_maximum_fusion.2.own_ref, bf16[4,512,512]{2,1,0:T(8,128)(2,1)} %maximum_select_fusion.1.after_ref), custom_call_target="tpu_custom_call" | custom-call | bytes 209715200 | tf_op jit(solution)/shard_map/gather_weights/pallas_call | solution.py:442
  186.7 2.5 copy.52
  193.6 10.8 %copy.51 = bf16[1024,2,2048]{2,0,1:T(8,128)(2,1)} copy(bf16[1024,2,2048]{2,1,0:T(2,128)(2,1)} %param.20) | data formatting | bytes 16777216 | tf_op jit(solution)/shard_map/optimization_barrier | solution.py:1569
  204.4 4.8 constant_dynamic-slice_fusion.4
  209.2 2.4 collective-permute-start.1
  211.6 43.3 %attend.1 = (bf16[1024,1536]{1,0:T(8,128)(2,1)}, bf16[1024,1024]{1,0:T(8,128)(2,1)S(1)}) custom-call(s32[1]{0:T(128)} %dynamic_slice.98.len_ref, bf16[1024,2048]{1,0:T(8,128)(2,1)} %copy-done.12, bf16[2048,1536]{1,0:T(8,128)(2,1)} %gather_weights.2.w_ref, f32[1024,256]{1,0:T(8,128)S(1)} %concatenate.38.cos_ref, f32[1024,256]{1,0:T(8,128)S(1)} %copy-done.10), custom_call_target="tpu_custom_call" | custom-call | flops 10737418240 | bytes 13631488 | tf_op jit(solution)/shard_map/attend/pallas_call | solution.py:552
  256.3 121.8 %gather_weights.3 = bf16[2048,1024]{1,0:T(8,128)(2,1)} custom-call(bf16[1024,256]{1,0:T(8,128)(2,1)} %constant_dynamic-slice_fusion.2.own_ref, bf16[1024,1024]{1,0:T(8,128)(2,1)} %copy-done.8), custom_call_target="tpu_custom_call" | custom-call | bytes 209715200 | tf_op jit(solution)/shard_map/gather_weights/pallas_call | solution.py:442
  378.1 7.4 convolution_convert_fusion.3
  388.3 6.5 slice_bitcast_fusion
  394.8 3.6 fusion.13
  401.4 33.5 %collective-permute-done.2.wd_far = bf16[512,2048]{1,0:T(8,128)(2,1)} collective-permute-done((bf16[512,2048]{1,0:T(8,128)(2,1)S(1)}, bf16[512,2048]{1,0:T(8,128)(2,1)}, u32[]{:S(2)}, u32[]{:S(2)}) %collective-permute-start.2) | collective-permute-done | bytes 2097184 | tf_op jit(solution)/shard_map/ppermute | solution.py:1571
  434.9 4.0 slice_bitcast_fusion.4
  439.5 6.2 collective-permute-done.4.wg_sib
  445.7 3.1 collective-permute-done.5.wu_sib
  449.4 279.8 %feed_forward.1 = (bf16[4,512,2048]{2,1,0:T(8,128)(2,1)}, bf16[4,512,4096]{2,1,0:T(8,128)(2,1)}, bf16[4,512,2048]{2,1,0:T(8,128)(2,1)}, bf16[3,512,2048]{2,1,0:T...) custom-call(bf16[512,2048]{1,0:T(8,128)(2,1)} %multiply_convert_fusi, ...), custom_call_target="tpu_custom_call" | custom-call | flops 154618822656 | bytes 838860800 | tf_op jit(solution)/shard_map/feed_forward/pallas_call | solution.py:1167
  729.3 4.8 convert_reduce_fusion
  735.3 4.4 multiply_convert_fusion
  744.0 8.3 convolution_convert_fusion.4.dz_ref
  752.3 63.7 %attend_back.1 = bf16[1024,1536]{1,0:T(8,128)(2,1)} custom-call(s32[1]{0:T(128)} %dynamic_slice.98.len_ref, bf16[1024,1536]{1,0:T(8,128)(2,1)} %get-tuple-element.71.qkv_ref, bf16[1024,1024]{1,0:T(8,128)(2,1)S(1)} %convolution_convert_fusion.4.dz_ref, f32[1024,256]{1,0:T(8,128)S(1)} %concatenate.38.cos_ref, f32[1024,256]{1,0:T(8,128)S(1)} %copy-done.11), custom_call_target="tpu_custom_call" | custom-call | flops 10737418240 | bytes 8388608 | tf_op jit(solution)/shard_map/attend_back/pallas_call | solution.py:659
  816.1 8.6 convolution_convert_fusion.1
  826.9 8.8 convolution_convert_fusion
  835.7 9.6 convolution_convert_fusion.2
  845.3 2.9 add_convert_fusion
  862.2 178.4 %finish.1 = (bf16[4,512,512]{2,1,0:T(8,128)(2,1)S(1)}, f32[2,256,384]{2,1,0:T(8,128)S(1)}, f32[2,256,256]{2,1,0:T(8,128)S(1)}, f32[8,512]{1,0:T(8,128)S(1)}) custom-call(bf16[512,2048]{1,0:T(8,128)(2,1)S(1)} %fusion.4.ig_ref, bf16[2,2,2,256,1536]{4,3,2,1,0:T(8,128)(2,1)} %bitcast.83, bf16[2,2,2,256,1024]{4,3,2,1,0:T(8,128)(2,1)S(1)} %bitcast.79, ...), custom_call_target="tpu_custom_call" | custom-call | bytes 314572800 | tf_op jit(solution)/shard_map/finish/pallas_call | solution.py:1468
  1046.2 2.4 collective-permute-start.13
  1048.6 2.4 convert_add_fusion.4
  1051.1 3.5 convert_add_fusion.3
  1057.0 5.2 copy.57
  1062.3 2.6 convert_element_type.135
  1066.3 2.3 convert_select_fusion
  (170 shorter events, 66.7 us)
Async XLA Ops:
  7.2 87.9 %copy-start = (bf16[1024,512]{1,0:T(8,128)(2,1)S(1)}, bf16[1024,512]{1,0:T(8,128)(2,1)}, u32[]{:S(2)}) copy-start(bf16[1024,512]{1,0:T(8,128)(2,1)} %param.17) | copy-start | bytes 3145732
  7.2 63.4 %all-gather.3.cloned.1.call-start = ((), (), s32[]{:S(2)}) async-start(), calls=%async_computation.1 | async-start | bytes 10485760 | tf_op jit(solution)/shard_map/all_gather | solution.py:1559
  7.9 441.5 %all-gather.5.cloned.1.call-start = ((), (), s32[]{:S(2)}) async-start(), calls=%async_computation.2 | async-start | bytes 10485760 | tf_op jit(solution)/shard_map/all_gather | solution.py:1566
  68.7 326.2 %copy-start.2 = (bf16[512,2048]{1,0:T(8,128)(2,1)}, bf16[512,2048]{1,0:T(8,128)(2,1)S(1)}, u32[]{:S(2)}) copy-start(bf16[512,2048]{1,0:T(8,128)(2,1)S(1)} %get-tuple-element.52) | copy-start | bytes 6291460
  73.8 108.2 %collective-permute-start = (bf16[4,512,512]{2,1,0:T(8,128)(2,1)}, bf16[4,512,512]{2,1,0:T(8,128)(2,1)}, u32[]{:S(2)}, u32[]{:S(2)}) collective-permute-start(bf16[4,512,512]{2,1,0:T(8,128)(2,1)} %maximum_select_fusion.1.after_ref), channel_id=1, source_target_pairs={{0,0},{4,8},{8,4},{12,12},{16,16},{20,24},{24,20},{28,28},{1,1},{5... | collective-permute-start | bytes 6291464 | tf_op jit(solution)/shard_map/ppermute | solution.py:1563
  97.1 85.0 %copy-start.34 = (s32[16]{0:T(128)S(1)}, s32[16]{0:T(128)}, u32[]{:S(2)}) copy-start(s32[16]{0:T(128)} %param.13) | copy-start | bytes 196
  182.0 864.2 %reduce-scatter.2.cloned.1.call-start = ((), (), s32[]{:S(2)}) async-start(), calls=%async_computation.3 | async-start | bytes 10485760 | tf_op jit(solution)/shard_map/reduce_scatter | solution.py:1615
  204.4 7.2 copy-start.10
  209.2 225.7 %collective-permute-start.1 = (bf16[512,2,2048]{2,0,1:T(8,128)(2,1)}, bf16[512,2,2048]{2,0,1:T(8,128)(2,1)}, u32[]{:S(2)}, u32[]{:S(2)}) collective-permute-start(bf16[512,2,2048]{2,0,1:T(8,128)(2,1)} %constant_dynamic-slice_fusion.4), channel_id=1, source_target_pairs={{0,4},{4,0},{1,5},{5,1},{2,6},{6,2},{3,7},{7,3},{8,12},{12,8},{9,1... | collective-permute-start | bytes 12582920 | tf_op jit(solution)/shard_map/ppermute | solution.py:1570
  378.1 7.6 copy-start.33
  385.7 9.2 collective-permute-start.3
  387.7 12.0 %copy-start.25 = (f32[2048]{0:T(1024)}, f32[2048]{0:T(1024)S(1)}, u32[]{:S(2)}) copy-start(f32[2048]{0:T(1024)S(1)} %convert_element_type.114) | copy-start | bytes 24580
  387.8 47.1 %collective-permute-start.2 = (bf16[512,2048]{1,0:T(8,128)(2,1)S(1)}, bf16[512,2048]{1,0:T(8,128)(2,1)}, u32[]{:S(2)}, u32[]{:S(2)}) collective-permute-start(bf16[512,2048]{1,0:T(8,128)(2,1)S(1)} %constant_dynamic-slice_fusion.3), channel_id=1, source_target_pairs={{0,4},{4,0},{1,5},{5,1},{2,6},{6,2},{3,7},{7,3},{8,12},{12,8},{9,1... | collective-permute-start | bytes 6291464 | tf_op jit(solution)/shard_map/ppermute | solution.py:1571
  399.7 39.2 %copy-start.27 = (f32[512]{0:T(512)}, f32[512]{0:T(512)S(1)}, u32[]{:S(2)}) copy-start(f32[512]{0:T(512)S(1)} %get-tuple-element.155) | copy-start | bytes 6148
  438.9 10.5 copy-start.23
  438.9 6.8 collective-permute-start.4
  438.9 9.9 collective-permute-start.5
  439.4 10.0 collective-permute-start.6
  739.7 4.3 collective-permute-start.9
  739.7 105.6 %collective-permute-start.8 = (bf16[2,256,3072]{2,1,0:T(8,128)(2,1)}, bf16[2,256,3072]{2,1,0:T(8,128)(2,1)}, u32[]{:S(2)}, u32[]{:S(2)}) collective-permute-start(bf16[2,256,3072]{2,1,0:T(8,128)(2,1)} %get-tuple-element.69), channel_id=1, source_target_pairs={{0,16},{16,0},{8,24},{24,8},{1,17},{17,1},{9,25},{25,9},{2,18},{18... | collective-permute-start | bytes 9437192 | tf_op jit(solution)/shard_map/ppermute | solution.py:1621
  741.2 11.1 %copy-start.11 = (f32[1024,256]{1,0:T(8,128)S(1)}, f32[1024,256]{1,0:T(8,128)}, u32[]{:S(2)}) copy-start(f32[1024,256]{1,0:T(8,128)} %concatenate.40.sin_ref) | copy-start | bytes 3145732
  741.2 107.0 %collective-permute-start.7 = (bf16[2,256,3072]{2,1,0:T(8,128)(2,1)}, bf16[2,256,3072]{2,1,0:T(8,128)(2,1)S(1)}, u32[]{:S(2)}, u32[]{:S(2)}) collective-permute-start(bf16[2,256,3072]{2,1,0:T(8,128)(2,1)} %get-tuple-element.67), channel_id=1, source_target_pairs={{0,4},{4,0},{1,5},{5,1},{2,6},{6,2},{3,7},{7,3},{8,12},{12,8},{9,1... | collective-permute-start | bytes 9437192 | tf_op jit(solution)/shard_map/ppermute | solution.py:1620
  744.0 72.1 %slice-start.2 = ((s8[6291456]{0:T(1024)(128)(4,1)}), s8[4194304]{0:T(1024)(128)(4,1)S(1)}, s32[]{:S(2)}) async-start(s8[6291456]{0:T(1024)(128)(4,1)} %bitcast.81), calls=%async_computation.6 | async-start | bytes 8388608
  752.3 63.7 %slice-start.3 = ((s8[6291456]{0:T(1024)(128)(4,1)}), s8[2097152]{0:T(1024)(128)(4,1)S(1)}, s32[]{:S(2)}) async-start(s8[6291456]{0:T(1024)(128)(4,1)} %bitcast.81), calls=%async_computation.7 | async-start | bytes 4194304
  816.0 9.1 copy-start.35
  825.0 10.7 copy-start.9
  825.0 24.5 %collective-permute-start.10 = (bf16[512,2048]{1,0:T(8,128)(2,1)S(1)}, bf16[512,2048]{1,0:T(8,128)(2,1)S(1)}, u32[]{:S(2)}, u32[]{:S(2)}) collective-permute-start(bf16[512,2048]{1,0:T(8,128)(2,1)S(1)} %constant_dynamic-slice_fusion), channel_id=1, source_target_pairs={{0,8},{8,0},{16,24},{24,16},{1,9},{9,1},{17,25},{25,17},{2,10},{10... | collective-permute-start | bytes 6291464 | tf_op jit(solution)/shard_map/ppermute | solution.py:1537
  835.7 9.6 copy-start.22
  849.4 7.8 copy-start.20
  856.5 189.7 %collective-permute-start.12 = (bf16[256,3072]{1,0:T(8,128)(2,1)}, bf16[256,3072]{1,0:T(8,128)(2,1)}, u32[]{:S(2)}, u32[]{:S(2)}) collective-permute-start(bf16[256,3072]{1,0:T(8,128)(2,1)} %dynamic-slice_bitcast_fusion), channel_id=1, source_target_pairs={{0,4},{4,0},{1,5},{5,1},{2,6},{6,2},{3,7},{7,3},{8,12},{12,8},{9,1... | collective-permute-start | bytes 4718600 | tf_op jit(solution)/shard_map/ppermute | solution.py:1655
  858.4 187.8 %collective-permute-start.11 = (bf16[256,3072]{1,0:T(8,128)(2,1)}, bf16[256,3072]{1,0:T(8,128)(2,1)}, u32[]{:S(2)}, u32[]{:S(2)}) collective-permute-start(bf16[256,3072]{1,0:T(8,128)(2,1)} %dynamic-slice_bitcast_fusion.1), channel_id=1, source_target_pairs={{0,16},{16,0},{8,24},{24,8},{1,17},{17,1},{9,25},{25,9},{2,18},{18... | collective-permute-start | bytes 4718600 | tf_op jit(solution)/shard_map/ppermute | solution.py:1654
  1046.2 20.2 %collective-permute-start.13 = (bf16[4,512,512]{2,1,0:T(8,128)(2,1)}, bf16[4,512,512]{2,1,0:T(8,128)(2,1)S(1)}, u32[]{:S(2)}, u32[]{:S(2)}) collective-permute-start(bf16[4,512,512]{2,1,0:T(8,128)(2,1)} %reduce-scatter.2.cloned.1.call-done), channel_id=1, source_target_pairs={{0,0},{4,8},{8,4},{12,12},{16,16},{20,24},{24,20},{28,28},{1,1},{5... | collective-permute-start | bytes 6291464 | tf_op jit(solution)/shard_map/ppermute | solution.py:1663
  (25 other events, 81.9 us)
Sparse Core Ops, SparseCore 0:
  9.6 60.9 all-gather.2
  182.1 171.1 all-gather.4
  729.4 147.8 reduce-scatter.1

commit v8 on v6

--- a/solution.py
+++ b/solution.py
@@ -363,13 +363,31 @@
 
 
 def gather_kernel(
-    cols, q_ref, o_ref, after_ref, wq_ref, wo_ref, q_send, q_recv, q_over, o_send, o_recv, o_over, local_sems
+    cols,
+    q_ref,
+    o_ref,
+    rows_ref,
+    wq_ref,
+    wo_ref,
+    crossed_ref,
+    q_send,
+    q_recv,
+    q_over,
+    o_send,
+    o_recv,
+    o_over,
+    cross_sems,
+    local_sems,
 ):
     group, core, mate, row, col = place()
     last = cols - 1
     over = (group, 1 - row, col)
     greet(over)
 
+    @pl.when(core != row)
+    def _():
+        greet((mate, core, col))
+
     @pl.when(col < last)
     def _():
         greet((group, row, col + 1))
@@ -380,8 +398,10 @@
 
     pl.semaphore_wait(
         pltpu.get_barrier_semaphore(),
-        1 + jnp.minimum(col, 1) + jnp.minimum(last - col, 1),
-    )
+        1 + jnp.minimum(col, 1) + jnp.minimum(last - col, 1) + (core - row) * (core - row),
+    )
+    cross = remote(rows_ref, crossed_ref, cross_sems, 0, (mate, core, col))
+    stay = pltpu.make_async_copy(rows_ref, crossed_ref, local_sems.at[2])
 
     def moves(own, full, send, recv, over_sems):
         tall, wide = own.shape
@@ -422,6 +442,15 @@
         across(own, row, col).start()
         own_copies.append(pltpu.make_async_copy(own, block(row, col), local_sems.at[at]))
         own_copies[-1].start()
+
+    @pl.when(core != row)
+    def _():
+        cross.start()
+
+    @pl.when(core == row)
+    def _():
+        stay.start()
+
     for at in range(1, cols):
         chunk = line_order(col, last, at)
         for own, (block, along, across) in both:
@@ -438,6 +467,15 @@
             across(block(row, chunk), row, chunk).start()
     for copy in own_copies:
         copy.wait()
+
+    @pl.when(core != row)
+    def _():
+        cross.wait()
+
+    @pl.when(core == row)
+    def _():
+        stay.wait()
+
     for own, (block, along, across) in both:
         for chunk in range(cols):
 
@@ -453,7 +491,7 @@
             across(own, 1 - row, chunk).wait_recv()
 
 
-def gather_weights(own_q, own_o, after, rows, cols):
+def gather_weights(own_q, own_o, token_rows, rows, cols):
     anywhere = pl.BlockSpec(memory_space=pl.ANY)
 
     def whole(own):
@@ -461,20 +499,24 @@
 
     return pl.pallas_call(
         functools.partial(gather_kernel, cols),
-        out_shape=(whole(own_q), whole(own_o)),
+        out_shape=(
+            whole(own_q),
+            whole(own_o),
+            jax.ShapeDtypeStruct(token_rows.shape, token_rows.dtype),
+        ),
         in_specs=[anywhere] * 3,
-        out_specs=(anywhere,) * 2,
+        out_specs=(anywhere,) * 3,
         scratch_shapes=[
             pltpu.SemaphoreType.DMA((2, cols)),
             pltpu.SemaphoreType.DMA((cols,)),
             pltpu.SemaphoreType.DMA((2, cols)),
         ]
         * 2
-        + [pltpu.SemaphoreType.DMA((2,))],
+        + [pltpu.SemaphoreType.DMA((2, 1)), pltpu.SemaphoreType.DMA((3,))],
         compiler_params=pltpu.CompilerParams(collective_id=4, has_side_effects=True),
         cost_estimate=pl.CostEstimate(flops=0, bytes_accessed=300 << 20, transcendentals=0),
         name="gather_weights",
-    )(own_q, own_o, after)
+    )(own_q, own_o, token_rows)
 
 
 def half_turn(wide):
@@ -750,6 +792,7 @@
     relay_recv,
     pair_sems,
     lane_sems,
+    tile_sems,
     io_sems,
 ):
     group, core, mate, row, col = place()
@@ -759,7 +802,7 @@
     half = depth // 2
     units = wg_own.shape[1]
     rows = own_ref.shape[0]
-    tile = min(512, units)
+    tile = units // cols
     beside = col + 1 - 2 * lax.rem(col, 2)
     facing = last - col
     inner = (col > 0) & (col < last)
@@ -978,8 +1021,6 @@
         ]
     for load in loads:
         load.start()
-    for load in loads:
-        load.wait()
 
     def relay(box, slot):
         hand_over(slot, facing, box, 3).wait_recv()
@@ -1078,15 +1119,30 @@
         return pltpu.make_async_copy(
             grad_ref.at[chunk, :, aligned(block, rows)],
             mlp_buf.at[:, part_of(chunk)],
-            w_sems.at[chunk],
+            tile_sems.at[chunk],
         )
 
     parts = range(3)
+
+    def block_of(at):
+        return 2 * lax.rem(at, 2) + jnp.where(at >= 2, core, 1 - core)
+
+    for chunk in range(cols):
+        grad_tile(block_of(0), chunk).start()
+    for chunk in range(cols):
+        b_turn[0, :, part_of(chunk)] = b_all[chunk, :, aligned(block_of(0), rows)].T
+    for chunk in range(cols):
+        grad_tile(block_of(0), chunk).wait()
+    for chunk in range(cols):
+        g_two[0, :, part_of(chunk)] = mlp_buf[:, part_of(chunk)].T
+    for load in loads:
+        load.wait()
 
     def one_block(at, unused):
         high = lax.rem(at, 2)
         is_own = at >= 2
-        block = 2 * high + jnp.where(is_own, core, 1 - core)
+        side = lax.rem(at, 2)
+        following = block_of(jnp.minimum(at + 1, 3))
 
         @pl.when(inner & (at == 1))
         def _():
@@ -1095,14 +1151,10 @@
             relay(1, last - col)
             deliver(last - col, facing, 2, 2).start()
 
-        for chunk in range(cols):
-            grad_tile(block, chunk).start()
-        for chunk in range(cols):
-            b_turn[:, part_of(chunk)] = b_all[chunk, :, aligned(block, rows)].T
-        for chunk in range(cols):
-            grad_tile(block, chunk).wait()
-        for chunk in range(cols):
-            g_two[0, :, part_of(chunk)] = mlp_buf[:, part_of(chunk)].T
+        @pl.when(at < 3)
+        def _():
+            for chunk in range(cols):
+                grad_tile(following, chunk).start()
 
         @pl.when((at == 1) | (at == 2))
         def _():
@@ -1121,17 +1173,25 @@
             for part in parts:
                 landed(high, part).wait()
 
-        @pl.loop(0, units // tile)
+        @pl.when(at < 3)
+        def _():
+            for chunk in range(cols):
+                grad_tile(following, chunk).wait()
+
+        @pl.loop(0, cols)
         def _(step):
             lanes = aligned(step, tile)
+            tokens = aligned(step, rows)
 
             def put(buffer, value):
                 other = jnp.where(is_own, buffer[:, lanes].astype(jnp.float32), 0.0)
                 buffer[:, lanes] = (other + value).astype(jnp.bfloat16)
 
-            put(dg_buf, dot_nn(b_turn[...], wg[:, lanes]))
-            put(du_buf, dot_nn(b_turn[...], wu[:, lanes]))
-            put(u_buf, RES_MULT * dot_nn(g_two[0], wd[:, lanes]))
+            put(dg_buf, dot_nn(b_turn[side], wg[:, lanes]))
+            b_turn[1 - side, :, tokens] = b_all[step, :, aligned(following, rows)].T
+            put(du_buf, dot_nn(b_turn[side], wu[:, lanes]))
+            g_two[1 - side, :, tokens] = mlp_buf[:, tokens].T
+            put(u_buf, RES_MULT * dot_nn(g_two[side], wd[:, lanes]))
 
         @pl.when(jnp.logical_not(is_own))
         def _():
@@ -1185,7 +1245,7 @@
             pltpu.VMEM((width, units), bf16),
             pltpu.VMEM((width, units), bf16),
             pltpu.VMEM((cols, rows, width), bf16),
-            pltpu.VMEM((rows, width), bf16),
+            pltpu.VMEM((2, rows, width), bf16),
             pltpu.VMEM((2, rows, width), bf16),
             pltpu.VMEM((rows, units), bf16),
             pltpu.VMEM((rows, units), bf16),
@@ -1200,6 +1260,7 @@
             pltpu.SemaphoreType.DMA((2,)),
             pltpu.SemaphoreType.DMA((2, 2, 3)),
             pltpu.SemaphoreType.DMA((8,)),
+            pltpu.SemaphoreType.DMA((cols,)),
             pltpu.SemaphoreType.DMA((9,)),
         ],
         compiler_params=pltpu.CompilerParams(
@@ -1220,9 +1281,7 @@
     gq_ref,
     go_ref,
     gain_ref,
-    out_ref,
     gin_ref,
-    crossed_ref,
     sq_ref,
     so_ref,
     gsum_ref,
@@ -1248,7 +1307,6 @@
     o_sems,
     qz_sems,
     oz_sems,
-    cross_sems,
     local_sems,
 ):
     group, core, mate, row, col = place()
@@ -1335,8 +1393,6 @@
         ig_ref.at[:, lanes(col, width)], gin_ref.at[col], local_sems.at[2]
     )
 
-    cross = remote(out_ref, crossed_ref, cross_sems, 0, (mate, core, col))
-    stay = pltpu.make_async_copy(out_ref, crossed_ref, local_sems.at[4])
     for m in range(2):
         copies[m]["s0"].start()
         copies[m]["a1"].start()
@@ -1344,7 +1400,6 @@
     @pl.when(core == row)
     def _():
         own_tokens.start()
-        stay.start()
         for step in range(1, cols):
             token_copy(step, col).start()
 
@@ -1386,7 +1441,6 @@
     def _():
         for step in range(cols):
             token_copy(step, col).start()
-        cross.start()
 
     gain_round(2)
     for m in range(2):
@@ -1449,15 +1503,13 @@
     def _():
         token_copy(0, col).wait_recv()
         token_copy(0, col).wait_send()
-        cross.wait()
 
     @pl.when(core == row)
     def _():
         own_tokens.wait()
-        stay.wait()
-
-
-def finish(input_grad, grad_q, grad_o, gains, output, cols):
+
+
+def finish(input_grad, grad_q, grad_o, gains, cols):
     anywhere = pl.BlockSpec(memory_space=pl.ANY)
     in_vmem = pl.BlockSpec(memory_space=pltpu.VMEM)
     bf16, f32 = jnp.bfloat16, jnp.float32
@@ -1480,13 +1532,12 @@
         functools.partial(finish_kernel, cols),
         out_shape=(
             jax.ShapeDtypeStruct((cols, length, full // cols), bf16),
-            jax.ShapeDtypeStruct(output.shape, bf16),
             jax.ShapeDtypeStruct((2, rows, wide_q // cols), f32),
             jax.ShapeDtypeStruct((2, rows, wide_o // cols), f32),
             jax.ShapeDtypeStruct(gains.shape, f32),
         ),
-        in_specs=[anywhere] * 5,
-        out_specs=(anywhere, anywhere, in_vmem, in_vmem, in_vmem),
+        in_specs=[anywhere] * 4,
+        out_specs=(anywhere, in_vmem, in_vmem, in_vmem),
         scratch_shapes=buffers(wide_q)
         + buffers(wide_o)
         + [
@@ -1498,8 +1549,7 @@
             pltpu.SemaphoreType.DMA((2, 5)),
             pltpu.SemaphoreType.DMA((2, 2, cols)),
             pltpu.SemaphoreType.DMA((2, 2, cols)),
-            pltpu.SemaphoreType.DMA((2, 1)),
-            pltpu.SemaphoreType.DMA((5,)),
+            pltpu.SemaphoreType.DMA((4,)),
         ],
         compiler_params=pltpu.CompilerParams(
             collective_id=3, has_side_effects=True, vmem_limit_bytes=40 << 20
@@ -1511,7 +1561,6 @@
         grad_q.reshape(2, 2, 2, rows, wide_q),
         grad_o.reshape(2, 2, 2, rows, wide_o),
         gains,
-        output,
     )
 
 
@@ -1574,9 +1623,9 @@
     everyone, attn_input = lax.optimization_barrier((everyone, attn_input))
     picked = pick_sequences(everyone, deal_order, group * seq_group, seq_group)
     picked = jnp.where(given_live, picked, jnp.zeros_like(picked))
-    given = lax.ppermute(picked, ("dp", "row"), CROSSED)
-    weights_qkv, weights_out = gather_weights(pack_q, pack_o, picked, row_count, col_count)
-    given, weights_qkv = lax.optimization_barrier((given, weights_qkv))
+    weights_qkv, weights_out, given = gather_weights(
+        pack_q, pack_o, picked, row_count, col_count
+    )
     line_cot = lax.all_gather(given, "col", axis=2, tiled=True)
     own_grad = lax.dynamic_index_in_dim(line_cot, col, keepdims=False).astype(jnp.float32)
 
@@ -1646,6 +1695,16 @@
     grad_projected = attend_back_fast(
         length, projected, grad_heads, cosines, sines, col_count
     )
+    a_sum, b_sum, grad_projected = lax.optimization_barrier(
+        (plus(a_keep, a_came), plus(b_keep, b_came), grad_projected)
+    )
+    high = group // 2
+
+    def one_of(pair, at):
+        return lax.dynamic_index_in_dim(pair, at, keepdims=False)
+
+    a_last = lax.ppermute(one_of(a_sum, 1 - high), "dp", OVER_Y)
+    b_last = lax.ppermute(one_of(b_sum, 1 - row), "row", OVER_X)
     grad_normed_one = summed_rows(expand_local(grad_projected, weights_qkv).astype(jnp.bfloat16))
     grad_qkv = token_outer(attn_input, grad_projected).astype(jnp.bfloat16)
     weighted_one = grad_normed_one * gain_one
@@ -1656,20 +1715,15 @@
         - own_float * scale_one**3 * inner_one / full_width
     ).astype(jnp.bfloat16)
     gain_one_part = jnp.sum(grad_normed_one * own_float * scale_one, axis=0)
-    a_sum, b_sum, own_input_grad = lax.optimization_barrier(
-        (plus(a_keep, a_came), plus(b_keep, b_came), own_input_grad)
-    )
-    high = group // 2
-
-    def one_of(pair, at):
-        return lax.dynamic_index_in_dim(pair, at, keepdims=False)
-
-    a_last = lax.ppermute(one_of(a_sum, 1 - high), "dp", OVER_Y)
-    b_last = lax.ppermute(one_of(b_sum, 1 - row), "row", OVER_X)
+    a_last, b_last, own_input_grad = lax.optimization_barrier((a_last, b_last, own_input_grad))
     gains = jnp.stack([gain_one_part, gain_two_part]).reshape(8, -1)
-    given_grad, given_out, sums_q, sums_o, gain_sums = finish(
-        own_input_grad, grad_qkv, grad_out, gains, out_cols, col_count
-    )
+    given_grad, sums_q, sums_o, gain_sums = finish(
+        own_input_grad, grad_qkv, grad_out, gains, col_count
+    )
+    out_cols, a_last, b_last, a_sum, b_sum, given_grad = lax.optimization_barrier(
+        (out_cols, a_last, b_last, a_sum, b_sum, given_grad)
+    )
+    given_out = lax.ppermute(out_cols, ("dp", "row"), CROSSED)
     layer_out = jnp.where(given_live, given_out.astype(jnp.float32), 0.0)
     input_grad = given_grad.astype(jnp.float32)
     a_total = one_of(a_sum, high).astype(jnp.float32) + a_last.astype(jnp.float32)

time: 1040 us -> 1040 us (level)
  Pallas kernels: 718 us -> 742 us
  starting transfers between devices: 26.2 us -> 11.4 us
  waiting for transfers between devices: 109 us -> 97.8 us
    pallas_call x1, Pallas kernels: 118 us -> 150 us  [gather_weights(): pl.pallas_call(functools.partial(gather_kernel, cols), out_shape=(whole(o...]
    ppermute x1, waiting for transfers between devices: 23.2 us -> 2.08 us  [one_sequence_body(): a_last = lax.ppermute(one_of(a_sum, 1 - high), 'dp', OVER_Y)]
    ppermute x1, waiting for transfers between devices: 0.13 us -> 17.8 us  [one_sequence_body(): b_last = lax.ppermute(one_of(b_sum, 1 - row), 'row', OVER_X)]
    ppermute x1, starting transfers between devices: 17.1 us -> 2.98 us  [one_sequence_body(): given_out = lax.ppermute(out_cols, ('dp', 'row'), CROSSED)]
    unnamed x87 -> x89, local copies, waits for them, and re-layouts: 23.1 us -> 18.4 us
  transfers between devices with their start and end apart: 16 -> 16, of which waited for: 8 -> 7; matrix products, arithmetic and copies ran while one was open for 11% -> 13% of each run, Pallas kernels for 26% -> 30%
where the time goes in v8:
time: 1040 us; the launch traced here: 1020 us
  Pallas kernels  742 us (71%)
  waiting for transfers between devices  97.8 us (9%)
  local copies, waits for them, and re-layouts  60.1 us (6%)
  other arithmetic  45.8 us (4%)
  matrix products  42.1 us (4%)
  between operations  22.4 us (2%)
  starting transfers between devices  11.4 us (1%)
    pallas_call x1, Pallas kernels, feed_forward(): pl.pallas_call(functools.partial(ffn_kernel, cols), out_shape=(jax.ShapeD...  281 us
    pallas_call x1, Pallas kernels, finish(): pl.pallas_call(functools.partial(finish_kernel, cols), out_shape=(jax.Sha...  159 us
    pallas_call x1, Pallas kernels, gather_weights(): pl.pallas_call(functools.partial(gather_kernel, cols), out_shape=(whole(o...  150 us
    ppermute x1, waiting for transfers between devices, one_sequence_body(): far_down = lax.ppermute(half_rows(w_down), 'row', OVER_X)  65.7 us
    pallas_call x1, Pallas kernels, attend_back_fast(): pl.pallas_call(functools.partial(attend_back_kernel, block), grid=(groups...  63.2 us
    pallas_call x1, Pallas kernels, start_exchange(): pl.pallas_call(functools.partial(start_kernel, cols), out_shape=(jax.Shap...  46 us
    pallas_call x1, Pallas kernels, attend_fast(): pl.pallas_call(functools.partial(attend_kernel, block), grid=(groups,), o...  43 us
  transfers between devices with their start and end apart: 16, of which 7 were waited for; matrix products, arithmetic and copies ran while one was open for 13% of the time, Pallas kernels for 30%

profile of v8, /device:TPU:0, one launch (start us, length us, event | category | flops | bytes accessed | tf_op | source)
XLA Modules:
  0.0 1021.7 jit_solution(10413465522439993817)
XLA Ops:
  15.9 2.1 fusion.14
  24.0 46.0 %start_exchange.1 = (bf16[512,2048]{1,0:T(8,128)(2,1)S(1)}, bf16[1024,2048]{1,0:T(8,128)(2,1)S(1)}) custom-call(bf16[4,512,512]{2,1,0:T(8,128)(2,1)S(1)} %copy-done.3, f32[1,2048]{1,0:T(1,128)S(1)} %bitcast.80), custom_call_target="tpu_custom_call" | custom-call | bytes 209715200 | tf_op jit(solution)/shard_map/start_exchange/pallas_call | solution.py:342
  72.1 2.8 constant_dynamic-slice_fusion.8
  79.3 149.8 %gather_weights.1 = (bf16[2048,1536]{1,0:T(8,128)(2,1)}, bf16[2048,1024]{1,0:T(8,128)(2,1)}, bf16[4,512,512]{2,1,0:T(8,128)(2,1)}) custom-call(bf16[1024,384]{1,0:T(8,128)(2,1)} %pad_maximum_fusion.2.q_ref, bf16[1024,256]{1,0:T(8,128)(2,1)} %get-tuple-element.170.o_ref, bf16[4,512,512]{2,1,0:T(8,128)(2,1)} %maximum_select_fusion.1.rows_ref), custom_call_target="tpu_custom_call" | custom-call | bytes 314572800 | tf_op jit(solution)/shard_map/gather_weights/pallas_call | solution.py:500
  234.4 2.4 concatenate.38.cos_ref
  236.9 11.4 %copy.51 = bf16[1024,2,2048]{2,0,1:T(8,128)(2,1)} copy(bf16[1024,2,2048]{2,1,0:T(2,128)(2,1)} %param.20) | data formatting | bytes 16777216 | tf_op jit(solution)/shard_map/optimization_barrier | solution.py:1632
  248.3 2.8 constant_dynamic-slice_fusion.3
  251.2 43.0 %attend.1 = (bf16[1024,1536]{1,0:T(8,128)(2,1)}, bf16[1024,1024]{1,0:T(8,128)(2,1)S(1)}) custom-call(s32[1]{0:T(128)} %dynamic_slice.99.len_ref, bf16[1024,2048]{1,0:T(8,128)(2,1)} %copy-done.8, bf16[2048,1536]{1,0:T(8,128)(2,1)} %get-tuple-element.58.w_ref, f32[1024,256]{1,0:T(8,128)S(1)} %copy-done.4, f32[1024,256]{1,0:T(8,128)S(1)} %concatenate.40.sin_ref), custom_call_target="tpu_custom_call" | custom-call | flops 10737418240 | bytes 13631488 | tf_op jit(solution)/shard_map/attend/pallas_call | solution.py:615
  294.3 9.1 convolution_convert_fusion.3
  308.5 3.9 slice_bitcast_fusion
  313.7 5.1 fusion.13
  321.7 65.7 %collective-permute-done.1.wd_far = bf16[512,2048]{1,0:T(8,128)(2,1)} collective-permute-done((bf16[512,2048]{1,0:T(8,128)(2,1)S(1)}, bf16[512,2048]{1,0:T(8,128)(2,1)}, u32[]{:S(2)}, u32[]{:S(2)}) %collective-permute-start.1) | collective-permute-done | bytes 2097184 | tf_op jit(solution)/shard_map/ppermute | solution.py:1634
  389.7 6.3 collective-permute-done.3.wg_sib
  396.0 3.1 collective-permute-done.4.wu_sib
  399.7 281.2 %feed_forward.1 = (bf16[4,512,2048]{2,1,0:T(8,128)(2,1)}, bf16[4,512,4096]{2,1,0:T(8,128)(2,1)}, bf16[4,512,2048]{2,1,0:T(8,128)(2,1)}, bf16[3,512,2048]{2,1,0:T...) custom-call(bf16[512,2048]{1,0:T(8,128)(2,1)} %multiply_convert_fusi, ...), custom_call_target="tpu_custom_call" | custom-call | flops 154618822656 | bytes 838860800 | tf_op jit(solution)/shard_map/feed_forward/pallas_call | solution.py:1230
  681.0 4.8 convert_reduce_fusion
  686.9 4.4 multiply_convert_fusion
  695.6 7.9 convolution_convert_fusion.4.dz_ref
  703.6 63.2 %attend_back.1 = bf16[1024,1536]{1,0:T(8,128)(2,1)} custom-call(s32[1]{0:T(128)} %dynamic_slice.99.len_ref, bf16[1024,1536]{1,0:T(8,128)(2,1)} %get-tuple-element.75.qkv_ref, bf16[1024,1024]{1,0:T(8,128)(2,1)S(1)} %convolution_convert_fusion.4.dz_ref, f32[1024,256]{1,0:T(8,128)S(1)} %copy-done.5, f32[1024,256]{1,0:T(8,128)S(1)} %concatenate.40.sin_ref), custom_call_target="tpu_custom_call" | custom-call | flops 10737418240 | bytes 8388608 | tf_op jit(solution)/shard_map/attend_back/pallas_call | solution.py:722
  766.8 9.1 convolution_convert_fusion.2
  781.7 6.9 convolution_convert_fusion.1
  794.2 9.1 convolution_convert_fusion
  805.0 4.6 fusion.4.ig_ref
  809.6 17.8 %collective-permute-done.10 = bf16[256,3072]{1,0:T(8,128)(2,1)} collective-permute-done((bf16[256,3072]{1,0:T(8,128)(2,1)}, bf16[256,3072]{1,0:T(8,128)(2,1)}, u32[]{:S(2)}, u32[]{:S(2)}) %collective-permute-start.10) | collective-permute-done | bytes 1572896 | tf_op jit(solution)/shard_map/ppermute | solution.py:1707
  827.4 2.1 collective-permute-done.9
  829.5 158.7 %finish.1 = (bf16[4,512,512]{2,1,0:T(8,128)(2,1)S(1)}, f32[2,256,384]{2,1,0:T(8,128)S(1)}, f32[2,256,256]{2,1,0:T(8,128)S(1)}, f32[8,512]{1,0:T(8,128)S(1)}) custom-call(bf16[512,2048]{1,0:T(8,128)(2,1)S(1)} %fusion.4.ig_ref, bf16[2,2,2,256,1536]{4,3,2,1,0:T(8,128)(2,1)} %bitcast.83, bf16[2,2,2,256,1024]{4,3,2,1,0:T(8,128)(2,1)S(1)} %bitcast.79, ...), custom_call_target="tpu_custom_call" | custom-call | bytes 314572800 | tf_op jit(solution)/shard_map/finish/pallas_call | solution.py:1531
  992.5 3.0 collective-permute-start.12
  995.5 2.4 convert_add_fusion.4
  997.9 3.1 convert_add_fusion.3
  1003.4 5.3 copy.57
  1008.6 2.6 convert_element_type.135
  1012.7 2.3 convert_select_fusion
  (175 shorter events, 57.3 us)
Async XLA Ops:
  7.2 68.8 %all-gather.3.cloned.1.call-start = ((), (), s32[]{:S(2)}) async-start(), calls=%async_computation.1 | async-start | bytes 10485760 | tf_op jit(solution)/shard_map/all_gather | solution.py:1622
  7.9 391.8 %all-gather.5.cloned.1.call-start = ((), (), s32[]{:S(2)}) async-start(), calls=%async_computation.2 | async-start | bytes 10485760 | tf_op jit(solution)/shard_map/all_gather | solution.py:1629
  15.2 59.7 %copy-start.6 = (f32[2048]{0:T(1024)}, f32[2048]{0:T(1024)S(1)}, u32[]{:S(2)}) copy-start(f32[2048]{0:T(1024)S(1)} %convert_element_type.108) | copy-start | bytes 24580
  72.1 241.6 %copy-start = (bf16[512,2048]{1,0:T(8,128)(2,1)}, bf16[512,2048]{1,0:T(8,128)(2,1)S(1)}, u32[]{:S(2)}) copy-start(bf16[512,2048]{1,0:T(8,128)(2,1)S(1)} %get-tuple-element.56) | copy-start | bytes 6291460
  77.7 151.4 %copy-start.36 = (s32[16]{0:T(128)S(1)}, s32[16]{0:T(128)}, u32[]{:S(2)}) copy-start(s32[16]{0:T(128)} %param.13) | copy-start | bytes 196
  229.1 763.4 %reduce-scatter.2.cloned.1.call-start = ((), (), s32[]{:S(2)}) async-start(), calls=%async_computation.3 | async-start | bytes 10485760 | tf_op jit(solution)/shard_map/reduce_scatter | solution.py:1677
  251.1 136.3 %collective-permute-start = (bf16[512,2,2048]{2,0,1:T(8,128)(2,1)S(1)}, bf16[512,2,2048]{2,0,1:T(8,128)(2,1)S(1)}, u32[]{:S(2)}, u32[]{:S(2)}) collective-permute-start(bf16[512,2,2048]{2,0,1:T(8,128)(2,1)S(1)} %constant_dynamic-slice_fusion.3), channel_id=1, source_target_pairs={{0,4},{4,0},{1,5},{5,1},{2,6},{6,2},{3,7},{7,3},{8,12},{12,8},{9,1... | collective-permute-start | bytes 12582920 | tf_op jit(solution)/shard_map/ppermute | solution.py:1633
  294.3 14.2 %slice-start = ((s8[8388608]{0:T(1024)(128)(4,1)}), s8[4194304]{0:T(1024)(128)(4,1)S(1)}, s32[]{:S(2)}) async-start(s8[8388608]{0:T(1024)(128)(4,1)} %bitcast.81), calls=%async_computation.4 | async-start | bytes 8388608
  294.3 11.3 %copy-start.35 = (bf16[2048]{0:T(1024)(128)(2,1)S(1)}, bf16[2048]{0:T(1024)(128)(2,1)}, u32[]{:S(2)}) copy-start(bf16[2048]{0:T(1024)(128)(2,1)} %param.16) | copy-start | bytes 12292
  294.3 14.2 %slice-start.1 = ((s8[8388608]{0:T(1024)(128)(4,1)}), s8[4194304]{0:T(1024)(128)(4,1)S(1)}, s32[]{:S(2)}) async-start(s8[8388608]{0:T(1024)(128)(4,1)} %bitcast.81), calls=%async_computation.5 | async-start | bytes 8388608
  305.4 7.0 collective-permute-start.2
  306.3 13.8 %copy-start.27 = (f32[2048]{0:T(1024)}, f32[2048]{0:T(1024)S(1)}, u32[]{:S(2)}) copy-start(f32[2048]{0:T(1024)S(1)} %convert_element_type.114) | copy-start | bytes 24580
  306.4 81.0 %collective-permute-start.1 = (bf16[512,2048]{1,0:T(8,128)(2,1)S(1)}, bf16[512,2048]{1,0:T(8,128)(2,1)}, u32[]{:S(2)}, u32[]{:S(2)}) collective-permute-start(bf16[512,2048]{1,0:T(8,128)(2,1)S(1)} %constant_dynamic-slice_fusion.2), channel_id=1, source_target_pairs={{0,4},{4,0},{1,5},{5,1},{2,6},{6,2},{3,7},{7,3},{8,12},{12,8},{9,1... | collective-permute-start | bytes 6291464 | tf_op jit(solution)/shard_map/ppermute | solution.py:1634
  320.0 69.2 %copy-start.29 = (f32[512]{0:T(512)}, f32[512]{0:T(512)S(1)}, u32[]{:S(2)}) copy-start(f32[512]{0:T(512)S(1)} %get-tuple-element.163) | copy-start | bytes 6148
  389.2 10.5 %copy-start.24 = (bf16[512,2048]{1,0:T(8,128)(2,1)}, bf16[512,2048]{1,0:T(8,128)(2,1)S(1)}, u32[]{:S(2)}) copy-start(bf16[512,2048]{1,0:T(8,128)(2,1)S(1)} %get-tuple-element.143.wu_far) | copy-start | bytes 6291460
  389.2 6.9 collective-permute-start.3
  389.2 9.9 collective-permute-start.4
  389.7 10.0 collective-permute-start.5
  691.3 4.3 collective-permute-start.8
  691.3 84.6 %collective-permute-start.7 = (bf16[2,256,3072]{2,1,0:T(8,128)(2,1)}, bf16[2,256,3072]{2,1,0:T(8,128)(2,1)S(1)}, u32[]{:S(2)}, u32[]{:S(2)}) collective-permute-start(bf16[2,256,3072]{2,1,0:T(8,128)(2,1)} %get-tuple-element.74), channel_id=1, source_target_pairs={{0,16},{16,0},{8,24},{24,8},{1,17},{17,1},{9,25},{25,9},{2,18},{18... | collective-permute-start | bytes 9437192 | tf_op jit(solution)/shard_map/ppermute | solution.py:1683
  692.9 10.7 %copy-start.5 = (f32[1024,256]{1,0:T(8,128)S(1)}, f32[1024,256]{1,0:T(8,128)}, u32[]{:S(2)}) copy-start(f32[1024,256]{1,0:T(8,128)} %concatenate.38.cos_ref) | copy-start | bytes 3145732
  692.9 84.2 %collective-permute-start.6 = (bf16[2,256,3072]{2,1,0:T(8,128)(2,1)}, bf16[2,256,3072]{2,1,0:T(8,128)(2,1)S(1)}, u32[]{:S(2)}, u32[]{:S(2)}) collective-permute-start(bf16[2,256,3072]{2,1,0:T(8,128)(2,1)} %get-tuple-element.72), channel_id=1, source_target_pairs={{0,4},{4,0},{1,5},{5,1},{2,6},{6,2},{3,7},{7,3},{8,12},{12,8},{9,1... | collective-permute-start | bytes 9437192 | tf_op jit(solution)/shard_map/ppermute | solution.py:1682
  703.6 63.2 %copy-start.11 = (bf16[1024,1024]{1,0:T(8,128)(2,1)S(1)}, bf16[1024,1024]{1,0:T(8,128)(2,1)}, u32[]{:S(2)}) copy-start(bf16[1024,1024]{1,0:T(8,128)(2,1)} %copy-done.10) | copy-start | bytes 6291460
  777.1 12.0 %copy-start.16 = (bf16[2,256,3072]{2,1,0:T(8,128)(2,1)}, bf16[2,256,3072]{2,1,0:T(8,128)(2,1)S(1)}, u32[]{:S(2)}) copy-start(bf16[2,256,3072]{2,1,0:T(8,128)(2,1)S(1)} %add_convert_fusion) | copy-start | bytes 9437188
  788.6 14.6 %copy-start.19 = (bf16[1024,2048]{1,0:T(8,128)(2,1)}, bf16[1024,2048]{1,0:T(8,128)(2,1)S(1)}, u32[]{:S(2)}) copy-start(bf16[1024,2048]{1,0:T(8,128)(2,1)S(1)} %convolution_convert_fusion.1) | copy-start | bytes 12582916
  788.9 14.4 %collective-permute-start.11 = (bf16[512,2048]{1,0:T(8,128)(2,1)S(1)}, bf16[512,2048]{1,0:T(8,128)(2,1)S(1)}, u32[]{:S(2)}, u32[]{:S(2)}) collective-permute-start(bf16[512,2048]{1,0:T(8,128)(2,1)S(1)} %constant_dynamic-slice_fusion), channel_id=1, source_target_pairs={{0,8},{8,0},{16,24},{24,16},{1,9},{9,1},{17,25},{25,17},{2,10},{10... | collective-permute-start | bytes 6291464 | tf_op jit(solution)/shard_map/ppermute | solution.py:1600
  790.4 37.0 %collective-permute-start.10 = (bf16[256,3072]{1,0:T(8,128)(2,1)}, bf16[256,3072]{1,0:T(8,128)(2,1)}, u32[]{:S(2)}, u32[]{:S(2)}) collective-permute-start(bf16[256,3072]{1,0:T(8,128)(2,1)} %dynamic-slice_bitcast_fusion), channel_id=1, source_target_pairs={{0,4},{4,0},{1,5},{5,1},{2,6},{6,2},{3,7},{7,3},{8,12},{12,8},{9,1... | collective-permute-start | bytes 4718600 | tf_op jit(solution)/shard_map/ppermute | solution.py:1707
  792.7 10.6 %copy-start.1 = (bf16[512,2048]{1,0:T(8,128)(2,1)S(1)}, bf16[512,2048]{1,0:T(8,128)(2,1)}, u32[]{:S(2)}) copy-start(bf16[512,2048]{1,0:T(8,128)(2,1)} %copy-done) | copy-start | bytes 6291460
  792.7 10.6 %copy-start.7 = (f32[2048]{0:T(1024)S(1)}, f32[2048]{0:T(1024)}, u32[]{:S(2)}) copy-start(f32[2048]{0:T(1024)} %copy-done.6) | copy-start | bytes 24580
  792.7 36.8 %collective-permute-start.9 = (bf16[256,3072]{1,0:T(8,128)(2,1)}, bf16[256,3072]{1,0:T(8,128)(2,1)}, u32[]{:S(2)}, u32[]{:S(2)}) collective-permute-start(bf16[256,3072]{1,0:T(8,128)(2,1)} %dynamic-slice_bitcast_fusion.1), channel_id=1, source_target_pairs={{0,16},{16,0},{8,24},{24,8},{1,17},{17,1},{9,25},{25,9},{2,18},{18... | collective-permute-start | bytes 4718600 | tf_op jit(solution)/shard_map/ppermute | solution.py:1706
  805.0 24.4 %copy-start.2 = (bf16[2048,1024]{1,0:T(8,128)(2,1)S(1)}, bf16[2048,1024]{1,0:T(8,128)(2,1)}, u32[]{:S(2)}) copy-start(bf16[2048,1024]{1,0:T(8,128)(2,1)} %convolution_convert_fusion.2) | copy-start | bytes 12582916
  992.5 20.2 %collective-permute-start.12 = (bf16[4,512,512]{2,1,0:T(8,128)(2,1)}, bf16[4,512,512]{2,1,0:T(8,128)(2,1)S(1)}, u32[]{:S(2)}, u32[]{:S(2)}) collective-permute-start(bf16[4,512,512]{2,1,0:T(8,128)(2,1)} %reduce-scatter.2.cloned.1.call-done), channel_id=1, source_target_pairs={{0,0},{4,8},{8,4},{12,12},{16,16},{20,24},{24,20},{28,28},{1,1},{5... | collective-permute-start | bytes 6291464 | tf_op jit(solution)/shard_map/ppermute | solution.py:1726
  (28 other events, 113.8 us)
Sparse Core Ops, SparseCore 0:
  9.6 60.9 all-gather.2
  229.2 149.2 all-gather.4
  681.1 143.0 reduce-scatter.1

commit v9 on v8

--- a/solution.py
+++ b/solution.py
@@ -373,16 +373,21 @@
     q_send,
     q_recv,
     q_over,
+    q_shared,
     o_send,
     o_recv,
     o_over,
+    o_shared,
     cross_sems,
     local_sems,
 ):
     group, core, mate, row, col = place()
     last = cols - 1
     over = (group, 1 - row, col)
+    high = (group - core) // 2
+    other_plane = (2 * (1 - high) + core, row, col)
     greet(over)
+    greet(other_plane)
 
     @pl.when(core != row)
     def _():
@@ -398,12 +403,12 @@
 
     pl.semaphore_wait(
         pltpu.get_barrier_semaphore(),
-        1 + jnp.minimum(col, 1) + jnp.minimum(last - col, 1) + (core - row) * (core - row),
+        2 + jnp.minimum(col, 1) + jnp.minimum(last - col, 1) + (core - row) * (core - row),
     )
     cross = remote(rows_ref, crossed_ref, cross_sems, 0, (mate, core, col))
     stay = pltpu.make_async_copy(rows_ref, crossed_ref, local_sems.at[2])
 
-    def moves(own, full, send, recv, over_sems):
+    def moves(own, full, send, recv, over_sems, shared_sems):
         tall, wide = own.shape
 
         def block(of_row, of_col):
@@ -422,14 +427,18 @@
         def across(src, of_row, chunk):
             return remote(src, block(of_row, chunk), over_sems, chunk, over)
 
-        return block, along, across
+        def share(chunk):
+            place_there = block(1 - row, chunk)
+            return remote(place_there, place_there, shared_sems, chunk, other_plane)
+
+        return block, along, across, share
 
     both = (
-        (q_ref, moves(q_ref, wq_ref, q_send, q_recv, q_over)),
-        (o_ref, moves(o_ref, wo_ref, o_send, o_recv, o_over)),
+        (q_ref, moves(q_ref, wq_ref, q_send, q_recv, q_over, q_shared)),
+        (o_ref, moves(o_ref, wo_ref, o_send, o_recv, o_over, o_shared)),
     )
     own_copies = []
-    for at, (own, (block, along, across)) in enumerate(both):
+    for at, (own, (block, along, across, share)) in enumerate(both):
 
         @pl.when(col < last)
         def _():
@@ -439,7 +448,10 @@
         def _():
             along(own, col, col - 1, 1).start()
 
-        across(own, row, col).start()
+        @pl.when(lax.rem(col, 2) == high)
+        def _():
+            across(own, row, col).start()
+
         own_copies.append(pltpu.make_async_copy(own, block(row, col), local_sems.at[at]))
         own_copies[-1].start()
 
@@ -453,7 +465,7 @@
 
     for at in range(1, cols):
         chunk = line_order(col, last, at)
-        for own, (block, along, across) in both:
+        for own, (block, along, across, share) in both:
             along(own, chunk, col, 0).wait_recv()
 
             @pl.when((chunk < col) & (col < last))
@@ -464,7 +476,15 @@
             def _():
                 along(block(row, chunk), chunk, col - 1, 1).start()
 
-            across(block(row, chunk), row, chunk).start()
+            @pl.when(lax.rem(chunk, 2) == high)
+            def _():
+                across(block(row, chunk), row, chunk).start()
+
+    for at in range(cols // 2):
+        for own, (block, along, across, share) in both:
+            chunk = 2 * at + high
+            across(own, 1 - row, chunk).wait_recv()
+            share(chunk).start()
     for copy in own_copies:
         copy.wait()
 
@@ -476,7 +496,7 @@
     def _():
         stay.wait()
 
-    for own, (block, along, across) in both:
+    for own, (block, along, across, share) in both:
         for chunk in range(cols):
 
             @pl.when((col >= chunk) & (col < last))
@@ -487,8 +507,10 @@
             def _():
                 along(own, chunk, col - 1, 1).wait_send()
 
-            across(own, row, chunk).wait_send()
-            across(own, 1 - row, chunk).wait_recv()
+        for at in range(cols // 2):
+            across(own, row, 2 * at + high).wait_send()
+            share(2 * at + high).wait_send()
+            share(2 * at + 1 - high).wait_recv()
 
 
 def gather_weights(own_q, own_o, token_rows, rows, cols):
@@ -509,6 +531,7 @@
         scratch_shapes=[
             pltpu.SemaphoreType.DMA((2, cols)),
             pltpu.SemaphoreType.DMA((cols,)),
+            pltpu.SemaphoreType.DMA((2, cols)),
             pltpu.SemaphoreType.DMA((2, cols)),
         ]
         * 2
@@ -760,9 +783,15 @@
     wg_far,
     wu_far,
     wd_far,
+    wg_far_y,
+    wu_far_y,
+    wd_far_y,
     wg_sib,
     wu_sib,
     wd_sib,
+    wg_sib_y,
+    wu_sib_y,
+    wd_sib_y,
     u_all,
     dgu_all,
     mlp_all,
@@ -837,26 +866,38 @@
         side = lax.rem(at, 2)
         return pltpu.make_async_copy(grad_ref.at[order(at)], g_two.at[side], io_sems.at[6 + side])
 
+    quarter = half // 2
+    high = (group - core) // 2
+
     def rows_at(first, size):
-        return pl.ds(pl.multiple_of(first, half), size)
+        return pl.ds(pl.multiple_of(first, quarter), size)
 
     own_copy = pltpu.make_async_copy(own_ref, b_all.at[col], io_sems.at[0])
     own_copy.start()
     load_resid = pltpu.make_async_copy(resid_ref, mlp_buf, io_sems.at[8])
     far = (1 - row) * depth
     loads = []
-    for at, (full, mine, across, shared) in enumerate(
-        ((wg, wg_own, wg_far, wg_sib), (wu, wu_own, wu_far, wu_sib), (wd, wd_own, wd_far, wd_sib))
+    for full, mine, pieces in (
+        (wg, wg_own, (wg_far, wg_far_y, wg_sib, wg_sib_y)),
+        (wu, wu_own, (wu_far, wu_far_y, wu_sib, wu_sib_y)),
+        (wd, wd_own, (wd_far, wd_far_y, wd_sib, wd_sib_y)),
     ):
-        loads += [
-            pltpu.make_async_copy(mine, full.at[rows_at(row * depth, depth)], w_sems.at[3 * at]),
+        places = [
+            far + of_core * half + of_plane * quarter
+            for of_core in (core, 1 - core)
+            for of_plane in (high, 1 - high)
+        ]
+        loads.append(
             pltpu.make_async_copy(
-                across, full.at[rows_at(far + core * half, half)], w_sems.at[3 * at + 1]
-            ),
-            pltpu.make_async_copy(
-                shared, full.at[rows_at(far + (1 - core) * half, half)], w_sems.at[3 * at + 2]
-            ),
-        ]
+                mine, full.at[rows_at(row * depth, depth)], w_sems.at[len(loads)]
+            )
+        )
+        for piece, first in zip(pieces, places):
+            loads.append(
+                pltpu.make_async_copy(
+                    piece, full.at[rows_at(first, quarter)], w_sems.at[len(loads)]
+                )
+            )
     for load in loads:
         load.start()
     load_g(0).start()
@@ -1238,7 +1279,7 @@
             jax.ShapeDtypeStruct((2, 3, rows, units), bf16),
         )
         + (lane,) * 4,
-        in_specs=[anywhere] * 12,
+        in_specs=[anywhere] * 18,
         out_specs=(anywhere,) * 10,
         scratch_shapes=[
             pltpu.VMEM((width, units), bf16),
@@ -1252,7 +1293,7 @@
             pltpu.VMEM((rows, units), bf16),
             pltpu.VMEM((rows, width), bf16),
             pltpu.VMEM((cols - 1, rows, width), bf16),
-            pltpu.SemaphoreType.DMA((12,)),
+            pltpu.SemaphoreType.DMA((15,)),
             pltpu.SemaphoreType.DMA((2, cols)),
             pltpu.SemaphoreType.DMA((cols,)),
             pltpu.SemaphoreType.DMA((cols,)),
@@ -1281,7 +1322,9 @@
     gq_ref,
     go_ref,
     gain_ref,
+    out_ref,
     gin_ref,
+    crossed_ref,
     sq_ref,
     so_ref,
     gsum_ref,
@@ -1307,6 +1350,7 @@
     o_sems,
     qz_sems,
     oz_sems,
+    cross_sems,
     local_sems,
 ):
     group, core, mate, row, col = place()
@@ -1393,6 +1437,8 @@
         ig_ref.at[:, lanes(col, width)], gin_ref.at[col], local_sems.at[2]
     )
 
+    cross = remote(out_ref, crossed_ref, cross_sems, 0, (mate, core, col))
+    stay = pltpu.make_async_copy(out_ref, crossed_ref, local_sems.at[4])
     for m in range(2):
         copies[m]["s0"].start()
         copies[m]["a1"].start()
@@ -1400,6 +1446,7 @@
     @pl.when(core == row)
     def _():
         own_tokens.start()
+        stay.start()
         for step in range(1, cols):
             token_copy(step, col).start()
 
@@ -1441,6 +1488,7 @@
     def _():
         for step in range(cols):
             token_copy(step, col).start()
+        cross.start()
 
     gain_round(2)
     for m in range(2):
@@ -1503,13 +1551,15 @@
     def _():
         token_copy(0, col).wait_recv()
         token_copy(0, col).wait_send()
+        cross.wait()
 
     @pl.when(core == row)
     def _():
         own_tokens.wait()
-
-
-def finish(input_grad, grad_q, grad_o, gains, cols):
+        stay.wait()
+
+
+def finish(input_grad, grad_q, grad_o, gains, output, cols):
     anywhere = pl.BlockSpec(memory_space=pl.ANY)
     in_vmem = pl.BlockSpec(memory_space=pltpu.VMEM)
     bf16, f32 = jnp.bfloat16, jnp.float32
@@ -1532,12 +1582,13 @@
         functools.partial(finish_kernel, cols),
         out_shape=(
             jax.ShapeDtypeStruct((cols, length, full // cols), bf16),
+            jax.ShapeDtypeStruct(output.shape, bf16),
             jax.ShapeDtypeStruct((2, rows, wide_q // cols), f32),
             jax.ShapeDtypeStruct((2, rows, wide_o // cols), f32),
             jax.ShapeDtypeStruct(gains.shape, f32),
         ),
-        in_specs=[anywhere] * 4,
-        out_specs=(anywhere, in_vmem, in_vmem, in_vmem),
+        in_specs=[anywhere] * 5,
+        out_specs=(anywhere, anywhere, in_vmem, in_vmem, in_vmem),
         scratch_shapes=buffers(wide_q)
         + buffers(wide_o)
         + [
@@ -1549,7 +1600,8 @@
             pltpu.SemaphoreType.DMA((2, 5)),
             pltpu.SemaphoreType.DMA((2, 2, cols)),
             pltpu.SemaphoreType.DMA((2, 2, cols)),
-            pltpu.SemaphoreType.DMA((4,)),
+            pltpu.SemaphoreType.DMA((2, 1)),
+            pltpu.SemaphoreType.DMA((5,)),
         ],
         compiler_params=pltpu.CompilerParams(
             collective_id=3, has_side_effects=True, vmem_limit_bytes=40 << 20
@@ -1561,6 +1613,7 @@
         grad_q.reshape(2, 2, 2, rows, wide_q),
         grad_o.reshape(2, 2, 2, rows, wide_o),
         gains,
+        output,
     )
 
 
@@ -1630,8 +1683,12 @@
     own_grad = lax.dynamic_index_in_dim(line_cot, col, keepdims=False).astype(jnp.float32)
 
     w_gate_up, w_down, weights_qkv = lax.optimization_barrier((w_gate_up, w_down, weights_qkv))
-    far_gate_up = lax.ppermute(half_rows(w_gate_up), "row", OVER_X)
-    far_down = lax.ppermute(half_rows(w_down), "row", OVER_X)
+    def quarter_rows(matrix):
+        count = matrix.shape[0] // 4
+        return lax.dynamic_slice_in_dim(matrix, (2 * core + group // 2) * count, count)
+
+    far_gate_up = lax.ppermute(quarter_rows(w_gate_up), "row", OVER_X)
+    far_down = lax.ppermute(quarter_rows(w_down), "row", OVER_X)
     own_mats = (w_gate_up[:, 0], w_gate_up[:, 1], w_down)
 
     cosine_table, sine_table = rope_tables(jnp.arange(slot_len, dtype=jnp.int32), HEAD_SIZE)
@@ -1660,10 +1717,15 @@
     scale_two = lax.rsqrt(jnp.mean(resid * resid, axis=1, keepdims=True) + EPSILON)
     own_ffn = (resid * scale_two * gain_two).astype(jnp.bfloat16)
 
-    far_gate_up, far_down, own_ffn, own_mats = lax.optimization_barrier(
-        (far_gate_up, far_down, own_ffn, own_mats)
+    shared_gate_up = lax.ppermute(far_gate_up, "dp", OVER_Y)
+    shared_down = lax.ppermute(far_down, "dp", OVER_Y)
+    own_ffn, own_mats, far_gate_up, far_down, shared_gate_up, shared_down = (
+        lax.optimization_barrier(
+            (own_ffn, own_mats, far_gate_up, far_down, shared_gate_up, shared_down)
+        )
     )
     far_mats = (far_gate_up[:, 0], far_gate_up[:, 1], far_down)
+    far_mats += (shared_gate_up[:, 0], shared_gate_up[:, 1], shared_down)
     sibling_mats = tuple(from_sibling(matrix) for matrix in far_mats)
     *unused, a_keep, a_send, b_keep, b_send = feed_forward(
         own_ffn,
@@ -1717,13 +1779,12 @@
     gain_one_part = jnp.sum(grad_normed_one * own_float * scale_one, axis=0)
     a_last, b_last, own_input_grad = lax.optimization_barrier((a_last, b_last, own_input_grad))
     gains = jnp.stack([gain_one_part, gain_two_part]).reshape(8, -1)
-    given_grad, sums_q, sums_o, gain_sums = finish(
-        own_input_grad, grad_qkv, grad_out, gains, col_count
-    )
-    out_cols, a_last, b_last, a_sum, b_sum, given_grad = lax.optimization_barrier(
-        (out_cols, a_last, b_last, a_sum, b_sum, given_grad)
-    )
-    given_out = lax.ppermute(out_cols, ("dp", "row"), CROSSED)
+    given_grad, given_out, sums_q, sums_o, gain_sums = finish(
+        own_input_grad, grad_qkv, grad_out, gains, out_cols, col_count
+    )
+    a_last, b_last, a_sum, b_sum, given_grad = lax.optimization_barrier(
+        (a_last, b_last, a_sum, b_sum, given_grad)
+    )
     layer_out = jnp.where(given_live, given_out.astype(jnp.float32), 0.0)
     input_grad = given_grad.astype(jnp.float32)
     a_total = one_of(a_sum, high).astype(jnp.float32) + a_last.astype(jnp.float32)

time: 1040 us -> 1040 us (level)
  waiting for transfers between devices: 97.8 us -> 84.2 us
  Pallas kernels: 742 us -> 755 us
  local copies, waits for them, and re-layouts: 60.1 us -> 73.1 us
    ppermute x3 -> x4, waiting for transfers between devices: 65.7 us -> 54.3 us  [the longest x1 36.7 us: one_sequence_body(): shared_down = lax.ppermute(far_down, 'dp', OVER_Y)]
    unnamed x89 -> x109, local copies, waits for them, and re-layouts: 18.4 us -> 26.3 us
  transfers between devices with their start and end apart: 16 -> 20, of which waited for: 7 -> 10; matrix products, arithmetic and copies ran while one was open for 13% -> 11% of each run, Pallas kernels for 30% -> 15%
where the time goes in v9:
time: 1040 us; the launch traced here: 1030 us
  Pallas kernels  755 us (73%)
  waiting for transfers between devices  84.2 us (8%)
  local copies, waits for them, and re-layouts  73.1 us (7%)
  other arithmetic  45 us (4%)
  matrix products  37.8 us (4%)
  between operations  22.8 us (2%)
    pallas_call x1, Pallas kernels, feed_forward(): pl.pallas_call(functools.partial(ffn_kernel, cols), out_shape=(jax.ShapeD...  286 us
    pallas_call x1, Pallas kernels, finish(): pl.pallas_call(functools.partial(finish_kernel, cols), out_shape=(jax.Sha...  159 us
    pallas_call x1, Pallas kernels, gather_weights(): pl.pallas_call(functools.partial(gather_kernel, cols), out_shape=(whole(o...  158 us
    pallas_call x1, Pallas kernels, attend_back_fast(): pl.pallas_call(functools.partial(attend_back_kernel, block), grid=(groups...  63.2 us
    pallas_call x1, Pallas kernels, start_exchange(): pl.pallas_call(functools.partial(start_kernel, cols), out_shape=(jax.Shap...  46 us
    pallas_call x1, Pallas kernels, attend_fast(): pl.pallas_call(functools.partial(attend_kernel, block), grid=(groups,), o...  43.1 us
    ppermute x1, waiting for transfers between devices, one_sequence_body(): shared_down = lax.ppermute(far_down, 'dp', OVER_Y)  36.7 us
    unnamed x109, local copies, waits for them, and re-layouts  26.3 us
  transfers between devices with their start and end apart: 20, of which 10 were waited for; matrix products, arithmetic and copies ran while one was open for 11% of the time, Pallas kernels for 15%

profile of v9, /device:TPU:0, one launch (start us, length us, event | category | flops | bytes accessed | tf_op | source)
XLA Modules:
  0.0 1028.8 jit_solution(14662465163114793639)
XLA Ops:
  15.9 2.1 fusion.14
  24.0 46.0 %start_exchange.1 = (bf16[512,2048]{1,0:T(8,128)(2,1)S(1)}, bf16[1024,2048]{1,0:T(8,128)(2,1)S(1)}) custom-call(bf16[4,512,512]{2,1,0:T(8,128)(2,1)S(1)} %copy-done.4, f32[1,2048]{1,0:T(1,128)S(1)} %bitcast.84), custom_call_target="tpu_custom_call" | custom-call | bytes 209715200 | tf_op jit(solution)/shard_map/start_exchange/pallas_call | solution.py:342
  72.1 2.8 constant_dynamic-slice_fusion.8
  79.3 158.4 %gather_weights.1 = (bf16[2048,1536]{1,0:T(8,128)(2,1)}, bf16[2048,1024]{1,0:T(8,128)(2,1)}, bf16[4,512,512]{2,1,0:T(8,128)(2,1)}) custom-call(bf16[1024,384]{1,0:T(8,128)(2,1)} %pad_maximum_fusion.2.q_ref, bf16[1024,256]{1,0:T(8,128)(2,1)} %get-tuple-element.176.o_ref, bf16[4,512,512]{2,1,0:T(8,128)(2,1)} %maximum_select_fusion.1.rows_ref), custom_call_target="tpu_custom_call" | custom-call | bytes 314572800 | tf_op jit(solution)/shard_map/gather_weights/pallas_call | solution.py:522
  243.1 2.3 concatenate.38.cos_ref
  245.3 10.8 %copy.53 = bf16[1024,2,2048]{2,0,1:T(8,128)(2,1)} copy(bf16[1024,2,2048]{2,1,0:T(2,128)(2,1)} %param.20) | data formatting | bytes 16777216 | tf_op jit(solution)/shard_map/optimization_barrier | solution.py:1685
  256.2 3.2 constant_dynamic-slice_fusion.2
  260.9 43.1 %attend.1 = (bf16[1024,1536]{1,0:T(8,128)(2,1)}, bf16[1024,1024]{1,0:T(8,128)(2,1)S(1)}) custom-call(s32[1]{0:T(128)} %dynamic_slice.83.len_ref, bf16[1024,2048]{1,0:T(8,128)(2,1)} %copy-done.10, bf16[2048,1536]{1,0:T(8,128)(2,1)} %get-tuple-element.58.w_ref, f32[1024,256]{1,0:T(8,128)S(1)} %copy-done.6, f32[1024,256]{1,0:T(8,128)S(1)} %concatenate.40.sin_ref), custom_call_target="tpu_custom_call" | custom-call | flops 10737418240 | bytes 13631488 | tf_op jit(solution)/shard_map/attend/pallas_call | solution.py:638
  304.0 4.8 convolution_convert_fusion.3
  311.4 2.3 constant_dynamic-slice_fusion.1
  315.3 6.8 slice_bitcast_fusion
  322.0 17.6 %collective-permute-done.2.wd_far = bf16[256,2048]{1,0:T(8,128)(2,1)} collective-permute-done((bf16[256,2048]{1,0:T(8,128)(2,1)}, bf16[256,2048]{1,0:T(8,128)(2,1)}, u32[]{:S(2)}, u32[]{:S(2)}) %collective-permute-start.2) | collective-permute-done | bytes 1048608 | tf_op jit(solution)/shard_map/ppermute | solution.py:1691
  340.3 5.2 fusion.13
  348.4 36.7 %collective-permute-done.4.wd_far_y = bf16[256,2048]{1,0:T(8,128)(2,1)S(1)} collective-permute-done((bf16[256,2048]{1,0:T(8,128)(2,1)}, bf16[256,2048]{1,0:T(8,128)(2,1)S(1)}, u32[]{:S(2)}, u32[]{:S(2)}) %collective-permute-start.4) | collective-permute-done | bytes 1048608 | tf_op jit(solution)/shard_map/ppermute | solution.py:1721
  385.1 2.1 slice_bitcast_fusion.6
  391.5 3.0 collective-permute-done.8.wg_sib_y
  398.4 285.6 %feed_forward.1 = (bf16[4,512,2048]{2,1,0:T(8,128)(2,1)}, bf16[4,512,4096]{2,1,0:T(8,128)(2,1)}, bf16[4,512,2048]{2,1,0:T(8,128)(2,1)}, bf16[3,512,2048]{2,1,0:T...) custom-call(bf16[512,2048]{1,0:T(8,128)(2,1)} %multiply_convert_fusi, ...), custom_call_target="tpu_custom_call" | custom-call | flops 154618822656 | bytes 838860800 | tf_op jit(solution)/shard_map/feed_forward/pallas_call | solution.py:1271
  684.1 4.8 convert_reduce_fusion
  690.0 4.4 multiply_convert_fusion
  698.7 7.9 convolution_convert_fusion.4.dz_ref
  706.6 63.2 %attend_back.1 = bf16[1024,1536]{1,0:T(8,128)(2,1)} custom-call(s32[1]{0:T(128)} %dynamic_slice.83.len_ref, bf16[1024,1536]{1,0:T(8,128)(2,1)} %get-tuple-element.78.qkv_ref, bf16[1024,1024]{1,0:T(8,128)(2,1)S(1)} %convolution_convert_fusion.4.dz_ref, f32[1024,256]{1,0:T(8,128)S(1)} %copy-done.7, f32[1024,256]{1,0:T(8,128)S(1)} %concatenate.40.sin_ref), custom_call_target="tpu_custom_call" | custom-call | flops 10737418240 | bytes 8388608 | tf_op jit(solution)/shard_map/attend_back/pallas_call | solution.py:745
  769.8 9.1 convolution_convert_fusion.2
  784.8 6.9 convolution_convert_fusion.1
  797.3 9.1 convolution_convert_fusion
  808.1 5.4 fusion.4.ig_ref
  813.5 17.0 %collective-permute-done.15 = bf16[256,3072]{1,0:T(8,128)(2,1)} collective-permute-done((bf16[256,3072]{1,0:T(8,128)(2,1)}, bf16[256,3072]{1,0:T(8,128)(2,1)}, u32[]{:S(2)}, u32[]{:S(2)}) %collective-permute-start.15) | collective-permute-done | bytes 1572896 | tf_op jit(solution)/shard_map/ppermute | solution.py:1769
  834.0 2.2 copy-done.3
  837.7 159.2 %finish.1 = (bf16[4,512,512]{2,1,0:T(8,128)(2,1)S(1)}, bf16[4,512,512]{2,1,0:T(8,128)(2,1)S(1)}, f32[2,256,384]{2,1,0:T(8,128)S(1)}, f32[2,256,256]{2,1,0:T(8,128)S(1)}, f32[8,512]{1,0:T(8,128)S(1)}) custom-call(bf16[512,2048]{1,0:T(8,128)(2,1)S(1)} %copy-done.2, bf16[2,2,2,256,1536]{4,3,2,1,0:T(8,128)(2,1)} %bitcast.85, ...), custom_call_target="tpu_custom_call" | custom-call | bytes 314572800 | tf_op jit(solution)/shard_map/finish/pallas_call | solution.py:1581
  999.1 2.9 copy-done.19
  1006.0 5.2 copy.57
  1012.4 2.6 convert_element_type.135
  1015.0 2.3 convert_select_fusion
  (203 shorter events, 71.0 us)
Async XLA Ops:
  7.2 68.8 %all-gather.3.cloned.1.call-start = ((), (), s32[]{:S(2)}) async-start(), calls=%async_computation.1 | async-start | bytes 10485760 | tf_op jit(solution)/shard_map/all_gather | solution.py:1675
  7.9 390.5 %all-gather.5.cloned.1.call-start = ((), (), s32[]{:S(2)}) async-start(), calls=%async_computation.2 | async-start | bytes 10485760 | tf_op jit(solution)/shard_map/all_gather | solution.py:1682
  15.2 59.7 %copy-start.8 = (f32[2048]{0:T(1024)}, f32[2048]{0:T(1024)S(1)}, u32[]{:S(2)}) copy-start(f32[2048]{0:T(1024)S(1)} %convert_element_type.108) | copy-start | bytes 24580
  72.1 268.2 %copy-start = (bf16[512,2048]{1,0:T(8,128)(2,1)}, bf16[512,2048]{1,0:T(8,128)(2,1)S(1)}, u32[]{:S(2)}) copy-start(bf16[512,2048]{1,0:T(8,128)(2,1)S(1)} %get-tuple-element.53) | copy-start | bytes 6291460
  77.7 160.1 %copy-start.48 = (s32[16]{0:T(128)S(1)}, s32[16]{0:T(128)}, u32[]{:S(2)}) copy-start(s32[16]{0:T(128)} %param.13) | copy-start | bytes 196
  237.7 594.7 %reduce-scatter.2.cloned.1.call-start = ((), (), s32[]{:S(2)}) async-start(), calls=%async_computation.3 | async-start | bytes 10485760 | tf_op jit(solution)/shard_map/reduce_scatter | solution.py:1739
  259.4 44.6 %copy-start.41 = (bf16[2048,1024]{1,0:T(8,128)(2,1)S(1)}, bf16[2048,1024]{1,0:T(8,128)(2,1)}, u32[]{:S(2)}) copy-start(bf16[2048,1024]{1,0:T(8,128)(2,1)} %get-tuple-element.62) | copy-start | bytes 12582916
  259.4 55.2 %collective-permute-start.1 = (bf16[256,2,2048]{2,0,1:T(8,128)(2,1)}, bf16[256,2,2048]{2,0,1:T(8,128)(2,1)}, u32[]{:S(2)}, u32[]{:S(2)}) collective-permute-start(bf16[256,2,2048]{2,0,1:T(8,128)(2,1)} %constant_dynamic-slice_fusion.2), channel_id=1, source_target_pairs={{0,4},{4,0},{1,5},{5,1},{2,6},{6,2},{3,7},{7,3},{8,12},{12,8},{9,1... | collective-permute-start | bytes 6291464 | tf_op jit(solution)/shard_map/ppermute | solution.py:1690
  311.4 28.9 %collective-permute-start = (bf16[512,2048]{1,0:T(8,128)(2,1)}, bf16[512,2048]{1,0:T(8,128)(2,1)}, u32[]{:S(2)}, u32[]{:S(2)}) collective-permute-start(bf16[512,2048]{1,0:T(8,128)(2,1)} %constant_dynamic-slice_fusion.3), channel_id=1, source_target_pairs={{0,8},{8,0},{16,24},{24,16},{1,9},{9,1},{17,25},{25,17},{2,10},{10... | collective-permute-start | bytes 6291464 | tf_op jit(solution)/shard_map/ppermute | solution.py:1653
  313.7 25.9 %collective-permute-start.2 = (bf16[256,2048]{1,0:T(8,128)(2,1)}, bf16[256,2048]{1,0:T(8,128)(2,1)}, u32[]{:S(2)}, u32[]{:S(2)}) collective-permute-start(bf16[256,2048]{1,0:T(8,128)(2,1)} %constant_dynamic-slice_fusion.1), channel_id=1, source_target_pairs={{0,4},{4,0},{1,5},{5,1},{2,6},{6,2},{3,7},{7,3},{8,12},{12,8},{9,1... | collective-permute-start | bytes 3145736 | tf_op jit(solution)/shard_map/ppermute | solution.py:1691
  314.6 32.1 %copy-start.32 = (f32[2048]{0:T(1024)}, f32[2048]{0:T(1024)S(1)}, u32[]{:S(2)}) copy-start(f32[2048]{0:T(1024)S(1)} %convert_element_type.114) | copy-start | bytes 24580
  314.6 25.7 %copy-start.25 = (bf16[1024,2048]{1,0:T(8,128)(2,1)S(1)}, bf16[1024,2048]{1,0:T(8,128)(2,1)}, u32[]{:S(2)}) copy-start(bf16[1024,2048]{1,0:T(8,128)(2,1)} %copy-done.24) | copy-start | bytes 12582916
  314.6 70.5 %collective-permute-start.3 = (bf16[256,2,2048]{2,0,1:T(8,128)(2,1)}, bf16[256,2,2048]{2,0,1:T(8,128)(2,1)S(1)}, u32[]{:S(2)}, u32[]{:S(2)}) collective-permute-start(bf16[256,2,2048]{2,0,1:T(8,128)(2,1)} %collective-permute-done.1), channel_id=1, source_target_pairs={{0,16},{16,0},{8,24},{24,8},{1,17},{17,1},{9,25},{25,9},{2,18},{18... | collective-permute-start | bytes 6291464 | tf_op jit(solution)/shard_map/ppermute | solution.py:1720
  339.6 45.5 %collective-permute-start.4 = (bf16[256,2048]{1,0:T(8,128)(2,1)}, bf16[256,2048]{1,0:T(8,128)(2,1)S(1)}, u32[]{:S(2)}, u32[]{:S(2)}) collective-permute-start(bf16[256,2048]{1,0:T(8,128)(2,1)} %collective-permute-done.2.wd_far), channel_id=1, source_target_pairs={{0,16},{16,0},{8,24},{24,8},{1,17},{17,1},{9,25},{25,9},{2,18},{18... | collective-permute-start | bytes 3145736 | tf_op jit(solution)/shard_map/ppermute | solution.py:1721
  346.7 38.5 %copy-start.34 = (f32[512]{0:T(512)}, f32[512]{0:T(512)S(1)}, u32[]{:S(2)}) copy-start(f32[512]{0:T(512)S(1)} %get-tuple-element.169) | copy-start | bytes 6148
  387.2 11.2 %copy-start.28 = (bf16[256,2048]{1,0:T(8,128)(2,1)}, bf16[256,2048]{1,0:T(8,128)(2,1)S(1)}, u32[]{:S(2)}) copy-start(bf16[256,2048]{1,0:T(8,128)(2,1)S(1)} %get-tuple-element.150.wu_far) | copy-start | bytes 3145732
  387.2 2.7 collective-permute-start.5
  387.3 4.1 collective-permute-start.6
  388.1 6.4 collective-permute-start.8
  388.2 7.7 collective-permute-start.9
  388.6 8.8 collective-permute-start.10
  390.0 8.5 collective-permute-start.7
  694.4 4.3 collective-permute-start.13
  694.4 84.6 %collective-permute-start.12 = (bf16[2,256,3072]{2,1,0:T(8,128)(2,1)}, bf16[2,256,3072]{2,1,0:T(8,128)(2,1)S(1)}, u32[]{:S(2)}, u32[]{:S(2)}) collective-permute-start(bf16[2,256,3072]{2,1,0:T(8,128)(2,1)} %get-tuple-element.77), channel_id=1, source_target_pairs={{0,16},{16,0},{8,24},{24,8},{1,17},{17,1},{9,25},{25,9},{2,18},{18... | collective-permute-start | bytes 9437192 | tf_op jit(solution)/shard_map/ppermute | solution.py:1745
  696.2 84.0 %collective-permute-start.11 = (bf16[2,256,3072]{2,1,0:T(8,128)(2,1)}, bf16[2,256,3072]{2,1,0:T(8,128)(2,1)S(1)}, u32[]{:S(2)}, u32[]{:S(2)}) collective-permute-start(bf16[2,256,3072]{2,1,0:T(8,128)(2,1)} %get-tuple-element.75), channel_id=1, source_target_pairs={{0,4},{4,0},{1,5},{5,1},{2,6},{6,2},{3,7},{7,3},{8,12},{12,8},{9,1... | collective-permute-start | bytes 9437192 | tf_op jit(solution)/shard_map/ppermute | solution.py:1744
  706.6 63.2 %copy-start.13 = (bf16[1024,1024]{1,0:T(8,128)(2,1)S(1)}, bf16[1024,1024]{1,0:T(8,128)(2,1)}, u32[]{:S(2)}) copy-start(bf16[1024,1024]{1,0:T(8,128)(2,1)} %copy-done.12) | copy-start | bytes 6291460
  780.2 12.0 %copy-start.18 = (bf16[2,256,3072]{2,1,0:T(8,128)(2,1)}, bf16[2,256,3072]{2,1,0:T(8,128)(2,1)S(1)}, u32[]{:S(2)}) copy-start(bf16[2,256,3072]{2,1,0:T(8,128)(2,1)S(1)} %add_convert_fusion) | copy-start | bytes 9437188
  791.7 14.7 %copy-start.22 = (bf16[1024,2048]{1,0:T(8,128)(2,1)}, bf16[1024,2048]{1,0:T(8,128)(2,1)S(1)}, u32[]{:S(2)}) copy-start(bf16[1024,2048]{1,0:T(8,128)(2,1)S(1)} %convolution_convert_fusion.1) | copy-start | bytes 12582916
  792.0 14.4 %collective-permute-start.16 = (bf16[512,2048]{1,0:T(8,128)(2,1)S(1)}, bf16[512,2048]{1,0:T(8,128)(2,1)S(1)}, u32[]{:S(2)}, u32[]{:S(2)}) collective-permute-start(bf16[512,2048]{1,0:T(8,128)(2,1)S(1)} %constant_dynamic-slice_fusion), channel_id=1, source_target_pairs={{0,8},{8,0},{16,24},{24,16},{1,9},{9,1},{17,25},{25,17},{2,10},{10... | collective-permute-start | bytes 6291464 | tf_op jit(solution)/shard_map/ppermute | solution.py:1653
  793.4 37.0 %collective-permute-start.15 = (bf16[256,3072]{1,0:T(8,128)(2,1)}, bf16[256,3072]{1,0:T(8,128)(2,1)}, u32[]{:S(2)}, u32[]{:S(2)}) collective-permute-start(bf16[256,3072]{1,0:T(8,128)(2,1)} %dynamic-slice_bitcast_fusion), channel_id=1, source_target_pairs={{0,4},{4,0},{1,5},{5,1},{2,6},{6,2},{3,7},{7,3},{8,12},{12,8},{9,1... | collective-permute-start | bytes 4718600 | tf_op jit(solution)/shard_map/ppermute | solution.py:1769
  795.7 36.7 %collective-permute-start.14 = (bf16[256,3072]{1,0:T(8,128)(2,1)}, bf16[256,3072]{1,0:T(8,128)(2,1)}, u32[]{:S(2)}, u32[]{:S(2)}) collective-permute-start(bf16[256,3072]{1,0:T(8,128)(2,1)} %dynamic-slice_bitcast_fusion.1), channel_id=1, source_target_pairs={{0,16},{16,0},{8,24},{24,8},{1,17},{17,1},{9,25},{25,9},{2,18},{18... | collective-permute-start | bytes 4718600 | tf_op jit(solution)/shard_map/ppermute | solution.py:1768
  837.7 159.2 %copy-start.21 = (bf16[2,256,3072]{2,1,0:T(8,128)(2,1)S(1)}, bf16[2,256,3072]{2,1,0:T(8,128)(2,1)}, u32[]{:S(2)}) copy-start(bf16[2,256,3072]{2,1,0:T(8,128)(2,1)} %copy-done.20) | copy-start | bytes 9437188
  (42 other events, 191.7 us)
Sparse Core Ops, SparseCore 0:
  9.6 60.9 all-gather.2
  237.8 153.7 all-gather.4
  684.2 142.9 reduce-scatter.1

commit v10 on v9

--- a/solution.py
+++ b/solution.py
@@ -363,35 +363,12 @@
 
 
 def gather_kernel(
-    cols,
-    q_ref,
-    o_ref,
-    rows_ref,
-    wq_ref,
-    wo_ref,
-    crossed_ref,
-    q_send,
-    q_recv,
-    q_over,
-    q_shared,
-    o_send,
-    o_recv,
-    o_over,
-    o_shared,
-    cross_sems,
-    local_sems,
+    cols, q_ref, o_ref, after_ref, wq_ref, wo_ref, q_send, q_recv, q_over, o_send, o_recv, o_over, local_sems
 ):
     group, core, mate, row, col = place()
     last = cols - 1
     over = (group, 1 - row, col)
-    high = (group - core) // 2
-    other_plane = (2 * (1 - high) + core, row, col)
     greet(over)
-    greet(other_plane)
-
-    @pl.when(core != row)
-    def _():
-        greet((mate, core, col))
 
     @pl.when(col < last)
     def _():
@@ -403,12 +380,10 @@
 
     pl.semaphore_wait(
         pltpu.get_barrier_semaphore(),
-        2 + jnp.minimum(col, 1) + jnp.minimum(last - col, 1) + (core - row) * (core - row),
-    )
-    cross = remote(rows_ref, crossed_ref, cross_sems, 0, (mate, core, col))
-    stay = pltpu.make_async_copy(rows_ref, crossed_ref, local_sems.at[2])
-
-    def moves(own, full, send, recv, over_sems, shared_sems):
+        1 + jnp.minimum(col, 1) + jnp.minimum(last - col, 1),
+    )
+
+    def moves(own, full, send, recv, over_sems):
         tall, wide = own.shape
 
         def block(of_row, of_col):
@@ -427,18 +402,14 @@
         def across(src, of_row, chunk):
             return remote(src, block(of_row, chunk), over_sems, chunk, over)
 
-        def share(chunk):
-            place_there = block(1 - row, chunk)
-            return remote(place_there, place_there, shared_sems, chunk, other_plane)
-
-        return block, along, across, share
+        return block, along, across
 
     both = (
-        (q_ref, moves(q_ref, wq_ref, q_send, q_recv, q_over, q_shared)),
-        (o_ref, moves(o_ref, wo_ref, o_send, o_recv, o_over, o_shared)),
+        (q_ref, moves(q_ref, wq_ref, q_send, q_recv, q_over)),
+        (o_ref, moves(o_ref, wo_ref, o_send, o_recv, o_over)),
     )
     own_copies = []
-    for at, (own, (block, along, across, share)) in enumerate(both):
+    for at, (own, (block, along, across)) in enumerate(both):
 
         @pl.when(col < last)
         def _():
@@ -448,24 +419,12 @@
         def _():
             along(own, col, col - 1, 1).start()
 
-        @pl.when(lax.rem(col, 2) == high)
-        def _():
-            across(own, row, col).start()
-
+        across(own, row, col).start()
         own_copies.append(pltpu.make_async_copy(own, block(row, col), local_sems.at[at]))
         own_copies[-1].start()
-
-    @pl.when(core != row)
-    def _():
-        cross.start()
-
-    @pl.when(core == row)
-    def _():
-        stay.start()
-
     for at in range(1, cols):
         chunk = line_order(col, last, at)
-        for own, (block, along, across, share) in both:
+        for own, (block, along, across) in both:
             along(own, chunk, col, 0).wait_recv()
 
             @pl.when((chunk < col) & (col < last))
@@ -476,27 +435,10 @@
             def _():
                 along(block(row, chunk), chunk, col - 1, 1).start()
 
-            @pl.when(lax.rem(chunk, 2) == high)
-            def _():
-                across(block(row, chunk), row, chunk).start()
-
-    for at in range(cols // 2):
-        for own, (block, along, across, share) in both:
-            chunk = 2 * at + high
-            across(own, 1 - row, chunk).wait_recv()
-            share(chunk).start()
+            across(block(row, chunk), row, chunk).start()
     for copy in own_copies:
         copy.wait()
-
-    @pl.when(core != row)
-    def _():
-        cross.wait()
-
-    @pl.when(core == row)
-    def _():
-        stay.wait()
-
-    for own, (block, along, across, share) in both:
+    for own, (block, along, across) in both:
         for chunk in range(cols):
 
             @pl.when((col >= chunk) & (col < last))
@@ -507,13 +449,11 @@
             def _():
                 along(own, chunk, col - 1, 1).wait_send()
 
-        for at in range(cols // 2):
-            across(own, row, 2 * at + high).wait_send()
-            share(2 * at + high).wait_send()
-            share(2 * at + 1 - high).wait_recv()
-
-
-def gather_weights(own_q, own_o, token_rows, rows, cols):
+            across(own, row, chunk).wait_send()
+            across(own, 1 - row, chunk).wait_recv()
+
+
+def gather_weights(own_q, own_o, after, rows, cols):
     anywhere = pl.BlockSpec(memory_space=pl.ANY)
 
     def whole(own):
@@ -521,25 +461,20 @@
 
     return pl.pallas_call(
         functools.partial(gather_kernel, cols),
-        out_shape=(
-            whole(own_q),
-            whole(own_o),
-            jax.ShapeDtypeStruct(token_rows.shape, token_rows.dtype),
-        ),
+        out_shape=(whole(own_q), whole(own_o)),
         in_specs=[anywhere] * 3,
-        out_specs=(anywhere,) * 3,
+        out_specs=(anywhere,) * 2,
         scratch_shapes=[
             pltpu.SemaphoreType.DMA((2, cols)),
             pltpu.SemaphoreType.DMA((cols,)),
             pltpu.SemaphoreType.DMA((2, cols)),
-            pltpu.SemaphoreType.DMA((2, cols)),
         ]
         * 2
-        + [pltpu.SemaphoreType.DMA((2, 1)), pltpu.SemaphoreType.DMA((3,))],
+        + [pltpu.SemaphoreType.DMA((2,))],
         compiler_params=pltpu.CompilerParams(collective_id=4, has_side_effects=True),
         cost_estimate=pl.CostEstimate(flops=0, bytes_accessed=300 << 20, transcendentals=0),
         name="gather_weights",
-    )(own_q, own_o, token_rows)
+    )(own_q, own_o, after)
 
 
 def half_turn(wide):
@@ -1439,10 +1374,10 @@
 
     cross = remote(out_ref, crossed_ref, cross_sems, 0, (mate, core, col))
     stay = pltpu.make_async_copy(out_ref, crossed_ref, local_sems.at[4])
-    for m in range(2):
+    for m in (1, 0):
         copies[m]["s0"].start()
-        copies[m]["a1"].start()
         copies[m]["own"].start()
+    copies[1]["a1"].start()
     @pl.when(core == row)
     def _():
         own_tokens.start()
@@ -1466,35 +1401,6 @@
         exchange.start()
         exchange.wait()
         gain_now[at + 1] = gain_now[at] + gain_in[at]
-
-    gain_round(0)
-    for m in range(2):
-        copies[m]["s0"].wait()
-        copies[m]["b1"].start()
-    gain_round(1)
-    for m in range(2):
-        grads, out, keep, sib, a1, a2, b1, b2, zb, sems, z_sems = matrices[m]
-        copies[m]["own"].wait()
-        copies[m]["a1"].wait()
-        rows_plus(keep.at[1 - high, row], a1.at[1 - high])
-        copies[m]["a2"].start()
-    for m in range(2):
-        grads, out, keep, sib, a1, a2, b1, b2, zb, sems, z_sems = matrices[m]
-        copies[m]["b1"].wait()
-        rows_plus(sib.at[high, 1 - row], b1.at[1 - row])
-        copies[m]["b2"].start()
-
-    @pl.when(core != row)
-    def _():
-        for step in range(cols):
-            token_copy(step, col).start()
-        cross.start()
-
-    gain_round(2)
-    for m in range(2):
-        grads, out, keep, sib, a1, a2, b1, b2, zb, sems, z_sems = matrices[m]
-        rows_plus(keep.at[high, row], a1.at[high])
-        rows_plus(sib.at[high, row], b1.at[row])
 
     def z_moves(m, side, source):
         grads, out, keep, sib, a1, a2, b1, b2, zb, sems, z_sems = matrices[m]
@@ -1512,18 +1418,52 @@
             for step in range(1, cols)
         ]
 
-    for side, last_copy in ((0, "a2"), (1, "b2")):
-        for m in range(2):
-            grads, out, keep, sib, a1, a2, b1, b2, zb, sems, z_sems = matrices[m]
+    def first_sums(m):
+        grads, out, keep, sib, a1, a2, b1, b2, zb, sems, z_sems = matrices[m]
+        copies[m]["own"].wait()
+        copies[m]["a1"].wait()
+        if m == 1:
+            copies[0]["a1"].start()
+        rows_plus(keep.at[1 - high, row], a1.at[1 - high])
+        copies[m]["a2"].start()
+        copies[m]["b1"].wait()
+        if m == 1:
+            copies[0]["b1"].start()
+        rows_plus(sib.at[high, 1 - row], b1.at[1 - row])
+        copies[m]["b2"].start()
+
+    def last_sums(m):
+        grads, out, keep, sib, a1, a2, b1, b2, zb, sems, z_sems = matrices[m]
+        rows_plus(keep.at[high, row], a1.at[high])
+        rows_plus(sib.at[high, row], b1.at[row])
+        for side, last_copy in ((0, "a2"), (1, "b2")):
             copies[m][last_copy].wait()
             rows_plus((keep, sib)[side].at[high, row], (a2, b2)[side])
             for copy in z_moves(m, side, lambda step: 0):
                 copy.start()
+
+    copies[1]["s0"].wait()
+    copies[1]["b1"].start()
+    gain_round(0)
+    copies[0]["s0"].wait()
+    first_sums(1)
+    gain_round(1)
+    last_sums(1)
+    gain_round(2)
+    first_sums(0)
+
+    @pl.when(core != row)
+    def _():
+        for step in range(cols):
+            token_copy(step, col).start()
+        cross.start()
+
     gain_round(3)
+    last_sums(0)
     gain_round(4)
     gsum_ref[...] = gain_now[5]
-    for side in range(2):
-        for m in range(2):
+    for m in (1, 0):
+        for side in range(2):
             grads, out, keep, sib, a1, a2, b1, b2, zb, sems, z_sems = matrices[m]
             for copy in z_moves(m, side, lambda step: 0):
                 copy.wait_send()
@@ -1676,9 +1616,9 @@
     everyone, attn_input = lax.optimization_barrier((everyone, attn_input))
     picked = pick_sequences(everyone, deal_order, group * seq_group, seq_group)
     picked = jnp.where(given_live, picked, jnp.zeros_like(picked))
-    weights_qkv, weights_out, given = gather_weights(
-        pack_q, pack_o, picked, row_count, col_count
-    )
+    given = lax.ppermute(picked, ("dp", "row"), CROSSED)
+    weights_qkv, weights_out = gather_weights(pack_q, pack_o, picked, row_count, col_count)
+    given, weights_qkv = lax.optimization_barrier((given, weights_qkv))
     line_cot = lax.all_gather(given, "col", axis=2, tiled=True)
     own_grad = lax.dynamic_index_in_dim(line_cot, col, keepdims=False).astype(jnp.float32)
 

time: 1040 us -> 1020 us (0.981); the launches traced: 1030 us -> 998 us
  Pallas kernels: 755 us -> 708 us
  starting transfers between devices: 10.3 us -> 27.4 us
    pallas_call x1, Pallas kernels: 158 us -> 118 us  [gather_weights(): pl.pallas_call(functools.partial(gather_kernel, cols), out_shape=(whole(o...]
    ppermute x0 -> x1, starting transfers between devices: none -> 17.1 us  [one_sequence_body(): given = lax.ppermute(picked, ('dp', 'row'), CROSSED)]
    pallas_call x1, Pallas kernels: 159 us -> 147 us  [finish(): pl.pallas_call(functools.partial(finish_kernel, cols), out_shape=(jax.Sha...]
    unnamed x109 -> x111, local copies, waits for them, and re-layouts: 26.3 us -> 26.1 us
  transfers between devices with their start and end apart: 20 -> 21, of which waited for: 10 -> 10; matrix products, arithmetic and copies ran while one was open for 11% -> 11% of each run, Pallas kernels for 15% -> 27%
where the time goes in v10:
time: 1020 us; the launch traced here: 998 us
  Pallas kernels  708 us (69%)
  waiting for transfers between devices  85 us (8%)
  local copies, waits for them, and re-layouts  71.4 us (7%)
  other arithmetic  45 us (4%)
  matrix products  37.8 us (4%)
  starting transfers between devices  27.4 us (3%)
  between operations  22.8 us (2%)
    pallas_call x1, Pallas kernels, feed_forward(): pl.pallas_call(functools.partial(ffn_kernel, cols), out_shape=(jax.ShapeD...  291 us
    pallas_call x1, Pallas kernels, finish(): pl.pallas_call(functools.partial(finish_kernel, cols), out_shape=(jax.Sha...  147 us
    pallas_call x1, Pallas kernels, gather_weights(): pl.pallas_call(functools.partial(gather_kernel, cols), out_shape=(whole(o...  118 us
    pallas_call x1, Pallas kernels, attend_back_fast(): pl.pallas_call(functools.partial(attend_back_kernel, block), grid=(groups...  63.2 us
    pallas_call x1, Pallas kernels, start_exchange(): pl.pallas_call(functools.partial(start_kernel, cols), out_shape=(jax.Shap...  46.2 us
    pallas_call x1, Pallas kernels, attend_fast(): pl.pallas_call(functools.partial(attend_kernel, block), grid=(groups,), o...  43 us
    ppermute x1, waiting for transfers between devices, one_sequence_body(): shared_down = lax.ppermute(far_down, 'dp', OVER_Y)  36.3 us
    unnamed x111, local copies, waits for them, and re-layouts  26.1 us
  transfers between devices with their start and end apart: 21, of which 10 were waited for; matrix products, arithmetic and copies ran while one was open for 11% of the time, Pallas kernels for 27%

profile of v10, /device:TPU:0, one launch (start us, length us, event | category | flops | bytes accessed | tf_op | source)
XLA Modules:
  0.0 997.9 jit_solution(11833270710282926113)
XLA Ops:
  20.4 46.2 %start_exchange.1 = (bf16[512,2048]{1,0:T(8,128)(2,1)S(1)}, bf16[1024,2048]{1,0:T(8,128)(2,1)S(1)}) custom-call(bf16[4,512,512]{2,1,0:T(8,128)(2,1)S(1)} %copy-done.4, f32[1,2048]{1,0:T(1,128)S(1)} %bitcast.84), custom_call_target="tpu_custom_call" | custom-call | bytes 209715200 | tf_op jit(solution)/shard_map/start_exchange/pallas_call | solution.py:342
  73.9 17.1 %collective-permute-start = (bf16[4,512,512]{2,1,0:T(8,128)(2,1)}, bf16[4,512,512]{2,1,0:T(8,128)(2,1)}, u32[]{:S(2)}, u32[]{:S(2)}) collective-permute-start(bf16[4,512,512]{2,1,0:T(8,128)(2,1)} %maximum_select_fusion.1.after_ref), channel_id=1, source_target_pairs={{0,0},{4,8},{8,4},{12,12},{16,16},{20,24},{24,20},{28,28},{1,1},{5... | collective-permute-start | bytes 6291464 | tf_op jit(solution)/shard_map/ppermute | solution.py:1619
  96.1 117.9 %gather_weights.1 = (bf16[2048,1536]{1,0:T(8,128)(2,1)}, bf16[2048,1024]{1,0:T(8,128)(2,1)}) custom-call(bf16[1024,384]{1,0:T(8,128)(2,1)} %pad_maximum_fusion.2.q_ref, bf16[1024,256]{1,0:T(8,128)(2,1)} %get-tuple-element.178.o_ref, bf16[4,512,512]{2,1,0:T(8,128)(2,1)} %maximum_select_fusion.1.after_ref), custom_call_target="tpu_custom_call" | custom-call | bytes 314572800 | tf_op jit(solution)/shard_map/gather_weights/pallas_call | solution.py:462
  219.4 2.3 concatenate.38.cos_ref
  221.7 11.2 %copy.53 = bf16[1024,2,2048]{2,0,1:T(8,128)(2,1)} copy(bf16[1024,2,2048]{2,1,0:T(2,128)(2,1)} %param.20) | data formatting | bytes 16777216 | tf_op jit(solution)/shard_map/optimization_barrier | solution.py:1625
  232.9 3.5 constant_dynamic-slice_fusion.2
  238.0 43.0 %attend.1 = (bf16[1024,1536]{1,0:T(8,128)(2,1)}, bf16[1024,1024]{1,0:T(8,128)(2,1)S(1)}) custom-call(s32[1]{0:T(128)} %dynamic_slice.83.len_ref, bf16[1024,2048]{1,0:T(8,128)(2,1)} %copy-done.10, bf16[2048,1536]{1,0:T(8,128)(2,1)} %get-tuple-element.60.w_ref, f32[1024,256]{1,0:T(8,128)S(1)} %copy-done.6, f32[1024,256]{1,0:T(8,128)S(1)} %concatenate.40.sin_ref), custom_call_target="tpu_custom_call" | custom-call | flops 10737418240 | bytes 13631488 | tf_op jit(solution)/shard_map/attend/pallas_call | solution.py:573
  281.1 4.8 convolution_convert_fusion.3
  288.5 2.3 constant_dynamic-slice_fusion.1
  292.9 6.4 slice_bitcast_fusion
  299.3 17.4 %collective-permute-done.3.wd_far = bf16[256,2048]{1,0:T(8,128)(2,1)} collective-permute-done((bf16[256,2048]{1,0:T(8,128)(2,1)}, bf16[256,2048]{1,0:T(8,128)(2,1)}, u32[]{:S(2)}, u32[]{:S(2)}) %collective-permute-start.3) | collective-permute-done | bytes 1048608 | tf_op jit(solution)/shard_map/ppermute | solution.py:1631
  317.6 5.2 fusion.13
  325.8 36.3 %collective-permute-done.5.wd_far_y = bf16[256,2048]{1,0:T(8,128)(2,1)S(1)} collective-permute-done((bf16[256,2048]{1,0:T(8,128)(2,1)}, bf16[256,2048]{1,0:T(8,128)(2,1)S(1)}, u32[]{:S(2)}, u32[]{:S(2)}) %collective-permute-start.5) | collective-permute-done | bytes 1048608 | tf_op jit(solution)/shard_map/ppermute | solution.py:1661
  362.3 2.6 slice_bitcast_fusion.6
  367.6 3.0 collective-permute-done.7.wu_sib
  374.6 291.0 %feed_forward.1 = (bf16[4,512,2048]{2,1,0:T(8,128)(2,1)}, bf16[4,512,4096]{2,1,0:T(8,128)(2,1)}, bf16[4,512,2048]{2,1,0:T(8,128)(2,1)}, bf16[3,512,2048]{2,1,0:T...) custom-call(bf16[512,2048]{1,0:T(8,128)(2,1)} %multiply_convert_fusi, ...), custom_call_target="tpu_custom_call" | custom-call | flops 154618822656 | bytes 838860800 | tf_op jit(solution)/shard_map/feed_forward/pallas_call | solution.py:1206
  665.6 4.8 convert_reduce_fusion
  671.6 4.4 multiply_convert_fusion
  678.1 2.2 collective-permute-done.14
  680.3 7.9 convolution_convert_fusion.4.dz_ref
  688.2 63.2 %attend_back.1 = bf16[1024,1536]{1,0:T(8,128)(2,1)} custom-call(s32[1]{0:T(128)} %dynamic_slice.83.len_ref, bf16[1024,1536]{1,0:T(8,128)(2,1)} %get-tuple-element.80.qkv_ref, bf16[1024,1024]{1,0:T(8,128)(2,1)S(1)} %convolution_convert_fusion.4.dz_ref, f32[1024,256]{1,0:T(8,128)S(1)} %copy-done.7, f32[1024,256]{1,0:T(8,128)S(1)} %concatenate.40.sin_ref), custom_call_target="tpu_custom_call" | custom-call | flops 10737418240 | bytes 8388608 | tf_op jit(solution)/shard_map/attend_back/pallas_call | solution.py:680
  751.5 9.1 convolution_convert_fusion.2
  766.4 6.9 convolution_convert_fusion.1
  778.4 9.1 convolution_convert_fusion
  789.2 5.4 fusion.4.ig_ref
  794.6 17.4 %collective-permute-done.16 = bf16[256,3072]{1,0:T(8,128)(2,1)} collective-permute-done((bf16[256,3072]{1,0:T(8,128)(2,1)}, bf16[256,3072]{1,0:T(8,128)(2,1)}, u32[]{:S(2)}, u32[]{:S(2)}) %collective-permute-start.16) | collective-permute-done | bytes 1572896 | tf_op jit(solution)/shard_map/ppermute | solution.py:1709
  815.2 2.2 copy-done.3
  819.0 147.1 %finish.1 = (bf16[4,512,512]{2,1,0:T(8,128)(2,1)S(1)}, bf16[4,512,512]{2,1,0:T(8,128)(2,1)S(1)}, f32[2,256,384]{2,1,0:T(8,128)S(1)}, f32[2,256,256]{2,1,0:T(8,128)S(1)}, f32[8,512]{1,0:T(8,128)S(1)}) custom-call(bf16[512,2048]{1,0:T(8,128)(2,1)S(1)} %copy-done.2, bf16[2,2,2,256,1536]{4,3,2,1,0:T(8,128)(2,1)} %bitcast.85, ...), custom_call_target="tpu_custom_call" | custom-call | bytes 314572800 | tf_op jit(solution)/shard_map/finish/pallas_call | solution.py:1521
  968.2 2.9 copy-done.19
  975.1 5.2 copy.57
  981.6 2.6 convert_element_type.135
  984.2 2.3 convert_select_fusion
  (207 shorter events, 72.3 us)
Async XLA Ops:
  7.2 63.4 %all-gather.3.cloned.1.call-start = ((), (), s32[]{:S(2)}) async-start(), calls=%async_computation.1 | async-start | bytes 10485760 | tf_op jit(solution)/shard_map/all_gather | solution.py:1615
  7.9 366.7 %all-gather.5.cloned.1.call-start = ((), (), s32[]{:S(2)}) async-start(), calls=%async_computation.2 | async-start | bytes 10485760 | tf_op jit(solution)/shard_map/all_gather | solution.py:1622
  15.2 58.7 %copy-start.8 = (f32[2048]{0:T(1024)}, f32[2048]{0:T(1024)S(1)}, u32[]{:S(2)}) copy-start(f32[2048]{0:T(1024)S(1)} %convert_element_type.108) | copy-start | bytes 24580
  68.7 249.0 %copy-start = (bf16[512,2048]{1,0:T(8,128)(2,1)}, bf16[512,2048]{1,0:T(8,128)(2,1)S(1)}, u32[]{:S(2)}) copy-start(bf16[512,2048]{1,0:T(8,128)(2,1)S(1)} %get-tuple-element.54) | copy-start | bytes 6291460
  70.6 20.4 %copy-start.28 = (bf16[1024,2,128]{2,1,0:T(2,128)(2,1)S(1)}, bf16[1024,2,128]{2,1,0:T(2,128)(2,1)}, u32[]{:S(2)}) copy-start(bf16[1024,2,128]{2,1,0:T(2,128)(2,1)} %param.18) | copy-start | bytes 1572868
  73.9 140.1 %collective-permute-start = (bf16[4,512,512]{2,1,0:T(8,128)(2,1)}, bf16[4,512,512]{2,1,0:T(8,128)(2,1)}, u32[]{:S(2)}, u32[]{:S(2)}) collective-permute-start(bf16[4,512,512]{2,1,0:T(8,128)(2,1)} %maximum_select_fusion.1.after_ref), channel_id=1, source_target_pairs={{0,0},{4,8},{8,4},{12,12},{16,16},{20,24},{24,20},{28,28},{1,1},{5... | collective-permute-start | bytes 6291464 | tf_op jit(solution)/shard_map/ppermute | solution.py:1619
  95.1 119.1 %copy-start.49 = (s32[16]{0:T(128)S(1)}, s32[16]{0:T(128)}, u32[]{:S(2)}) copy-start(s32[16]{0:T(128)} %param.13) | copy-start | bytes 196
  214.0 599.6 %reduce-scatter.2.cloned.1.call-start = ((), (), s32[]{:S(2)}) async-start(), calls=%async_computation.3 | async-start | bytes 10485760 | tf_op jit(solution)/shard_map/reduce_scatter | solution.py:1679
  236.3 44.7 %copy-start.42 = (bf16[2048,1024]{1,0:T(8,128)(2,1)S(1)}, bf16[2048,1024]{1,0:T(8,128)(2,1)}, u32[]{:S(2)}) copy-start(bf16[2048,1024]{1,0:T(8,128)(2,1)} %get-tuple-element.64) | copy-start | bytes 12582916
  236.3 55.2 %collective-permute-start.2 = (bf16[256,2,2048]{2,0,1:T(8,128)(2,1)}, bf16[256,2,2048]{2,0,1:T(8,128)(2,1)}, u32[]{:S(2)}, u32[]{:S(2)}) collective-permute-start(bf16[256,2,2048]{2,0,1:T(8,128)(2,1)} %constant_dynamic-slice_fusion.2), channel_id=1, source_target_pairs={{0,4},{4,0},{1,5},{5,1},{2,6},{6,2},{3,7},{7,3},{8,12},{12,8},{9,1... | collective-permute-start | bytes 6291464 | tf_op jit(solution)/shard_map/ppermute | solution.py:1630
  288.5 29.1 %collective-permute-start.1 = (bf16[512,2048]{1,0:T(8,128)(2,1)}, bf16[512,2048]{1,0:T(8,128)(2,1)}, u32[]{:S(2)}, u32[]{:S(2)}) collective-permute-start(bf16[512,2048]{1,0:T(8,128)(2,1)} %constant_dynamic-slice_fusion.3), channel_id=1, source_target_pairs={{0,8},{8,0},{16,24},{24,16},{1,9},{9,1},{17,25},{25,17},{2,10},{10... | collective-permute-start | bytes 6291464 | tf_op jit(solution)/shard_map/ppermute | solution.py:1593
  290.8 25.9 %collective-permute-start.3 = (bf16[256,2048]{1,0:T(8,128)(2,1)}, bf16[256,2048]{1,0:T(8,128)(2,1)}, u32[]{:S(2)}, u32[]{:S(2)}) collective-permute-start(bf16[256,2048]{1,0:T(8,128)(2,1)} %constant_dynamic-slice_fusion.1), channel_id=1, source_target_pairs={{0,4},{4,0},{1,5},{5,1},{2,6},{6,2},{3,7},{7,3},{8,12},{12,8},{9,1... | collective-permute-start | bytes 3145736 | tf_op jit(solution)/shard_map/ppermute | solution.py:1631
  291.5 32.5 %copy-start.33 = (f32[2048]{0:T(1024)}, f32[2048]{0:T(1024)S(1)}, u32[]{:S(2)}) copy-start(f32[2048]{0:T(1024)S(1)} %convert_element_type.114) | copy-start | bytes 24580
  291.5 26.1 %copy-start.25 = (bf16[1024,2048]{1,0:T(8,128)(2,1)S(1)}, bf16[1024,2048]{1,0:T(8,128)(2,1)}, u32[]{:S(2)}) copy-start(bf16[1024,2048]{1,0:T(8,128)(2,1)} %copy-done.24) | copy-start | bytes 12582916
  291.6 70.5 %collective-permute-start.4 = (bf16[256,2,2048]{2,0,1:T(8,128)(2,1)}, bf16[256,2,2048]{2,0,1:T(8,128)(2,1)S(1)}, u32[]{:S(2)}, u32[]{:S(2)}) collective-permute-start(bf16[256,2,2048]{2,0,1:T(8,128)(2,1)} %collective-permute-done.2), channel_id=1, source_target_pairs={{0,16},{16,0},{8,24},{24,8},{1,17},{17,1},{9,25},{25,9},{2,18},{18... | collective-permute-start | bytes 6291464 | tf_op jit(solution)/shard_map/ppermute | solution.py:1660
  316.7 45.3 %collective-permute-start.5 = (bf16[256,2048]{1,0:T(8,128)(2,1)}, bf16[256,2048]{1,0:T(8,128)(2,1)S(1)}, u32[]{:S(2)}, u32[]{:S(2)}) collective-permute-start(bf16[256,2048]{1,0:T(8,128)(2,1)} %collective-permute-done.3.wd_far), channel_id=1, source_target_pairs={{0,16},{16,0},{8,24},{24,8},{1,17},{17,1},{9,25},{25,9},{2,18},{18... | collective-permute-start | bytes 3145736 | tf_op jit(solution)/shard_map/ppermute | solution.py:1661
  324.0 38.2 %copy-start.35 = (f32[512]{0:T(512)}, f32[512]{0:T(512)S(1)}, u32[]{:S(2)}) copy-start(f32[512]{0:T(512)S(1)} %get-tuple-element.171) | copy-start | bytes 6148
  362.2 3.8 collective-permute-start.10
  364.9 2.7 collective-permute-start.6
  365.0 5.6 collective-permute-start.7
  365.5 6.6 collective-permute-start.9
  365.6 8.1 collective-permute-start.11
  366.0 8.6 collective-permute-start.8
  676.0 4.3 collective-permute-start.14
  676.0 84.6 %collective-permute-start.13 = (bf16[2,256,3072]{2,1,0:T(8,128)(2,1)}, bf16[2,256,3072]{2,1,0:T(8,128)(2,1)S(1)}, u32[]{:S(2)}, u32[]{:S(2)}) collective-permute-start(bf16[2,256,3072]{2,1,0:T(8,128)(2,1)} %get-tuple-element.79), channel_id=1, source_target_pairs={{0,16},{16,0},{8,24},{24,8},{1,17},{17,1},{9,25},{25,9},{2,18},{18... | collective-permute-start | bytes 9437192 | tf_op jit(solution)/shard_map/ppermute | solution.py:1685
  677.5 84.3 %collective-permute-start.12 = (bf16[2,256,3072]{2,1,0:T(8,128)(2,1)}, bf16[2,256,3072]{2,1,0:T(8,128)(2,1)S(1)}, u32[]{:S(2)}, u32[]{:S(2)}) collective-permute-start(bf16[2,256,3072]{2,1,0:T(8,128)(2,1)} %get-tuple-element.77), channel_id=1, source_target_pairs={{0,4},{4,0},{1,5},{5,1},{2,6},{6,2},{3,7},{7,3},{8,12},{12,8},{9,1... | collective-permute-start | bytes 9437192 | tf_op jit(solution)/shard_map/ppermute | solution.py:1684
  688.2 63.2 %copy-start.13 = (bf16[1024,1024]{1,0:T(8,128)(2,1)S(1)}, bf16[1024,1024]{1,0:T(8,128)(2,1)}, u32[]{:S(2)}) copy-start(bf16[1024,1024]{1,0:T(8,128)(2,1)} %copy-done.12) | copy-start | bytes 6291460
  773.3 14.2 %copy-start.22 = (bf16[1024,2048]{1,0:T(8,128)(2,1)}, bf16[1024,2048]{1,0:T(8,128)(2,1)S(1)}, u32[]{:S(2)}) copy-start(bf16[1024,2048]{1,0:T(8,128)(2,1)S(1)} %convolution_convert_fusion.1) | copy-start | bytes 12582916
  773.6 13.9 %collective-permute-start.17 = (bf16[512,2048]{1,0:T(8,128)(2,1)S(1)}, bf16[512,2048]{1,0:T(8,128)(2,1)S(1)}, u32[]{:S(2)}, u32[]{:S(2)}) collective-permute-start(bf16[512,2048]{1,0:T(8,128)(2,1)S(1)} %constant_dynamic-slice_fusion), channel_id=1, source_target_pairs={{0,8},{8,0},{16,24},{24,16},{1,9},{9,1},{17,25},{25,17},{2,10},{10... | collective-permute-start | bytes 6291464 | tf_op jit(solution)/shard_map/ppermute | solution.py:1593
  775.0 37.1 %collective-permute-start.16 = (bf16[256,3072]{1,0:T(8,128)(2,1)}, bf16[256,3072]{1,0:T(8,128)(2,1)}, u32[]{:S(2)}, u32[]{:S(2)}) collective-permute-start(bf16[256,3072]{1,0:T(8,128)(2,1)} %dynamic-slice_bitcast_fusion), channel_id=1, source_target_pairs={{0,4},{4,0},{1,5},{5,1},{2,6},{6,2},{3,7},{7,3},{8,12},{12,8},{9,1... | collective-permute-start | bytes 4718600 | tf_op jit(solution)/shard_map/ppermute | solution.py:1709
  777.0 36.7 %collective-permute-start.15 = (bf16[256,3072]{1,0:T(8,128)(2,1)}, bf16[256,3072]{1,0:T(8,128)(2,1)}, u32[]{:S(2)}, u32[]{:S(2)}) collective-permute-start(bf16[256,3072]{1,0:T(8,128)(2,1)} %dynamic-slice_bitcast_fusion.1), channel_id=1, source_target_pairs={{0,16},{16,0},{8,24},{24,8},{1,17},{17,1},{9,25},{25,9},{2,18},{18... | collective-permute-start | bytes 4718600 | tf_op jit(solution)/shard_map/ppermute | solution.py:1708
  819.0 147.1 %copy-start.21 = (bf16[2,256,3072]{2,1,0:T(8,128)(2,1)S(1)}, bf16[2,256,3072]{2,1,0:T(8,128)(2,1)}, u32[]{:S(2)}) copy-start(bf16[2,256,3072]{2,1,0:T(8,128)(2,1)} %copy-done.20) | copy-start | bytes 9437188
  (44 other events, 222.8 us)
Sparse Core Ops, SparseCore 0:
  9.6 60.9 all-gather.2
  214.2 159.4 all-gather.4
  665.7 142.5 reduce-scatter.1

commit v11 on v10

--- a/solution.py
+++ b/solution.py
@@ -355,7 +355,7 @@
             pltpu.SemaphoreType.DMA((3,)),
         ],
         compiler_params=pltpu.CompilerParams(
-            collective_id=1, has_side_effects=True, vmem_limit_bytes=16 << 20
+            collective_id=1, has_side_effects=True, vmem_limit_bytes=60 << 20
         ),
         cost_estimate=pl.CostEstimate(flops=0, bytes_accessed=200 << 20, transcendentals=0),
         name="start_exchange",
@@ -1544,7 +1544,7 @@
             pltpu.SemaphoreType.DMA((5,)),
         ],
         compiler_params=pltpu.CompilerParams(
-            collective_id=3, has_side_effects=True, vmem_limit_bytes=40 << 20
+            collective_id=3, has_side_effects=True, vmem_limit_bytes=60 << 20
         ),
         cost_estimate=pl.CostEstimate(flops=0, bytes_accessed=300 << 20, transcendentals=0),
         name="finish",
@@ -1693,7 +1693,6 @@
     own_attn_grad = (RES_MULT * grad_resid).astype(jnp.bfloat16)
     grad_attn = joined(own_attn_grad, from_sibling(own_attn_grad), core)
     grad_heads = contract_local(grad_attn, weights_out).astype(jnp.bfloat16)
-    grad_out = token_outer(grad_attn, heads_out).astype(jnp.bfloat16)
     grad_projected = attend_back_fast(
         length, projected, grad_heads, cosines, sines, col_count
     )
@@ -1707,7 +1706,13 @@
 
     a_last = lax.ppermute(one_of(a_sum, 1 - high), "dp", OVER_Y)
     b_last = lax.ppermute(one_of(b_sum, 1 - row), "row", OVER_X)
-    grad_normed_one = summed_rows(expand_local(grad_projected, weights_qkv).astype(jnp.bfloat16))
+    input_partial = expand_local(grad_projected, weights_qkv).astype(jnp.bfloat16)
+    grad_attn, heads_out, input_partial = lax.optimization_barrier(
+        (grad_attn, heads_out, input_partial)
+    )
+    grad_out = token_outer(grad_attn, heads_out).astype(jnp.bfloat16)
+    grad_normed_one = summed_rows(input_partial)
+    attn_input, grad_normed_one = lax.optimization_barrier((attn_input, grad_normed_one))
     grad_qkv = token_outer(attn_input, grad_projected).astype(jnp.bfloat16)
     weighted_one = grad_normed_one * gain_one
     inner_one = jnp.sum(weighted_one * own_float, axis=1, keepdims=True)
@@ -1717,20 +1722,19 @@
         - own_float * scale_one**3 * inner_one / full_width
     ).astype(jnp.bfloat16)
     gain_one_part = jnp.sum(grad_normed_one * own_float * scale_one, axis=0)
-    a_last, b_last, own_input_grad = lax.optimization_barrier((a_last, b_last, own_input_grad))
-    gains = jnp.stack([gain_one_part, gain_two_part]).reshape(8, -1)
-    given_grad, given_out, sums_q, sums_o, gain_sums = finish(
-        own_input_grad, grad_qkv, grad_out, gains, out_cols, col_count
-    )
-    a_last, b_last, a_sum, b_sum, given_grad = lax.optimization_barrier(
-        (a_last, b_last, a_sum, b_sum, given_grad)
-    )
-    layer_out = jnp.where(given_live, given_out.astype(jnp.float32), 0.0)
-    input_grad = given_grad.astype(jnp.float32)
     a_total = one_of(a_sum, high).astype(jnp.float32) + a_last.astype(jnp.float32)
     b_total = one_of(b_sum, row).astype(jnp.float32) + b_last.astype(jnp.float32)
     sums_gate_up = jnp.stack([a_total[:, :hidden], b_total[:, :hidden]], axis=1)
     sums_down = jnp.concatenate([a_total[:, hidden:], b_total[:, hidden:]], axis=1)
+    sums_gate_up, sums_down, own_input_grad = lax.optimization_barrier(
+        (sums_gate_up, sums_down, own_input_grad)
+    )
+    gains = jnp.stack([gain_one_part, gain_two_part]).reshape(8, -1)
+    given_grad, given_out, sums_q, sums_o, gain_sums = finish(
+        own_input_grad, grad_qkv, grad_out, gains, out_cols, col_count
+    )
+    layer_out = jnp.where(given_live, given_out.astype(jnp.float32), 0.0)
+    input_grad = given_grad.astype(jnp.float32)
     grad_gain_attn, grad_gain_ffn = gain_sums.reshape(2, full_width)
 
     def both_cores(sums):

time: 1020 us -> 1010 us (level)
  starting transfers between devices: 27.4 us -> 10.1 us
  local copies, waits for them, and re-layouts: 71.4 us -> 54.8 us
  waiting for transfers between devices: 85 us -> 98.9 us
  Pallas kernels: 708 us -> 721 us
    ppermute x1, waiting for transfers between devices: 1.55 us -> 27.5 us  [one_sequence_body(): a_last = lax.ppermute(one_of(a_sum, 1 - high), 'dp', OVER_Y)]
    pallas_call x1, Pallas kernels: 118 us -> 133 us  [gather_weights(): pl.pallas_call(functools.partial(gather_kernel, cols), out_shape=(whole(o...]
    ppermute x1, waiting for transfers between devices: 17.4 us -> 1.93 us  [one_sequence_body(): b_last = lax.ppermute(one_of(b_sum, 1 - row), 'row', OVER_X)]
    ppermute x1, starting transfers between devices: 17.1 us -> 1.98 us  [one_sequence_body(): given = lax.ppermute(picked, ('dp', 'row'), CROSSED)]
    unnamed x111 -> x77, local copies, waits for them, and re-layouts: 26.1 us -> 12 us
  transfers between devices with their start and end apart: 21 -> 21, of which waited for: 10 -> 12; matrix products, arithmetic and copies ran while one was open for 11% -> 11% of each run, Pallas kernels for 27% -> 29%
where the time goes in v11:
time: 1010 us; the launch traced here: 992 us
  Pallas kernels  721 us (71%)
  waiting for transfers between devices  98.9 us (10%)
  local copies, waits for them, and re-layouts  54.8 us (5%)
  other arithmetic  51.7 us (5%)
  matrix products  32.8 us (3%)
  between operations  22.7 us (2%)
  starting transfers between devices  10.1 us (1%)
    pallas_call x1, Pallas kernels, feed_forward(): pl.pallas_call(functools.partial(ffn_kernel, cols), out_shape=(jax.ShapeD...  286 us
    pallas_call x1, Pallas kernels, finish(): pl.pallas_call(functools.partial(finish_kernel, cols), out_shape=(jax.Sha...  146 us
    pallas_call x1, Pallas kernels, gather_weights(): pl.pallas_call(functools.partial(gather_kernel, cols), out_shape=(whole(o...  133 us
    pallas_call x1, Pallas kernels, attend_back_fast(): pl.pallas_call(functools.partial(attend_back_kernel, block), grid=(groups...  63.3 us
    pallas_call x1, Pallas kernels, start_exchange(): pl.pallas_call(functools.partial(start_kernel, cols), out_shape=(jax.Shap...  47.1 us
    pallas_call x1, Pallas kernels, attend_fast(): pl.pallas_call(functools.partial(attend_kernel, block), grid=(groups,), o...  44.1 us
    ppermute x1, waiting for transfers between devices, one_sequence_body(): shared_down = lax.ppermute(far_down, 'dp', OVER_Y)  37.7 us
    ppermute x1, waiting for transfers between devices, one_sequence_body(): a_last = lax.ppermute(one_of(a_sum, 1 - high), 'dp', OVER_Y)  27.5 us
  transfers between devices with their start and end apart: 21, of which 12 were waited for; matrix products, arithmetic and copies ran while one was open for 11% of the time, Pallas kernels for 29%

profile of v11, /device:TPU:0, one launch (start us, length us, event | category | flops | bytes accessed | tf_op | source)
XLA Modules:
  0.0 991.6 jit_solution(17146211565572612305)
XLA Ops:
  19.2 47.1 %start_exchange.1 = (bf16[512,2048]{1,0:T(8,128)(2,1)}, bf16[1024,2048]{1,0:T(8,128)(2,1)}) custom-call(bf16[4,512,512]{2,1,0:T(8,128)(2,1)} %tok_ref.1, f32[1,2048]{1,0:T(1,128)} %bitcast.91), custom_call_target="tpu_custom_call" | custom-call | bytes 209715200 | tf_op jit(solution)/shard_map/start_exchange/pallas_call | solution.py:342
  66.3 4.3 all-gather.3.cloned.1.call-done
  76.8 2.1 constant_dynamic-slice_fusion.4
  79.9 133.5 %gather_weights.1 = (bf16[2048,1536]{1,0:T(8,128)(2,1)}, bf16[2048,1024]{1,0:T(8,128)(2,1)}) custom-call(bf16[1024,384]{1,0:T(8,128)(2,1)} %pad_maximum_fusion.2.q_ref, bf16[1024,256]{1,0:T(8,128)(2,1)} %get-tuple-element.178.o_ref, bf16[4,512,512]{2,1,0:T(8,128)(2,1)} %copy-done.8), custom_call_target="tpu_custom_call" | custom-call | bytes 314572800 | tf_op jit(solution)/shard_map/gather_weights/pallas_call | solution.py:462
  215.8 10.6 %copy.53 = bf16[1024,2,2048]{2,0,1:T(8,128)(2,1)} copy(bf16[1024,2,2048]{2,1,0:T(2,128)(2,1)} %param.20) | data formatting | bytes 16777216 | tf_op jit(solution)/shard_map/optimization_barrier | solution.py:1625
  226.4 3.4 constant_dynamic-slice_fusion.2
  229.9 44.1 %attend.1 = (bf16[1024,1536]{1,0:T(8,128)(2,1)}, bf16[1024,1024]{1,0:T(8,128)(2,1)S(1)}) custom-call(s32[1]{0:T(128)} %dynamic_slice.83.len_ref, bf16[1024,2048]{1,0:T(8,128)(2,1)} %get-tuple-element.88.a_ref, bf16[2048,1536]{1,0:T(8,128)(2,1)} %get-tuple-element.60.w_ref, f32[1024,256]{1,0:T(8,128)S(1)} %concatenate.38.cos_ref, ...), custom_call_target="tpu_custom_call" | custom-call | flops 10737418240 | bytes 13631488 | tf_op jit(solution)/shard_map/attend/pallas_call | solution.py:573
  274.0 4.8 convolution_convert_fusion.3
  284.6 7.1 slice_bitcast_fusion
  291.7 16.8 %collective-permute-done.3.wd_far = bf16[256,2048]{1,0:T(8,128)(2,1)} collective-permute-done((bf16[256,2048]{1,0:T(8,128)(2,1)S(1)}, bf16[256,2048]{1,0:T(8,128)(2,1)}, u32[]{:S(2)}, u32[]{:S(2)}) %collective-permute-start.3) | collective-permute-done | bytes 1048608 | tf_op jit(solution)/shard_map/ppermute | solution.py:1631
  309.1 5.2 fusion.10
  317.2 37.7 %collective-permute-done.5.wd_far_y = bf16[256,2048]{1,0:T(8,128)(2,1)} collective-permute-done((bf16[256,2048]{1,0:T(8,128)(2,1)}, bf16[256,2048]{1,0:T(8,128)(2,1)}, u32[]{:S(2)}, u32[]{:S(2)}) %collective-permute-start.5) | collective-permute-done | bytes 1048608 | tf_op jit(solution)/shard_map/ppermute | solution.py:1661
  356.1 3.5 slice_bitcast_fusion.6
  369.4 286.0 %feed_forward.1 = (bf16[4,512,2048]{2,1,0:T(8,128)(2,1)}, bf16[4,512,4096]{2,1,0:T(8,128)(2,1)}, bf16[4,512,2048]{2,1,0:T(8,128)(2,1)}, bf16[3,512,2048]{2,1,0:T...) custom-call(bf16[512,2048]{1,0:T(8,128)(2,1)} %multiply_convert_fusi, ...), custom_call_target="tpu_custom_call" | custom-call | flops 154618822656 | bytes 838860800 | tf_op jit(solution)/shard_map/feed_forward/pallas_call | solution.py:1206
  655.4 4.8 convert_reduce_fusion
  661.3 4.8 multiply_convert_fusion
  668.3 2.3 collective-permute-done.14
  670.6 5.1 maximum_select_fusion
  675.8 4.7 convolution_convert_fusion.4.dz_ref
  680.5 63.3 %attend_back.1 = bf16[1024,1536]{1,0:T(8,128)(2,1)} custom-call(s32[1]{0:T(128)} %dynamic_slice.83.len_ref, bf16[1024,1536]{1,0:T(8,128)(2,1)} %get-tuple-element.80.qkv_ref, bf16[1024,1024]{1,0:T(8,128)(2,1)S(1)} %convolution_convert_fusion.4.dz_ref, f32[1024,256]{1,0:T(8,128)S(1)} %concatenate.38.cos_ref, f32[1024,256]{1,0:T(8,128)S(1)} %concatenate.40.sin_ref), custom_call_target="tpu_custom_call" | custom-call | flops 10737418240 | bytes 8388608 | tf_op jit(solution)/shard_map/attend_back/pallas_call | solution.py:680
  743.9 3.2 add_convert_fusion
  748.9 8.3 convolution_convert_fusion.1
  760.1 6.2 convolution_convert_fusion.2
  766.4 27.5 %collective-permute-done.15 = bf16[256,3072]{1,0:T(8,128)(2,1)S(1)} collective-permute-done((bf16[256,3072]{1,0:T(8,128)(2,1)S(1)}, bf16[256,3072]{1,0:T(8,128)(2,1)S(1)}, u32[]{:S(2)}, u32[]{:S(2)}) %collective-permute-start.15) | collective-permute-done | bytes 1572896 | tf_op jit(solution)/shard_map/ppermute | solution.py:1707
  798.9 2.2 pad_maximum_fusion
  802.0 2.0 copy-done.4
  805.9 5.5 fusion.4.ig_ref
  811.5 5.2 copy.57
  816.7 8.8 convolution_convert_fusion
  825.5 146.5 %finish.1 = (bf16[4,512,512]{2,1,0:T(8,128)(2,1)}, bf16[4,512,512]{2,1,0:T(8,128)(2,1)}, f32[2,256,384]{2,1,0:T(8,128)}, f32[2,256,256]{2,1,0:T(8,128)}, f32[8,512]{1,0:T(8,128)}) custom-call(bf16[512,2048]{1,0:T(8,128)(2,1)} %fusion.4.ig_ref, bf16[2,2,2,256,1536]{4,3,2,1,0:T(8,128)(2,1)} %bitcast.85, bf16[2,2,2,256,1024]{4,3,2,1,0:T(8,128)(2,1)} %bitcast.86, ...), custom_call_target="tpu_custom_call" | custom-call | bytes 314572800 | tf_op jit(solution)/shard_map/finish/pallas_call | solution.py:1521
  976.7 2.6 convert_element_type.141
  979.3 2.3 convert_select_fusion
  (173 shorter events, 57.1 us)
Async XLA Ops:
  7.2 63.4 %all-gather.3.cloned.1.call-start = ((), (), s32[]{:S(2)}) async-start(), calls=%async_computation.1 | async-start | bytes 10485760 | tf_op jit(solution)/shard_map/all_gather | solution.py:1615
  7.9 361.4 %all-gather.5.cloned.1.call-start = ((), (), s32[]{:S(2)}) async-start(), calls=%async_computation.2 | async-start | bytes 10485760 | tf_op jit(solution)/shard_map/all_gather | solution.py:1622
  66.3 6.5 copy-start.22
  72.8 7.1 copy-start.8
  72.8 140.6 %collective-permute-start = (bf16[4,512,512]{2,1,0:T(8,128)(2,1)S(1)}, bf16[4,512,512]{2,1,0:T(8,128)(2,1)}, u32[]{:S(2)}, u32[]{:S(2)}) collective-permute-start(bf16[4,512,512]{2,1,0:T(8,128)(2,1)S(1)} %maximum_select_fusion.1.after_ref), channel_id=1, source_target_pairs={{0,0},{4,8},{8,4},{12,12},{16,16},{20,24},{24,20},{28,28},{1,1},{5... | collective-permute-start | bytes 6291464 | tf_op jit(solution)/shard_map/ppermute | solution.py:1619
  78.9 134.7 %copy-start.32 = (s32[16]{0:T(128)S(1)}, s32[16]{0:T(128)}, u32[]{:S(2)}) copy-start(s32[16]{0:T(128)} %param.13) | copy-start | bytes 196
  213.5 612.0 %reduce-scatter.2.cloned.1.call-start = ((), (), s32[]{:S(2)}) async-start(), calls=%async_computation.3 | async-start | bytes 10485760 | tf_op jit(solution)/shard_map/reduce_scatter | solution.py:1679
  229.9 44.2 %copy-start.29 = (bf16[2048,1024]{1,0:T(8,128)(2,1)S(1)}, bf16[2048,1024]{1,0:T(8,128)(2,1)}, u32[]{:S(2)}) copy-start(bf16[2048,1024]{1,0:T(8,128)(2,1)} %get-tuple-element.64) | copy-start | bytes 12582916
  229.9 54.4 %collective-permute-start.2 = (bf16[256,2,2048]{2,0,1:T(8,128)(2,1)}, bf16[256,2,2048]{2,0,1:T(8,128)(2,1)}, u32[]{:S(2)}, u32[]{:S(2)}) collective-permute-start(bf16[256,2,2048]{2,0,1:T(8,128)(2,1)} %constant_dynamic-slice_fusion.2), channel_id=1, source_target_pairs={{0,4},{4,0},{1,5},{5,1},{2,6},{6,2},{3,7},{7,3},{8,12},{12,8},{9,1... | collective-permute-start | bytes 6291464 | tf_op jit(solution)/shard_map/ppermute | solution.py:1630
  281.5 27.6 %collective-permute-start.1 = (bf16[512,2048]{1,0:T(8,128)(2,1)}, bf16[512,2048]{1,0:T(8,128)(2,1)}, u32[]{:S(2)}, u32[]{:S(2)}) collective-permute-start(bf16[512,2048]{1,0:T(8,128)(2,1)} %constant_dynamic-slice_fusion.3), channel_id=1, source_target_pairs={{0,8},{8,0},{16,24},{24,16},{1,9},{9,1},{17,25},{25,17},{2,10},{10... | collective-permute-start | bytes 6291464 | tf_op jit(solution)/shard_map/ppermute | solution.py:1593
  282.8 25.7 %collective-permute-start.3 = (bf16[256,2048]{1,0:T(8,128)(2,1)S(1)}, bf16[256,2048]{1,0:T(8,128)(2,1)}, u32[]{:S(2)}, u32[]{:S(2)}) collective-permute-start(bf16[256,2048]{1,0:T(8,128)(2,1)S(1)} %constant_dynamic-slice_fusion.1), channel_id=1, source_target_pairs={{0,4},{4,0},{1,5},{5,1},{2,6},{6,2},{3,7},{7,3},{8,12},{12,8},{9,1... | collective-permute-start | bytes 3145736 | tf_op jit(solution)/shard_map/ppermute | solution.py:1631
  284.3 31.2 %copy-start.18 = (f32[2048]{0:T(1024)}, f32[2048]{0:T(1024)S(1)}, u32[]{:S(2)}) copy-start(f32[2048]{0:T(1024)S(1)} %convert_element_type.114) | copy-start | bytes 24580
  284.3 24.8 %copy-start.5 = (bf16[512,2048]{1,0:T(8,128)(2,1)S(1)}, bf16[512,2048]{1,0:T(8,128)(2,1)}, u32[]{:S(2)}) copy-start(bf16[512,2048]{1,0:T(8,128)(2,1)} %get-tuple-element.54) | copy-start | bytes 6291460
  284.3 24.8 %copy-start.10 = (bf16[1024,2048]{1,0:T(8,128)(2,1)S(1)}, bf16[1024,2048]{1,0:T(8,128)(2,1)}, u32[]{:S(2)}) copy-start(bf16[1024,2048]{1,0:T(8,128)(2,1)} %copy-done.9) | copy-start | bytes 12582916
  284.3 70.6 %collective-permute-start.4 = (bf16[256,2,2048]{2,0,1:T(8,128)(2,1)}, bf16[256,2,2048]{2,0,1:T(8,128)(2,1)S(1)}, u32[]{:S(2)}, u32[]{:S(2)}) collective-permute-start(bf16[256,2,2048]{2,0,1:T(8,128)(2,1)} %collective-permute-done.2), channel_id=1, source_target_pairs={{0,16},{16,0},{8,24},{24,8},{1,17},{17,1},{9,25},{25,9},{2,18},{18... | collective-permute-start | bytes 6291464 | tf_op jit(solution)/shard_map/ppermute | solution.py:1660
  308.5 46.4 %collective-permute-start.5 = (bf16[256,2048]{1,0:T(8,128)(2,1)}, bf16[256,2048]{1,0:T(8,128)(2,1)}, u32[]{:S(2)}, u32[]{:S(2)}) collective-permute-start(bf16[256,2048]{1,0:T(8,128)(2,1)} %collective-permute-done.3.wd_far), channel_id=1, source_target_pairs={{0,16},{16,0},{8,24},{24,8},{1,17},{17,1},{9,25},{25,9},{2,18},{18... | collective-permute-start | bytes 3145736 | tf_op jit(solution)/shard_map/ppermute | solution.py:1661
  315.5 39.5 %copy-start.20 = (f32[512]{0:T(512)}, f32[512]{0:T(512)S(1)}, u32[]{:S(2)}) copy-start(f32[512]{0:T(512)S(1)} %get-tuple-element.171) | copy-start | bytes 6148
  356.1 13.2 %copy-start.16 = (bf16[256,2048]{1,0:T(8,128)(2,1)}, bf16[256,2048]{1,0:T(8,128)(2,1)S(1)}, u32[]{:S(2)}) copy-start(bf16[256,2048]{1,0:T(8,128)(2,1)S(1)} %get-tuple-element.150.wu_far_y) | copy-start | bytes 3145732
  356.1 4.5 collective-permute-start.10
  359.6 3.0 collective-permute-start.6
  359.8 4.4 collective-permute-start.7
  360.1 5.5 collective-permute-start.9
  360.3 6.8 collective-permute-start.11
  361.6 7.0 collective-permute-start.8
  666.1 4.5 collective-permute-start.14
  666.2 77.7 %collective-permute-start.13 = (bf16[2,256,3072]{2,1,0:T(8,128)(2,1)}, bf16[2,256,3072]{2,1,0:T(8,128)(2,1)}, u32[]{:S(2)}, u32[]{:S(2)}) collective-permute-start(bf16[2,256,3072]{2,1,0:T(8,128)(2,1)} %get-tuple-element.79), channel_id=1, source_target_pairs={{0,16},{16,0},{8,24},{24,8},{1,17},{17,1},{9,25},{25,9},{2,18},{18... | collective-permute-start | bytes 9437192 | tf_op jit(solution)/shard_map/ppermute | solution.py:1685
  667.8 7.9 copy-start.30
  667.8 79.3 %collective-permute-start.12 = (bf16[2,256,3072]{2,1,0:T(8,128)(2,1)}, bf16[2,256,3072]{2,1,0:T(8,128)(2,1)S(1)}, u32[]{:S(2)}, u32[]{:S(2)}) collective-permute-start(bf16[2,256,3072]{2,1,0:T(8,128)(2,1)} %get-tuple-element.77), channel_id=1, source_target_pairs={{0,4},{4,0},{1,5},{5,1},{2,6},{6,2},{3,7},{7,3},{8,12},{12,8},{9,1... | collective-permute-start | bytes 9437192 | tf_op jit(solution)/shard_map/ppermute | solution.py:1684
  680.5 63.4 %copy-start.12 = (bf16[2,256,3072]{2,1,0:T(8,128)(2,1)S(1)}, bf16[2,256,3072]{2,1,0:T(8,128)(2,1)}, u32[]{:S(2)}) copy-start(bf16[2,256,3072]{2,1,0:T(8,128)(2,1)} %get-tuple-element.78) | copy-start | bytes 9437188
  757.4 36.5 %collective-permute-start.15 = (bf16[256,3072]{1,0:T(8,128)(2,1)S(1)}, bf16[256,3072]{1,0:T(8,128)(2,1)S(1)}, u32[]{:S(2)}, u32[]{:S(2)}) collective-permute-start(bf16[256,3072]{1,0:T(8,128)(2,1)S(1)} %dynamic-slice_bitcast_fusion.1), channel_id=1, source_target_pairs={{0,16},{16,0},{8,24},{24,8},{1,17},{17,1},{9,25},{25,9},{2,18},{18... | collective-permute-start | bytes 4718600 | tf_op jit(solution)/shard_map/ppermute | solution.py:1707
  759.2 41.9 %collective-permute-start.17 = (bf16[512,2048]{1,0:T(8,128)(2,1)S(1)}, bf16[512,2048]{1,0:T(8,128)(2,1)S(1)}, u32[]{:S(2)}, u32[]{:S(2)}) collective-permute-start(bf16[512,2048]{1,0:T(8,128)(2,1)S(1)} %constant_dynamic-slice_fusion), channel_id=1, source_target_pairs={{0,8},{8,0},{16,24},{24,16},{1,9},{9,1},{17,25},{25,17},{2,10},{10... | collective-permute-start | bytes 6291464 | tf_op jit(solution)/shard_map/ppermute | solution.py:1593
  759.4 36.8 %collective-permute-start.16 = (bf16[256,3072]{1,0:T(8,128)(2,1)S(1)}, bf16[256,3072]{1,0:T(8,128)(2,1)S(1)}, u32[]{:S(2)}, u32[]{:S(2)}) collective-permute-start(bf16[256,3072]{1,0:T(8,128)(2,1)S(1)} %dynamic-slice_bitcast_fusion), channel_id=1, source_target_pairs={{0,4},{4,0},{1,5},{5,1},{2,6},{6,2},{3,7},{7,3},{8,12},{12,8},{9,1... | collective-permute-start | bytes 4718600 | tf_op jit(solution)/shard_map/ppermute | solution.py:1708
  (25 other events, 89.0 us)
Sparse Core Ops, SparseCore 0:
  9.6 60.9 all-gather.2
  213.6 155.6 all-gather.4
  666.3 142.8 reduce-scatter.1

commit v12 on v11

--- a/solution.py
+++ b/solution.py
@@ -1722,6 +1722,9 @@
         - own_float * scale_one**3 * inner_one / full_width
     ).astype(jnp.bfloat16)
     gain_one_part = jnp.sum(grad_normed_one * own_float * scale_one, axis=0)
+    a_last, b_last, grad_qkv, own_input_grad = lax.optimization_barrier(
+        (a_last, b_last, grad_qkv, own_input_grad)
+    )
     a_total = one_of(a_sum, high).astype(jnp.float32) + a_last.astype(jnp.float32)
     b_total = one_of(b_sum, row).astype(jnp.float32) + b_last.astype(jnp.float32)
     sums_gate_up = jnp.stack([a_total[:, :hidden], b_total[:, :hidden]], axis=1)

time: 1010 us -> 1000 us (0.990)
  waiting for transfers between devices: 98.9 us -> 76.5 us
    ppermute x1, waiting for transfers between devices: 27.5 us -> 3.43 us  [one_sequence_body(): a_last = lax.ppermute(one_of(a_sum, 1 - high), 'dp', OVER_Y)]
  transfers between devices with their start and end apart: 21 -> 21, of which waited for: 12 -> 12; matrix products, arithmetic and copies ran while one was open for 11% -> 12% of each run, Pallas kernels for 29% -> 29%
where the time goes in v12:
time: 1000 us; the launch traced here: 985 us
  Pallas kernels  722 us (72%)
  waiting for transfers between devices  76.5 us (8%)
  local copies, waits for them, and re-layouts  64.4 us (6%)
  other arithmetic  57.3 us (6%)
  matrix products  31.7 us (3%)
  between operations  22.7 us (2%)
  starting transfers between devices  10.4 us (1%)
    pallas_call x1, Pallas kernels, feed_forward(): pl.pallas_call(functools.partial(ffn_kernel, cols), out_shape=(jax.ShapeD...  286 us
    pallas_call x1, Pallas kernels, finish(): pl.pallas_call(functools.partial(finish_kernel, cols), out_shape=(jax.Sha...  148 us
    pallas_call x1, Pallas kernels, gather_weights(): pl.pallas_call(functools.partial(gather_kernel, cols), out_shape=(whole(o...  133 us
    pallas_call x1, Pallas kernels, attend_back_fast(): pl.pallas_call(functools.partial(attend_back_kernel, block), grid=(groups...  63.3 us
    pallas_call x1, Pallas kernels, start_exchange(): pl.pallas_call(functools.partial(start_kernel, cols), out_shape=(jax.Shap...  47.1 us
    pallas_call x1, Pallas kernels, attend_fast(): pl.pallas_call(functools.partial(attend_kernel, block), grid=(groups,), o...  44.1 us
    ppermute x1, waiting for transfers between devices, one_sequence_body(): shared_down = lax.ppermute(far_down, 'dp', OVER_Y)  37.7 us
  transfers between devices with their start and end apart: 21, of which 12 were waited for; matrix products, arithmetic and copies ran while one was open for 12% of the time, Pallas kernels for 29%

profile of v12, /device:TPU:0, one launch (start us, length us, event | category | flops | bytes accessed | tf_op | source)
XLA Modules:
  0.0 984.6 jit_solution(5108373372612184536)
XLA Ops:
  19.2 47.1 %start_exchange.1 = (bf16[512,2048]{1,0:T(8,128)(2,1)}, bf16[1024,2048]{1,0:T(8,128)(2,1)}) custom-call(bf16[4,512,512]{2,1,0:T(8,128)(2,1)} %tok_ref.1, f32[1,2048]{1,0:T(1,128)} %bitcast.91), custom_call_target="tpu_custom_call" | custom-call | bytes 209715200 | tf_op jit(solution)/shard_map/start_exchange/pallas_call | solution.py:342
  66.3 4.3 all-gather.3.cloned.1.call-done
  79.9 133.5 %gather_weights.1 = (bf16[2048,1536]{1,0:T(8,128)(2,1)}, bf16[2048,1024]{1,0:T(8,128)(2,1)}) custom-call(bf16[1024,384]{1,0:T(8,128)(2,1)} %pad_maximum_fusion.2.q_ref, bf16[1024,256]{1,0:T(8,128)(2,1)} %get-tuple-element.186.o_ref, bf16[4,512,512]{2,1,0:T(8,128)(2,1)} %copy-done.9), custom_call_target="tpu_custom_call" | custom-call | bytes 314572800 | tf_op jit(solution)/shard_map/gather_weights/pallas_call | solution.py:462
  215.8 10.6 %copy.53 = bf16[1024,2,2048]{2,0,1:T(8,128)(2,1)} copy(bf16[1024,2,2048]{2,1,0:T(2,128)(2,1)} %param.20) | data formatting | bytes 16777216 | tf_op jit(solution)/shard_map/optimization_barrier | solution.py:1625
  226.4 3.4 constant_dynamic-slice_fusion.2
  229.9 44.1 %attend.1 = (bf16[1024,1536]{1,0:T(8,128)(2,1)}, bf16[1024,1024]{1,0:T(8,128)(2,1)S(1)}) custom-call(s32[1]{0:T(128)} %dynamic_slice.83.len_ref, bf16[1024,2048]{1,0:T(8,128)(2,1)} %get-tuple-element.90.a_ref, bf16[2048,1536]{1,0:T(8,128)(2,1)} %get-tuple-element.64.w_ref, f32[1024,256]{1,0:T(8,128)S(1)} %concatenate.38.cos_ref, ...), custom_call_target="tpu_custom_call" | custom-call | flops 10737418240 | bytes 13631488 | tf_op jit(solution)/shard_map/attend/pallas_call | solution.py:573
  274.0 4.8 convolution_convert_fusion.3
  284.6 7.1 slice_bitcast_fusion
  291.7 16.8 %collective-permute-done.3.wd_far = bf16[256,2048]{1,0:T(8,128)(2,1)} collective-permute-done((bf16[256,2048]{1,0:T(8,128)(2,1)S(1)}, bf16[256,2048]{1,0:T(8,128)(2,1)}, u32[]{:S(2)}, u32[]{:S(2)}) %collective-permute-start.3) | collective-permute-done | bytes 1048608 | tf_op jit(solution)/shard_map/ppermute | solution.py:1631
  309.1 5.2 fusion.10
  317.2 37.7 %collective-permute-done.5.wd_far_y = bf16[256,2048]{1,0:T(8,128)(2,1)} collective-permute-done((bf16[256,2048]{1,0:T(8,128)(2,1)}, bf16[256,2048]{1,0:T(8,128)(2,1)}, u32[]{:S(2)}, u32[]{:S(2)}) %collective-permute-start.5) | collective-permute-done | bytes 1048608 | tf_op jit(solution)/shard_map/ppermute | solution.py:1661
  356.1 3.5 slice_bitcast_fusion.6
  369.4 286.0 %feed_forward.1 = (bf16[4,512,2048]{2,1,0:T(8,128)(2,1)}, bf16[4,512,4096]{2,1,0:T(8,128)(2,1)}, bf16[4,512,2048]{2,1,0:T(8,128)(2,1)}, bf16[3,512,2048]{2,1,0:T...) custom-call(bf16[512,2048]{1,0:T(8,128)(2,1)} %multiply_convert_fusi, ...), custom_call_target="tpu_custom_call" | custom-call | flops 154618822656 | bytes 838860800 | tf_op jit(solution)/shard_map/feed_forward/pallas_call | solution.py:1206
  655.4 4.8 convert_reduce_fusion
  661.3 4.8 multiply_convert_fusion
  670.7 4.8 maximum_select_fusion
  675.5 4.7 convolution_convert_fusion.4.dz_ref
  680.2 63.3 %attend_back.1 = bf16[1024,1536]{1,0:T(8,128)(2,1)} custom-call(s32[1]{0:T(128)} %dynamic_slice.83.len_ref, bf16[1024,1536]{1,0:T(8,128)(2,1)} %get-tuple-element.84.qkv_ref, bf16[1024,1024]{1,0:T(8,128)(2,1)S(1)} %convolution_convert_fusion.4.dz_ref, f32[1024,256]{1,0:T(8,128)S(1)} %concatenate.38.cos_ref, f32[1024,256]{1,0:T(8,128)S(1)} %concatenate.40.sin_ref), custom_call_target="tpu_custom_call" | custom-call | flops 10737418240 | bytes 8388608 | tf_op jit(solution)/shard_map/attend_back/pallas_call | solution.py:680
  743.5 4.9 add_convert_fusion
  748.5 2.8 add_convert_fusion.1
  751.8 6.9 convolution_convert_fusion.1
  762.5 2.8 dynamic-slice_bitcast_fusion
  766.2 2.7 dynamic-slice_bitcast_fusion.1
  770.5 6.2 convolution_convert_fusion.2
  776.7 2.5 convert_add_fusion.2
  783.1 5.3 fusion.4.ig_ref
  789.6 9.1 convolution_convert_fusion
  798.7 3.6 collective-permute-done.16
  802.2 3.4 collective-permute-done.15
  812.1 5.3 copy.57
  817.4 147.7 %finish.1 = (bf16[4,512,512]{2,1,0:T(8,128)(2,1)}, bf16[4,512,512]{2,1,0:T(8,128)(2,1)}, f32[2,256,384]{2,1,0:T(8,128)}, f32[2,256,256]{2,1,0:T(8,128)}, f32[8,512]{1,0:T(8,128)}) custom-call(bf16[512,2048]{1,0:T(8,128)(2,1)} %fusion.4.ig_ref, bf16[2,2,2,256,1536]{4,3,2,1,0:T(8,128)(2,1)} %bitcast.85, bf16[2,2,2,256,1024]{4,3,2,1,0:T(8,128)(2,1)} %bitcast.86, ...), custom_call_target="tpu_custom_call" | custom-call | bytes 314572800 | tf_op jit(solution)/shard_map/finish/pallas_call | solution.py:1521
  969.8 2.6 convert_element_type.141
  (185 shorter events, 69.6 us)
Async XLA Ops:
  7.2 63.4 %all-gather.3.cloned.1.call-start = ((), (), s32[]{:S(2)}) async-start(), calls=%async_computation.1 | async-start | bytes 10485760 | tf_op jit(solution)/shard_map/all_gather | solution.py:1615
  7.9 361.4 %all-gather.5.cloned.1.call-start = ((), (), s32[]{:S(2)}) async-start(), calls=%async_computation.2 | async-start | bytes 10485760 | tf_op jit(solution)/shard_map/all_gather | solution.py:1622
  72.8 140.6 %collective-permute-start = (bf16[4,512,512]{2,1,0:T(8,128)(2,1)S(1)}, bf16[4,512,512]{2,1,0:T(8,128)(2,1)}, u32[]{:S(2)}, u32[]{:S(2)}) collective-permute-start(bf16[4,512,512]{2,1,0:T(8,128)(2,1)S(1)} %maximum_select_fusion.1.after_ref), channel_id=1, source_target_pairs={{0,0},{4,8},{8,4},{12,12},{16,16},{20,24},{24,20},{28,28},{1,1},{5... | collective-permute-start | bytes 6291464 | tf_op jit(solution)/shard_map/ppermute | solution.py:1619
  78.9 134.7 %copy-start.37 = (s32[16]{0:T(128)S(1)}, s32[16]{0:T(128)}, u32[]{:S(2)}) copy-start(s32[16]{0:T(128)} %param.13) | copy-start | bytes 196
  213.5 603.9 %reduce-scatter.2.cloned.1.call-start = ((), (), s32[]{:S(2)}) async-start(), calls=%async_computation.3 | async-start | bytes 10485760 | tf_op jit(solution)/shard_map/reduce_scatter | solution.py:1679
  229.9 44.2 %copy-start.34 = (bf16[2048,1024]{1,0:T(8,128)(2,1)S(1)}, bf16[2048,1024]{1,0:T(8,128)(2,1)}, u32[]{:S(2)}) copy-start(bf16[2048,1024]{1,0:T(8,128)(2,1)} %get-tuple-element.68) | copy-start | bytes 12582916
  229.9 54.4 %collective-permute-start.2 = (bf16[256,2,2048]{2,0,1:T(8,128)(2,1)}, bf16[256,2,2048]{2,0,1:T(8,128)(2,1)}, u32[]{:S(2)}, u32[]{:S(2)}) collective-permute-start(bf16[256,2,2048]{2,0,1:T(8,128)(2,1)} %constant_dynamic-slice_fusion.2), channel_id=1, source_target_pairs={{0,4},{4,0},{1,5},{5,1},{2,6},{6,2},{3,7},{7,3},{8,12},{12,8},{9,1... | collective-permute-start | bytes 6291464 | tf_op jit(solution)/shard_map/ppermute | solution.py:1630
  281.5 27.6 %collective-permute-start.1 = (bf16[512,2048]{1,0:T(8,128)(2,1)}, bf16[512,2048]{1,0:T(8,128)(2,1)}, u32[]{:S(2)}, u32[]{:S(2)}) collective-permute-start(bf16[512,2048]{1,0:T(8,128)(2,1)} %constant_dynamic-slice_fusion.3), channel_id=1, source_target_pairs={{0,8},{8,0},{16,24},{24,16},{1,9},{9,1},{17,25},{25,17},{2,10},{10... | collective-permute-start | bytes 6291464 | tf_op jit(solution)/shard_map/ppermute | solution.py:1593
  282.8 25.7 %collective-permute-start.3 = (bf16[256,2048]{1,0:T(8,128)(2,1)S(1)}, bf16[256,2048]{1,0:T(8,128)(2,1)}, u32[]{:S(2)}, u32[]{:S(2)}) collective-permute-start(bf16[256,2048]{1,0:T(8,128)(2,1)S(1)} %constant_dynamic-slice_fusion.1), channel_id=1, source_target_pairs={{0,4},{4,0},{1,5},{5,1},{2,6},{6,2},{3,7},{7,3},{8,12},{12,8},{9,1... | collective-permute-start | bytes 3145736 | tf_op jit(solution)/shard_map/ppermute | solution.py:1631
  284.3 31.2 %copy-start.23 = (f32[2048]{0:T(1024)}, f32[2048]{0:T(1024)S(1)}, u32[]{:S(2)}) copy-start(f32[2048]{0:T(1024)S(1)} %convert_element_type.114) | copy-start | bytes 24580
  284.3 24.8 %copy-start.5 = (bf16[512,2048]{1,0:T(8,128)(2,1)S(1)}, bf16[512,2048]{1,0:T(8,128)(2,1)}, u32[]{:S(2)}) copy-start(bf16[512,2048]{1,0:T(8,128)(2,1)} %get-tuple-element.58) | copy-start | bytes 6291460
  284.3 24.8 %copy-start.15 = (bf16[1024,2048]{1,0:T(8,128)(2,1)S(1)}, bf16[1024,2048]{1,0:T(8,128)(2,1)}, u32[]{:S(2)}) copy-start(bf16[1024,2048]{1,0:T(8,128)(2,1)} %copy-done.14) | copy-start | bytes 12582916
  284.3 70.6 %collective-permute-start.4 = (bf16[256,2,2048]{2,0,1:T(8,128)(2,1)}, bf16[256,2,2048]{2,0,1:T(8,128)(2,1)S(1)}, u32[]{:S(2)}, u32[]{:S(2)}) collective-permute-start(bf16[256,2,2048]{2,0,1:T(8,128)(2,1)} %collective-permute-done.2), channel_id=1, source_target_pairs={{0,16},{16,0},{8,24},{24,8},{1,17},{17,1},{9,25},{25,9},{2,18},{18... | collective-permute-start | bytes 6291464 | tf_op jit(solution)/shard_map/ppermute | solution.py:1660
  308.5 46.4 %collective-permute-start.5 = (bf16[256,2048]{1,0:T(8,128)(2,1)}, bf16[256,2048]{1,0:T(8,128)(2,1)}, u32[]{:S(2)}, u32[]{:S(2)}) collective-permute-start(bf16[256,2048]{1,0:T(8,128)(2,1)} %collective-permute-done.3.wd_far), channel_id=1, source_target_pairs={{0,16},{16,0},{8,24},{24,8},{1,17},{17,1},{9,25},{25,9},{2,18},{18... | collective-permute-start | bytes 3145736 | tf_op jit(solution)/shard_map/ppermute | solution.py:1661
  315.5 39.5 %copy-start.25 = (f32[512]{0:T(512)}, f32[512]{0:T(512)S(1)}, u32[]{:S(2)}) copy-start(f32[512]{0:T(512)S(1)} %get-tuple-element.179) | copy-start | bytes 6148
  356.1 13.2 %copy-start.21 = (bf16[256,2048]{1,0:T(8,128)(2,1)}, bf16[256,2048]{1,0:T(8,128)(2,1)S(1)}, u32[]{:S(2)}) copy-start(bf16[256,2048]{1,0:T(8,128)(2,1)S(1)} %get-tuple-element.158.wu_far_y) | copy-start | bytes 3145732
  356.1 4.5 collective-permute-start.10
  359.6 3.0 collective-permute-start.6
  359.7 4.4 collective-permute-start.7
  360.1 5.5 collective-permute-start.9
  360.3 6.9 collective-permute-start.11
  361.6 7.0 collective-permute-start.8
  666.1 4.5 collective-permute-start.14
  666.2 77.3 %collective-permute-start.13 = (bf16[2,256,3072]{2,1,0:T(8,128)(2,1)}, bf16[2,256,3072]{2,1,0:T(8,128)(2,1)}, u32[]{:S(2)}, u32[]{:S(2)}) collective-permute-start(bf16[2,256,3072]{2,1,0:T(8,128)(2,1)} %get-tuple-element.83), channel_id=1, source_target_pairs={{0,16},{16,0},{8,24},{24,8},{1,17},{17,1},{9,25},{25,9},{2,18},{18... | collective-permute-start | bytes 9437192 | tf_op jit(solution)/shard_map/ppermute | solution.py:1685
  667.9 80.6 %collective-permute-start.12 = (bf16[2,256,3072]{2,1,0:T(8,128)(2,1)}, bf16[2,256,3072]{2,1,0:T(8,128)(2,1)S(1)}, u32[]{:S(2)}, u32[]{:S(2)}) collective-permute-start(bf16[2,256,3072]{2,1,0:T(8,128)(2,1)} %get-tuple-element.81), channel_id=1, source_target_pairs={{0,4},{4,0},{1,5},{5,1},{2,6},{6,2},{3,7},{7,3},{8,12},{12,8},{9,1... | collective-permute-start | bytes 9437192 | tf_op jit(solution)/shard_map/ppermute | solution.py:1684
  680.2 63.3 %copy-start.17 = (bf16[2,256,3072]{2,1,0:T(8,128)(2,1)S(1)}, bf16[2,256,3072]{2,1,0:T(8,128)(2,1)}, u32[]{:S(2)}) copy-start(bf16[2,256,3072]{2,1,0:T(8,128)(2,1)} %get-tuple-element.82) | copy-start | bytes 9437188
  762.2 8.3 copy-start.1
  762.2 14.5 %collective-permute-start.17 = (bf16[512,2048]{1,0:T(8,128)(2,1)}, bf16[512,2048]{1,0:T(8,128)(2,1)}, u32[]{:S(2)}, u32[]{:S(2)}) collective-permute-start(bf16[512,2048]{1,0:T(8,128)(2,1)} %constant_dynamic-slice_fusion), channel_id=1, source_target_pairs={{0,8},{8,0},{16,24},{24,16},{1,9},{9,1},{17,25},{25,17},{2,10},{10... | collective-permute-start | bytes 6291464 | tf_op jit(solution)/shard_map/ppermute | solution.py:1593
  765.3 36.9 %collective-permute-start.16 = (bf16[256,3072]{1,0:T(8,128)(2,1)}, bf16[256,3072]{1,0:T(8,128)(2,1)}, u32[]{:S(2)}, u32[]{:S(2)}) collective-permute-start(bf16[256,3072]{1,0:T(8,128)(2,1)} %dynamic-slice_bitcast_fusion), channel_id=1, source_target_pairs={{0,4},{4,0},{1,5},{5,1},{2,6},{6,2},{3,7},{7,3},{8,12},{12,8},{9,1... | collective-permute-start | bytes 4718600 | tf_op jit(solution)/shard_map/ppermute | solution.py:1708
  768.9 36.8 %collective-permute-start.15 = (bf16[256,3072]{1,0:T(8,128)(2,1)}, bf16[256,3072]{1,0:T(8,128)(2,1)}, u32[]{:S(2)}, u32[]{:S(2)}) collective-permute-start(bf16[256,3072]{1,0:T(8,128)(2,1)} %dynamic-slice_bitcast_fusion.1), channel_id=1, source_target_pairs={{0,16},{16,0},{8,24},{24,8},{1,17},{17,1},{9,25},{25,9},{2,18},{18... | collective-permute-start | bytes 4718600 | tf_op jit(solution)/shard_map/ppermute | solution.py:1707
  789.6 16.1 %copy-start.8 = (bf16[2,256,3072]{2,1,0:T(8,128)(2,1)S(1)}, bf16[2,256,3072]{2,1,0:T(8,128)(2,1)}, u32[]{:S(2)}) copy-start(bf16[2,256,3072]{2,1,0:T(8,128)(2,1)} %add_convert_fusion.1) | copy-start | bytes 9437188
  798.7 9.0 copy-start.7
  (31 other events, 138.6 us)
Sparse Core Ops, SparseCore 0:
  9.6 60.9 all-gather.2
  213.6 155.6 all-gather.4
  666.3 142.8 reduce-scatter.1

commit v13 on v12

--- a/solution.py
+++ b/solution.py
@@ -929,8 +929,10 @@
             dg_buf[:, lanes] = (back * upward * slope).astype(jnp.bfloat16)
             du_buf[:, lanes] = (back * silu).astype(jnp.bfloat16)
 
-        for copy in outputs(chunk):
-            copy.start()
+        @pl.when(at < last)
+        def _():
+            for copy in outputs(chunk):
+                copy.start()
 
         @pl.when(at > 0)
         def _():
@@ -979,24 +981,25 @@
         return unused
 
     lax.fori_loop(0, cols, one_chunk, 0)
-    for copy in outputs(order(last)):
-        copy.wait()
-    mlp_out(order(last)).wait()
 
     loads = []
-    for chunk in range(cols):
-        here = slice(chunk * rows, (chunk + 1) * rows)
-        loads += [
-            pltpu.make_async_copy(
-                dgu_all.at[chunk, :, 0:units], wg.at[here], w_sems.at[chunk]
-            ),
-            pltpu.make_async_copy(
-                dgu_all.at[chunk, :, units : 2 * units], wu.at[here], w_sems.at[cols + chunk]
-            ),
-            pltpu.make_async_copy(u_all.at[chunk], wd.at[here], w_sems.at[2 * cols + chunk]),
-        ]
+    for at in range(cols):
+        chunk = order(at)
+        here = aligned(chunk, rows)
+        sources = (dg_buf, du_buf, u_buf)
+        if at < last:
+            sources = (
+                dgu_all.at[chunk, :, 0:units],
+                dgu_all.at[chunk, :, units : 2 * units],
+                u_all.at[chunk],
+            )
+        for part, (source, full) in enumerate(zip(sources, (wg, wu, wd))):
+            loads.append(
+                pltpu.make_async_copy(source, full.at[here], w_sems.at[part * cols + at])
+            )
     for load in loads:
         load.start()
+    mlp_out(order(last)).wait()
 
     def relay(box, slot):
         hand_over(slot, facing, box, 3).wait_recv()

time: 1000 us -> 1000 us (level)
  no operation moved by 1% of the time
where the time goes in v13:
time: 1000 us; the launch traced here: 982 us
  Pallas kernels  719 us (72%)
  waiting for transfers between devices  76.5 us (8%)
  local copies, waits for them, and re-layouts  64.4 us (6%)
  other arithmetic  57.3 us (6%)
  matrix products  31.7 us (3%)
  between operations  22.7 us (2%)
  starting transfers between devices  10.4 us (1%)
    pallas_call x1, Pallas kernels, feed_forward(): pl.pallas_call(functools.partial(ffn_kernel, cols), out_shape=(jax.ShapeD...  284 us
    pallas_call x1, Pallas kernels, finish(): pl.pallas_call(functools.partial(finish_kernel, cols), out_shape=(jax.Sha...  148 us
    pallas_call x1, Pallas kernels, gather_weights(): pl.pallas_call(functools.partial(gather_kernel, cols), out_shape=(whole(o...  133 us
    pallas_call x1, Pallas kernels, attend_back_fast(): pl.pallas_call(functools.partial(attend_back_kernel, block), grid=(groups...  63.3 us
    pallas_call x1, Pallas kernels, start_exchange(): pl.pallas_call(functools.partial(start_kernel, cols), out_shape=(jax.Shap...  47.1 us
    pallas_call x1, Pallas kernels, attend_fast(): pl.pallas_call(functools.partial(attend_kernel, block), grid=(groups,), o...  44.1 us
    ppermute x1, waiting for transfers between devices, one_sequence_body(): shared_down = lax.ppermute(far_down, 'dp', OVER_Y)  37.7 us
  transfers between devices with their start and end apart: 21, of which 12 were waited for; matrix products, arithmetic and copies ran while one was open for 12% of the time, Pallas kernels for 29%

profile of v13, /device:TPU:0, one launch (start us, length us, event | category | flops | bytes accessed | tf_op | source)
XLA Modules:
  0.0 982.2 jit_solution(12927313140427582714)
XLA Ops:
  19.2 47.1 %start_exchange.1 = (bf16[512,2048]{1,0:T(8,128)(2,1)}, bf16[1024,2048]{1,0:T(8,128)(2,1)}) custom-call(bf16[4,512,512]{2,1,0:T(8,128)(2,1)} %tok_ref.1, f32[1,2048]{1,0:T(1,128)} %bitcast.91), custom_call_target="tpu_custom_call" | custom-call | bytes 209715200 | tf_op jit(solution)/shard_map/start_exchange/pallas_call | solution.py:342
  66.3 4.3 all-gather.3.cloned.1.call-done
  79.9 133.5 %gather_weights.1 = (bf16[2048,1536]{1,0:T(8,128)(2,1)}, bf16[2048,1024]{1,0:T(8,128)(2,1)}) custom-call(bf16[1024,384]{1,0:T(8,128)(2,1)} %pad_maximum_fusion.2.q_ref, bf16[1024,256]{1,0:T(8,128)(2,1)} %get-tuple-element.186.o_ref, bf16[4,512,512]{2,1,0:T(8,128)(2,1)} %copy-done.9), custom_call_target="tpu_custom_call" | custom-call | bytes 314572800 | tf_op jit(solution)/shard_map/gather_weights/pallas_call | solution.py:462
  215.8 10.6 %copy.53 = bf16[1024,2,2048]{2,0,1:T(8,128)(2,1)} copy(bf16[1024,2,2048]{2,1,0:T(2,128)(2,1)} %param.20) | data formatting | bytes 16777216 | tf_op jit(solution)/shard_map/optimization_barrier | solution.py:1628
  226.4 3.4 constant_dynamic-slice_fusion.2
  229.9 44.1 %attend.1 = (bf16[1024,1536]{1,0:T(8,128)(2,1)}, bf16[1024,1024]{1,0:T(8,128)(2,1)S(1)}) custom-call(s32[1]{0:T(128)} %dynamic_slice.83.len_ref, bf16[1024,2048]{1,0:T(8,128)(2,1)} %get-tuple-element.90.a_ref, bf16[2048,1536]{1,0:T(8,128)(2,1)} %get-tuple-element.64.w_ref, f32[1024,256]{1,0:T(8,128)S(1)} %concatenate.38.cos_ref, ...), custom_call_target="tpu_custom_call" | custom-call | flops 10737418240 | bytes 13631488 | tf_op jit(solution)/shard_map/attend/pallas_call | solution.py:573
  274.0 4.8 convolution_convert_fusion.3
  284.6 7.1 slice_bitcast_fusion
  291.7 16.8 %collective-permute-done.3.wd_far = bf16[256,2048]{1,0:T(8,128)(2,1)} collective-permute-done((bf16[256,2048]{1,0:T(8,128)(2,1)S(1)}, bf16[256,2048]{1,0:T(8,128)(2,1)}, u32[]{:S(2)}, u32[]{:S(2)}) %collective-permute-start.3) | collective-permute-done | bytes 1048608 | tf_op jit(solution)/shard_map/ppermute | solution.py:1634
  309.1 5.2 fusion.10
  317.2 37.7 %collective-permute-done.5.wd_far_y = bf16[256,2048]{1,0:T(8,128)(2,1)} collective-permute-done((bf16[256,2048]{1,0:T(8,128)(2,1)}, bf16[256,2048]{1,0:T(8,128)(2,1)}, u32[]{:S(2)}, u32[]{:S(2)}) %collective-permute-start.5) | collective-permute-done | bytes 1048608 | tf_op jit(solution)/shard_map/ppermute | solution.py:1664
  356.1 3.5 slice_bitcast_fusion.6
  369.4 283.6 %feed_forward.1 = (bf16[4,512,2048]{2,1,0:T(8,128)(2,1)}, bf16[4,512,4096]{2,1,0:T(8,128)(2,1)}, bf16[4,512,2048]{2,1,0:T(8,128)(2,1)}, bf16[3,512,2048]{2,1,0:T...) custom-call(bf16[512,2048]{1,0:T(8,128)(2,1)} %multiply_convert_fusi, ...), custom_call_target="tpu_custom_call" | custom-call | flops 154618822656 | bytes 838860800 | tf_op jit(solution)/shard_map/feed_forward/pallas_call | solution.py:1209
  653.0 4.8 convert_reduce_fusion
  658.9 4.8 multiply_convert_fusion
  668.3 4.8 maximum_select_fusion
  673.1 4.7 convolution_convert_fusion.4.dz_ref
  677.9 63.3 %attend_back.1 = bf16[1024,1536]{1,0:T(8,128)(2,1)} custom-call(s32[1]{0:T(128)} %dynamic_slice.83.len_ref, bf16[1024,1536]{1,0:T(8,128)(2,1)} %get-tuple-element.84.qkv_ref, bf16[1024,1024]{1,0:T(8,128)(2,1)S(1)} %convolution_convert_fusion.4.dz_ref, f32[1024,256]{1,0:T(8,128)S(1)} %concatenate.38.cos_ref, f32[1024,256]{1,0:T(8,128)S(1)} %concatenate.40.sin_ref), custom_call_target="tpu_custom_call" | custom-call | flops 10737418240 | bytes 8388608 | tf_op jit(solution)/shard_map/attend_back/pallas_call | solution.py:680
  741.2 4.9 add_convert_fusion
  746.1 2.8 add_convert_fusion.1
  749.5 6.9 convolution_convert_fusion.1
  760.1 2.8 dynamic-slice_bitcast_fusion
  763.8 2.7 dynamic-slice_bitcast_fusion.1
  768.1 6.2 convolution_convert_fusion.2
  774.3 2.5 convert_add_fusion.2
  780.7 5.3 fusion.4.ig_ref
  787.2 9.1 convolution_convert_fusion
  796.3 3.6 collective-permute-done.16
  799.9 3.4 collective-permute-done.15
  809.8 5.3 copy.57
  815.0 147.7 %finish.1 = (bf16[4,512,512]{2,1,0:T(8,128)(2,1)}, bf16[4,512,512]{2,1,0:T(8,128)(2,1)}, f32[2,256,384]{2,1,0:T(8,128)}, f32[2,256,256]{2,1,0:T(8,128)}, f32[8,512]{1,0:T(8,128)}) custom-call(bf16[512,2048]{1,0:T(8,128)(2,1)} %fusion.4.ig_ref, bf16[2,2,2,256,1536]{4,3,2,1,0:T(8,128)(2,1)} %bitcast.85, bf16[2,2,2,256,1024]{4,3,2,1,0:T(8,128)(2,1)} %bitcast.86, ...), custom_call_target="tpu_custom_call" | custom-call | bytes 314572800 | tf_op jit(solution)/shard_map/finish/pallas_call | solution.py:1524
  967.4 2.6 convert_element_type.141
  (185 shorter events, 69.5 us)
Async XLA Ops:
  7.2 63.4 %all-gather.3.cloned.1.call-start = ((), (), s32[]{:S(2)}) async-start(), calls=%async_computation.1 | async-start | bytes 10485760 | tf_op jit(solution)/shard_map/all_gather | solution.py:1618
  7.9 361.4 %all-gather.5.cloned.1.call-start = ((), (), s32[]{:S(2)}) async-start(), calls=%async_computation.2 | async-start | bytes 10485760 | tf_op jit(solution)/shard_map/all_gather | solution.py:1625
  72.8 140.6 %collective-permute-start = (bf16[4,512,512]{2,1,0:T(8,128)(2,1)S(1)}, bf16[4,512,512]{2,1,0:T(8,128)(2,1)}, u32[]{:S(2)}, u32[]{:S(2)}) collective-permute-start(bf16[4,512,512]{2,1,0:T(8,128)(2,1)S(1)} %maximum_select_fusion.1.after_ref), channel_id=1, source_target_pairs={{0,0},{4,8},{8,4},{12,12},{16,16},{20,24},{24,20},{28,28},{1,1},{5... | collective-permute-start | bytes 6291464 | tf_op jit(solution)/shard_map/ppermute | solution.py:1622
  78.9 134.7 %copy-start.37 = (s32[16]{0:T(128)S(1)}, s32[16]{0:T(128)}, u32[]{:S(2)}) copy-start(s32[16]{0:T(128)} %param.13) | copy-start | bytes 196
  213.5 601.6 %reduce-scatter.2.cloned.1.call-start = ((), (), s32[]{:S(2)}) async-start(), calls=%async_computation.3 | async-start | bytes 10485760 | tf_op jit(solution)/shard_map/reduce_scatter | solution.py:1682
  229.9 44.2 %copy-start.34 = (bf16[2048,1024]{1,0:T(8,128)(2,1)S(1)}, bf16[2048,1024]{1,0:T(8,128)(2,1)}, u32[]{:S(2)}) copy-start(bf16[2048,1024]{1,0:T(8,128)(2,1)} %get-tuple-element.68) | copy-start | bytes 12582916
  229.9 54.4 %collective-permute-start.2 = (bf16[256,2,2048]{2,0,1:T(8,128)(2,1)}, bf16[256,2,2048]{2,0,1:T(8,128)(2,1)}, u32[]{:S(2)}, u32[]{:S(2)}) collective-permute-start(bf16[256,2,2048]{2,0,1:T(8,128)(2,1)} %constant_dynamic-slice_fusion.2), channel_id=1, source_target_pairs={{0,4},{4,0},{1,5},{5,1},{2,6},{6,2},{3,7},{7,3},{8,12},{12,8},{9,1... | collective-permute-start | bytes 6291464 | tf_op jit(solution)/shard_map/ppermute | solution.py:1633
  281.5 27.6 %collective-permute-start.1 = (bf16[512,2048]{1,0:T(8,128)(2,1)}, bf16[512,2048]{1,0:T(8,128)(2,1)}, u32[]{:S(2)}, u32[]{:S(2)}) collective-permute-start(bf16[512,2048]{1,0:T(8,128)(2,1)} %constant_dynamic-slice_fusion.3), channel_id=1, source_target_pairs={{0,8},{8,0},{16,24},{24,16},{1,9},{9,1},{17,25},{25,17},{2,10},{10... | collective-permute-start | bytes 6291464 | tf_op jit(solution)/shard_map/ppermute | solution.py:1596
  282.8 25.7 %collective-permute-start.3 = (bf16[256,2048]{1,0:T(8,128)(2,1)S(1)}, bf16[256,2048]{1,0:T(8,128)(2,1)}, u32[]{:S(2)}, u32[]{:S(2)}) collective-permute-start(bf16[256,2048]{1,0:T(8,128)(2,1)S(1)} %constant_dynamic-slice_fusion.1), channel_id=1, source_target_pairs={{0,4},{4,0},{1,5},{5,1},{2,6},{6,2},{3,7},{7,3},{8,12},{12,8},{9,1... | collective-permute-start | bytes 3145736 | tf_op jit(solution)/shard_map/ppermute | solution.py:1634
  284.3 31.2 %copy-start.23 = (f32[2048]{0:T(1024)}, f32[2048]{0:T(1024)S(1)}, u32[]{:S(2)}) copy-start(f32[2048]{0:T(1024)S(1)} %convert_element_type.114) | copy-start | bytes 24580
  284.3 24.8 %copy-start.5 = (bf16[512,2048]{1,0:T(8,128)(2,1)S(1)}, bf16[512,2048]{1,0:T(8,128)(2,1)}, u32[]{:S(2)}) copy-start(bf16[512,2048]{1,0:T(8,128)(2,1)} %get-tuple-element.58) | copy-start | bytes 6291460
  284.3 24.8 %copy-start.15 = (bf16[1024,2048]{1,0:T(8,128)(2,1)S(1)}, bf16[1024,2048]{1,0:T(8,128)(2,1)}, u32[]{:S(2)}) copy-start(bf16[1024,2048]{1,0:T(8,128)(2,1)} %copy-done.14) | copy-start | bytes 12582916
  284.3 70.6 %collective-permute-start.4 = (bf16[256,2,2048]{2,0,1:T(8,128)(2,1)}, bf16[256,2,2048]{2,0,1:T(8,128)(2,1)S(1)}, u32[]{:S(2)}, u32[]{:S(2)}) collective-permute-start(bf16[256,2,2048]{2,0,1:T(8,128)(2,1)} %collective-permute-done.2), channel_id=1, source_target_pairs={{0,16},{16,0},{8,24},{24,8},{1,17},{17,1},{9,25},{25,9},{2,18},{18... | collective-permute-start | bytes 6291464 | tf_op jit(solution)/shard_map/ppermute | solution.py:1663
  308.5 46.4 %collective-permute-start.5 = (bf16[256,2048]{1,0:T(8,128)(2,1)}, bf16[256,2048]{1,0:T(8,128)(2,1)}, u32[]{:S(2)}, u32[]{:S(2)}) collective-permute-start(bf16[256,2048]{1,0:T(8,128)(2,1)} %collective-permute-done.3.wd_far), channel_id=1, source_target_pairs={{0,16},{16,0},{8,24},{24,8},{1,17},{17,1},{9,25},{25,9},{2,18},{18... | collective-permute-start | bytes 3145736 | tf_op jit(solution)/shard_map/ppermute | solution.py:1664
  315.5 39.5 %copy-start.25 = (f32[512]{0:T(512)}, f32[512]{0:T(512)S(1)}, u32[]{:S(2)}) copy-start(f32[512]{0:T(512)S(1)} %get-tuple-element.179) | copy-start | bytes 6148
  356.1 13.2 %copy-start.21 = (bf16[256,2048]{1,0:T(8,128)(2,1)}, bf16[256,2048]{1,0:T(8,128)(2,1)S(1)}, u32[]{:S(2)}) copy-start(bf16[256,2048]{1,0:T(8,128)(2,1)S(1)} %get-tuple-element.158.wu_far_y) | copy-start | bytes 3145732
  356.1 4.5 collective-permute-start.10
  359.6 3.0 collective-permute-start.6
  359.7 4.4 collective-permute-start.7
  360.1 5.5 collective-permute-start.9
  360.3 6.9 collective-permute-start.11
  361.6 7.0 collective-permute-start.8
  663.8 4.5 collective-permute-start.14
  663.8 77.3 %collective-permute-start.13 = (bf16[2,256,3072]{2,1,0:T(8,128)(2,1)}, bf16[2,256,3072]{2,1,0:T(8,128)(2,1)}, u32[]{:S(2)}, u32[]{:S(2)}) collective-permute-start(bf16[2,256,3072]{2,1,0:T(8,128)(2,1)} %get-tuple-element.83), channel_id=1, source_target_pairs={{0,16},{16,0},{8,24},{24,8},{1,17},{17,1},{9,25},{25,9},{2,18},{18... | collective-permute-start | bytes 9437192 | tf_op jit(solution)/shard_map/ppermute | solution.py:1688
  665.5 80.6 %collective-permute-start.12 = (bf16[2,256,3072]{2,1,0:T(8,128)(2,1)}, bf16[2,256,3072]{2,1,0:T(8,128)(2,1)S(1)}, u32[]{:S(2)}, u32[]{:S(2)}) collective-permute-start(bf16[2,256,3072]{2,1,0:T(8,128)(2,1)} %get-tuple-element.81), channel_id=1, source_target_pairs={{0,4},{4,0},{1,5},{5,1},{2,6},{6,2},{3,7},{7,3},{8,12},{12,8},{9,1... | collective-permute-start | bytes 9437192 | tf_op jit(solution)/shard_map/ppermute | solution.py:1687
  677.9 63.3 %copy-start.17 = (bf16[2,256,3072]{2,1,0:T(8,128)(2,1)S(1)}, bf16[2,256,3072]{2,1,0:T(8,128)(2,1)}, u32[]{:S(2)}) copy-start(bf16[2,256,3072]{2,1,0:T(8,128)(2,1)} %get-tuple-element.82) | copy-start | bytes 9437188
  759.9 8.2 copy-start.1
  759.9 14.4 %collective-permute-start.17 = (bf16[512,2048]{1,0:T(8,128)(2,1)}, bf16[512,2048]{1,0:T(8,128)(2,1)}, u32[]{:S(2)}, u32[]{:S(2)}) collective-permute-start(bf16[512,2048]{1,0:T(8,128)(2,1)} %constant_dynamic-slice_fusion), channel_id=1, source_target_pairs={{0,8},{8,0},{16,24},{24,16},{1,9},{9,1},{17,25},{25,17},{2,10},{10... | collective-permute-start | bytes 6291464 | tf_op jit(solution)/shard_map/ppermute | solution.py:1596
  763.0 36.9 %collective-permute-start.16 = (bf16[256,3072]{1,0:T(8,128)(2,1)}, bf16[256,3072]{1,0:T(8,128)(2,1)}, u32[]{:S(2)}, u32[]{:S(2)}) collective-permute-start(bf16[256,3072]{1,0:T(8,128)(2,1)} %dynamic-slice_bitcast_fusion), channel_id=1, source_target_pairs={{0,4},{4,0},{1,5},{5,1},{2,6},{6,2},{3,7},{7,3},{8,12},{12,8},{9,1... | collective-permute-start | bytes 4718600 | tf_op jit(solution)/shard_map/ppermute | solution.py:1711
  766.5 36.8 %collective-permute-start.15 = (bf16[256,3072]{1,0:T(8,128)(2,1)}, bf16[256,3072]{1,0:T(8,128)(2,1)}, u32[]{:S(2)}, u32[]{:S(2)}) collective-permute-start(bf16[256,3072]{1,0:T(8,128)(2,1)} %dynamic-slice_bitcast_fusion.1), channel_id=1, source_target_pairs={{0,16},{16,0},{8,24},{24,8},{1,17},{17,1},{9,25},{25,9},{2,18},{18... | collective-permute-start | bytes 4718600 | tf_op jit(solution)/shard_map/ppermute | solution.py:1710
  787.2 16.1 %copy-start.8 = (bf16[2,256,3072]{2,1,0:T(8,128)(2,1)S(1)}, bf16[2,256,3072]{2,1,0:T(8,128)(2,1)}, u32[]{:S(2)}) copy-start(bf16[2,256,3072]{2,1,0:T(8,128)(2,1)} %add_convert_fusion.1) | copy-start | bytes 9437188
  796.3 9.1 copy-start.7
  (31 other events, 138.5 us)
Sparse Core Ops, SparseCore 0:
  9.6 60.9 all-gather.2
  213.6 155.6 all-gather.4
  663.9 142.8 reduce-scatter.1
